TPU v7x, 512 devices: a whole 4x4x16 slice. The times are simulated.
512 devices in a mesh: seq: 32 (over x, z_hi, y), head: 16 (over z_lo, core).
Axes of the slice: x: 4, y: 4, z: 16 (z_hi: 2, z_lo: 8; z = z_hi * 8 + z_lo), core: 2. Of those that a mesh axis runs over, the one named last changes fastest.
Arguments:
- queries: bfloat16 [4096, 8192], P('seq', 'head'), may hold values from -40 to 40
- long_keys: bfloat16 [4096, 128], P(('seq', 'head')), may hold values from -6 to 6
- long_values: bfloat16 [4096, 128], P(('seq', 'head')), may hold values from -6 to 6
- short_keys: bfloat16 [4096, 128], P(('seq', 'head')), may hold values from -6 to 6
- short_values: bfloat16 [4096, 128], P(('seq', 'head')), may hold values from -6 to 6
- w_out: bfloat16 [8192, 8192], P('head', 'seq'), may hold values from -0.375 to 0.375
Outputs:
- projected: bfloat16 [4096, 8192], P('seq', 'head')
All inputs are finite; a program needn't handle non-finite values.
Results may differ from a plain program's by a relative error of at most 0.024.
Values may be sent and summed in bfloat16 or wider, within the bound.
No kernel may reach another device: no remote copies, remote signals or barrier semaphores. Data moves between devices by JAX's collectives and lax.ppermute only.
A program may use at most 64 MiB of HBM per device.

v0:
```python
import math

import jax
import jax.numpy as jnp
from jax import lax
from jax.sharding import PartitionSpec as P

W1 = 512
W2 = 32
QB = 32


def passed_along(value, axis, steps):
    count = lax.axis_size(axis)
    first, last = (max(0, -steps), min(count, count - steps))
    return lax.ppermute(value, axis, [(source, source + steps) for source in range(first, last)])


def attend(chosen, first_keys, first_values, second_keys, second_values, first):
    rows = chosen.shape[0]
    span = second_keys.shape[0] - rows + 1
    reach = first_keys.shape[0] - rows
    width = chosen.shape[1]
    key_window = jnp.stack(
        [second_keys[span - 1 - offset : span - 1 - offset + rows] for offset in range(span)],
        axis=1,
    )
    value_window = jnp.stack(
        [second_values[span - 1 - offset : span - 1 - offset + rows] for offset in range(span)],
        axis=1,
    )
    mixed = (chosen.astype(jnp.float32)[:, None, :] * key_window.astype(jnp.float32)).astype(
        jnp.bfloat16
    )
    scores = jnp.dot(
        mixed.reshape(rows * span, width), first_keys.T, preferred_element_type=jnp.float32
    ) * (2.5 / math.sqrt(width))
    scores = scores.reshape(rows, span, reach + rows)
    row_ids = jnp.arange(rows, dtype=jnp.int32)[:, None, None]
    offsets = jnp.arange(span, dtype=jnp.int32)[None, :, None]
    columns = jnp.arange(reach + rows, dtype=jnp.int32)[None, None, :]
    valid = (
        (columns >= row_ids + 1)
        & (columns <= reach + row_ids)
        & (first - reach + columns >= 0)
        & (first + row_ids - offsets >= 0)
    )
    scores = jnp.where(valid, scores, -jnp.inf)
    top = jnp.max(scores, axis=(1, 2), keepdims=True)
    weights = jnp.exp(scores - top)
    total = jnp.sum(weights, axis=(1, 2))
    probs = weights.astype(jnp.bfloat16)
    carried = jnp.dot(
        probs.reshape(rows * span, reach + rows), first_values, preferred_element_type=jnp.float32
    ).reshape(rows, span, width)
    attended = jnp.sum(carried * value_window.astype(jnp.float32), axis=1) / total[:, None]
    return attended.astype(jnp.bfloat16)


def earlier_blocks(paired, count):
    blocks = []
    moving = paired
    for distance in range(count):
        moving = passed_along(moving, "seq", 1)
        blocks.append(moving)
    return jnp.stack(blocks[::-1], axis=0)


def per_device(queries, long_keys, long_values, short_keys, short_values, w_out):
    width = long_keys.shape[1]
    tok_rows = queries.shape[0]
    heads_here = queries.shape[1] // width
    blocks_back = W1 // tok_rows
    rim_rows = W2 - 1
    first_piece = jnp.stack([long_keys, long_values], axis=0)
    second_piece = jnp.stack([short_keys, short_values], axis=0)
    first_own, second_own = (
        lax.all_gather(first_piece, "head", axis=1, tiled=True),
        lax.all_gather(second_piece, "head", axis=1, tiled=True),
    )
    earlier = earlier_blocks(first_own, blocks_back)
    rim = passed_along(second_own[:, tok_rows - rim_rows :], "seq", 1)
    window_keys = jnp.concatenate(
        [earlier[:, 0].reshape(blocks_back * tok_rows, width), first_own[0]], axis=0
    )
    window_values = jnp.concatenate(
        [earlier[:, 1].reshape(blocks_back * tok_rows, width), first_own[1]], axis=0
    )
    near_keys = jnp.concatenate([rim[0], second_own[0]], axis=0)
    near_values = jnp.concatenate([rim[1], second_own[1]], axis=0)
    seq_start = lax.axis_index("seq") * tok_rows
    per_block = tok_rows // QB

    def one_item(number):
        which_head = number // per_block
        start = number % per_block * QB
        chosen = lax.dynamic_slice(queries, (start, which_head * width), (QB, width))
        keys_one = lax.dynamic_slice_in_dim(window_keys, start, W1 + QB, 0)
        values_one = lax.dynamic_slice_in_dim(window_values, start, W1 + QB, 0)
        keys_two = lax.dynamic_slice_in_dim(near_keys, start, QB + rim_rows, 0)
        values_two = lax.dynamic_slice_in_dim(near_values, start, QB + rim_rows, 0)
        return attend(chosen, keys_one, values_one, keys_two, values_two, seq_start + start)

    results = lax.map(one_item, jnp.arange(heads_here * per_block, dtype=jnp.int32))
    attended = (
        results.reshape(heads_here, tok_rows, width)
        .transpose(1, 0, 2)
        .reshape(tok_rows, heads_here * width)
    )
    partial_sums = jnp.dot(
        attended,
        lax.all_gather(w_out, "seq", axis=1, tiled=True),
        preferred_element_type=jnp.float32,
    )
    summed = lax.psum_scatter(
        partial_sums.astype(jnp.bfloat16), "head", scatter_dimension=1, tiled=True
    )
    return summed


def solution(mesh):
    return jax.shard_map(
        per_device,
        mesh=mesh,
        in_specs=(
            P("seq", "head"),
            P(("seq", "head"), None),
            P(("seq", "head"), None),
            P(("seq", "head"), None),
            P(("seq", "head"), None),
            P("head", "seq"),
        ),
        out_specs=P("seq", "head"),
        check_vma=False,
    )
```

profile of v0, /device:TPU:1, one launch (start us, length us, event | category | flops | bytes accessed | tf_op | source)
XLA Modules:
  0.0 493.7 jit_solution(419667374991351333)
XLA Ops:
  7.2 37.7 %all_gather.10 = bf16[2,128,128]{2,1,0:T(8,128)(2,1)S(1)} all-gather(bf16[2,8,128]{2,1,0:T(8,128)(2,1)S(1)} %pad_maximum_fusion.6), channel_id=1, replica_groups=mesh['seq'=32,'head'=16] {'head'}, dimensions={1}, use_global_device_ids=true | all-gather | bytes 69632 | tf_op jit(solution)/shard_map/all_gather | solution.py:78
  45.0 3.2 collective-permute-start.1
  48.9 25.5 %all_gather.9 = bf16[2,128,128]{2,1,0:T(8,128)(2,1)S(1)} all-gather(bf16[2,8,128]{2,1,0:T(8,128)(2,1)S(1)} %pad_maximum_fusion.5), channel_id=1, replica_groups=mesh['seq'=32,'head'=16] {'head'}, dimensions={1}, use_global_device_ids=true | all-gather | bytes 69632 | tf_op jit(solution)/shard_map/all_gather | solution.py:79
  74.4 3.2 collective-permute-start
  77.7 2.9 collective-permute-start.2
  81.9 7.6 %collective-permute-start.3 = (bf16[2,128,128]{2,1,0:T(8,128)(2,1)S(1)}, bf16[2,128,128]{2,1,0:T(8,128)(2,1)S(1)}, u32[]{:S(2)}, u32[]{:S(2)}) collective-permute-start(bf16[2,128,128]{2,1,0:T(8,128)(2,1)S(1)} %collective-permute-done.2), channel_id=1, source_target_pairs={{0,16},{16,32},{32,48},{48,64},{64,80},{80,96},{96,112},{112,128},... | collective-permute-start | bytes 196616 | tf_op jit(solution)/shard_map/ppermute | solution.py:16
  90.8 3.7 collective-permute-start.4
  96.7 213.6 %while.12 = (s32[]{:T(128)}, bf16[16,32,128]{2,1,0:T(8,128)(2,1)}, s32[16]{0:T(128)S(1)}, s32[]{:T(128)}, bf16[128,512]{1,0:T(8,128)(2,1)}, /*index=5*/bf16[159,...) while((s32[]{:T(128)}, bf16[16,32,128]{2,1,0:T(8,128)(2,1)}, ...), condition=%wide.region_6.7_spmd, body=%wide.region_0.6_spmd.sunk | while | flops 289979552 | bytes 15264006 | solution.py:104
  102.9 1.5 fusion.94
  116.2 1.5 fusion.94
  121.1 1.4 fusion.98
  129.6 1.5 fusion.94
  142.9 1.5 fusion.94
  147.8 1.4 fusion.98
  156.3 1.5 fusion.94
  161.1 1.4 fusion.98
  169.6 1.5 fusion.94
  183.0 1.5 fusion.94
  187.8 1.4 fusion.98
  196.3 1.5 fusion.94
  209.7 1.5 fusion.94
  214.5 1.4 fusion.98
  223.0 1.5 fusion.94
  236.4 1.5 fusion.94
  249.7 1.5 fusion.94
  263.1 1.5 fusion.94
  276.4 1.5 fusion.94
  289.8 1.5 fusion.94
  303.1 1.5 fusion.94
  311.3 58.8 %all-gather.2.cloned.1.call-done = bf16[512,8192]{1,0:T(8,128)(2,1)} async-done(((bf16[512,256]{1,0:T(8,128)(2,1)}), bf16[512,8192]{1,0:T(8,128)(2,1)}) %all-gather.2.cloned.1.call-update) | async-done | bytes 8388624 | tf_op jit(solution)/shard_map/all_gather | solution.py:112
  370.1 6.0 %convolution_convert_fusion = bf16[128,8192]{1,0:T(8,128)(2,1)} fusion(bf16[128,512]{0,1:T(8,128)(2,1)S(1)} %bitcast.324, bf16[512,8192]{1,0:T(8,128)(2,1)} %all-gather.2.cloned.1.call-done), kind=kOutput, calls=%fused_computation.185 | convolution fusion | flops 1074790400 | bytes 10616832 | tf_op jit(solution)/shard_map/dot_general | solution.py:110
  376.2 110.6 %reduce-scatter.2.cloned.1.call-done = bf16[128,512]{1,0:T(8,128)(2,1)} async-done(((bf16[128,8192]{1,0:T(8,128)(2,1)}), bf16[128,512]{1,0:T(8,128)(2,1)}) %reduce-scatter.2.cloned.1.call-update) | async-done | bytes 131088 | tf_op jit(solution)/shard_map/reduce_scatter | solution.py:115
  (1441 shorter events, 141.8 us)
Async XLA Ops:
  6.5 363.6 %all-gather.2.cloned.1.call-start = ((), (), s32[]{:S(2)}) async-start(), calls=%async_computation.1 | async-start | bytes 8650752 | tf_op jit(solution)/shard_map/all_gather | solution.py:112
  45.0 32.7 %collective-permute-start.1 = (bf16[2,128,128]{2,1,0:T(8,128)(2,1)S(1)}, bf16[2,128,128]{2,1,0:T(8,128)(2,1)S(1)}, u32[]{:S(2)}, u32[]{:S(2)}) collective-permute-start(bf16[2,128,128]{2,1,0:T(8,128)(2,1)S(1)} %all_gather.10), channel_id=1, source_target_pairs={{0,16},{16,32},{32,48},{48,64},{64,80},{80,96},{96,112},{112,128},... | collective-permute-start | bytes 196616 | tf_op jit(solution)/shard_map/ppermute | solution.py:16
  74.4 15.1 %collective-permute-start = (bf16[2,31,128]{2,1,0:T(8,128)(2,1)S(1)}, bf16[2,31,128]{2,1,0:T(8,128)(2,1)S(1)}, u32[]{:S(2)}, u32[]{:S(2)}) collective-permute-start(bf16[2,31,128]{2,1,0:T(8,128)(2,1)S(1)} %slice.420), channel_id=1, source_target_pairs={{0,16},{16,32},{32,48},{48,64},{64,80},{80,96},{96,112},{112,128},... | collective-permute-start | bytes 47624 | tf_op jit(solution)/shard_map/ppermute | solution.py:16
  77.6 409.2 %reduce-scatter.2.cloned.1.call-start = ((), (), s32[]{:S(2)}) async-start(), calls=%async_computation.2 | async-start | bytes 2228224 | tf_op jit(solution)/shard_map/reduce_scatter | solution.py:115
  77.7 4.2 collective-permute-start.2
  81.9 8.9 %collective-permute-start.3 = (bf16[2,128,128]{2,1,0:T(8,128)(2,1)S(1)}, bf16[2,128,128]{2,1,0:T(8,128)(2,1)S(1)}, u32[]{:S(2)}, u32[]{:S(2)}) collective-permute-start(bf16[2,128,128]{2,1,0:T(8,128)(2,1)S(1)} %collective-permute-done.2), channel_id=1, source_target_pairs={{0,16},{16,32},{32,48},{48,64},{64,80},{80,96},{96,112},{112,128},... | collective-permute-start | bytes 196616 | tf_op jit(solution)/shard_map/ppermute | solution.py:16
  90.8 5.0 %collective-permute-start.4 = (bf16[2,128,128]{2,1,0:T(8,128)(2,1)S(1)}, bf16[2,128,128]{2,1,0:T(8,128)(2,1)S(1)}, u32[]{:S(2)}, u32[]{:S(2)}) collective-permute-start(bf16[2,128,128]{2,1,0:T(8,128)(2,1)S(1)} %collective-permute-done.3), channel_id=1, source_target_pairs={{0,16},{16,32},{32,48},{48,64},{64,80},{80,96},{96,112},{112,128},... | collective-permute-start | bytes 196616 | tf_op jit(solution)/shard_map/ppermute | solution.py:16
Sparse Core Ops, SparseCore 0:
  77.7 292.3 all-gather.1
  376.3 110.4 reduce-scatter.1
where the time goes:
time: 503 us; the launch traced here: 494 us
  waiting for transfers between devices  173 us (34%)
  local copies, waits for them, and re-layouts  83.8 us (17%)
  blocking collectives  63.2 us (13%)
  matrix products  52.7 us (10%)
  loops' own time  48.1 us (10%)
  other arithmetic  38.4 us (8%)
  starting transfers between devices  20.6 us (4%)
  between operations  13.5 us (3%)
    reduce_scatter x1, waiting for transfers between devices, per_device(): lax.psum_scatter(partial_sums.astype(jnp.bfloat16), 'head', scatter_dimen...  111 us
    all_gather x1, waiting for transfers between devices, per_device(): lax.all_gather(w_out, 'seq', axis=1, tiled=True)  58.8 us
    another operation x1, loops' own time, per_device(): lax.map(one_item, jnp.arange(heads_here * per_block, dtype=jnp.int32))  48.1 us
    all_gather x1, blocking collectives, per_device(): lax.all_gather(first_piece, 'head', axis=1, tiled=True)  37.7 us
    another operation x560, local copies, waits for them, and re-layouts, attend(): jnp.stack([second_values[span - 1 - offset:span - 1 - offset + rows] for...  25.7 us
    all_gather x1, blocking collectives, per_device(): lax.all_gather(second_piece, 'head', axis=1, tiled=True)  25.5 us
    dot_general x16, matrix products, attend(): jnp.dot(mixed.reshape(rows * span, width), first_keys.T, preferred_elemen...  23.8 us
    dot_general x16, matrix products, attend(): jnp.dot(probs.reshape(rows * span, reach + rows), first_values, preferred...  22.9 us
  transfers between devices with their start and end apart: 7, of which 5 were waited for; matrix products, arithmetic and copies ran while one was open for 34% of the time, Pallas kernels for 0%

commit v1 on v0

v1 whole, which is shorter than its diff:
```python
import functools
import math

import jax
import jax.numpy as jnp
from jax import lax
from jax.experimental import pallas as pl
from jax.experimental.pallas import tpu as pltpu
from jax.sharding import PartitionSpec as P

W1 = 512
W2 = 32
XS, HS, YS, ZS, CS = 4, 2, 4, 8, 2
BOTH = ("seq", "head")


def seq_of(x, half, y):
    return (x % XS) * HS * YS + (half % HS) * YS + y % YS


def moved(value, target):
    pairs = []
    for x in range(XS):
        for half in range(HS):
            for y in range(YS):
                for z in range(ZS):
                    for c in range(CS):
                        to = target(x, half, y, z, c)
                        if to is None:
                            continue
                        source = seq_of(x, half, y) * ZS * CS + z * CS + c
                        pairs.append((source, seq_of(*to[:3]) * ZS * CS + to[3] * CS + to[4]))
    return lax.ppermute(value, BOTH, pairs)


def later(value, steps):
    count = XS * HS * YS
    return lax.ppermute(value, "seq", [(s, s + steps) for s in range(count - steps)])


def attention_kernel(origin, q_ref, k_ref, v_ref, sk_ref, sv_ref, out_ref, q32, out32, *, tokens):
    rows, wide = q_ref.shape
    width = k_ref.shape[1]
    heads = wide // width
    span = sk_ref.shape[0] - rows
    factor = 2.5 / math.sqrt(width) * math.log2(math.e)
    q32[...] = q_ref[...].astype(jnp.float32)
    lanes = lax.broadcasted_iota(jnp.int32, (tokens, span, width), 2)
    token_of = lax.broadcasted_iota(jnp.int32, (tokens, span, width), 0)
    back = span - 1 - lax.broadcasted_iota(jnp.int32, (tokens, span, width), 1)

    def block(number, carry):
        start = pl.multiple_of(number * tokens, tokens)
        late = (lanes > start + token_of).reshape(tokens * span, width)
        counted = (origin[0] + start + token_of >= back).astype(jnp.float32)
        keys = jnp.stack([sk_ref[pl.ds(start + 1 + i, span), :] for i in range(tokens)])
        values = jnp.stack([sv_ref[pl.ds(start + 1 + i, span), :] for i in range(tokens)])
        for head in range(heads):
            cols = slice(head * width, (head + 1) * width)
            chosen = q32[pl.ds(start, tokens), cols]
            mixed = (chosen[:, None, :] * keys).astype(jnp.bfloat16).reshape(tokens * span, width)
            scores = lax.dot_general(
                mixed, k_ref[...], (((1,), (1,)), ((), ())), preferred_element_type=jnp.float32
            )
            parts = [scores[:, i * width : (i + 1) * width] for i in range(5)]
            parts = [jnp.where(late, parts[0], parts[4])] + parts[1:4]
            top = jnp.maximum(jnp.maximum(parts[0], parts[1]), jnp.maximum(parts[2], parts[3]))
            top = jnp.max(top.reshape(tokens, span, width), axis=1)
            top = jnp.max(top, axis=1, keepdims=True)
            top = jnp.broadcast_to(top[:, :, None], (tokens, span, width))
            top = top.reshape(tokens * span, width)
            weights = [jnp.exp2((p - top) * factor) for p in parts]
            probs = [jnp.where(late, weights[0], 0.0)] + weights[1:]
            probs = probs + [jnp.where(late, 0.0, weights[0])]
            probs = jnp.concatenate([p.astype(jnp.bfloat16) for p in probs], axis=1)
            carried = jnp.dot(probs, v_ref[...], preferred_element_type=jnp.float32)
            above = jnp.sum(carried[:, :width].reshape(tokens, span, width) * values, axis=1)
            below = jnp.sum(carried[:, width:].reshape(tokens, span, width) * counted, axis=1)
            out32[pl.ds(start, tokens), cols] = above / below
        return carry

    lax.fori_loop(0, rows // tokens, block, 0)
    out_ref[...] = out32[...].astype(jnp.bfloat16)


def attention(origin, q, k, v, sk, sv):
    rows, wide = q.shape
    return pl.pallas_call(
        functools.partial(attention_kernel, tokens=16),
        out_shape=jax.ShapeDtypeStruct((rows, wide), jnp.bfloat16),
        in_specs=[pl.BlockSpec(memory_space=pltpu.SMEM)]
        + [pl.BlockSpec(memory_space=pltpu.VMEM)] * 5,
        out_specs=pl.BlockSpec(memory_space=pltpu.VMEM),
        scratch_shapes=[pltpu.VMEM((rows, wide), jnp.float32)] * 2,
        compiler_params=pltpu.CompilerParams(vmem_limit_bytes=40 * 2**20),
        cost_estimate=pl.CostEstimate(
            flops=20_000_000_000, bytes_accessed=2**20, transcendentals=0
        ),
    )(origin, q, k, v, sk, sv)


def in_order(first, second, swap):
    return jnp.where(swap, second, first), jnp.where(swap, first, second)


def per_device(queries, long_keys, long_values, short_keys, short_values, w_out):
    rows = queries.shape[0]
    width = long_keys.shape[1]
    seq = lax.axis_index("seq")
    head = lax.axis_index("head")
    x, half, y = seq // (HS * YS), seq // YS % HS, seq % YS
    c = head % CS
    origin = seq * rows

    piece = jnp.stack([long_keys, long_values, short_keys, short_values])
    before = later(piece, 1)
    older = [later(piece[:2], steps) for steps in range(2, W1 // rows + 1)]
    blocks = older[::-1] + [before[:2], piece[:2]]
    mine = jnp.concatenate(
        [jnp.stack([b[0] for b in blocks]), jnp.stack([b[1] for b in blocks]), before[2:], piece[2:]]
    )
    gathered = lax.all_gather(mine, "head", axis=1, tiled=True)
    spots = len(blocks)
    reach = (spots - 1) * rows
    keys = gathered[:spots].reshape(spots * rows, width)
    values = gathered[spots : 2 * spots].reshape(spots * rows, width)
    place = origin - reach + jnp.arange(spots * rows, dtype=jnp.int32)[:, None]
    first_key = lax.dynamic_slice_in_dim(keys, jnp.maximum(reach - origin, 0), 1, 0)
    keys = jnp.where(place >= 0, keys, first_key)
    ones = (place >= 0).astype(jnp.bfloat16) * jnp.ones((1, width), jnp.bfloat16)
    values = jnp.concatenate([values, ones], axis=1)
    near = gathered[2 * spots :].astype(jnp.float32)
    near_keys = jnp.concatenate([near[0, rows - W2 :], near[2]])
    near_values = jnp.concatenate([near[1, rows - W2 :], near[3]])
    near_place = origin - W2 + jnp.arange(W2 + rows, dtype=jnp.int32)[:, None]
    near_keys = jnp.where(near_place >= 0, near_keys, near_keys[W2 : W2 + 1])

    other = moved(w_out, lambda x, h, y, z, c: (x, h + 1, y, z, c))
    pair = jnp.stack(in_order(w_out, other, half == 1))
    pair, keys = lax.optimization_barrier((pair, keys))
    from_x = [pair] + [
        moved(pair, lambda x, h, y, z, c, d=d: (x - d, h, y, z, c)) for d in (1, 2, 3)
    ]
    attended = attention(
        origin.reshape(1), queries, keys, values, near_keys, near_values
    )

    attended, from_x = lax.optimization_barrier((attended, from_x))

    from_y = [attended] + [
        moved(attended, lambda x, h, y, z, c, d=d: (x, h, y - d, z, c)) for d in (1, 2, 3)
    ]
    twice = jnp.concatenate(from_y + from_y[:3])
    tokens = lax.dynamic_slice_in_dim(twice, (2 * c - y) % YS * rows, YS * rows, 0)
    twice = jnp.concatenate(from_x + from_x[:3])
    columns = lax.dynamic_slice_in_dim(twice, (XS - x) % XS * HS, XS * HS, 0)
    count = YS // 2 * rows
    product = functools.partial(
        jnp.einsum, "tk,nkc->ntc", preferred_element_type=jnp.float32
    )
    away = product(tokens[count:], columns).astype(jnp.bfloat16)
    came = moved(away, lambda x, h, y, z, c: (x, h, y, z, 1 - c))
    kept = (product(tokens[:count], columns) + came.astype(jnp.float32)).astype(jnp.bfloat16)
    groups = [[z * CS + core for z in range(ZS)] for core in range(CS)]
    parts = lax.all_to_all(kept, "head", 0, 0, axis_index_groups=groups, tiled=True)
    summed = jnp.sum(parts.astype(jnp.float32), axis=0).astype(jnp.bfloat16)
    summed = summed.reshape(YS // 2, rows, summed.shape[-1])
    odd = y % 2 == 1
    sent = in_order(summed[0], summed[1], odd)
    landed = [
        moved(
            sent[j],
            lambda x, h, y, z, c, j=j: (x, h, 2 * c + (j ^ (y % 2)), z, y // 2),
        )
        for j in range(2)
    ]
    return jnp.concatenate(in_order(landed[0], landed[1], odd), axis=1)


def solution(mesh):
    return jax.shard_map(
        per_device,
        mesh=mesh,
        in_specs=(
            P("seq", "head"),
            P(("seq", "head"), None),
            P(("seq", "head"), None),
            P(("seq", "head"), None),
            P(("seq", "head"), None),
            P("head", "seq"),
        ),
        out_specs=P("seq", "head"),
        check_vma=False,
    )
```

time: 503 us -> 226 us (0.45); the launches traced: 494 us -> 225 us
  waiting for transfers between devices: 173 us -> 69.8 us
  local copies, waits for them, and re-layouts: 83.8 us -> 5.21 us
  starting transfers between devices: 20.6 us -> 87.2 us
  matrix products: 52.7 us -> 2.48 us
  loops' own time: 48.1 us -> 0 us
  other arithmetic: 38.4 us -> 2.08 us
  blocking collectives: 63.2 us -> 40.4 us
  Pallas kernels: 0 us -> 17.6 us
  between operations: 13.5 us -> 0.61 us
    reduce_scatter x1 -> x0, waiting for transfers between devices: 111 us -> none  [per_device(): lax.psum_scatter(partial_sums.astype(jnp.bfloat16), 'head', scatter_dimen...]
    ppermute x5 -> x14, starting transfers between devices: 20.6 us -> 83.7 us  [the longest x10 58.2 us: moved(): return lax.ppermute(value, BOTH, pairs)]
    all_gather x1 -> x0, waiting for transfers between devices: 58.8 us -> none  [per_device(): lax.all_gather(w_out, 'seq', axis=1, tiled=True)]
    all_to_all x0 -> x1, waiting for transfers between devices: none -> 50.8 us  [per_device(): lax.all_to_all(kept, 'head', 0, 0, axis_index_groups=groups, tiled=True)]
    dot_general x33 -> x2, matrix products: 52.7 us -> 2.48 us  [the longest x1 1.72 us: per_device(): product(tokens[:count], columns) + came.astype(jnp.float32)]
    another operation x1 -> x0, loops' own time: 48.1 us -> none  [per_device(): lax.map(one_item, jnp.arange(heads_here * per_block, dtype=jnp.int32))]
    another operation x576 -> x0, local copies, waits for them, and re-layouts: 26.2 us -> none  [the longest x560 25.7 us: attend(): jnp.stack([second_values[span - 1 - offset:span - 1 - offset + rows] for...]
    all_gather x2 -> x1, blocking collectives: 63.2 us -> 40.4 us  [per_device(): gathered = lax.all_gather(mine, 'head', axis=1, tiled=True)]
  transfers between devices with their start and end apart: 7 -> 15, of which waited for: 5 -> 8; matrix products, arithmetic and copies ran while one was open for 34% -> 2% of each run, Pallas kernels for 0% -> 8%
where the time goes in v1:
time: 226 us; the launch traced here: 225 us
  starting transfers between devices  87.2 us (39%)
  waiting for transfers between devices  69.8 us (31%)
  blocking collectives  40.4 us (18%)
  Pallas kernels  17.6 us (8%)
  local copies, waits for them, and re-layouts  5.21 us (2%)
  matrix products  2.48 us (1%)
    ppermute x10, starting transfers between devices, moved(): return lax.ppermute(value, BOTH, pairs)  58.2 us
    all_to_all x1, waiting for transfers between devices, per_device(): lax.all_to_all(kept, 'head', 0, 0, axis_index_groups=groups, tiled=True)  50.8 us
    all_gather x1, blocking collectives, per_device(): gathered = lax.all_gather(mine, 'head', axis=1, tiled=True)  40.4 us
    ppermute x4, starting transfers between devices, later(): lax.ppermute(value, 'seq', [(s, s + steps) for s in range(count - steps)])  25.5 us
    ppermute x10, waiting for transfers between devices, moved(): return lax.ppermute(value, BOTH, pairs)  18.4 us
    pallas_call x1, Pallas kernels, attention(): pl.pallas_call(functools.partial(attention_kernel, tokens=16), out_shape=...  17.6 us
  transfers between devices with their start and end apart: 15, of which 8 were waited for; matrix products, arithmetic and copies ran while one was open for 2% of the time, Pallas kernels for 8%

profile of v1, /device:TPU:1, one launch (start us, length us, event | category | flops | bytes accessed | tf_op | source)
XLA Modules:
  0.0 225.4 jit_solution(1393243431085310624)
XLA Ops:
  0.0 0.7 pad_maximum_fusion.5
  0.7 16.3 %collective-permute-start.1 = (bf16[2,8,128]{2,1,0:T(8,128)(2,1)S(1)}, bf16[2,8,128]{2,1,0:T(8,128)(2,1)S(1)}, u32[]{:S(2)}, u32[]{:S(2)}) collective-permute-start(bf16[2,8,128]{2,1,0:T(8,128)(2,1)S(1)} %pad_maximum_fusion.5), channel_id=1, source_target_pairs={{0,64},{16,80},{32,96},{48,112},{64,128},{80,144},{96,160},{112,17... | collective-permute-start | bytes 12296 | tf_op jit(solution)/shard_map/ppermute | solution.py:38
  17.0 4.6 %collective-permute-start.2 = (bf16[2,8,128]{2,1,0:T(8,128)(2,1)S(1)}, bf16[2,8,128]{2,1,0:T(8,128)(2,1)S(1)}, u32[]{:S(2)}, u32[]{:S(2)}) collective-permute-start(bf16[2,8,128]{2,1,0:T(8,128)(2,1)S(1)} %pad_maximum_fusion.5), channel_id=1, source_target_pairs={{0,48},{16,64},{32,80},{48,96},{64,112},{80,128},{96,144},{112,160... | collective-permute-start | bytes 12296 | tf_op jit(solution)/shard_map/ppermute | solution.py:38
  21.7 2.0 collective-permute-start.3
  23.6 1.1 copy.10
  24.7 13.0 %collective-permute-start = (bf16[512,256]{0,1:T(8,128)(2,1)S(1)}, bf16[512,256]{0,1:T(8,128)(2,1)S(1)}, u32[]{:S(2)}, u32[]{:S(2)}) collective-permute-start(bf16[512,256]{0,1:T(8,128)(2,1)S(1)} %copy.10), channel_id=1, source_target_pairs={{0,64},{1,65},{2,66},{3,67},{4,68},{5,69},{6,70},{7,71},{8,72},{9,... | collective-permute-start | bytes 786440 | tf_op jit(solution)/shard_map/ppermute | solution.py:33
  37.8 0.7 pad_maximum_fusion.4
  38.5 2.6 %collective-permute-start.4 = (bf16[4,8,128]{2,1,0:T(8,128)(2,1)S(1)}, bf16[4,8,128]{2,1,0:T(8,128)(2,1)S(1)}, u32[]{:S(2)}, u32[]{:S(2)}) collective-permute-start(bf16[4,8,128]{2,1,0:T(8,128)(2,1)S(1)} %pad_maximum_fusion.4), channel_id=1, source_target_pairs={{0,16},{16,32},{32,48},{48,64},{64,80},{80,96},{96,112},{112,128},... | collective-permute-start | bytes 24584 | tf_op jit(solution)/shard_map/ppermute | solution.py:38
  41.9 0.7 constant_dynamic-update-slice_fusion.8
  42.6 0.7 constant_dynamic-update-slice_fusion.3
  43.3 0.7 constant_dynamic-update-slice_fusion.1
  44.7 40.4 %all_gather.3 = bf16[14,128,128]{2,1,0:T(8,128)(2,1)S(1)} all-gather(bf16[14,8,128]{2,1,0:T(8,128)(2,1)S(1)} %constant_dynamic-update-slice_fusion), channel_id=1, replica_groups=mesh['seq'=32,'head'=16] {'head'}, dimensions={1}, use_global_device_ids=true | all-gather | bytes 487424 | tf_op jit(solution)/shard_map/all_gather | solution.py:122
  85.7 23.3 %collective-permute-start.5 = (bf16[2,512,256]{1,2,0:T(8,128)(2,1)S(1)}, bf16[2,512,256]{1,2,0:T(8,128)(2,1)S(1)}, u32[]{:S(2)}, u32[]{:S(2)}) collective-permute-start(bf16[2,512,256]{1,2,0:T(8,128)(2,1)S(1)} %pad_maximum_fusion), channel_id=1, source_target_pairs={{0,384},{1,385},{2,386},{3,387},{4,388},{5,389},{6,390},{7,391},{8... | collective-permute-start | bytes 1572872 | tf_op jit(solution)/shard_map/ppermute | solution.py:33
  109.1 2.1 collective-permute-start.6
  111.2 2.5 %collective-permute-start.7 = (bf16[2,512,256]{1,2,0:T(8,128)(2,1)S(1)}, bf16[2,512,256]{1,2,0:T(8,128)(2,1)S(1)}, u32[]{:S(2)}, u32[]{:S(2)}) collective-permute-start(bf16[2,512,256]{1,2,0:T(8,128)(2,1)S(1)} %pad_maximum_fusion), channel_id=1, source_target_pairs={{0,128},{1,129},{2,130},{3,131},{4,132},{5,133},{6,134},{7,135},{8... | collective-permute-start | bytes 1572872 | tf_op jit(solution)/shard_map/ppermute | solution.py:33
  113.7 17.6 %shard_map.64 = bf16[128,512]{1,0:T(8,128)(2,1)S(1)} custom-call(s32[1]{0:T(128)} %bitcast.origin, bf16[128,512]{1,0:T(8,128)(2,1)S(1)} %copy-done, bf16[640,128]{1,0:T(8,128)(2,1)S(1)} %broadcast_select_fusion.k_ref, bf16[640,256]{1,0:T(8,128)(2,1)S(1)} %pad_maximum_fusion.1.v_ref, f32[160,128]{1,0:T(8,128)S(1)} %get-tuple-element.31.sk_ref, ...), custom_call_target="tpu_custom_call" | custom-call | flops 20000000000 | bytes 1048576 | tf_op jit(solution)/shard_map/pallas_call | solution.py:88
  131.4 6.2 %collective-permute-done.7 = bf16[2,512,256]{1,2,0:T(8,128)(2,1)S(1)} collective-permute-done((bf16[2,512,256]{1,2,0:T(8,128)(2,1)S(1)}, bf16[2,512,256]{1,2,0:T(8,128)(2,1)S(1)}, u32[]{:S(2)}, u32[]{:S(2)}) %collective-permute-start.7) | collective-permute-done | bytes 524320 | tf_op jit(solution)/shard_map/ppermute | solution.py:33
  137.6 1.9 collective-permute-start.8
  139.5 1.9 collective-permute-start.9
  141.4 3.4 %collective-permute-start.10 = (bf16[128,512]{1,0:T(8,128)(2,1)S(1)}, bf16[128,512]{1,0:T(8,128)(2,1)S(1)}, u32[]{:S(2)}, u32[]{:S(2)}) collective-permute-start(bf16[128,512]{1,0:T(8,128)(2,1)S(1)} %shard_map.64), channel_id=1, source_target_pairs={{0,16},{1,17},{2,18},{3,19},{4,20},{5,21},{6,22},{7,23},{8,24},{9,... | collective-permute-start | bytes 393224 | tf_op jit(solution)/shard_map/ppermute | solution.py:33
  145.1 2.3 %collective-permute-done.9 = bf16[128,512]{1,0:T(8,128)(2,1)S(1)} collective-permute-done((bf16[128,512]{1,0:T(8,128)(2,1)S(1)}, bf16[128,512]{1,0:T(8,128)(2,1)S(1)}, u32[]{:S(2)}, u32[]{:S(2)}) %collective-permute-start.9) | collective-permute-done | bytes 131104 | tf_op jit(solution)/shard_map/ppermute | solution.py:33
  147.5 2.5 %collective-permute-done.10 = bf16[128,512]{1,0:T(8,128)(2,1)S(1)} collective-permute-done((bf16[128,512]{1,0:T(8,128)(2,1)S(1)}, bf16[128,512]{1,0:T(8,128)(2,1)S(1)}, u32[]{:S(2)}, u32[]{:S(2)}) %collective-permute-start.10) | collective-permute-done | bytes 131104 | tf_op jit(solution)/shard_map/ppermute | solution.py:33
  150.0 0.8 fusion.10
  150.8 3.6 %collective-permute-start.11 = (bf16[8,256,256]{1,2,0:T(8,128)(2,1)S(1)}, bf16[8,256,256]{1,2,0:T(8,128)(2,1)S(1)}, u32[]{:S(2)}, u32[]{:S(2)}) collective-permute-start(bf16[8,256,256]{1,2,0:T(8,128)(2,1)S(1)} %fusion.10), channel_id=1, source_target_pairs={{0,1},{1,0},{2,3},{3,2},{4,5},{5,4},{6,7},{7,6},{8,9},{9,8},{10,11... | collective-permute-start | bytes 3145736 | tf_op jit(solution)/shard_map/ppermute | solution.py:33
  154.3 2.3 %collective-permute-done.11 = bf16[8,256,256]{1,2,0:T(8,128)(2,1)S(1)} collective-permute-done((bf16[8,256,256]{1,2,0:T(8,128)(2,1)S(1)}, bf16[8,256,256]{1,2,0:T(8,128)(2,1)S(1)}, u32[]{:S(2)}, u32[]{:S(2)}) %collective-permute-start.11) | collective-permute-done | bytes 1048608 | tf_op jit(solution)/shard_map/ppermute | solution.py:33
  156.6 1.7 fusion
  158.3 3.6 %all-to-all-start = ((bf16[8,256,256]{1,2,0:T(8,128)(2,1)}), bf16[8,256,256]{1,2,0:T(8,128)(2,1)S(1)}, u32[]{:S(2)}, u32[]{:S(2)}) async-start(bf16[8,256,256]{1,2,0:T(8,128)(2,1)} %fusion), calls=%async_computation | async-start | bytes 2097152 | tf_op jit(solution)/shard_map/all_to_all | solution.py:165
  161.9 50.8 %all-to-all-done = bf16[8,256,256]{1,2,0:T(8,128)(2,1)S(1)} async-done(((bf16[8,256,256]{1,2,0:T(8,128)(2,1)}), bf16[8,256,256]{1,2,0:T(8,128)(2,1)S(1)}, u32[]{:S(2)}, u32[]{:S(2)}) %all-to-all-start) | async-done | bytes 1048608 | tf_op jit(solution)/shard_map/all_to_all | solution.py:165
  212.9 4.6 %collective-permute-start.12 = (bf16[128,256]{0,1:T(8,128)(2,1)S(1)}, bf16[128,256]{0,1:T(8,128)(2,1)S(1)}, u32[]{:S(2)}, u32[]{:S(2)}) collective-permute-start(bf16[128,256]{0,1:T(8,128)(2,1)S(1)} %get-tuple-element.29), channel_id=1, source_target_pairs={{0,16},{1,48},{2,18},{3,50},{4,20},{5,52},{6,22},{7,54},{8,24},{9,... | collective-permute-start | bytes 196616 | tf_op jit(solution)/shard_map/ppermute | solution.py:33
  217.5 1.9 collective-permute-start.13
  219.7 4.9 %collective-permute-done.13 = bf16[128,256]{0,1:T(8,128)(2,1)S(1)} collective-permute-done((bf16[128,256]{0,1:T(8,128)(2,1)S(1)}, bf16[128,256]{0,1:T(8,128)(2,1)S(1)}, u32[]{:S(2)}, u32[]{:S(2)}) %collective-permute-start.13) | collective-permute-done | bytes 65568 | tf_op jit(solution)/shard_map/ppermute | solution.py:33
  224.6 0.8 copy.13
  (54 shorter events, 2.7 us)
Async XLA Ops:
  0.0 113.7 %copy-start = (bf16[128,512]{1,0:T(8,128)(2,1)S(1)}, bf16[128,512]{1,0:T(8,128)(2,1)}, u32[]{:S(2)}) copy-start(bf16[128,512]{1,0:T(8,128)(2,1)} %q_ref.1) | copy-start | bytes 393220
  0.7 40.5 %collective-permute-start.1 = (bf16[2,8,128]{2,1,0:T(8,128)(2,1)S(1)}, bf16[2,8,128]{2,1,0:T(8,128)(2,1)S(1)}, u32[]{:S(2)}, u32[]{:S(2)}) collective-permute-start(bf16[2,8,128]{2,1,0:T(8,128)(2,1)S(1)} %pad_maximum_fusion.5), channel_id=1, source_target_pairs={{0,64},{16,80},{32,96},{48,112},{64,128},{80,144},{96,160},{112,17... | collective-permute-start | bytes 12296 | tf_op jit(solution)/shard_map/ppermute | solution.py:38
  17.0 24.3 %collective-permute-start.2 = (bf16[2,8,128]{2,1,0:T(8,128)(2,1)S(1)}, bf16[2,8,128]{2,1,0:T(8,128)(2,1)S(1)}, u32[]{:S(2)}, u32[]{:S(2)}) collective-permute-start(bf16[2,8,128]{2,1,0:T(8,128)(2,1)S(1)} %pad_maximum_fusion.5), channel_id=1, source_target_pairs={{0,48},{16,64},{32,80},{48,96},{64,112},{80,128},{96,144},{112,160... | collective-permute-start | bytes 12296 | tf_op jit(solution)/shard_map/ppermute | solution.py:38
  21.7 19.7 %collective-permute-start.3 = (bf16[2,8,128]{2,1,0:T(8,128)(2,1)S(1)}, bf16[2,8,128]{2,1,0:T(8,128)(2,1)S(1)}, u32[]{:S(2)}, u32[]{:S(2)}) collective-permute-start(bf16[2,8,128]{2,1,0:T(8,128)(2,1)S(1)} %pad_maximum_fusion.5), channel_id=1, source_target_pairs={{0,32},{16,48},{32,64},{48,80},{64,96},{80,112},{96,128},{112,144}... | collective-permute-start | bytes 12296 | tf_op jit(solution)/shard_map/ppermute | solution.py:38
  24.7 60.9 %collective-permute-start = (bf16[512,256]{0,1:T(8,128)(2,1)S(1)}, bf16[512,256]{0,1:T(8,128)(2,1)S(1)}, u32[]{:S(2)}, u32[]{:S(2)}) collective-permute-start(bf16[512,256]{0,1:T(8,128)(2,1)S(1)} %copy.10), channel_id=1, source_target_pairs={{0,64},{1,65},{2,66},{3,67},{4,68},{5,69},{6,70},{7,71},{8,72},{9,... | collective-permute-start | bytes 786440 | tf_op jit(solution)/shard_map/ppermute | solution.py:33
  38.5 3.4 %collective-permute-start.4 = (bf16[4,8,128]{2,1,0:T(8,128)(2,1)S(1)}, bf16[4,8,128]{2,1,0:T(8,128)(2,1)S(1)}, u32[]{:S(2)}, u32[]{:S(2)}) collective-permute-start(bf16[4,8,128]{2,1,0:T(8,128)(2,1)S(1)} %pad_maximum_fusion.4), channel_id=1, source_target_pairs={{0,16},{16,32},{32,48},{48,64},{64,80},{80,96},{96,112},{112,128},... | collective-permute-start | bytes 24584 | tf_op jit(solution)/shard_map/ppermute | solution.py:38
  85.7 45.6 %collective-permute-start.5 = (bf16[2,512,256]{1,2,0:T(8,128)(2,1)S(1)}, bf16[2,512,256]{1,2,0:T(8,128)(2,1)S(1)}, u32[]{:S(2)}, u32[]{:S(2)}) collective-permute-start(bf16[2,512,256]{1,2,0:T(8,128)(2,1)S(1)} %pad_maximum_fusion), channel_id=1, source_target_pairs={{0,384},{1,385},{2,386},{3,387},{4,388},{5,389},{6,390},{7,391},{8... | collective-permute-start | bytes 1572872 | tf_op jit(solution)/shard_map/ppermute | solution.py:33
  109.1 22.3 %collective-permute-start.6 = (bf16[2,512,256]{1,2,0:T(8,128)(2,1)S(1)}, bf16[2,512,256]{1,2,0:T(8,128)(2,1)S(1)}, u32[]{:S(2)}, u32[]{:S(2)}) collective-permute-start(bf16[2,512,256]{1,2,0:T(8,128)(2,1)S(1)} %pad_maximum_fusion), channel_id=1, source_target_pairs={{0,256},{1,257},{2,258},{3,259},{4,260},{5,261},{6,262},{7,263},{8... | collective-permute-start | bytes 1572872 | tf_op jit(solution)/shard_map/ppermute | solution.py:33
  111.2 26.3 %collective-permute-start.7 = (bf16[2,512,256]{1,2,0:T(8,128)(2,1)S(1)}, bf16[2,512,256]{1,2,0:T(8,128)(2,1)S(1)}, u32[]{:S(2)}, u32[]{:S(2)}) collective-permute-start(bf16[2,512,256]{1,2,0:T(8,128)(2,1)S(1)} %pad_maximum_fusion), channel_id=1, source_target_pairs={{0,128},{1,129},{2,130},{3,131},{4,132},{5,133},{6,134},{7,135},{8... | collective-permute-start | bytes 1572872 | tf_op jit(solution)/shard_map/ppermute | solution.py:33
  137.6 7.5 %collective-permute-start.8 = (bf16[128,512]{1,0:T(8,128)(2,1)S(1)}, bf16[128,512]{1,0:T(8,128)(2,1)S(1)}, u32[]{:S(2)}, u32[]{:S(2)}) collective-permute-start(bf16[128,512]{1,0:T(8,128)(2,1)S(1)} %shard_map.64), channel_id=1, source_target_pairs={{0,48},{1,49},{2,50},{3,51},{4,52},{5,53},{6,54},{7,55},{8,56},{9,... | collective-permute-start | bytes 393224 | tf_op jit(solution)/shard_map/ppermute | solution.py:33
  139.5 8.0 %collective-permute-start.9 = (bf16[128,512]{1,0:T(8,128)(2,1)S(1)}, bf16[128,512]{1,0:T(8,128)(2,1)S(1)}, u32[]{:S(2)}, u32[]{:S(2)}) collective-permute-start(bf16[128,512]{1,0:T(8,128)(2,1)S(1)} %shard_map.64), channel_id=1, source_target_pairs={{0,32},{1,33},{2,34},{3,35},{4,36},{5,37},{6,38},{7,39},{8,40},{9,... | collective-permute-start | bytes 393224 | tf_op jit(solution)/shard_map/ppermute | solution.py:33
  141.4 8.5 %collective-permute-start.10 = (bf16[128,512]{1,0:T(8,128)(2,1)S(1)}, bf16[128,512]{1,0:T(8,128)(2,1)S(1)}, u32[]{:S(2)}, u32[]{:S(2)}) collective-permute-start(bf16[128,512]{1,0:T(8,128)(2,1)S(1)} %shard_map.64), channel_id=1, source_target_pairs={{0,16},{1,17},{2,18},{3,19},{4,20},{5,21},{6,22},{7,23},{8,24},{9,... | collective-permute-start | bytes 393224 | tf_op jit(solution)/shard_map/ppermute | solution.py:33
  150.8 5.8 %collective-permute-start.11 = (bf16[8,256,256]{1,2,0:T(8,128)(2,1)S(1)}, bf16[8,256,256]{1,2,0:T(8,128)(2,1)S(1)}, u32[]{:S(2)}, u32[]{:S(2)}) collective-permute-start(bf16[8,256,256]{1,2,0:T(8,128)(2,1)S(1)} %fusion.10), channel_id=1, source_target_pairs={{0,1},{1,0},{2,3},{3,2},{4,5},{5,4},{6,7},{7,6},{8,9},{9,8},{10,11... | collective-permute-start | bytes 3145736 | tf_op jit(solution)/shard_map/ppermute | solution.py:33
  158.3 54.4 %all-to-all-start = ((bf16[8,256,256]{1,2,0:T(8,128)(2,1)}), bf16[8,256,256]{1,2,0:T(8,128)(2,1)S(1)}, u32[]{:S(2)}, u32[]{:S(2)}) async-start(bf16[8,256,256]{1,2,0:T(8,128)(2,1)} %fusion), calls=%async_computation | async-start | bytes 2097152 | tf_op jit(solution)/shard_map/all_to_all | solution.py:165
  212.9 6.8 %collective-permute-start.12 = (bf16[128,256]{0,1:T(8,128)(2,1)S(1)}, bf16[128,256]{0,1:T(8,128)(2,1)S(1)}, u32[]{:S(2)}, u32[]{:S(2)}) collective-permute-start(bf16[128,256]{0,1:T(8,128)(2,1)S(1)} %get-tuple-element.29), channel_id=1, source_target_pairs={{0,16},{1,48},{2,18},{3,50},{4,20},{5,52},{6,22},{7,54},{8,24},{9,... | collective-permute-start | bytes 196616 | tf_op jit(solution)/shard_map/ppermute | solution.py:33
  217.5 7.1 %collective-permute-start.13 = (bf16[128,256]{0,1:T(8,128)(2,1)S(1)}, bf16[128,256]{0,1:T(8,128)(2,1)S(1)}, u32[]{:S(2)}, u32[]{:S(2)}) collective-permute-start(bf16[128,256]{0,1:T(8,128)(2,1)S(1)} %get-tuple-element.30), channel_id=1, source_target_pairs={{0,0},{1,32},{2,2},{3,34},{4,4},{5,36},{6,6},{7,38},{8,8},{9,40},{... | collective-permute-start | bytes 196616 | tf_op jit(solution)/shard_map/ppermute | solution.py:33

commit v2 on v1

--- a/solution.py
+++ b/solution.py
@@ -38,10 +38,43 @@
     return lax.ppermute(value, "seq", [(s, s + steps) for s in range(count - steps)])
 
 
-def attention_kernel(origin, q_ref, k_ref, v_ref, sk_ref, sv_ref, out_ref, q32, out32, *, tokens):
+def attention_kernel(
+    place, q_ref, mine_ref, other_ref, out_ref, k_ref, v_ref, sk_ref, sv_ref, q32, out32, *, tokens
+):
     rows, wide = q_ref.shape
     width = k_ref.shape[1]
     heads = wide // width
+    block_now, core = place[0], place[1]
+    spots = W1 // rows + 1
+
+    def whole(number):
+        mine = mine_ref[:, number].astype(jnp.float32)
+        other = other_ref[:, number].astype(jnp.float32)
+        first, second = jnp.where(core == 1, other, mine), jnp.where(core == 1, mine, other)
+        return jnp.concatenate([first[:, None], second[:, None]], axis=1).reshape(rows, width)
+
+    for spot in reversed(range(spots)):
+        there = block_now + spot >= spots - 1
+        span = pl.ds(spot * rows, rows)
+        k_ref[span, :] = whole(spot).astype(jnp.bfloat16)
+        v_ref[span, :width] = whole(spots + spot).astype(jnp.bfloat16)
+        v_ref[span, width:] = jnp.full((rows, width), jnp.where(there, 1.0, 0.0)).astype(jnp.bfloat16)
+    for spot in range(1, spots):
+
+        @pl.when(block_now == spots - 1 - spot)
+        def _():
+            key = whole(spot)[:1]
+            filler = jnp.broadcast_to(key, (spot * rows, width))
+            k_ref[: spot * rows, :] = filler.astype(jnp.bfloat16)
+
+    short = whole(2 * spots + 2)
+    sk_ref[W2:, :] = short
+    edge = whole(2 * spots)[rows - W2 :]
+    sk_ref[:W2, :] = jnp.where(block_now == 0, jnp.broadcast_to(short[:1], edge.shape), edge)
+    sv_ref[W2:, :] = whole(2 * spots + 3)
+    sv_ref[:W2, :] = whole(2 * spots + 1)[rows - W2 :]
+    origin = block_now * rows
+
     span = sk_ref.shape[0] - rows
     factor = 2.5 / math.sqrt(width) * math.log2(math.e)
     q32[...] = q_ref[...].astype(jnp.float32)
@@ -52,7 +85,7 @@
     def block(number, carry):
         start = pl.multiple_of(number * tokens, tokens)
         late = (lanes > start + token_of).reshape(tokens * span, width)
-        counted = (origin[0] + start + token_of >= back).astype(jnp.float32)
+        counted = (origin + start + token_of >= back).astype(jnp.float32)
         keys = jnp.stack([sk_ref[pl.ds(start + 1 + i, span), :] for i in range(tokens)])
         values = jnp.stack([sv_ref[pl.ds(start + 1 + i, span), :] for i in range(tokens)])
         for head in range(heads):
@@ -83,20 +116,77 @@
     out_ref[...] = out32[...].astype(jnp.bfloat16)
 
 
-def attention(origin, q, k, v, sk, sv):
+def attention(place, q, mine, other):
     rows, wide = q.shape
+    width = mine.shape[-1]
+    spots = W1 // rows + 1
     return pl.pallas_call(
         functools.partial(attention_kernel, tokens=16),
         out_shape=jax.ShapeDtypeStruct((rows, wide), jnp.bfloat16),
         in_specs=[pl.BlockSpec(memory_space=pltpu.SMEM)]
-        + [pl.BlockSpec(memory_space=pltpu.VMEM)] * 5,
+        + [pl.BlockSpec(memory_space=pltpu.VMEM)] * 3,
         out_specs=pl.BlockSpec(memory_space=pltpu.VMEM),
-        scratch_shapes=[pltpu.VMEM((rows, wide), jnp.float32)] * 2,
+        scratch_shapes=[
+            pltpu.VMEM((spots * rows, width), jnp.bfloat16),
+            pltpu.VMEM((spots * rows, 2 * width), jnp.bfloat16),
+            pltpu.VMEM((W2 + rows, width), jnp.float32),
+            pltpu.VMEM((W2 + rows, width), jnp.float32),
+            pltpu.VMEM((rows, wide), jnp.float32),
+            pltpu.VMEM((rows, wide), jnp.float32),
+        ],
         compiler_params=pltpu.CompilerParams(vmem_limit_bytes=40 * 2**20),
         cost_estimate=pl.CostEstimate(
             flops=20_000_000_000, bytes_accessed=2**20, transcendentals=0
         ),
-    )(origin, q, k, v, sk, sv)
+    )(place, q, mine, other)
+
+
+def pack_kernel(count, *refs):
+    own, before, older, out_ref = refs[:4], refs[4], refs[5:-1], refs[-1]
+    for to in range(out_ref.shape[0]):
+        for kind in range(2):
+            line = [ref.at[kind] for ref in older[::-1]] + [before.at[kind], own[kind]]
+            for spot, ref in enumerate(line):
+                out_ref[to, kind * count + spot] = ref[...]
+            out_ref[to, 2 * count + kind] = before[2 + kind]
+            out_ref[to, 2 * count + 2 + kind] = own[2 + kind][...]
+
+
+def pack(own, before, older):
+    count = len(older) + 2
+    return pl.pallas_call(
+        functools.partial(pack_kernel, count),
+        out_shape=jax.ShapeDtypeStruct((ZS, 2 * count + 4) + own[0].shape, own[0].dtype),
+        in_specs=[pl.BlockSpec(memory_space=pltpu.VMEM)] * (5 + len(older)),
+        out_specs=pl.BlockSpec(memory_space=pltpu.VMEM),
+    )(*own, before, *older)
+
+
+def project_kernel(place, *refs):
+    tokens, columns, out_ref = refs[:YS], refs[YS : YS + XS], refs[-1]
+    x, y, c = place[0], place[1], place[2]
+    for d in range(XS):
+        to = lax.rem(x + d, XS)
+        for e in range(YS):
+            slot = lax.rem(y + e + YS - 2 * c, YS)
+            total = jnp.dot(tokens[e][0], columns[d][0], preferred_element_type=jnp.float32)
+            total += jnp.dot(tokens[e][1], columns[d][1], preferred_element_type=jnp.float32)
+            out_ref[slot // 2, to, slot % 2] = total.astype(jnp.bfloat16)
+
+
+def project(place, tokens, columns):
+    rows, wide = tokens[0].shape[1], columns[0].shape[2]
+    return pl.pallas_call(
+        project_kernel,
+        out_shape=jax.ShapeDtypeStruct((2, XS, YS // 2, rows, wide), jnp.bfloat16),
+        in_specs=[pl.BlockSpec(memory_space=pltpu.SMEM)]
+        + [pl.BlockSpec(memory_space=pltpu.VMEM)] * (XS + YS),
+        out_specs=pl.BlockSpec(memory_space=pltpu.VMEM),
+        compiler_params=pltpu.CompilerParams(vmem_limit_bytes=40 * 2**20),
+        cost_estimate=pl.CostEstimate(
+            flops=1_100_000_000, bytes_accessed=4 * 2**20, transcendentals=0
+        ),
+    )(place, *tokens, *columns)
 
 
 def in_order(first, second, swap):
@@ -105,66 +195,55 @@
 
 def per_device(queries, long_keys, long_values, short_keys, short_values, w_out):
     rows = queries.shape[0]
-    width = long_keys.shape[1]
     seq = lax.axis_index("seq")
     head = lax.axis_index("head")
     x, half, y = seq // (HS * YS), seq // YS % HS, seq % YS
-    c = head % CS
-    origin = seq * rows
+    z, c = head // CS, head % CS
+
+    def first_hop(x, h, y, z, c):
+        return (x, h, y, z ^ 1, c) if h != z % 2 else (x, h + 1, y, z, c)
+
+    def second_hop(x, h, y, z, c):
+        return (x, h + 1, y, z ^ 1, c) if h != z % 2 else None
+
+    one_way = moved(w_out, first_hop)
+    other_way = moved(w_out, second_hop)
 
     piece = jnp.stack([long_keys, long_values, short_keys, short_values])
     before = later(piece, 1)
     older = [later(piece[:2], steps) for steps in range(2, W1 // rows + 1)]
-    blocks = older[::-1] + [before[:2], piece[:2]]
-    mine = jnp.concatenate(
-        [jnp.stack([b[0] for b in blocks]), jnp.stack([b[1] for b in blocks]), before[2:], piece[2:]]
+    mine = pack((long_keys, long_values, short_keys, short_values), before, older)
+    lines = [[z * CS + core for z in range(ZS)] for core in range(CS)]
+    over_z = lax.all_to_all(mine, "head", 0, 0, axis_index_groups=lines, tiled=True)
+    over_core = moved(over_z, lambda x, h, y, z, c: (x, h, y, z, 1 - c))
+
+    near_by = half == z % 2
+    pair = jnp.stack(
+        [jnp.where(near_by, w_out, one_way), jnp.where(near_by, one_way, other_way)]
     )
-    gathered = lax.all_gather(mine, "head", axis=1, tiled=True)
-    spots = len(blocks)
-    reach = (spots - 1) * rows
-    keys = gathered[:spots].reshape(spots * rows, width)
-    values = gathered[spots : 2 * spots].reshape(spots * rows, width)
-    place = origin - reach + jnp.arange(spots * rows, dtype=jnp.int32)[:, None]
-    first_key = lax.dynamic_slice_in_dim(keys, jnp.maximum(reach - origin, 0), 1, 0)
-    keys = jnp.where(place >= 0, keys, first_key)
-    ones = (place >= 0).astype(jnp.bfloat16) * jnp.ones((1, width), jnp.bfloat16)
-    values = jnp.concatenate([values, ones], axis=1)
-    near = gathered[2 * spots :].astype(jnp.float32)
-    near_keys = jnp.concatenate([near[0, rows - W2 :], near[2]])
-    near_values = jnp.concatenate([near[1, rows - W2 :], near[3]])
-    near_place = origin - W2 + jnp.arange(W2 + rows, dtype=jnp.int32)[:, None]
-    near_keys = jnp.where(near_place >= 0, near_keys, near_keys[W2 : W2 + 1])
-
-    other = moved(w_out, lambda x, h, y, z, c: (x, h + 1, y, z, c))
-    pair = jnp.stack(in_order(w_out, other, half == 1))
-    pair, keys = lax.optimization_barrier((pair, keys))
+    pair, over_core = lax.optimization_barrier((pair, over_core))
     from_x = [pair] + [
         moved(pair, lambda x, h, y, z, c, d=d: (x - d, h, y, z, c)) for d in (1, 2, 3)
     ]
-    attended = attention(
-        origin.reshape(1), queries, keys, values, near_keys, near_values
-    )
-
+
+    attended = attention(jnp.stack([seq, c]), queries, over_z, over_core)
     attended, from_x = lax.optimization_barrier((attended, from_x))
 
+    beside = moved(attended, lambda x, h, y, z, c: (x, h, y, z ^ 1, c))
+    attended = jnp.stack([attended, beside])
     from_y = [attended] + [
         moved(attended, lambda x, h, y, z, c, d=d: (x, h, y - d, z, c)) for d in (1, 2, 3)
     ]
-    twice = jnp.concatenate(from_y + from_y[:3])
-    tokens = lax.dynamic_slice_in_dim(twice, (2 * c - y) % YS * rows, YS * rows, 0)
-    twice = jnp.concatenate(from_x + from_x[:3])
-    columns = lax.dynamic_slice_in_dim(twice, (XS - x) % XS * HS, XS * HS, 0)
-    count = YS // 2 * rows
-    product = functools.partial(
-        jnp.einsum, "tk,nkc->ntc", preferred_element_type=jnp.float32
-    )
-    away = product(tokens[count:], columns).astype(jnp.bfloat16)
-    came = moved(away, lambda x, h, y, z, c: (x, h, y, z, 1 - c))
-    kept = (product(tokens[:count], columns) + came.astype(jnp.float32)).astype(jnp.bfloat16)
-    groups = [[z * CS + core for z in range(ZS)] for core in range(CS)]
+    sums = project(jnp.stack([x, y, c]), from_y, from_x)
+    came = moved(sums[1], lambda x, h, y, z, c: (x, h, y, z, 1 - c))
+    kept = (sums[0].astype(jnp.float32) + came.astype(jnp.float32)).astype(jnp.bfloat16)
+    groups = [
+        [(2 * far + low) * CS + core for far in range(ZS // 2)]
+        for low in range(2)
+        for core in range(CS)
+    ]
     parts = lax.all_to_all(kept, "head", 0, 0, axis_index_groups=groups, tiled=True)
     summed = jnp.sum(parts.astype(jnp.float32), axis=0).astype(jnp.bfloat16)
-    summed = summed.reshape(YS // 2, rows, summed.shape[-1])
     odd = y % 2 == 1
     sent = in_order(summed[0], summed[1], odd)
     landed = [

time: 226 us -> 220 us (0.973); the launches traced: 225 us -> 217 us
  starting transfers between devices: 87.2 us -> 143 us
  blocking collectives: 40.4 us -> 0 us
  waiting for transfers between devices: 69.8 us -> 47.2 us
  Pallas kernels: 17.6 us -> 21.4 us
  local copies, waits for them, and re-layouts: 5.21 us -> 1.94 us
  matrix products: 2.48 us -> 0 us
    ppermute x10 -> x13, starting transfers between devices: 58.2 us -> 103 us  [moved(): return lax.ppermute(value, BOTH, pairs)]
    all_gather x1 -> x0, blocking collectives: 40.4 us -> none  [per_device(): gathered = lax.all_gather(mine, 'head', axis=1, tiled=True)]
    all_to_all x1, waiting for transfers between devices: 50.8 us -> 28.2 us  [per_device(): lax.all_to_all(kept, 'head', 0, 0, axis_index_groups=groups, tiled=True)]
    all_to_all x0 -> x1, starting transfers between devices: none -> 9.94 us  [per_device(): lax.all_to_all(mine, 'head', 0, 0, axis_index_groups=lines, tiled=True)]
    pallas_call x0 -> x2, Pallas kernels: none -> 3.3 us  [the longest x1 1.81 us: project(): pl.pallas_call(project_kernel, out_shape=jax.ShapeDtypeStruct((2, XS, YS...]
    dot_general x2 -> x0, matrix products: 2.48 us -> none  [the longest x1 1.72 us: per_device(): product(tokens[:count], columns) + came.astype(jnp.float32)]
    ppermute x10 -> x13, waiting for transfers between devices: 18.4 us -> 18.4 us  [moved(): return lax.ppermute(value, BOTH, pairs)]
  transfers between devices with their start and end apart: 15 -> 19, of which waited for: 8 -> 9; matrix products, arithmetic and copies ran while one was open for 2% -> 0% of each run, Pallas kernels for 8% -> 8%
where the time goes in v2:
time: 220 us; the launch traced here: 217 us
  starting transfers between devices  143 us (65%)
  waiting for transfers between devices  47.2 us (21%)
  Pallas kernels  21.4 us (10%)
  other arithmetic  2.7 us (1%)
    ppermute x13, starting transfers between devices, moved(): return lax.ppermute(value, BOTH, pairs)  103 us
    all_to_all x1, waiting for transfers between devices, per_device(): lax.all_to_all(kept, 'head', 0, 0, axis_index_groups=groups, tiled=True)  28.2 us
    ppermute x4, starting transfers between devices, later(): lax.ppermute(value, 'seq', [(s, s + steps) for s in range(count - steps)])  26.1 us
    ppermute x13, waiting for transfers between devices, moved(): return lax.ppermute(value, BOTH, pairs)  18.4 us
    pallas_call x1, Pallas kernels, attention(): pl.pallas_call(functools.partial(attention_kernel, tokens=16), out_shape=...  18.1 us
    all_to_all x1, starting transfers between devices, per_device(): lax.all_to_all(mine, 'head', 0, 0, axis_index_groups=lines, tiled=True)  9.94 us
  transfers between devices with their start and end apart: 19, of which 9 were waited for; matrix products, arithmetic and copies ran while one was open for 0% of the time, Pallas kernels for 8%

profile of v2, /device:TPU:1, one launch (start us, length us, event | category | flops | bytes accessed | tf_op | source)
XLA Modules:
  0.0 216.7 jit_solution(3291848696983904031)
XLA Ops:
  0.7 0.7 pad_maximum_fusion.3
  1.4 4.0 %collective-permute-start = (bf16[4,8,128]{2,1,0:T(8,128)(2,1)S(1)}, bf16[4,8,128]{2,1,0:T(8,128)(2,1)S(1)}, u32[]{:S(2)}, u32[]{:S(2)}) collective-permute-start(bf16[4,8,128]{2,1,0:T(8,128)(2,1)S(1)} %pad_maximum_fusion.3), channel_id=1, source_target_pairs={{0,16},{16,32},{32,48},{48,64},{64,80},{80,96},{96,112},{112,128},... | collective-permute-start | bytes 24584 | tf_op jit(solution)/shard_map/ppermute | solution.py:38
  5.4 15.4 %collective-permute-start.3 = (bf16[2,8,128]{2,1,0:T(8,128)(2,1)S(1)}, bf16[2,8,128]{2,1,0:T(8,128)(2,1)S(1)}, u32[]{:S(2)}, u32[]{:S(2)}) collective-permute-start(bf16[2,8,128]{2,1,0:T(8,128)(2,1)S(1)} %pad_maximum_fusion.4), channel_id=1, source_target_pairs={{0,64},{16,80},{32,96},{48,112},{64,128},{80,144},{96,160},{112,17... | collective-permute-start | bytes 12296 | tf_op jit(solution)/shard_map/ppermute | solution.py:38
  20.9 3.4 %collective-permute-start.2 = (bf16[2,8,128]{2,1,0:T(8,128)(2,1)S(1)}, bf16[2,8,128]{2,1,0:T(8,128)(2,1)S(1)}, u32[]{:S(2)}, u32[]{:S(2)}) collective-permute-start(bf16[2,8,128]{2,1,0:T(8,128)(2,1)S(1)} %pad_maximum_fusion.4), channel_id=1, source_target_pairs={{0,48},{16,64},{32,80},{48,96},{64,112},{80,128},{96,144},{112,160... | collective-permute-start | bytes 12296 | tf_op jit(solution)/shard_map/ppermute | solution.py:38
  24.3 3.3 %collective-permute-start.1 = (bf16[2,8,128]{2,1,0:T(8,128)(2,1)S(1)}, bf16[2,8,128]{2,1,0:T(8,128)(2,1)S(1)}, u32[]{:S(2)}, u32[]{:S(2)}) collective-permute-start(bf16[2,8,128]{2,1,0:T(8,128)(2,1)S(1)} %pad_maximum_fusion.4), channel_id=1, source_target_pairs={{0,32},{16,48},{32,64},{48,80},{64,96},{80,112},{96,128},{112,144}... | collective-permute-start | bytes 12296 | tf_op jit(solution)/shard_map/ppermute | solution.py:38
  27.6 0.7 collective-permute-done.1.refs_5_
  29.5 1.5 shard_map.64
  31.0 9.9 %all-to-all-start = ((bf16[8,14,8,128]{3,2,1,0:T(8,128)(2,1)}), bf16[8,14,8,128]{3,2,1,0:T(8,128)(2,1)S(1)}, u32[]{:S(2)}, u32[]{:S(2)}) async-start(bf16[8,14,8,128]{3,2,1,0:T(8,128)(2,1)} %shard_map.64), calls=%async_computation | async-start | bytes 458752 | tf_op jit(solution)/shard_map/all_to_all | solution.py:217
  40.9 19.1 %collective-permute-start.4 = (bf16[512,256]{1,0:T(8,128)(2,1)S(1)}, bf16[512,256]{1,0:T(8,128)(2,1)S(1)}, u32[]{:S(2)}, u32[]{:S(2)}) collective-permute-start(bf16[512,256]{1,0:T(8,128)(2,1)S(1)} %copy-done.1), channel_id=1, source_target_pairs={{0,64},{1,65},{2,0},{3,1},{4,68},{5,69},{6,4},{7,5},{8,72},{9,73},... | collective-permute-start | bytes 786440 | tf_op jit(solution)/shard_map/ppermute | solution.py:33
  60.0 0.7 collective-permute-start.5
  60.8 5.1 %collective-permute-start.6 = (bf16[8,14,8,128]{3,2,1,0:T(8,128)(2,1)S(1)}, bf16[8,14,8,128]{3,2,1,0:T(8,128)(2,1)S(1)}, u32[]{:S(2)}, u32[]{:S(2)}) collective-permute-start(bf16[8,14,8,128]{3,2,1,0:T(8,128)(2,1)S(1)} %all-to-all-done.mine_ref), channel_id=1, source_target_pairs={{0,1},{1,0},{2,3},{3,2},{4,5},{5,4},{6,7},{7,6},{8,9},{9,8},{10,11... | collective-permute-start | bytes 688136 | tf_op jit(solution)/shard_map/ppermute | solution.py:33
  66.1 0.9 collective-permute-done.6.other_ref
  67.0 15.0 %collective-permute-start.9 = (bf16[2,512,256]{2,1,0:T(8,128)(2,1)S(1)}, bf16[2,512,256]{2,1,0:T(8,128)(2,1)S(1)}, u32[]{:S(2)}, u32[]{:S(2)}) collective-permute-start(bf16[2,512,256]{2,1,0:T(8,128)(2,1)S(1)} %pad_maximum_fusion.refs_4_), channel_id=1, source_target_pairs={{0,128},{1,129},{2,130},{3,131},{4,132},{5,133},{6,134},{7,135},{8... | collective-permute-start | bytes 1572872 | tf_op jit(solution)/shard_map/ppermute | solution.py:33
  82.1 3.2 %collective-permute-start.8 = (bf16[2,512,256]{2,1,0:T(8,128)(2,1)S(1)}, bf16[2,512,256]{2,1,0:T(8,128)(2,1)S(1)}, u32[]{:S(2)}, u32[]{:S(2)}) collective-permute-start(bf16[2,512,256]{2,1,0:T(8,128)(2,1)S(1)} %pad_maximum_fusion.refs_4_), channel_id=1, source_target_pairs={{0,256},{1,257},{2,258},{3,259},{4,260},{5,261},{6,262},{7,263},{8... | collective-permute-start | bytes 1572872 | tf_op jit(solution)/shard_map/ppermute | solution.py:33
  85.2 4.0 %collective-permute-start.7 = (bf16[2,512,256]{2,1,0:T(8,128)(2,1)S(1)}, bf16[2,512,256]{2,1,0:T(8,128)(2,1)S(1)}, u32[]{:S(2)}, u32[]{:S(2)}) collective-permute-start(bf16[2,512,256]{2,1,0:T(8,128)(2,1)S(1)} %pad_maximum_fusion.refs_4_), channel_id=1, source_target_pairs={{0,384},{1,385},{2,386},{3,387},{4,388},{5,389},{6,390},{7,391},{8... | collective-permute-start | bytes 1572872 | tf_op jit(solution)/shard_map/ppermute | solution.py:33
  89.2 18.1 %shard_map.65 = bf16[128,512]{1,0:T(8,128)(2,1)S(1)} custom-call(s32[2]{0:T(128)S(1)} %pad_add_fusion.1.place, bf16[128,512]{1,0:T(8,128)(2,1)S(1)} %copy-done, bf16[8,14,8,128]{3,2,1,0:T(8,128)(2,1)S(1)} %all-to-all-done.mine_ref, bf16[8,14,8,128]{3,2,1,0:T(8,128)(2,1)S(1)} %collective-permute-done.6.other_ref), custom_call_target="tpu_custom_call" | custom-call | flops 20000000000 | bytes 1048576 | tf_op jit(solution)/shard_map/pallas_call | solution.py:123
  107.8 34.7 %collective-permute-start.10 = (bf16[128,512]{1,0:T(8,128)(2,1)S(1)}, bf16[128,512]{1,0:T(8,128)(2,1)S(1)}, u32[]{:S(2)}, u32[]{:S(2)}) collective-permute-start(bf16[128,512]{1,0:T(8,128)(2,1)S(1)} %shard_map.65), channel_id=1, source_target_pairs={{0,2},{1,3},{2,0},{3,1},{4,6},{5,7},{6,4},{7,5},{8,10},{9,11},{10,... | collective-permute-start | bytes 393224 | tf_op jit(solution)/shard_map/ppermute | solution.py:33
  142.5 2.3 %collective-permute-done.10 = bf16[128,512]{1,0:T(8,128)(2,1)S(1)} collective-permute-done((bf16[128,512]{1,0:T(8,128)(2,1)S(1)}, bf16[128,512]{1,0:T(8,128)(2,1)S(1)}, u32[]{:S(2)}, u32[]{:S(2)}) %collective-permute-start.10) | collective-permute-done | bytes 131104 | tf_op jit(solution)/shard_map/ppermute | solution.py:33
  144.9 2.0 collective-permute-start.13
  146.9 1.9 collective-permute-start.12
  148.8 4.5 %collective-permute-start.11 = (bf16[2,128,512]{2,1,0:T(8,128)(2,1)S(1)}, bf16[2,128,512]{2,1,0:T(8,128)(2,1)S(1)}, u32[]{:S(2)}, u32[]{:S(2)}) collective-permute-start(bf16[2,128,512]{2,1,0:T(8,128)(2,1)S(1)} %pad_maximum_fusion.1.refs_0_), channel_id=1, source_target_pairs={{0,48},{1,49},{2,50},{3,51},{4,52},{5,53},{6,54},{7,55},{8,56},{9,... | collective-permute-start | bytes 786440 | tf_op jit(solution)/shard_map/ppermute | solution.py:33
  153.5 3.2 %collective-permute-done.13.refs_3_ = bf16[2,128,512]{2,1,0:T(8,128)(2,1)S(1)} collective-permute-done((bf16[2,128,512]{2,1,0:T(8,128)(2,1)S(1)}, bf16[2,128,512]{2,1,0:T(8,128)(2,1)S(1)}, u32[]{:S(2)}, u32[]{:S(2)}) %collective-permute-start.13) | collective-permute-done | bytes 262176 | tf_op jit(solution)/shard_map/ppermute | solution.py:33
  156.7 4.7 %collective-permute-done.11.refs_1_ = bf16[2,128,512]{2,1,0:T(8,128)(2,1)S(1)} collective-permute-done((bf16[2,128,512]{2,1,0:T(8,128)(2,1)S(1)}, bf16[2,128,512]{2,1,0:T(8,128)(2,1)S(1)}, u32[]{:S(2)}, u32[]{:S(2)}) %collective-permute-start.11) | collective-permute-done | bytes 262176 | tf_op jit(solution)/shard_map/ppermute | solution.py:33
  161.4 1.8 shard_map.66
  163.2 5.4 %collective-permute-start.14 = (bf16[4,2,128,256]{3,2,1,0:T(8,128)(2,1)S(1)}, bf16[4,2,128,256]{3,2,1,0:T(8,128)(2,1)S(1)}, u32[]{:S(2)}, u32[]{:S(2)}) collective-permute-start(bf16[4,2,128,256]{3,2,1,0:T(8,128)(2,1)S(1)} %slice_bitcast_fusion), channel_id=1, source_target_pairs={{0,1},{1,0},{2,3},{3,2},{4,5},{5,4},{6,7},{7,6},{8,9},{9,8},{10,11... | collective-permute-start | bytes 1572872 | tf_op jit(solution)/shard_map/ppermute | solution.py:33
  168.6 1.5 collective-permute-done.14
  170.1 1.0 fusion
  171.1 3.8 %all-to-all-start.1 = ((bf16[4,2,128,256]{3,2,1,0:T(8,128)(2,1)}), bf16[4,2,128,256]{3,2,1,0:T(8,128)(2,1)S(1)}, u32[]{:S(2)}, u32[]{:S(2)}) async-start(bf16[4,2,128,256]{3,2,1,0:T(8,128)(2,1)} %fusion), calls=%async_computation.1 | async-start | bytes 1048576 | tf_op jit(solution)/shard_map/all_to_all | solution.py:245
  174.9 28.2 %all-to-all-done.1 = bf16[4,2,128,256]{3,2,1,0:T(8,128)(2,1)S(1)} async-done(((bf16[4,2,128,256]{3,2,1,0:T(8,128)(2,1)}), bf16[4,2,128,256]{3,2,1,0:T(8,128)(2,1)S(1)}, u32[]{:S(2)}, u32[]{:S(2)}) %all-to-all-start.1) | async-done | bytes 524320 | tf_op jit(solution)/shard_map/all_to_all | solution.py:245
  203.2 5.7 %collective-permute-start.15 = (bf16[128,256]{1,0:T(8,128)(2,1)S(1)}, bf16[128,256]{1,0:T(8,128)(2,1)S(1)}, u32[]{:S(2)}, u32[]{:S(2)}) collective-permute-start(bf16[128,256]{1,0:T(8,128)(2,1)S(1)} %get-tuple-element.23), channel_id=1, source_target_pairs={{0,16},{1,48},{2,18},{3,50},{4,20},{5,52},{6,22},{7,54},{8,24},{9,... | collective-permute-start | bytes 196616 | tf_op jit(solution)/shard_map/ppermute | solution.py:33
  208.9 1.9 collective-permute-start.16
  210.8 5.2 %collective-permute-done.16 = bf16[128,256]{1,0:T(8,128)(2,1)S(1)} collective-permute-done((bf16[128,256]{1,0:T(8,128)(2,1)S(1)}, bf16[128,256]{1,0:T(8,128)(2,1)S(1)}, u32[]{:S(2)}, u32[]{:S(2)}) %collective-permute-start.16) | collective-permute-done | bytes 65568 | tf_op jit(solution)/shard_map/ppermute | solution.py:33
  (40 shorter events, 3.5 us)
Async XLA Ops:
  0.0 0.7 copy-start.4
  0.0 0.7 copy-start.3
  0.0 0.7 copy-start.2
  1.4 26.9 %collective-permute-start = (bf16[4,8,128]{2,1,0:T(8,128)(2,1)S(1)}, bf16[4,8,128]{2,1,0:T(8,128)(2,1)S(1)}, u32[]{:S(2)}, u32[]{:S(2)}) collective-permute-start(bf16[4,8,128]{2,1,0:T(8,128)(2,1)S(1)} %pad_maximum_fusion.3), channel_id=1, source_target_pairs={{0,16},{16,32},{32,48},{48,64},{64,80},{80,96},{96,112},{112,128},... | collective-permute-start | bytes 24584 | tf_op jit(solution)/shard_map/ppermute | solution.py:38
  5.4 22.1 %collective-permute-start.3 = (bf16[2,8,128]{2,1,0:T(8,128)(2,1)S(1)}, bf16[2,8,128]{2,1,0:T(8,128)(2,1)S(1)}, u32[]{:S(2)}, u32[]{:S(2)}) collective-permute-start(bf16[2,8,128]{2,1,0:T(8,128)(2,1)S(1)} %pad_maximum_fusion.4), channel_id=1, source_target_pairs={{0,64},{16,80},{32,96},{48,112},{64,128},{80,144},{96,160},{112,17... | collective-permute-start | bytes 12296 | tf_op jit(solution)/shard_map/ppermute | solution.py:38
  20.9 6.7 %collective-permute-start.2 = (bf16[2,8,128]{2,1,0:T(8,128)(2,1)S(1)}, bf16[2,8,128]{2,1,0:T(8,128)(2,1)S(1)}, u32[]{:S(2)}, u32[]{:S(2)}) collective-permute-start(bf16[2,8,128]{2,1,0:T(8,128)(2,1)S(1)} %pad_maximum_fusion.4), channel_id=1, source_target_pairs={{0,48},{16,64},{32,80},{48,96},{64,112},{80,128},{96,144},{112,160... | collective-permute-start | bytes 12296 | tf_op jit(solution)/shard_map/ppermute | solution.py:38
  24.3 4.0 %collective-permute-start.1 = (bf16[2,8,128]{2,1,0:T(8,128)(2,1)S(1)}, bf16[2,8,128]{2,1,0:T(8,128)(2,1)S(1)}, u32[]{:S(2)}, u32[]{:S(2)}) collective-permute-start(bf16[2,8,128]{2,1,0:T(8,128)(2,1)S(1)} %pad_maximum_fusion.4), channel_id=1, source_target_pairs={{0,32},{16,48},{32,64},{48,80},{64,96},{80,112},{96,128},{112,144}... | collective-permute-start | bytes 12296 | tf_op jit(solution)/shard_map/ppermute | solution.py:38
  27.5 0.7 copy-start.6
  27.6 0.7 copy-start.7
  28.3 0.6 copy-start.8
  28.9 0.6 copy-start.5
  31.0 9.9 %copy-start.1 = (bf16[512,256]{1,0:T(8,128)(2,1)S(1)}, bf16[512,256]{1,0:T(8,128)(2,1)}, u32[]{:S(2)}) copy-start(bf16[512,256]{1,0:T(8,128)(2,1)} %param.11) | copy-start | bytes 786436
  31.0 29.8 %all-to-all-start = ((bf16[8,14,8,128]{3,2,1,0:T(8,128)(2,1)}), bf16[8,14,8,128]{3,2,1,0:T(8,128)(2,1)S(1)}, u32[]{:S(2)}, u32[]{:S(2)}) async-start(bf16[8,14,8,128]{3,2,1,0:T(8,128)(2,1)} %shard_map.64), calls=%async_computation | async-start | bytes 458752 | tf_op jit(solution)/shard_map/all_to_all | solution.py:217
  40.9 25.0 %collective-permute-start.4 = (bf16[512,256]{1,0:T(8,128)(2,1)S(1)}, bf16[512,256]{1,0:T(8,128)(2,1)S(1)}, u32[]{:S(2)}, u32[]{:S(2)}) collective-permute-start(bf16[512,256]{1,0:T(8,128)(2,1)S(1)} %copy-done.1), channel_id=1, source_target_pairs={{0,64},{1,65},{2,0},{3,1},{4,68},{5,69},{6,4},{7,5},{8,72},{9,73},... | collective-permute-start | bytes 786440 | tf_op jit(solution)/shard_map/ppermute | solution.py:33
  60.0 6.0 %collective-permute-start.5 = (bf16[512,256]{1,0:T(8,128)(2,1)S(1)}, bf16[512,256]{1,0:T(8,128)(2,1)S(1)}, u32[]{:S(2)}, u32[]{:S(2)}) collective-permute-start(bf16[512,256]{1,0:T(8,128)(2,1)S(1)} %copy-done.1), channel_id=1, source_target_pairs={{2,64},{3,65},{6,68},{7,69},{10,72},{11,73},{14,76},{15,77},{18,80... | collective-permute-start | bytes 786440 | tf_op jit(solution)/shard_map/ppermute | solution.py:33
  60.8 6.2 %collective-permute-start.6 = (bf16[8,14,8,128]{3,2,1,0:T(8,128)(2,1)S(1)}, bf16[8,14,8,128]{3,2,1,0:T(8,128)(2,1)S(1)}, u32[]{:S(2)}, u32[]{:S(2)}) collective-permute-start(bf16[8,14,8,128]{3,2,1,0:T(8,128)(2,1)S(1)} %all-to-all-done.mine_ref), channel_id=1, source_target_pairs={{0,1},{1,0},{2,3},{3,2},{4,5},{5,4},{6,7},{7,6},{8,9},{9,8},{10,11... | collective-permute-start | bytes 688136 | tf_op jit(solution)/shard_map/ppermute | solution.py:33
  66.0 23.2 %copy-start = (bf16[128,512]{1,0:T(8,128)(2,1)S(1)}, bf16[128,512]{1,0:T(8,128)(2,1)}, u32[]{:S(2)}) copy-start(bf16[128,512]{1,0:T(8,128)(2,1)} %q_ref.1) | copy-start | bytes 393220
  67.0 40.3 %collective-permute-start.9 = (bf16[2,512,256]{2,1,0:T(8,128)(2,1)S(1)}, bf16[2,512,256]{2,1,0:T(8,128)(2,1)S(1)}, u32[]{:S(2)}, u32[]{:S(2)}) collective-permute-start(bf16[2,512,256]{2,1,0:T(8,128)(2,1)S(1)} %pad_maximum_fusion.refs_4_), channel_id=1, source_target_pairs={{0,128},{1,129},{2,130},{3,131},{4,132},{5,133},{6,134},{7,135},{8... | collective-permute-start | bytes 1572872 | tf_op jit(solution)/shard_map/ppermute | solution.py:33
  82.1 25.3 %collective-permute-start.8 = (bf16[2,512,256]{2,1,0:T(8,128)(2,1)S(1)}, bf16[2,512,256]{2,1,0:T(8,128)(2,1)S(1)}, u32[]{:S(2)}, u32[]{:S(2)}) collective-permute-start(bf16[2,512,256]{2,1,0:T(8,128)(2,1)S(1)} %pad_maximum_fusion.refs_4_), channel_id=1, source_target_pairs={{0,256},{1,257},{2,258},{3,259},{4,260},{5,261},{6,262},{7,263},{8... | collective-permute-start | bytes 1572872 | tf_op jit(solution)/shard_map/ppermute | solution.py:33
  85.2 22.6 %collective-permute-start.7 = (bf16[2,512,256]{2,1,0:T(8,128)(2,1)S(1)}, bf16[2,512,256]{2,1,0:T(8,128)(2,1)S(1)}, u32[]{:S(2)}, u32[]{:S(2)}) collective-permute-start(bf16[2,512,256]{2,1,0:T(8,128)(2,1)S(1)} %pad_maximum_fusion.refs_4_), channel_id=1, source_target_pairs={{0,384},{1,385},{2,386},{3,387},{4,388},{5,389},{6,390},{7,391},{8... | collective-permute-start | bytes 1572872 | tf_op jit(solution)/shard_map/ppermute | solution.py:33
  107.8 37.0 %collective-permute-start.10 = (bf16[128,512]{1,0:T(8,128)(2,1)S(1)}, bf16[128,512]{1,0:T(8,128)(2,1)S(1)}, u32[]{:S(2)}, u32[]{:S(2)}) collective-permute-start(bf16[128,512]{1,0:T(8,128)(2,1)S(1)} %shard_map.65), channel_id=1, source_target_pairs={{0,2},{1,3},{2,0},{3,1},{4,6},{5,7},{6,4},{7,5},{8,10},{9,11},{10,... | collective-permute-start | bytes 393224 | tf_op jit(solution)/shard_map/ppermute | solution.py:33
  144.9 11.8 %collective-permute-start.13 = (bf16[2,128,512]{2,1,0:T(8,128)(2,1)S(1)}, bf16[2,128,512]{2,1,0:T(8,128)(2,1)S(1)}, u32[]{:S(2)}, u32[]{:S(2)}) collective-permute-start(bf16[2,128,512]{2,1,0:T(8,128)(2,1)S(1)} %pad_maximum_fusion.1.refs_0_), channel_id=1, source_target_pairs={{0,16},{1,17},{2,18},{3,19},{4,20},{5,21},{6,22},{7,23},{8,24},{9,... | collective-permute-start | bytes 786440 | tf_op jit(solution)/shard_map/ppermute | solution.py:33
  146.9 9.8 %collective-permute-start.12 = (bf16[2,128,512]{2,1,0:T(8,128)(2,1)S(1)}, bf16[2,128,512]{2,1,0:T(8,128)(2,1)S(1)}, u32[]{:S(2)}, u32[]{:S(2)}) collective-permute-start(bf16[2,128,512]{2,1,0:T(8,128)(2,1)S(1)} %pad_maximum_fusion.1.refs_0_), channel_id=1, source_target_pairs={{0,32},{1,33},{2,34},{3,35},{4,36},{5,37},{6,38},{7,39},{8,40},{9,... | collective-permute-start | bytes 786440 | tf_op jit(solution)/shard_map/ppermute | solution.py:33
  148.8 12.5 %collective-permute-start.11 = (bf16[2,128,512]{2,1,0:T(8,128)(2,1)S(1)}, bf16[2,128,512]{2,1,0:T(8,128)(2,1)S(1)}, u32[]{:S(2)}, u32[]{:S(2)}) collective-permute-start(bf16[2,128,512]{2,1,0:T(8,128)(2,1)S(1)} %pad_maximum_fusion.1.refs_0_), channel_id=1, source_target_pairs={{0,48},{1,49},{2,50},{3,51},{4,52},{5,53},{6,54},{7,55},{8,56},{9,... | collective-permute-start | bytes 786440 | tf_op jit(solution)/shard_map/ppermute | solution.py:33
  163.2 6.9 %collective-permute-start.14 = (bf16[4,2,128,256]{3,2,1,0:T(8,128)(2,1)S(1)}, bf16[4,2,128,256]{3,2,1,0:T(8,128)(2,1)S(1)}, u32[]{:S(2)}, u32[]{:S(2)}) collective-permute-start(bf16[4,2,128,256]{3,2,1,0:T(8,128)(2,1)S(1)} %slice_bitcast_fusion), channel_id=1, source_target_pairs={{0,1},{1,0},{2,3},{3,2},{4,5},{5,4},{6,7},{7,6},{8,9},{9,8},{10,11... | collective-permute-start | bytes 1572872 | tf_op jit(solution)/shard_map/ppermute | solution.py:33
  171.1 32.0 %all-to-all-start.1 = ((bf16[4,2,128,256]{3,2,1,0:T(8,128)(2,1)}), bf16[4,2,128,256]{3,2,1,0:T(8,128)(2,1)S(1)}, u32[]{:S(2)}, u32[]{:S(2)}) async-start(bf16[4,2,128,256]{3,2,1,0:T(8,128)(2,1)} %fusion), calls=%async_computation.1 | async-start | bytes 1048576 | tf_op jit(solution)/shard_map/all_to_all | solution.py:245
  203.2 7.7 %collective-permute-start.15 = (bf16[128,256]{1,0:T(8,128)(2,1)S(1)}, bf16[128,256]{1,0:T(8,128)(2,1)S(1)}, u32[]{:S(2)}, u32[]{:S(2)}) collective-permute-start(bf16[128,256]{1,0:T(8,128)(2,1)S(1)} %get-tuple-element.23), channel_id=1, source_target_pairs={{0,16},{1,48},{2,18},{3,50},{4,20},{5,52},{6,22},{7,54},{8,24},{9,... | collective-permute-start | bytes 196616 | tf_op jit(solution)/shard_map/ppermute | solution.py:33
  208.9 7.1 %collective-permute-start.16 = (bf16[128,256]{1,0:T(8,128)(2,1)S(1)}, bf16[128,256]{1,0:T(8,128)(2,1)S(1)}, u32[]{:S(2)}, u32[]{:S(2)}) collective-permute-start(bf16[128,256]{1,0:T(8,128)(2,1)S(1)} %get-tuple-element.24), channel_id=1, source_target_pairs={{0,0},{1,32},{2,2},{3,34},{4,4},{5,36},{6,6},{7,38},{8,8},{9,40},{... | collective-permute-start | bytes 196616 | tf_op jit(solution)/shard_map/ppermute | solution.py:33

commit v3 on v2

--- a/solution.py
+++ b/solution.py
@@ -200,26 +200,51 @@
     x, half, y = seq // (HS * YS), seq // YS % HS, seq % YS
     z, c = head // CS, head % CS
 
-    def first_hop(x, h, y, z, c):
-        return (x, h, y, z ^ 1, c) if h != z % 2 else (x, h + 1, y, z, c)
-
-    def second_hop(x, h, y, z, c):
-        return (x, h + 1, y, z ^ 1, c) if h != z % 2 else None
-
-    one_way = moved(w_out, first_hop)
-    other_way = moved(w_out, second_hop)
+    def along(steps):
+        def target(x, h, y, z, c):
+            to = (h * ZS + z + steps) % (HS * ZS)
+            return (x, to // ZS, y, to % ZS, c)
+
+        return target
+
+    def kept_here(h, z):
+        return h == z % 2
+
+    def first_up(x, h, y, z, c):
+        return along(4)(x, h, y, z, c) if kept_here(h, z) else None
+
+    def first_down(x, h, y, z, c):
+        return None if kept_here(h, z) else along(-4)(x, h, y, z, c)
+
+    def second_up(x, h, y, z, c):
+        spot = (h * ZS + z - 4) % (HS * ZS)
+        return along(4)(x, h, y, z, c) if kept_here(spot // ZS, spot % ZS) else None
+
+    def second_down(x, h, y, z, c):
+        spot = (h * ZS + z + 4) % (HS * ZS)
+        if kept_here(spot // ZS, spot % ZS):
+            return None
+        return along(-5 if spot < ZS else -3)(x, h, y, z, c)
+
+    def near(x, h, y, z, c):
+        return None if kept_here(h, z) else (x, h, y, z ^ 1, c)
+
+    upward, downward = moved(w_out, first_up), moved(w_out, first_down)
 
     piece = jnp.stack([long_keys, long_values, short_keys, short_values])
     before = later(piece, 1)
     older = [later(piece[:2], steps) for steps in range(2, W1 // rows + 1)]
     mine = pack((long_keys, long_values, short_keys, short_values), before, older)
     lines = [[z * CS + core for z in range(ZS)] for core in range(CS)]
+    mine, upward, downward = lax.optimization_barrier((mine, upward, downward))
+    upward, downward = moved(upward, second_up), moved(downward, second_down)
+    beside = moved(w_out, near)
     over_z = lax.all_to_all(mine, "head", 0, 0, axis_index_groups=lines, tiled=True)
     over_core = moved(over_z, lambda x, h, y, z, c: (x, h, y, z, 1 - c))
 
     near_by = half == z % 2
     pair = jnp.stack(
-        [jnp.where(near_by, w_out, one_way), jnp.where(near_by, one_way, other_way)]
+        [jnp.where(near_by, w_out, upward), jnp.where(near_by, beside, downward)]
     )
     pair, over_core = lax.optimization_barrier((pair, over_core))
     from_x = [pair] + [

time: 220 us -> 203 us (0.923)
  starting transfers between devices: 143 us -> 120 us
  waiting for transfers between devices: 47.2 us -> 53.6 us
    ppermute x13 -> x16, starting transfers between devices: 103 us -> 75.8 us  [moved(): return lax.ppermute(value, BOTH, pairs)]
    all_to_all x1, waiting for transfers between devices: 0.01 us -> 8.43 us  [per_device(): lax.all_to_all(mine, 'head', 0, 0, axis_index_groups=lines, tiled=True)]
    all_to_all x1, starting transfers between devices: 3.8 us -> 11.1 us  [per_device(): lax.all_to_all(kept, 'head', 0, 0, axis_index_groups=groups, tiled=True)]
    ppermute x4, starting transfers between devices: 26.1 us -> 22.9 us  [later(): lax.ppermute(value, 'seq', [(s, s + steps) for s in range(count - steps)])]
    ppermute x13 -> x16, waiting for transfers between devices: 18.4 us -> 15.5 us  [moved(): return lax.ppermute(value, BOTH, pairs)]
  transfers between devices with their start and end apart: 19 -> 22, of which waited for: 9 -> 11; matrix products, arithmetic and copies ran while one was open for 0% -> 0% of each run, Pallas kernels for 8% -> 10%
where the time goes in v3:
time: 203 us; the launch traced here: 199 us
  starting transfers between devices  120 us (59%)
  waiting for transfers between devices  53.6 us (26%)
  Pallas kernels  21.4 us (11%)
  other arithmetic  2.69 us (1%)
    ppermute x16, starting transfers between devices, moved(): return lax.ppermute(value, BOTH, pairs)  75.8 us
    all_to_all x1, waiting for transfers between devices, per_device(): lax.all_to_all(kept, 'head', 0, 0, axis_index_groups=groups, tiled=True)  28.9 us
    ppermute x4, starting transfers between devices, later(): lax.ppermute(value, 'seq', [(s, s + steps) for s in range(count - steps)])  22.9 us
    pallas_call x1, Pallas kernels, attention(): pl.pallas_call(functools.partial(attention_kernel, tokens=16), out_shape=...  18.1 us
    ppermute x16, waiting for transfers between devices, moved(): return lax.ppermute(value, BOTH, pairs)  15.5 us
    all_to_all x1, starting transfers between devices, per_device(): lax.all_to_all(kept, 'head', 0, 0, axis_index_groups=groups, tiled=True)  11.1 us
    all_to_all x1, starting transfers between devices, per_device(): lax.all_to_all(mine, 'head', 0, 0, axis_index_groups=lines, tiled=True)  10.1 us
    all_to_all x1, waiting for transfers between devices, per_device(): lax.all_to_all(mine, 'head', 0, 0, axis_index_groups=lines, tiled=True)  8.43 us
  transfers between devices with their start and end apart: 22, of which 11 were waited for; matrix products, arithmetic and copies ran while one was open for 0% of the time, Pallas kernels for 10%

profile of v3, /device:TPU:1, one launch (start us, length us, event | category | flops | bytes accessed | tf_op | source)
XLA Modules:
  0.0 199.3 jit_solution(7179942087492766723)
XLA Ops:
  0.0 0.8 collective-permute-start.5
  0.8 10.3 %collective-permute-start.4 = (bf16[512,256]{1,0:T(8,128)(2,1)}, bf16[512,256]{1,0:T(8,128)(2,1)S(1)}, u32[]{:S(2)}, u32[]{:S(2)}) collective-permute-start(bf16[512,256]{1,0:T(8,128)(2,1)} %param.11), channel_id=1, source_target_pairs={{0,8},{1,9},{4,12},{5,13},{8,64},{9,65},{12,68},{13,69},{16,24},{1... | collective-permute-start | bytes 786440 | tf_op jit(solution)/shard_map/ppermute | solution.py:33
  11.8 8.6 %collective-permute-start.3 = (bf16[2,8,128]{2,1,0:T(8,128)(2,1)S(1)}, bf16[2,8,128]{2,1,0:T(8,128)(2,1)S(1)}, u32[]{:S(2)}, u32[]{:S(2)}) collective-permute-start(bf16[2,8,128]{2,1,0:T(8,128)(2,1)S(1)} %pad_maximum_fusion.4), channel_id=1, source_target_pairs={{0,64},{16,80},{32,96},{48,112},{64,128},{80,144},{96,160},{112,17... | collective-permute-start | bytes 12296 | tf_op jit(solution)/shard_map/ppermute | solution.py:38
  20.5 3.2 %collective-permute-start = (bf16[4,8,128]{2,1,0:T(8,128)(2,1)S(1)}, bf16[4,8,128]{2,1,0:T(8,128)(2,1)S(1)}, u32[]{:S(2)}, u32[]{:S(2)}) collective-permute-start(bf16[4,8,128]{2,1,0:T(8,128)(2,1)S(1)} %pad_maximum_fusion.3), channel_id=1, source_target_pairs={{0,16},{16,32},{32,48},{48,64},{64,80},{80,96},{96,112},{112,128},... | collective-permute-start | bytes 24584 | tf_op jit(solution)/shard_map/ppermute | solution.py:38
  23.7 7.5 %collective-permute-start.2 = (bf16[2,8,128]{2,1,0:T(8,128)(2,1)S(1)}, bf16[2,8,128]{2,1,0:T(8,128)(2,1)S(1)}, u32[]{:S(2)}, u32[]{:S(2)}) collective-permute-start(bf16[2,8,128]{2,1,0:T(8,128)(2,1)S(1)} %pad_maximum_fusion.4), channel_id=1, source_target_pairs={{0,48},{16,64},{32,80},{48,96},{64,112},{80,128},{96,144},{112,160... | collective-permute-start | bytes 12296 | tf_op jit(solution)/shard_map/ppermute | solution.py:38
  31.3 3.6 %collective-permute-start.1 = (bf16[2,8,128]{2,1,0:T(8,128)(2,1)S(1)}, bf16[2,8,128]{2,1,0:T(8,128)(2,1)S(1)}, u32[]{:S(2)}, u32[]{:S(2)}) collective-permute-start(bf16[2,8,128]{2,1,0:T(8,128)(2,1)S(1)} %pad_maximum_fusion.4), channel_id=1, source_target_pairs={{0,32},{16,48},{32,64},{48,80},{64,96},{80,112},{96,128},{112,144}... | collective-permute-start | bytes 12296 | tf_op jit(solution)/shard_map/ppermute | solution.py:38
  36.8 1.5 shard_map.64
  38.3 10.1 %all-to-all-start = ((bf16[8,14,8,128]{3,2,1,0:T(8,128)(2,1)}), bf16[8,14,8,128]{3,2,1,0:T(8,128)(2,1)S(1)}, u32[]{:S(2)}, u32[]{:S(2)}) async-start(bf16[8,14,8,128]{3,2,1,0:T(8,128)(2,1)} %shard_map.64), calls=%async_computation | async-start | bytes 458752 | tf_op jit(solution)/shard_map/all_to_all | solution.py:242
  49.1 1.3 collective-permute-start.7
  51.2 8.4 %all-to-all-done.mine_ref = bf16[8,14,8,128]{3,2,1,0:T(8,128)(2,1)S(1)} async-done(((bf16[8,14,8,128]{3,2,1,0:T(8,128)(2,1)}), bf16[8,14,8,128]{3,2,1,0:T(8,128)(2,1)S(1)}, u32[]{:S(2)}, u32[]{:S(2)}) %all-to-all-start) | async-done | bytes 229408 | tf_op jit(solution)/shard_map/all_to_all | solution.py:242
  59.6 6.3 %collective-permute-start.9 = (bf16[8,14,8,128]{3,2,1,0:T(8,128)(2,1)S(1)}, bf16[8,14,8,128]{3,2,1,0:T(8,128)(2,1)S(1)}, u32[]{:S(2)}, u32[]{:S(2)}) collective-permute-start(bf16[8,14,8,128]{3,2,1,0:T(8,128)(2,1)S(1)} %all-to-all-done.mine_ref), channel_id=1, source_target_pairs={{0,1},{1,0},{2,3},{3,2},{4,5},{5,4},{6,7},{7,6},{8,9},{9,8},{10,11... | collective-permute-start | bytes 688136 | tf_op jit(solution)/shard_map/ppermute | solution.py:33
  66.1 1.0 collective-permute-done.9.other_ref
  67.0 15.6 %collective-permute-start.12 = (bf16[2,512,256]{2,1,0:T(8,128)(2,1)S(1)}, bf16[2,512,256]{2,1,0:T(8,128)(2,1)S(1)}, u32[]{:S(2)}, u32[]{:S(2)}) collective-permute-start(bf16[2,512,256]{2,1,0:T(8,128)(2,1)S(1)} %pad_maximum_fusion.refs_4_), channel_id=1, source_target_pairs={{0,128},{1,129},{2,130},{3,131},{4,132},{5,133},{6,134},{7,135},{8... | collective-permute-start | bytes 1572872 | tf_op jit(solution)/shard_map/ppermute | solution.py:33
  82.6 3.2 %collective-permute-start.11 = (bf16[2,512,256]{2,1,0:T(8,128)(2,1)S(1)}, bf16[2,512,256]{2,1,0:T(8,128)(2,1)S(1)}, u32[]{:S(2)}, u32[]{:S(2)}) collective-permute-start(bf16[2,512,256]{2,1,0:T(8,128)(2,1)S(1)} %pad_maximum_fusion.refs_4_), channel_id=1, source_target_pairs={{0,256},{1,257},{2,258},{3,259},{4,260},{5,261},{6,262},{7,263},{8... | collective-permute-start | bytes 1572872 | tf_op jit(solution)/shard_map/ppermute | solution.py:33
  85.8 4.0 %collective-permute-start.10 = (bf16[2,512,256]{2,1,0:T(8,128)(2,1)S(1)}, bf16[2,512,256]{2,1,0:T(8,128)(2,1)S(1)}, u32[]{:S(2)}, u32[]{:S(2)}) collective-permute-start(bf16[2,512,256]{2,1,0:T(8,128)(2,1)S(1)} %pad_maximum_fusion.refs_4_), channel_id=1, source_target_pairs={{0,384},{1,385},{2,386},{3,387},{4,388},{5,389},{6,390},{7,391},{8... | collective-permute-start | bytes 1572872 | tf_op jit(solution)/shard_map/ppermute | solution.py:33
  89.8 18.1 %shard_map.65 = bf16[128,512]{1,0:T(8,128)(2,1)S(1)} custom-call(s32[2]{0:T(128)S(1)} %pad_add_fusion.1.place, bf16[128,512]{1,0:T(8,128)(2,1)S(1)} %copy-done, bf16[8,14,8,128]{3,2,1,0:T(8,128)(2,1)S(1)} %all-to-all-done.mine_ref, bf16[8,14,8,128]{3,2,1,0:T(8,128)(2,1)S(1)} %collective-permute-done.9.other_ref), custom_call_target="tpu_custom_call" | custom-call | flops 20000000000 | bytes 1048576 | tf_op jit(solution)/shard_map/pallas_call | solution.py:123
  108.0 9.5 %collective-permute-start.13 = (bf16[128,512]{1,0:T(8,128)(2,1)S(1)}, bf16[128,512]{1,0:T(8,128)(2,1)S(1)}, u32[]{:S(2)}, u32[]{:S(2)}) collective-permute-start(bf16[128,512]{1,0:T(8,128)(2,1)S(1)} %shard_map.65), channel_id=1, source_target_pairs={{0,2},{1,3},{2,0},{3,1},{4,6},{5,7},{6,4},{7,5},{8,10},{9,11},{10,... | collective-permute-start | bytes 393224 | tf_op jit(solution)/shard_map/ppermute | solution.py:33
  117.5 2.3 %collective-permute-done.13 = bf16[128,512]{1,0:T(8,128)(2,1)S(1)} collective-permute-done((bf16[128,512]{1,0:T(8,128)(2,1)S(1)}, bf16[128,512]{1,0:T(8,128)(2,1)S(1)}, u32[]{:S(2)}, u32[]{:S(2)}) %collective-permute-start.13) | collective-permute-done | bytes 131104 | tf_op jit(solution)/shard_map/ppermute | solution.py:33
  119.9 2.0 %collective-permute-start.16 = (bf16[2,128,512]{2,1,0:T(8,128)(2,1)S(1)}, bf16[2,128,512]{2,1,0:T(8,128)(2,1)S(1)}, u32[]{:S(2)}, u32[]{:S(2)}) collective-permute-start(bf16[2,128,512]{2,1,0:T(8,128)(2,1)S(1)} %pad_maximum_fusion.1.refs_0_), channel_id=1, source_target_pairs={{0,16},{1,17},{2,18},{3,19},{4,20},{5,21},{6,22},{7,23},{8,24},{9,... | collective-permute-start | bytes 786440 | tf_op jit(solution)/shard_map/ppermute | solution.py:33
  121.9 1.9 collective-permute-start.15
  123.8 4.5 %collective-permute-start.14 = (bf16[2,128,512]{2,1,0:T(8,128)(2,1)S(1)}, bf16[2,128,512]{2,1,0:T(8,128)(2,1)S(1)}, u32[]{:S(2)}, u32[]{:S(2)}) collective-permute-start(bf16[2,128,512]{2,1,0:T(8,128)(2,1)S(1)} %pad_maximum_fusion.1.refs_0_), channel_id=1, source_target_pairs={{0,48},{1,49},{2,50},{3,51},{4,52},{5,53},{6,54},{7,55},{8,56},{9,... | collective-permute-start | bytes 786440 | tf_op jit(solution)/shard_map/ppermute | solution.py:33
  128.4 2.6 %collective-permute-done.16.refs_3_ = bf16[2,128,512]{2,1,0:T(8,128)(2,1)S(1)} collective-permute-done((bf16[2,128,512]{2,1,0:T(8,128)(2,1)S(1)}, bf16[2,128,512]{2,1,0:T(8,128)(2,1)S(1)}, u32[]{:S(2)}, u32[]{:S(2)}) %collective-permute-start.16) | collective-permute-done | bytes 262176 | tf_op jit(solution)/shard_map/ppermute | solution.py:33
  131.0 2.8 %collective-permute-done.14.refs_1_ = bf16[2,128,512]{2,1,0:T(8,128)(2,1)S(1)} collective-permute-done((bf16[2,128,512]{2,1,0:T(8,128)(2,1)S(1)}, bf16[2,128,512]{2,1,0:T(8,128)(2,1)S(1)}, u32[]{:S(2)}, u32[]{:S(2)}) %collective-permute-start.14) | collective-permute-done | bytes 262176 | tf_op jit(solution)/shard_map/ppermute | solution.py:33
  133.8 1.8 shard_map.66
  135.7 8.6 %collective-permute-start.17 = (bf16[4,2,128,256]{3,2,1,0:T(8,128)(2,1)S(1)}, bf16[4,2,128,256]{3,2,1,0:T(8,128)(2,1)S(1)}, u32[]{:S(2)}, u32[]{:S(2)}) collective-permute-start(bf16[4,2,128,256]{3,2,1,0:T(8,128)(2,1)S(1)} %slice_bitcast_fusion), channel_id=1, source_target_pairs={{0,1},{1,0},{2,3},{3,2},{4,5},{5,4},{6,7},{7,6},{8,9},{9,8},{10,11... | collective-permute-start | bytes 1572872 | tf_op jit(solution)/shard_map/ppermute | solution.py:33
  144.3 1.5 collective-permute-done.17
  145.8 0.9 fusion
  146.7 11.1 %all-to-all-start.1 = ((bf16[4,2,128,256]{3,2,1,0:T(8,128)(2,1)}), bf16[4,2,128,256]{3,2,1,0:T(8,128)(2,1)S(1)}, u32[]{:S(2)}, u32[]{:S(2)}) async-start(bf16[4,2,128,256]{3,2,1,0:T(8,128)(2,1)} %fusion), calls=%async_computation.1 | async-start | bytes 1048576 | tf_op jit(solution)/shard_map/all_to_all | solution.py:270
  157.8 28.9 %all-to-all-done.1 = bf16[4,2,128,256]{3,2,1,0:T(8,128)(2,1)S(1)} async-done(((bf16[4,2,128,256]{3,2,1,0:T(8,128)(2,1)}), bf16[4,2,128,256]{3,2,1,0:T(8,128)(2,1)S(1)}, u32[]{:S(2)}, u32[]{:S(2)}) %all-to-all-start.1) | async-done | bytes 524320 | tf_op jit(solution)/shard_map/all_to_all | solution.py:270
  186.8 4.7 %collective-permute-start.18 = (bf16[128,256]{1,0:T(8,128)(2,1)S(1)}, bf16[128,256]{1,0:T(8,128)(2,1)S(1)}, u32[]{:S(2)}, u32[]{:S(2)}) collective-permute-start(bf16[128,256]{1,0:T(8,128)(2,1)S(1)} %get-tuple-element.27), channel_id=1, source_target_pairs={{0,16},{1,48},{2,18},{3,50},{4,20},{5,52},{6,22},{7,54},{8,24},{9,... | collective-permute-start | bytes 196616 | tf_op jit(solution)/shard_map/ppermute | solution.py:33
  191.5 1.9 collective-permute-start.19
  193.6 5.0 %collective-permute-done.19 = bf16[128,256]{1,0:T(8,128)(2,1)S(1)} collective-permute-done((bf16[128,256]{1,0:T(8,128)(2,1)S(1)}, bf16[128,256]{1,0:T(8,128)(2,1)S(1)}, u32[]{:S(2)}, u32[]{:S(2)}) %collective-permute-start.19) | collective-permute-done | bytes 65568 | tf_op jit(solution)/shard_map/ppermute | solution.py:33
  (49 shorter events, 5.4 us)
Async XLA Ops:
  0.0 11.1 %copy-start.2 = (bf16[8,128]{1,0:T(8,128)(2,1)S(1)}, bf16[8,128]{1,0:T(8,128)(2,1)}, u32[]{:S(2)}) copy-start(bf16[8,128]{1,0:T(8,128)(2,1)} %refs_0_.1) | copy-start | bytes 6148
  0.0 38.3 %collective-permute-start.5 = (bf16[512,256]{1,0:T(8,128)(2,1)}, bf16[512,256]{1,0:T(8,128)(2,1)S(1)}, u32[]{:S(2)}, u32[]{:S(2)}) collective-permute-start(bf16[512,256]{1,0:T(8,128)(2,1)} %param.11), channel_id=1, source_target_pairs={{2,74},{3,75},{6,78},{7,79},{10,2},{11,3},{14,6},{15,7},{18,90},{1... | collective-permute-start | bytes 786440 | tf_op jit(solution)/shard_map/ppermute | solution.py:33
  0.8 37.5 %collective-permute-start.4 = (bf16[512,256]{1,0:T(8,128)(2,1)}, bf16[512,256]{1,0:T(8,128)(2,1)S(1)}, u32[]{:S(2)}, u32[]{:S(2)}) collective-permute-start(bf16[512,256]{1,0:T(8,128)(2,1)} %param.11), channel_id=1, source_target_pairs={{0,8},{1,9},{4,12},{5,13},{8,64},{9,65},{12,68},{13,69},{16,24},{1... | collective-permute-start | bytes 786440 | tf_op jit(solution)/shard_map/ppermute | solution.py:33
  11.1 9.4 %copy-start.4 = (bf16[8,128]{1,0:T(8,128)(2,1)S(1)}, bf16[8,128]{1,0:T(8,128)(2,1)}, u32[]{:S(2)}) copy-start(bf16[8,128]{1,0:T(8,128)(2,1)} %refs_2_.1) | copy-start | bytes 6148
  11.1 9.4 %copy-start.5 = (bf16[8,128]{1,0:T(8,128)(2,1)S(1)}, bf16[8,128]{1,0:T(8,128)(2,1)}, u32[]{:S(2)}) copy-start(bf16[8,128]{1,0:T(8,128)(2,1)} %refs_3_.1) | copy-start | bytes 6148
  11.8 8.7 %copy-start.3 = (bf16[8,128]{1,0:T(8,128)(2,1)S(1)}, bf16[8,128]{1,0:T(8,128)(2,1)}, u32[]{:S(2)}) copy-start(bf16[8,128]{1,0:T(8,128)(2,1)} %refs_1_.1) | copy-start | bytes 6148
  11.8 19.4 %collective-permute-start.3 = (bf16[2,8,128]{2,1,0:T(8,128)(2,1)S(1)}, bf16[2,8,128]{2,1,0:T(8,128)(2,1)S(1)}, u32[]{:S(2)}, u32[]{:S(2)}) collective-permute-start(bf16[2,8,128]{2,1,0:T(8,128)(2,1)S(1)} %pad_maximum_fusion.4), channel_id=1, source_target_pairs={{0,64},{16,80},{32,96},{48,112},{64,128},{80,144},{96,160},{112,17... | collective-permute-start | bytes 12296 | tf_op jit(solution)/shard_map/ppermute | solution.py:38
  20.5 15.1 %collective-permute-start = (bf16[4,8,128]{2,1,0:T(8,128)(2,1)S(1)}, bf16[4,8,128]{2,1,0:T(8,128)(2,1)S(1)}, u32[]{:S(2)}, u32[]{:S(2)}) collective-permute-start(bf16[4,8,128]{2,1,0:T(8,128)(2,1)S(1)} %pad_maximum_fusion.3), channel_id=1, source_target_pairs={{0,16},{16,32},{32,48},{48,64},{64,80},{80,96},{96,112},{112,128},... | collective-permute-start | bytes 24584 | tf_op jit(solution)/shard_map/ppermute | solution.py:38
  23.7 11.1 %collective-permute-start.2 = (bf16[2,8,128]{2,1,0:T(8,128)(2,1)S(1)}, bf16[2,8,128]{2,1,0:T(8,128)(2,1)S(1)}, u32[]{:S(2)}, u32[]{:S(2)}) collective-permute-start(bf16[2,8,128]{2,1,0:T(8,128)(2,1)S(1)} %pad_maximum_fusion.4), channel_id=1, source_target_pairs={{0,48},{16,64},{32,80},{48,96},{64,112},{80,128},{96,144},{112,160... | collective-permute-start | bytes 12296 | tf_op jit(solution)/shard_map/ppermute | solution.py:38
  31.2 4.4 %copy-start.7 = (bf16[2,8,128]{2,1,0:T(8,128)(2,1)}, bf16[2,8,128]{2,1,0:T(8,128)(2,1)S(1)}, u32[]{:S(2)}) copy-start(bf16[2,8,128]{2,1,0:T(8,128)(2,1)S(1)} %collective-permute-done.3.refs_7_) | copy-start | bytes 12292
  31.3 4.4 %collective-permute-start.1 = (bf16[2,8,128]{2,1,0:T(8,128)(2,1)S(1)}, bf16[2,8,128]{2,1,0:T(8,128)(2,1)S(1)}, u32[]{:S(2)}, u32[]{:S(2)}) collective-permute-start(bf16[2,8,128]{2,1,0:T(8,128)(2,1)S(1)} %pad_maximum_fusion.4), channel_id=1, source_target_pairs={{0,32},{16,48},{32,64},{48,80},{64,96},{80,112},{96,128},{112,144}... | collective-permute-start | bytes 12296 | tf_op jit(solution)/shard_map/ppermute | solution.py:38
  34.9 0.7 copy-start.8
  35.6 0.6 copy-start.9
  36.2 0.6 copy-start.6
  38.3 10.8 %copy-start.1 = (bf16[512,256]{1,0:T(8,128)(2,1)S(1)}, bf16[512,256]{1,0:T(8,128)(2,1)}, u32[]{:S(2)}) copy-start(bf16[512,256]{1,0:T(8,128)(2,1)} %param.11) | copy-start | bytes 786436
  38.3 21.4 %all-to-all-start = ((bf16[8,14,8,128]{3,2,1,0:T(8,128)(2,1)}), bf16[8,14,8,128]{3,2,1,0:T(8,128)(2,1)S(1)}, u32[]{:S(2)}, u32[]{:S(2)}) async-start(bf16[8,14,8,128]{3,2,1,0:T(8,128)(2,1)} %shard_map.64), calls=%async_computation | async-start | bytes 458752 | tf_op jit(solution)/shard_map/all_to_all | solution.py:242
  48.4 2.8 %collective-permute-start.6 = (bf16[512,256]{1,0:T(8,128)(2,1)S(1)}, bf16[512,256]{1,0:T(8,128)(2,1)S(1)}, u32[]{:S(2)}, u32[]{:S(2)}) collective-permute-start(bf16[512,256]{1,0:T(8,128)(2,1)S(1)} %collective-permute-done.4), channel_id=1, source_target_pairs={{2,10},{3,11},{6,14},{7,15},{8,64},{9,65},{12,68},{13,69},{18,26},... | collective-permute-start | bytes 786440 | tf_op jit(solution)/shard_map/ppermute | solution.py:33
  49.1 16.8 %collective-permute-start.7 = (bf16[512,256]{1,0:T(8,128)(2,1)S(1)}, bf16[512,256]{1,0:T(8,128)(2,1)S(1)}, u32[]{:S(2)}, u32[]{:S(2)}) collective-permute-start(bf16[512,256]{1,0:T(8,128)(2,1)S(1)} %copy-done.1), channel_id=1, source_target_pairs={{2,0},{3,1},{6,4},{7,5},{10,8},{11,9},{14,12},{15,13},{18,16},{19,... | collective-permute-start | bytes 786440 | tf_op jit(solution)/shard_map/ppermute | solution.py:33
  50.4 15.5 %collective-permute-start.8 = (bf16[512,256]{1,0:T(8,128)(2,1)S(1)}, bf16[512,256]{1,0:T(8,128)(2,1)S(1)}, u32[]{:S(2)}, u32[]{:S(2)}) collective-permute-start(bf16[512,256]{1,0:T(8,128)(2,1)S(1)} %collective-permute-done.5), channel_id=1, source_target_pairs={{2,72},{3,73},{6,76},{7,77},{8,2},{9,3},{12,6},{13,7},{18,88},{19,... | collective-permute-start | bytes 786440 | tf_op jit(solution)/shard_map/ppermute | solution.py:33
  59.6 7.4 %collective-permute-start.9 = (bf16[8,14,8,128]{3,2,1,0:T(8,128)(2,1)S(1)}, bf16[8,14,8,128]{3,2,1,0:T(8,128)(2,1)S(1)}, u32[]{:S(2)}, u32[]{:S(2)}) collective-permute-start(bf16[8,14,8,128]{3,2,1,0:T(8,128)(2,1)S(1)} %all-to-all-done.mine_ref), channel_id=1, source_target_pairs={{0,1},{1,0},{2,3},{3,2},{4,5},{5,4},{6,7},{7,6},{8,9},{9,8},{10,11... | collective-permute-start | bytes 688136 | tf_op jit(solution)/shard_map/ppermute | solution.py:33
  66.0 23.8 %copy-start = (bf16[128,512]{1,0:T(8,128)(2,1)S(1)}, bf16[128,512]{1,0:T(8,128)(2,1)}, u32[]{:S(2)}) copy-start(bf16[128,512]{1,0:T(8,128)(2,1)} %q_ref.1) | copy-start | bytes 393220
  67.0 40.9 %collective-permute-start.12 = (bf16[2,512,256]{2,1,0:T(8,128)(2,1)S(1)}, bf16[2,512,256]{2,1,0:T(8,128)(2,1)S(1)}, u32[]{:S(2)}, u32[]{:S(2)}) collective-permute-start(bf16[2,512,256]{2,1,0:T(8,128)(2,1)S(1)} %pad_maximum_fusion.refs_4_), channel_id=1, source_target_pairs={{0,128},{1,129},{2,130},{3,131},{4,132},{5,133},{6,134},{7,135},{8... | collective-permute-start | bytes 1572872 | tf_op jit(solution)/shard_map/ppermute | solution.py:33
  82.6 25.3 %collective-permute-start.11 = (bf16[2,512,256]{2,1,0:T(8,128)(2,1)S(1)}, bf16[2,512,256]{2,1,0:T(8,128)(2,1)S(1)}, u32[]{:S(2)}, u32[]{:S(2)}) collective-permute-start(bf16[2,512,256]{2,1,0:T(8,128)(2,1)S(1)} %pad_maximum_fusion.refs_4_), channel_id=1, source_target_pairs={{0,256},{1,257},{2,258},{3,259},{4,260},{5,261},{6,262},{7,263},{8... | collective-permute-start | bytes 1572872 | tf_op jit(solution)/shard_map/ppermute | solution.py:33
  85.8 22.2 %collective-permute-start.10 = (bf16[2,512,256]{2,1,0:T(8,128)(2,1)S(1)}, bf16[2,512,256]{2,1,0:T(8,128)(2,1)S(1)}, u32[]{:S(2)}, u32[]{:S(2)}) collective-permute-start(bf16[2,512,256]{2,1,0:T(8,128)(2,1)S(1)} %pad_maximum_fusion.refs_4_), channel_id=1, source_target_pairs={{0,384},{1,385},{2,386},{3,387},{4,388},{5,389},{6,390},{7,391},{8... | collective-permute-start | bytes 1572872 | tf_op jit(solution)/shard_map/ppermute | solution.py:33
  108.0 11.8 %collective-permute-start.13 = (bf16[128,512]{1,0:T(8,128)(2,1)S(1)}, bf16[128,512]{1,0:T(8,128)(2,1)S(1)}, u32[]{:S(2)}, u32[]{:S(2)}) collective-permute-start(bf16[128,512]{1,0:T(8,128)(2,1)S(1)} %shard_map.65), channel_id=1, source_target_pairs={{0,2},{1,3},{2,0},{3,1},{4,6},{5,7},{6,4},{7,5},{8,10},{9,11},{10,... | collective-permute-start | bytes 393224 | tf_op jit(solution)/shard_map/ppermute | solution.py:33
  119.9 11.1 %collective-permute-start.16 = (bf16[2,128,512]{2,1,0:T(8,128)(2,1)S(1)}, bf16[2,128,512]{2,1,0:T(8,128)(2,1)S(1)}, u32[]{:S(2)}, u32[]{:S(2)}) collective-permute-start(bf16[2,128,512]{2,1,0:T(8,128)(2,1)S(1)} %pad_maximum_fusion.1.refs_0_), channel_id=1, source_target_pairs={{0,16},{1,17},{2,18},{3,19},{4,20},{5,21},{6,22},{7,23},{8,24},{9,... | collective-permute-start | bytes 786440 | tf_op jit(solution)/shard_map/ppermute | solution.py:33
  121.9 9.1 %collective-permute-start.15 = (bf16[2,128,512]{2,1,0:T(8,128)(2,1)S(1)}, bf16[2,128,512]{2,1,0:T(8,128)(2,1)S(1)}, u32[]{:S(2)}, u32[]{:S(2)}) collective-permute-start(bf16[2,128,512]{2,1,0:T(8,128)(2,1)S(1)} %pad_maximum_fusion.1.refs_0_), channel_id=1, source_target_pairs={{0,32},{1,33},{2,34},{3,35},{4,36},{5,37},{6,38},{7,39},{8,40},{9,... | collective-permute-start | bytes 786440 | tf_op jit(solution)/shard_map/ppermute | solution.py:33
  123.8 10.0 %collective-permute-start.14 = (bf16[2,128,512]{2,1,0:T(8,128)(2,1)S(1)}, bf16[2,128,512]{2,1,0:T(8,128)(2,1)S(1)}, u32[]{:S(2)}, u32[]{:S(2)}) collective-permute-start(bf16[2,128,512]{2,1,0:T(8,128)(2,1)S(1)} %pad_maximum_fusion.1.refs_0_), channel_id=1, source_target_pairs={{0,48},{1,49},{2,50},{3,51},{4,52},{5,53},{6,54},{7,55},{8,56},{9,... | collective-permute-start | bytes 786440 | tf_op jit(solution)/shard_map/ppermute | solution.py:33
  135.7 10.1 %collective-permute-start.17 = (bf16[4,2,128,256]{3,2,1,0:T(8,128)(2,1)S(1)}, bf16[4,2,128,256]{3,2,1,0:T(8,128)(2,1)S(1)}, u32[]{:S(2)}, u32[]{:S(2)}) collective-permute-start(bf16[4,2,128,256]{3,2,1,0:T(8,128)(2,1)S(1)} %slice_bitcast_fusion), channel_id=1, source_target_pairs={{0,1},{1,0},{2,3},{3,2},{4,5},{5,4},{6,7},{7,6},{8,9},{9,8},{10,11... | collective-permute-start | bytes 1572872 | tf_op jit(solution)/shard_map/ppermute | solution.py:33
  146.7 40.0 %all-to-all-start.1 = ((bf16[4,2,128,256]{3,2,1,0:T(8,128)(2,1)}), bf16[4,2,128,256]{3,2,1,0:T(8,128)(2,1)S(1)}, u32[]{:S(2)}, u32[]{:S(2)}) async-start(bf16[4,2,128,256]{3,2,1,0:T(8,128)(2,1)} %fusion), calls=%async_computation.1 | async-start | bytes 1048576 | tf_op jit(solution)/shard_map/all_to_all | solution.py:270
  186.8 6.8 %collective-permute-start.18 = (bf16[128,256]{1,0:T(8,128)(2,1)S(1)}, bf16[128,256]{1,0:T(8,128)(2,1)S(1)}, u32[]{:S(2)}, u32[]{:S(2)}) collective-permute-start(bf16[128,256]{1,0:T(8,128)(2,1)S(1)} %get-tuple-element.27), channel_id=1, source_target_pairs={{0,16},{1,48},{2,18},{3,50},{4,20},{5,52},{6,22},{7,54},{8,24},{9,... | collective-permute-start | bytes 196616 | tf_op jit(solution)/shard_map/ppermute | solution.py:33
  191.5 7.1 %collective-permute-start.19 = (bf16[128,256]{1,0:T(8,128)(2,1)S(1)}, bf16[128,256]{1,0:T(8,128)(2,1)S(1)}, u32[]{:S(2)}, u32[]{:S(2)}) collective-permute-start(bf16[128,256]{1,0:T(8,128)(2,1)S(1)} %get-tuple-element.28), channel_id=1, source_target_pairs={{0,0},{1,32},{2,2},{3,34},{4,4},{5,36},{6,6},{7,38},{8,8},{9,40},{... | collective-permute-start | bytes 196616 | tf_op jit(solution)/shard_map/ppermute | solution.py:33

commit v4 on v3

--- a/solution.py
+++ b/solution.py
@@ -38,12 +38,11 @@
     return lax.ppermute(value, "seq", [(s, s + steps) for s in range(count - steps)])
 
 
-def attention_kernel(
+def window_kernel(
     place, q_ref, mine_ref, other_ref, out_ref, k_ref, v_ref, sk_ref, sv_ref, q32, out32, *, tokens
 ):
-    rows, wide = q_ref.shape
+    rows = q_ref.shape[0]
     width = k_ref.shape[1]
-    heads = wide // width
     block_now, core = place[0], place[1]
     spots = W1 // rows + 1
 
@@ -73,8 +72,15 @@
     sk_ref[:W2, :] = jnp.where(block_now == 0, jnp.broadcast_to(short[:1], edge.shape), edge)
     sv_ref[W2:, :] = whole(2 * spots + 3)
     sv_ref[:W2, :] = whole(2 * spots + 1)[rows - W2 :]
-    origin = block_now * rows
-
+    attend_half(place, q_ref, k_ref, v_ref, sk_ref, sv_ref, q32, out32, tokens, 0)
+    out_ref[...] = out32[: rows // 2].astype(jnp.bfloat16)
+
+
+def attend_half(place, q_ref, k_ref, v_ref, sk_ref, sv_ref, q32, out32, tokens, part):
+    rows, wide = q_ref.shape
+    width = k_ref.shape[1]
+    heads = wide // width
+    origin = place[0] * rows
     span = sk_ref.shape[0] - rows
     factor = 2.5 / math.sqrt(width) * math.log2(math.e)
     q32[...] = q_ref[...].astype(jnp.float32)
@@ -112,33 +118,58 @@
             out32[pl.ds(start, tokens), cols] = above / below
         return carry
 
-    lax.fori_loop(0, rows // tokens, block, 0)
-    out_ref[...] = out32[...].astype(jnp.bfloat16)
-
-
-def attention(place, q, mine, other):
-    rows, wide = q.shape
-    width = mine.shape[-1]
-    spots = W1 // rows + 1
+    steps = rows // tokens // 2
+    lax.fori_loop(part * steps, (part + 1) * steps, block, 0)
+
+
+def rest_kernel(
+    place, q_ref, k_ref, v_ref, sk_ref, sv_ref, early_ref, out_ref, q32, out32, *, tokens
+):
+    half = q_ref.shape[0] // 2
+    attend_half(place, q_ref, k_ref, v_ref, sk_ref, sv_ref, q32, out32, tokens, 1)
+    out_ref[:half] = early_ref[...]
+    out_ref[half:] = out32[half:].astype(jnp.bfloat16)
+
+
+def attention_call(kernel, operands, out_shape):
+    rows, wide = operands[1].shape
     return pl.pallas_call(
-        functools.partial(attention_kernel, tokens=16),
-        out_shape=jax.ShapeDtypeStruct((rows, wide), jnp.bfloat16),
+        functools.partial(kernel, tokens=16),
+        out_shape=out_shape,
         in_specs=[pl.BlockSpec(memory_space=pltpu.SMEM)]
-        + [pl.BlockSpec(memory_space=pltpu.VMEM)] * 3,
-        out_specs=pl.BlockSpec(memory_space=pltpu.VMEM),
+        + [pl.BlockSpec(memory_space=pltpu.VMEM)] * (len(operands) - 1),
+        out_specs=jax.tree.map(lambda _: pl.BlockSpec(memory_space=pltpu.VMEM), out_shape),
         scratch_shapes=[
-            pltpu.VMEM((spots * rows, width), jnp.bfloat16),
-            pltpu.VMEM((spots * rows, 2 * width), jnp.bfloat16),
-            pltpu.VMEM((W2 + rows, width), jnp.float32),
-            pltpu.VMEM((W2 + rows, width), jnp.float32),
             pltpu.VMEM((rows, wide), jnp.float32),
             pltpu.VMEM((rows, wide), jnp.float32),
         ],
         compiler_params=pltpu.CompilerParams(vmem_limit_bytes=40 * 2**20),
         cost_estimate=pl.CostEstimate(
-            flops=20_000_000_000, bytes_accessed=2**20, transcendentals=0
+            flops=10_000_000_000, bytes_accessed=2**20, transcendentals=0
         ),
-    )(place, q, mine, other)
+    )(*operands)
+
+
+def first_attention(place, q, mine, other):
+    rows, wide = q.shape
+    width = mine.shape[-1]
+    spots = W1 // rows + 1
+    shapes = [
+        ((rows // 2, wide), jnp.bfloat16),
+        ((spots * rows, width), jnp.bfloat16),
+        ((spots * rows, 2 * width), jnp.bfloat16),
+        ((W2 + rows, width), jnp.float32),
+        ((W2 + rows, width), jnp.float32),
+    ]
+    shapes = [jax.ShapeDtypeStruct(*shape) for shape in shapes]
+    early, *window = attention_call(window_kernel, (place, q, mine, other), shapes)
+    return early, window
+
+
+def rest_attention(place, q, window, early):
+    return attention_call(
+        rest_kernel, (place, q, *window, early), jax.ShapeDtypeStruct(q.shape, jnp.bfloat16)
+    )
 
 
 def pack_kernel(count, *refs):
@@ -235,26 +266,29 @@
     before = later(piece, 1)
     older = [later(piece[:2], steps) for steps in range(2, W1 // rows + 1)]
     mine = pack((long_keys, long_values, short_keys, short_values), before, older)
+    mine, upward, downward = lax.optimization_barrier((mine, upward, downward))
     lines = [[z * CS + core for z in range(ZS)] for core in range(CS)]
-    mine, upward, downward = lax.optimization_barrier((mine, upward, downward))
+    over_z = lax.all_to_all(mine, "head", 0, 0, axis_index_groups=lines, tiled=True)
+    over_z, upward, downward = lax.optimization_barrier((over_z, upward, downward))
+    over_core = moved(over_z, lambda x, h, y, z, c: (x, h, y, z, 1 - c))
+    spot = jnp.stack([seq, c])
+    early, window = first_attention(spot, queries, over_z, over_core)
     upward, downward = moved(upward, second_up), moved(downward, second_down)
     beside = moved(w_out, near)
-    over_z = lax.all_to_all(mine, "head", 0, 0, axis_index_groups=lines, tiled=True)
-    over_core = moved(over_z, lambda x, h, y, z, c: (x, h, y, z, 1 - c))
 
     near_by = half == z % 2
     pair = jnp.stack(
         [jnp.where(near_by, w_out, upward), jnp.where(near_by, beside, downward)]
     )
-    pair, over_core = lax.optimization_barrier((pair, over_core))
+    pair, early = lax.optimization_barrier((pair, early))
     from_x = [pair] + [
         moved(pair, lambda x, h, y, z, c, d=d: (x - d, h, y, z, c)) for d in (1, 2, 3)
     ]
 
-    attended = attention(jnp.stack([seq, c]), queries, over_z, over_core)
-    attended, from_x = lax.optimization_barrier((attended, from_x))
+    attended = rest_attention(spot, queries, window, early)
 
     beside = moved(attended, lambda x, h, y, z, c: (x, h, y, z ^ 1, c))
+    beside, from_x = lax.optimization_barrier((beside, from_x))
     attended = jnp.stack([attended, beside])
     from_y = [attended] + [
         moved(attended, lambda x, h, y, z, c, d=d: (x, h, y - d, z, c)) for d in (1, 2, 3)

time: 203 us -> 206 us (1.015)
  blocking collectives: 0 us -> 21.3 us
  starting transfers between devices: 120 us -> 109 us
  waiting for transfers between devices: 53.6 us -> 46.3 us
    all_to_all x0 -> x1, blocking collectives: none -> 21.3 us  [per_device(): lax.all_to_all(mine, 'head', 0, 0, axis_index_groups=lines, tiled=True)]
    all_to_all x1 -> x0, starting transfers between devices: 10.1 us -> none  [per_device(): lax.all_to_all(mine, 'head', 0, 0, axis_index_groups=lines, tiled=True)]
    all_to_all x1 -> x0, waiting for transfers between devices: 8.43 us -> none  [per_device(): lax.all_to_all(mine, 'head', 0, 0, axis_index_groups=lines, tiled=True)]
    all_to_all x1, starting transfers between devices: 11.1 us -> 7.3 us  [per_device(): lax.all_to_all(kept, 'head', 0, 0, axis_index_groups=groups, tiled=True)]
    ppermute x16, starting transfers between devices: 75.8 us -> 79.1 us  [moved(): return lax.ppermute(value, BOTH, pairs)]
    pallas_call x1 -> x2, Pallas kernels: 18.1 us -> 18.8 us  [attention_call(): pl.pallas_call(functools.partial(kernel, tokens=16), out_shape=out_shape,...]
  transfers between devices with their start and end apart: 22 -> 21, of which waited for: 11 -> 7; matrix products, arithmetic and copies ran while one was open for 0% -> 0% of each run, Pallas kernels for 10% -> 10%
where the time goes in v4:
time: 206 us; the launch traced here: 204 us
  starting transfers between devices  109 us (53%)
  waiting for transfers between devices  46.3 us (22%)
  Pallas kernels  22.1 us (11%)
  blocking collectives  21.3 us (10%)
  other arithmetic  2.74 us (1%)
    ppermute x16, starting transfers between devices, moved(): return lax.ppermute(value, BOTH, pairs)  79.1 us
    all_to_all x1, waiting for transfers between devices, per_device(): lax.all_to_all(kept, 'head', 0, 0, axis_index_groups=groups, tiled=True)  28.2 us
    ppermute x4, starting transfers between devices, later(): lax.ppermute(value, 'seq', [(s, s + steps) for s in range(count - steps)])  22.9 us
    all_to_all x1, blocking collectives, per_device(): lax.all_to_all(mine, 'head', 0, 0, axis_index_groups=lines, tiled=True)  21.3 us
    pallas_call x2, Pallas kernels, attention_call(): pl.pallas_call(functools.partial(kernel, tokens=16), out_shape=out_shape,...  18.8 us
    ppermute x16, waiting for transfers between devices, moved(): return lax.ppermute(value, BOTH, pairs)  17.5 us
    all_to_all x1, starting transfers between devices, per_device(): lax.all_to_all(kept, 'head', 0, 0, axis_index_groups=groups, tiled=True)  7.3 us
  transfers between devices with their start and end apart: 21, of which 7 were waited for; matrix products, arithmetic and copies ran while one was open for 0% of the time, Pallas kernels for 10%

profile of v4, /device:TPU:1, one launch (start us, length us, event | category | flops | bytes accessed | tf_op | source)
XLA Modules:
  0.0 203.6 jit_solution(16664072627290031743)
XLA Ops:
  0.0 0.8 collective-permute-start.5
  0.8 10.3 %collective-permute-start.4 = (bf16[512,256]{1,0:T(8,128)(2,1)}, bf16[512,256]{1,0:T(8,128)(2,1)S(1)}, u32[]{:S(2)}, u32[]{:S(2)}) collective-permute-start(bf16[512,256]{1,0:T(8,128)(2,1)} %param.11), channel_id=1, source_target_pairs={{0,8},{1,9},{4,12},{5,13},{8,64},{9,65},{12,68},{13,69},{16,24},{1... | collective-permute-start | bytes 786440 | tf_op jit(solution)/shard_map/ppermute | solution.py:33
  11.8 8.6 %collective-permute-start.3 = (bf16[2,8,128]{2,1,0:T(8,128)(2,1)S(1)}, bf16[2,8,128]{2,1,0:T(8,128)(2,1)S(1)}, u32[]{:S(2)}, u32[]{:S(2)}) collective-permute-start(bf16[2,8,128]{2,1,0:T(8,128)(2,1)S(1)} %pad_maximum_fusion.4), channel_id=1, source_target_pairs={{0,64},{16,80},{32,96},{48,112},{64,128},{80,144},{96,160},{112,17... | collective-permute-start | bytes 12296 | tf_op jit(solution)/shard_map/ppermute | solution.py:38
  20.5 3.2 %collective-permute-start = (bf16[4,8,128]{2,1,0:T(8,128)(2,1)S(1)}, bf16[4,8,128]{2,1,0:T(8,128)(2,1)S(1)}, u32[]{:S(2)}, u32[]{:S(2)}) collective-permute-start(bf16[4,8,128]{2,1,0:T(8,128)(2,1)S(1)} %pad_maximum_fusion.3), channel_id=1, source_target_pairs={{0,16},{16,32},{32,48},{48,64},{64,80},{80,96},{96,112},{112,128},... | collective-permute-start | bytes 24584 | tf_op jit(solution)/shard_map/ppermute | solution.py:38
  23.7 7.5 %collective-permute-start.2 = (bf16[2,8,128]{2,1,0:T(8,128)(2,1)S(1)}, bf16[2,8,128]{2,1,0:T(8,128)(2,1)S(1)}, u32[]{:S(2)}, u32[]{:S(2)}) collective-permute-start(bf16[2,8,128]{2,1,0:T(8,128)(2,1)S(1)} %pad_maximum_fusion.4), channel_id=1, source_target_pairs={{0,48},{16,64},{32,80},{48,96},{64,112},{80,128},{96,144},{112,160... | collective-permute-start | bytes 12296 | tf_op jit(solution)/shard_map/ppermute | solution.py:38
  31.3 3.6 %collective-permute-start.1 = (bf16[2,8,128]{2,1,0:T(8,128)(2,1)S(1)}, bf16[2,8,128]{2,1,0:T(8,128)(2,1)S(1)}, u32[]{:S(2)}, u32[]{:S(2)}) collective-permute-start(bf16[2,8,128]{2,1,0:T(8,128)(2,1)S(1)} %pad_maximum_fusion.4), channel_id=1, source_target_pairs={{0,32},{16,48},{32,64},{48,80},{64,96},{80,112},{96,128},{112,144}... | collective-permute-start | bytes 12296 | tf_op jit(solution)/shard_map/ppermute | solution.py:38
  34.9 0.7 collective-permute-done.1.refs_5_
  36.8 1.5 shard_map.64
  38.3 21.3 %all_to_all.10.mine_ref = bf16[8,14,8,128]{3,2,1,0:T(8,128)(2,1)S(1)} all-to-all(bf16[8,14,8,128]{3,2,1,0:T(8,128)(2,1)} %shard_map.64), channel_id=1, replica_groups={{0,2,4,6,8,10,12,14},{1,3,5,7,9,11,13,15},{16,18,20,22,24,26,28,30},{17..., dimensions={0} | all-to-all | bytes 458752 | tf_op jit(solution)/shard_map/all_to_all | solution.py:271
  59.6 6.2 %collective-permute-start.6 = (bf16[8,14,8,128]{3,2,1,0:T(8,128)(2,1)S(1)}, bf16[8,14,8,128]{3,2,1,0:T(8,128)(2,1)S(1)}, u32[]{:S(2)}, u32[]{:S(2)}) collective-permute-start(bf16[8,14,8,128]{3,2,1,0:T(8,128)(2,1)S(1)} %all_to_all.10.mine_ref), channel_id=1, source_target_pairs={{0,1},{1,0},{2,3},{3,2},{4,5},{5,4},{6,7},{7,6},{8,9},{9,8},{10,11... | collective-permute-start | bytes 688136 | tf_op jit(solution)/shard_map/ppermute | solution.py:33
  65.9 1.3 collective-permute-start.8
  68.7 9.5 %shard_map.65 = (bf16[64,512]{1,0:T(8,128)(2,1)S(1)}, bf16[640,128]{1,0:T(8,128)(2,1)S(1)}, bf16[640,256]{1,0:T(8,128)(2,1)S(1)}, f32[160,128]{1,0:T(8,128)S(1)}, f32[160,128]{1,0:T(8,128)S(1)}) custom-call(s32[2]{0:T(128)S(1)} %pad_add_fusion.1.place, bf16[128,512]{1,0:T(8,128)(2,1)S(1)} %copy-done, bf16[8,14,8,128]{3,2,1,0:T(8,128)(2,1)S(1)} %all_to_all.10.mine_ref, ...), custom_call_target="tpu_custom_call" | custom-call | flops 10000000000 | bytes 1048576 | tf_op jit(solution)/shard_map/pallas_call | solution.py:136
  78.3 15.5 %collective-permute-start.13 = (bf16[2,512,256]{2,1,0:T(8,128)(2,1)S(1)}, bf16[2,512,256]{2,1,0:T(8,128)(2,1)S(1)}, u32[]{:S(2)}, u32[]{:S(2)}) collective-permute-start(bf16[2,512,256]{2,1,0:T(8,128)(2,1)S(1)} %pad_maximum_fusion.refs_4_), channel_id=1, source_target_pairs={{0,128},{1,129},{2,130},{3,131},{4,132},{5,133},{6,134},{7,135},{8... | collective-permute-start | bytes 1572872 | tf_op jit(solution)/shard_map/ppermute | solution.py:33
  93.8 3.2 %collective-permute-start.12 = (bf16[2,512,256]{2,1,0:T(8,128)(2,1)S(1)}, bf16[2,512,256]{2,1,0:T(8,128)(2,1)S(1)}, u32[]{:S(2)}, u32[]{:S(2)}) collective-permute-start(bf16[2,512,256]{2,1,0:T(8,128)(2,1)S(1)} %pad_maximum_fusion.refs_4_), channel_id=1, source_target_pairs={{0,256},{1,257},{2,258},{3,259},{4,260},{5,261},{6,262},{7,263},{8... | collective-permute-start | bytes 1572872 | tf_op jit(solution)/shard_map/ppermute | solution.py:33
  97.0 4.0 %collective-permute-start.11 = (bf16[2,512,256]{2,1,0:T(8,128)(2,1)S(1)}, bf16[2,512,256]{2,1,0:T(8,128)(2,1)S(1)}, u32[]{:S(2)}, u32[]{:S(2)}) collective-permute-start(bf16[2,512,256]{2,1,0:T(8,128)(2,1)S(1)} %pad_maximum_fusion.refs_4_), channel_id=1, source_target_pairs={{0,384},{1,385},{2,386},{3,387},{4,388},{5,389},{6,390},{7,391},{8... | collective-permute-start | bytes 1572872 | tf_op jit(solution)/shard_map/ppermute | solution.py:33
  100.9 9.4 %shard_map.66 = bf16[128,512]{1,0:T(8,128)(2,1)S(1)} custom-call(s32[2]{0:T(128)S(1)} %pad_add_fusion.1.place, bf16[128,512]{1,0:T(8,128)(2,1)S(1)} %copy-done, bf16[640,128]{1,0:T(8,128)(2,1)S(1)} %get-tuple-element.27.k_ref, bf16[640,256]{1,0:T(8,128)(2,1)S(1)} %get-tuple-element.28.v_ref, f32[160,128]{1,0:T(8,128)S(1)} %get-tuple-element.29.sk_ref, ...), custom_call_target="tpu_custom_call" | custom-call | flops 10000000000 | bytes 1048576 | tf_op jit(solution)/shard_map/pallas_call | solution.py:136
  110.3 15.7 %collective-permute-start.10 = (bf16[128,512]{1,0:T(8,128)(2,1)S(1)}, bf16[128,512]{1,0:T(8,128)(2,1)S(1)}, u32[]{:S(2)}, u32[]{:S(2)}) collective-permute-start(bf16[128,512]{1,0:T(8,128)(2,1)S(1)} %shard_map.66), channel_id=1, source_target_pairs={{0,2},{1,3},{2,0},{3,1},{4,6},{5,7},{6,4},{7,5},{8,10},{9,11},{10,... | collective-permute-start | bytes 393224 | tf_op jit(solution)/shard_map/ppermute | solution.py:33
  126.0 2.3 %collective-permute-done.10 = bf16[128,512]{1,0:T(8,128)(2,1)S(1)} collective-permute-done((bf16[128,512]{1,0:T(8,128)(2,1)S(1)}, bf16[128,512]{1,0:T(8,128)(2,1)S(1)}, u32[]{:S(2)}, u32[]{:S(2)}) %collective-permute-start.10) | collective-permute-done | bytes 131104 | tf_op jit(solution)/shard_map/ppermute | solution.py:33
  128.4 2.0 collective-permute-start.16
  130.4 1.9 collective-permute-start.15
  132.4 4.5 %collective-permute-start.14 = (bf16[2,128,512]{2,1,0:T(8,128)(2,1)S(1)}, bf16[2,128,512]{2,1,0:T(8,128)(2,1)S(1)}, u32[]{:S(2)}, u32[]{:S(2)}) collective-permute-start(bf16[2,128,512]{2,1,0:T(8,128)(2,1)S(1)} %pad_maximum_fusion.1.refs_0_), channel_id=1, source_target_pairs={{0,48},{1,49},{2,50},{3,51},{4,52},{5,53},{6,54},{7,55},{8,56},{9,... | collective-permute-start | bytes 786440 | tf_op jit(solution)/shard_map/ppermute | solution.py:33
  137.0 6.0 %collective-permute-done.16.refs_3_ = bf16[2,128,512]{2,1,0:T(8,128)(2,1)S(1)} collective-permute-done((bf16[2,128,512]{2,1,0:T(8,128)(2,1)S(1)}, bf16[2,128,512]{2,1,0:T(8,128)(2,1)S(1)}, u32[]{:S(2)}, u32[]{:S(2)}) %collective-permute-start.16) | collective-permute-done | bytes 262176 | tf_op jit(solution)/shard_map/ppermute | solution.py:33
  143.0 2.4 %collective-permute-done.14.refs_1_ = bf16[2,128,512]{2,1,0:T(8,128)(2,1)S(1)} collective-permute-done((bf16[2,128,512]{2,1,0:T(8,128)(2,1)S(1)}, bf16[2,128,512]{2,1,0:T(8,128)(2,1)S(1)}, u32[]{:S(2)}, u32[]{:S(2)}) %collective-permute-start.14) | collective-permute-done | bytes 262176 | tf_op jit(solution)/shard_map/ppermute | solution.py:33
  145.4 1.8 shard_map.67
  147.2 4.9 %collective-permute-start.17 = (bf16[4,2,128,256]{3,2,1,0:T(8,128)(2,1)S(1)}, bf16[4,2,128,256]{3,2,1,0:T(8,128)(2,1)S(1)}, u32[]{:S(2)}, u32[]{:S(2)}) collective-permute-start(bf16[4,2,128,256]{3,2,1,0:T(8,128)(2,1)S(1)} %slice_bitcast_fusion), channel_id=1, source_target_pairs={{0,1},{1,0},{2,3},{3,2},{4,5},{5,4},{6,7},{7,6},{8,9},{9,8},{10,11... | collective-permute-start | bytes 1572872 | tf_op jit(solution)/shard_map/ppermute | solution.py:33
  152.1 1.5 collective-permute-done.17
  153.6 1.0 fusion
  154.6 7.3 %all-to-all-start.1 = ((bf16[4,2,128,256]{3,2,1,0:T(8,128)(2,1)}), bf16[4,2,128,256]{3,2,1,0:T(8,128)(2,1)S(1)}, u32[]{:S(2)}, u32[]{:S(2)}) async-start(bf16[4,2,128,256]{3,2,1,0:T(8,128)(2,1)} %fusion), calls=%async_computation.1 | async-start | bytes 1048576 | tf_op jit(solution)/shard_map/all_to_all | solution.py:304
  161.9 28.2 %all-to-all-done.1 = bf16[4,2,128,256]{3,2,1,0:T(8,128)(2,1)S(1)} async-done(((bf16[4,2,128,256]{3,2,1,0:T(8,128)(2,1)}), bf16[4,2,128,256]{3,2,1,0:T(8,128)(2,1)S(1)}, u32[]{:S(2)}, u32[]{:S(2)}) %all-to-all-start.1) | async-done | bytes 524320 | tf_op jit(solution)/shard_map/all_to_all | solution.py:304
  190.2 5.7 %collective-permute-start.18 = (bf16[128,256]{1,0:T(8,128)(2,1)S(1)}, bf16[128,256]{1,0:T(8,128)(2,1)S(1)}, u32[]{:S(2)}, u32[]{:S(2)}) collective-permute-start(bf16[128,256]{1,0:T(8,128)(2,1)S(1)} %get-tuple-element.43), channel_id=1, source_target_pairs={{0,16},{1,48},{2,18},{3,50},{4,20},{5,52},{6,22},{7,54},{8,24},{9,... | collective-permute-start | bytes 196616 | tf_op jit(solution)/shard_map/ppermute | solution.py:33
  195.8 1.9 collective-permute-start.19
  197.8 5.2 %collective-permute-done.19 = bf16[128,256]{1,0:T(8,128)(2,1)S(1)} collective-permute-done((bf16[128,256]{1,0:T(8,128)(2,1)S(1)}, bf16[128,256]{1,0:T(8,128)(2,1)S(1)}, u32[]{:S(2)}, u32[]{:S(2)}) %collective-permute-start.19) | collective-permute-done | bytes 65568 | tf_op jit(solution)/shard_map/ppermute | solution.py:33
  (49 shorter events, 4.4 us)
Async XLA Ops:
  0.0 11.1 %copy-start.2 = (bf16[8,128]{1,0:T(8,128)(2,1)S(1)}, bf16[8,128]{1,0:T(8,128)(2,1)}, u32[]{:S(2)}) copy-start(bf16[8,128]{1,0:T(8,128)(2,1)} %refs_0_.1) | copy-start | bytes 6148
  0.0 38.3 %collective-permute-start.5 = (bf16[512,256]{1,0:T(8,128)(2,1)}, bf16[512,256]{1,0:T(8,128)(2,1)S(1)}, u32[]{:S(2)}, u32[]{:S(2)}) collective-permute-start(bf16[512,256]{1,0:T(8,128)(2,1)} %param.11), channel_id=1, source_target_pairs={{2,74},{3,75},{6,78},{7,79},{10,2},{11,3},{14,6},{15,7},{18,90},{1... | collective-permute-start | bytes 786440 | tf_op jit(solution)/shard_map/ppermute | solution.py:33
  0.8 37.5 %collective-permute-start.4 = (bf16[512,256]{1,0:T(8,128)(2,1)}, bf16[512,256]{1,0:T(8,128)(2,1)S(1)}, u32[]{:S(2)}, u32[]{:S(2)}) collective-permute-start(bf16[512,256]{1,0:T(8,128)(2,1)} %param.11), channel_id=1, source_target_pairs={{0,8},{1,9},{4,12},{5,13},{8,64},{9,65},{12,68},{13,69},{16,24},{1... | collective-permute-start | bytes 786440 | tf_op jit(solution)/shard_map/ppermute | solution.py:33
  11.1 9.4 %copy-start.4 = (bf16[8,128]{1,0:T(8,128)(2,1)S(1)}, bf16[8,128]{1,0:T(8,128)(2,1)}, u32[]{:S(2)}) copy-start(bf16[8,128]{1,0:T(8,128)(2,1)} %refs_2_.1) | copy-start | bytes 6148
  11.1 9.4 %copy-start.5 = (bf16[8,128]{1,0:T(8,128)(2,1)S(1)}, bf16[8,128]{1,0:T(8,128)(2,1)}, u32[]{:S(2)}) copy-start(bf16[8,128]{1,0:T(8,128)(2,1)} %refs_3_.1) | copy-start | bytes 6148
  11.8 8.7 %copy-start.3 = (bf16[8,128]{1,0:T(8,128)(2,1)S(1)}, bf16[8,128]{1,0:T(8,128)(2,1)}, u32[]{:S(2)}) copy-start(bf16[8,128]{1,0:T(8,128)(2,1)} %refs_1_.1) | copy-start | bytes 6148
  11.8 19.4 %collective-permute-start.3 = (bf16[2,8,128]{2,1,0:T(8,128)(2,1)S(1)}, bf16[2,8,128]{2,1,0:T(8,128)(2,1)S(1)}, u32[]{:S(2)}, u32[]{:S(2)}) collective-permute-start(bf16[2,8,128]{2,1,0:T(8,128)(2,1)S(1)} %pad_maximum_fusion.4), channel_id=1, source_target_pairs={{0,64},{16,80},{32,96},{48,112},{64,128},{80,144},{96,160},{112,17... | collective-permute-start | bytes 12296 | tf_op jit(solution)/shard_map/ppermute | solution.py:38
  20.5 15.1 %collective-permute-start = (bf16[4,8,128]{2,1,0:T(8,128)(2,1)S(1)}, bf16[4,8,128]{2,1,0:T(8,128)(2,1)S(1)}, u32[]{:S(2)}, u32[]{:S(2)}) collective-permute-start(bf16[4,8,128]{2,1,0:T(8,128)(2,1)S(1)} %pad_maximum_fusion.3), channel_id=1, source_target_pairs={{0,16},{16,32},{32,48},{48,64},{64,80},{80,96},{96,112},{112,128},... | collective-permute-start | bytes 24584 | tf_op jit(solution)/shard_map/ppermute | solution.py:38
  23.7 11.1 %collective-permute-start.2 = (bf16[2,8,128]{2,1,0:T(8,128)(2,1)S(1)}, bf16[2,8,128]{2,1,0:T(8,128)(2,1)S(1)}, u32[]{:S(2)}, u32[]{:S(2)}) collective-permute-start(bf16[2,8,128]{2,1,0:T(8,128)(2,1)S(1)} %pad_maximum_fusion.4), channel_id=1, source_target_pairs={{0,48},{16,64},{32,80},{48,96},{64,112},{80,128},{96,144},{112,160... | collective-permute-start | bytes 12296 | tf_op jit(solution)/shard_map/ppermute | solution.py:38
  31.2 4.4 %copy-start.7 = (bf16[2,8,128]{2,1,0:T(8,128)(2,1)}, bf16[2,8,128]{2,1,0:T(8,128)(2,1)S(1)}, u32[]{:S(2)}) copy-start(bf16[2,8,128]{2,1,0:T(8,128)(2,1)S(1)} %collective-permute-done.3.refs_7_) | copy-start | bytes 12292
  31.3 4.4 %collective-permute-start.1 = (bf16[2,8,128]{2,1,0:T(8,128)(2,1)S(1)}, bf16[2,8,128]{2,1,0:T(8,128)(2,1)S(1)}, u32[]{:S(2)}, u32[]{:S(2)}) collective-permute-start(bf16[2,8,128]{2,1,0:T(8,128)(2,1)S(1)} %pad_maximum_fusion.4), channel_id=1, source_target_pairs={{0,32},{16,48},{32,64},{48,80},{64,96},{80,112},{96,128},{112,144}... | collective-permute-start | bytes 12296 | tf_op jit(solution)/shard_map/ppermute | solution.py:38
  34.9 0.7 copy-start.8
  35.6 0.6 copy-start.9
  36.2 0.6 copy-start.6
  38.3 27.6 %copy-start.1 = (bf16[512,256]{1,0:T(8,128)(2,1)S(1)}, bf16[512,256]{1,0:T(8,128)(2,1)}, u32[]{:S(2)}) copy-start(bf16[512,256]{1,0:T(8,128)(2,1)} %param.11) | copy-start | bytes 786436
  38.3 30.4 %copy-start = (bf16[128,512]{1,0:T(8,128)(2,1)S(1)}, bf16[128,512]{1,0:T(8,128)(2,1)}, u32[]{:S(2)}) copy-start(bf16[128,512]{1,0:T(8,128)(2,1)} %q_ref.3) | copy-start | bytes 393220
  59.6 9.0 %collective-permute-start.6 = (bf16[8,14,8,128]{3,2,1,0:T(8,128)(2,1)S(1)}, bf16[8,14,8,128]{3,2,1,0:T(8,128)(2,1)S(1)}, u32[]{:S(2)}, u32[]{:S(2)}) collective-permute-start(bf16[8,14,8,128]{3,2,1,0:T(8,128)(2,1)S(1)} %all_to_all.10.mine_ref), channel_id=1, source_target_pairs={{0,1},{1,0},{2,3},{3,2},{4,5},{5,4},{6,7},{7,6},{8,9},{9,8},{10,11... | collective-permute-start | bytes 688136 | tf_op jit(solution)/shard_map/ppermute | solution.py:33
  65.9 12.3 %collective-permute-start.8 = (bf16[512,256]{1,0:T(8,128)(2,1)S(1)}, bf16[512,256]{1,0:T(8,128)(2,1)S(1)}, u32[]{:S(2)}, u32[]{:S(2)}) collective-permute-start(bf16[512,256]{1,0:T(8,128)(2,1)S(1)} %copy-done.1), channel_id=1, source_target_pairs={{2,0},{3,1},{6,4},{7,5},{10,8},{11,9},{14,12},{15,13},{18,16},{19,... | collective-permute-start | bytes 786440 | tf_op jit(solution)/shard_map/ppermute | solution.py:33
  67.3 10.9 %collective-permute-start.7 = (bf16[512,256]{1,0:T(8,128)(2,1)S(1)}, bf16[512,256]{1,0:T(8,128)(2,1)S(1)}, u32[]{:S(2)}, u32[]{:S(2)}) collective-permute-start(bf16[512,256]{1,0:T(8,128)(2,1)S(1)} %collective-permute-done.4), channel_id=1, source_target_pairs={{2,10},{3,11},{6,14},{7,15},{8,64},{9,65},{12,68},{13,69},{18,26},... | collective-permute-start | bytes 786440 | tf_op jit(solution)/shard_map/ppermute | solution.py:33
  68.0 10.2 %collective-permute-start.9 = (bf16[512,256]{1,0:T(8,128)(2,1)S(1)}, bf16[512,256]{1,0:T(8,128)(2,1)S(1)}, u32[]{:S(2)}, u32[]{:S(2)}) collective-permute-start(bf16[512,256]{1,0:T(8,128)(2,1)S(1)} %collective-permute-done.5), channel_id=1, source_target_pairs={{2,72},{3,73},{6,76},{7,77},{8,2},{9,3},{12,6},{13,7},{18,88},{19,... | collective-permute-start | bytes 786440 | tf_op jit(solution)/shard_map/ppermute | solution.py:33
  78.3 50.1 %collective-permute-start.13 = (bf16[2,512,256]{2,1,0:T(8,128)(2,1)S(1)}, bf16[2,512,256]{2,1,0:T(8,128)(2,1)S(1)}, u32[]{:S(2)}, u32[]{:S(2)}) collective-permute-start(bf16[2,512,256]{2,1,0:T(8,128)(2,1)S(1)} %pad_maximum_fusion.refs_4_), channel_id=1, source_target_pairs={{0,128},{1,129},{2,130},{3,131},{4,132},{5,133},{6,134},{7,135},{8... | collective-permute-start | bytes 1572872 | tf_op jit(solution)/shard_map/ppermute | solution.py:33
  93.8 34.6 %collective-permute-start.12 = (bf16[2,512,256]{2,1,0:T(8,128)(2,1)S(1)}, bf16[2,512,256]{2,1,0:T(8,128)(2,1)S(1)}, u32[]{:S(2)}, u32[]{:S(2)}) collective-permute-start(bf16[2,512,256]{2,1,0:T(8,128)(2,1)S(1)} %pad_maximum_fusion.refs_4_), channel_id=1, source_target_pairs={{0,256},{1,257},{2,258},{3,259},{4,260},{5,261},{6,262},{7,263},{8... | collective-permute-start | bytes 1572872 | tf_op jit(solution)/shard_map/ppermute | solution.py:33
  97.0 31.4 %collective-permute-start.11 = (bf16[2,512,256]{2,1,0:T(8,128)(2,1)S(1)}, bf16[2,512,256]{2,1,0:T(8,128)(2,1)S(1)}, u32[]{:S(2)}, u32[]{:S(2)}) collective-permute-start(bf16[2,512,256]{2,1,0:T(8,128)(2,1)S(1)} %pad_maximum_fusion.refs_4_), channel_id=1, source_target_pairs={{0,384},{1,385},{2,386},{3,387},{4,388},{5,389},{6,390},{7,391},{8... | collective-permute-start | bytes 1572872 | tf_op jit(solution)/shard_map/ppermute | solution.py:33
  110.3 18.1 %collective-permute-start.10 = (bf16[128,512]{1,0:T(8,128)(2,1)S(1)}, bf16[128,512]{1,0:T(8,128)(2,1)S(1)}, u32[]{:S(2)}, u32[]{:S(2)}) collective-permute-start(bf16[128,512]{1,0:T(8,128)(2,1)S(1)} %shard_map.66), channel_id=1, source_target_pairs={{0,2},{1,3},{2,0},{3,1},{4,6},{5,7},{6,4},{7,5},{8,10},{9,11},{10,... | collective-permute-start | bytes 393224 | tf_op jit(solution)/shard_map/ppermute | solution.py:33
  128.4 14.6 %collective-permute-start.16 = (bf16[2,128,512]{2,1,0:T(8,128)(2,1)S(1)}, bf16[2,128,512]{2,1,0:T(8,128)(2,1)S(1)}, u32[]{:S(2)}, u32[]{:S(2)}) collective-permute-start(bf16[2,128,512]{2,1,0:T(8,128)(2,1)S(1)} %pad_maximum_fusion.1.refs_0_), channel_id=1, source_target_pairs={{0,16},{1,17},{2,18},{3,19},{4,20},{5,21},{6,22},{7,23},{8,24},{9,... | collective-permute-start | bytes 786440 | tf_op jit(solution)/shard_map/ppermute | solution.py:33
  130.4 12.6 %collective-permute-start.15 = (bf16[2,128,512]{2,1,0:T(8,128)(2,1)S(1)}, bf16[2,128,512]{2,1,0:T(8,128)(2,1)S(1)}, u32[]{:S(2)}, u32[]{:S(2)}) collective-permute-start(bf16[2,128,512]{2,1,0:T(8,128)(2,1)S(1)} %pad_maximum_fusion.1.refs_0_), channel_id=1, source_target_pairs={{0,32},{1,33},{2,34},{3,35},{4,36},{5,37},{6,38},{7,39},{8,40},{9,... | collective-permute-start | bytes 786440 | tf_op jit(solution)/shard_map/ppermute | solution.py:33
  132.4 13.0 %collective-permute-start.14 = (bf16[2,128,512]{2,1,0:T(8,128)(2,1)S(1)}, bf16[2,128,512]{2,1,0:T(8,128)(2,1)S(1)}, u32[]{:S(2)}, u32[]{:S(2)}) collective-permute-start(bf16[2,128,512]{2,1,0:T(8,128)(2,1)S(1)} %pad_maximum_fusion.1.refs_0_), channel_id=1, source_target_pairs={{0,48},{1,49},{2,50},{3,51},{4,52},{5,53},{6,54},{7,55},{8,56},{9,... | collective-permute-start | bytes 786440 | tf_op jit(solution)/shard_map/ppermute | solution.py:33
  147.2 6.4 %collective-permute-start.17 = (bf16[4,2,128,256]{3,2,1,0:T(8,128)(2,1)S(1)}, bf16[4,2,128,256]{3,2,1,0:T(8,128)(2,1)S(1)}, u32[]{:S(2)}, u32[]{:S(2)}) collective-permute-start(bf16[4,2,128,256]{3,2,1,0:T(8,128)(2,1)S(1)} %slice_bitcast_fusion), channel_id=1, source_target_pairs={{0,1},{1,0},{2,3},{3,2},{4,5},{5,4},{6,7},{7,6},{8,9},{9,8},{10,11... | collective-permute-start | bytes 1572872 | tf_op jit(solution)/shard_map/ppermute | solution.py:33
  154.6 35.5 %all-to-all-start.1 = ((bf16[4,2,128,256]{3,2,1,0:T(8,128)(2,1)}), bf16[4,2,128,256]{3,2,1,0:T(8,128)(2,1)S(1)}, u32[]{:S(2)}, u32[]{:S(2)}) async-start(bf16[4,2,128,256]{3,2,1,0:T(8,128)(2,1)} %fusion), calls=%async_computation.1 | async-start | bytes 1048576 | tf_op jit(solution)/shard_map/all_to_all | solution.py:304
  190.2 7.6 %collective-permute-start.18 = (bf16[128,256]{1,0:T(8,128)(2,1)S(1)}, bf16[128,256]{1,0:T(8,128)(2,1)S(1)}, u32[]{:S(2)}, u32[]{:S(2)}) collective-permute-start(bf16[128,256]{1,0:T(8,128)(2,1)S(1)} %get-tuple-element.43), channel_id=1, source_target_pairs={{0,16},{1,48},{2,18},{3,50},{4,20},{5,52},{6,22},{7,54},{8,24},{9,... | collective-permute-start | bytes 196616 | tf_op jit(solution)/shard_map/ppermute | solution.py:33
  195.8 7.1 %collective-permute-start.19 = (bf16[128,256]{1,0:T(8,128)(2,1)S(1)}, bf16[128,256]{1,0:T(8,128)(2,1)S(1)}, u32[]{:S(2)}, u32[]{:S(2)}) collective-permute-start(bf16[128,256]{1,0:T(8,128)(2,1)S(1)} %get-tuple-element.44), channel_id=1, source_target_pairs={{0,0},{1,32},{2,2},{3,34},{4,4},{5,36},{6,6},{7,38},{8,8},{9,40},{... | collective-permute-start | bytes 196616 | tf_op jit(solution)/shard_map/ppermute | solution.py:33

commit v5 on v3

--- a/solution.py
+++ b/solution.py
@@ -164,9 +164,9 @@
 
 def project_kernel(place, *refs):
     tokens, columns, out_ref = refs[:YS], refs[YS : YS + XS], refs[-1]
-    x, y, c = place[0], place[1], place[2]
+    x, y, far, c = place[0], place[1], place[2], place[3]
     for d in range(XS):
-        to = lax.rem(x + d, XS)
+        to = lax.rem(x + d, XS) ^ far
         for e in range(YS):
             slot = lax.rem(y + e + YS - 2 * c, YS)
             total = jnp.dot(tokens[e][0], columns[d][0], preferred_element_type=jnp.float32)
@@ -252,23 +252,19 @@
     ]
 
     attended = attention(jnp.stack([seq, c]), queries, over_z, over_core)
-    attended, from_x = lax.optimization_barrier((attended, from_x))
-
     beside = moved(attended, lambda x, h, y, z, c: (x, h, y, z ^ 1, c))
+    beside, from_x = lax.optimization_barrier((beside, from_x))
     attended = jnp.stack([attended, beside])
     from_y = [attended] + [
         moved(attended, lambda x, h, y, z, c, d=d: (x, h, y - d, z, c)) for d in (1, 2, 3)
     ]
-    sums = project(jnp.stack([x, y, c]), from_y, from_x)
+    sums = project(jnp.stack([x, y, z // 2, c]), from_y, from_x)
     came = moved(sums[1], lambda x, h, y, z, c: (x, h, y, z, 1 - c))
     kept = (sums[0].astype(jnp.float32) + came.astype(jnp.float32)).astype(jnp.bfloat16)
-    groups = [
-        [(2 * far + low) * CS + core for far in range(ZS // 2)]
-        for low in range(2)
-        for core in range(CS)
-    ]
-    parts = lax.all_to_all(kept, "head", 0, 0, axis_index_groups=groups, tiled=True)
-    summed = jnp.sum(parts.astype(jnp.float32), axis=0).astype(jnp.bfloat16)
+    parts = [kept[0]] + [
+        moved(kept[k], lambda x, h, y, z, c, k=k: (x, h, y, z ^ (2 * k), c)) for k in (3, 2, 1)
+    ]
+    summed = sum(part.astype(jnp.float32) for part in parts).astype(jnp.bfloat16)
     odd = y % 2 == 1
     sent = in_order(summed[0], summed[1], odd)
     landed = [

time: 203 us -> 192 us (0.946); the launches traced: 199 us -> 191 us
  waiting for transfers between devices: 53.6 us -> 42 us
  starting transfers between devices: 120 us -> 124 us
    all_to_all x1 -> x0, waiting for transfers between devices: 28.9 us -> none  [per_device(): lax.all_to_all(kept, 'head', 0, 0, axis_index_groups=groups, tiled=True)]
    ppermute x16 -> x19, waiting for transfers between devices: 15.5 us -> 32.9 us  [moved(): return lax.ppermute(value, BOTH, pairs)]
    ppermute x16 -> x19, starting transfers between devices: 75.8 us -> 91.3 us  [moved(): return lax.ppermute(value, BOTH, pairs)]
    all_to_all x1 -> x0, starting transfers between devices: 11.1 us -> none  [per_device(): lax.all_to_all(kept, 'head', 0, 0, axis_index_groups=groups, tiled=True)]
  transfers between devices with their start and end apart: 22 -> 24, of which waited for: 11 -> 11; matrix products, arithmetic and copies ran while one was open for 0% -> 1% of each run, Pallas kernels for 10% -> 10%
where the time goes in v5:
time: 192 us; the launch traced here: 191 us
  starting transfers between devices  124 us (65%)
  waiting for transfers between devices  42 us (22%)
  Pallas kernels  21.4 us (11%)
    ppermute x19, starting transfers between devices, moved(): return lax.ppermute(value, BOTH, pairs)  91.3 us
    ppermute x19, waiting for transfers between devices, moved(): return lax.ppermute(value, BOTH, pairs)  32.9 us
    ppermute x4, starting transfers between devices, later(): lax.ppermute(value, 'seq', [(s, s + steps) for s in range(count - steps)])  22.9 us
    pallas_call x1, Pallas kernels, attention(): pl.pallas_call(functools.partial(attention_kernel, tokens=16), out_shape=...  18.1 us
    all_to_all x1, starting transfers between devices, per_device(): lax.all_to_all(mine, 'head', 0, 0, axis_index_groups=lines, tiled=True)  10.1 us
    all_to_all x1, waiting for transfers between devices, per_device(): lax.all_to_all(mine, 'head', 0, 0, axis_index_groups=lines, tiled=True)  8.43 us
  transfers between devices with their start and end apart: 24, of which 11 were waited for; matrix products, arithmetic and copies ran while one was open for 1% of the time, Pallas kernels for 10%

profile of v5, /device:TPU:1, one launch (start us, length us, event | category | flops | bytes accessed | tf_op | source)
XLA Modules:
  0.0 191.5 jit_solution(17240872895352071222)
XLA Ops:
  0.8 10.3 %collective-permute-start.4 = (bf16[512,256]{1,0:T(8,128)(2,1)}, bf16[512,256]{1,0:T(8,128)(2,1)S(1)}, u32[]{:S(2)}, u32[]{:S(2)}) collective-permute-start(bf16[512,256]{1,0:T(8,128)(2,1)} %param.11), channel_id=1, source_target_pairs={{0,8},{1,9},{4,12},{5,13},{8,64},{9,65},{12,68},{13,69},{16,24},{1... | collective-permute-start | bytes 786440 | tf_op jit(solution)/shard_map/ppermute | solution.py:33
  11.8 8.6 %collective-permute-start.3 = (bf16[2,8,128]{2,1,0:T(8,128)(2,1)S(1)}, bf16[2,8,128]{2,1,0:T(8,128)(2,1)S(1)}, u32[]{:S(2)}, u32[]{:S(2)}) collective-permute-start(bf16[2,8,128]{2,1,0:T(8,128)(2,1)S(1)} %pad_maximum_fusion.4), channel_id=1, source_target_pairs={{0,64},{16,80},{32,96},{48,112},{64,128},{80,144},{96,160},{112,17... | collective-permute-start | bytes 12296 | tf_op jit(solution)/shard_map/ppermute | solution.py:38
  20.5 3.2 %collective-permute-start = (bf16[4,8,128]{2,1,0:T(8,128)(2,1)S(1)}, bf16[4,8,128]{2,1,0:T(8,128)(2,1)S(1)}, u32[]{:S(2)}, u32[]{:S(2)}) collective-permute-start(bf16[4,8,128]{2,1,0:T(8,128)(2,1)S(1)} %pad_maximum_fusion.3), channel_id=1, source_target_pairs={{0,16},{16,32},{32,48},{48,64},{64,80},{80,96},{96,112},{112,128},... | collective-permute-start | bytes 24584 | tf_op jit(solution)/shard_map/ppermute | solution.py:38
  23.7 7.5 %collective-permute-start.2 = (bf16[2,8,128]{2,1,0:T(8,128)(2,1)S(1)}, bf16[2,8,128]{2,1,0:T(8,128)(2,1)S(1)}, u32[]{:S(2)}, u32[]{:S(2)}) collective-permute-start(bf16[2,8,128]{2,1,0:T(8,128)(2,1)S(1)} %pad_maximum_fusion.4), channel_id=1, source_target_pairs={{0,48},{16,64},{32,80},{48,96},{64,112},{80,128},{96,144},{112,160... | collective-permute-start | bytes 12296 | tf_op jit(solution)/shard_map/ppermute | solution.py:38
  31.3 3.6 %collective-permute-start.1 = (bf16[2,8,128]{2,1,0:T(8,128)(2,1)S(1)}, bf16[2,8,128]{2,1,0:T(8,128)(2,1)S(1)}, u32[]{:S(2)}, u32[]{:S(2)}) collective-permute-start(bf16[2,8,128]{2,1,0:T(8,128)(2,1)S(1)} %pad_maximum_fusion.4), channel_id=1, source_target_pairs={{0,32},{16,48},{32,64},{48,80},{64,96},{80,112},{96,128},{112,144}... | collective-permute-start | bytes 12296 | tf_op jit(solution)/shard_map/ppermute | solution.py:38
  36.8 1.5 shard_map.64
  38.3 10.1 %all-to-all-start = ((bf16[8,14,8,128]{3,2,1,0:T(8,128)(2,1)}), bf16[8,14,8,128]{3,2,1,0:T(8,128)(2,1)S(1)}, u32[]{:S(2)}, u32[]{:S(2)}) async-start(bf16[8,14,8,128]{3,2,1,0:T(8,128)(2,1)} %shard_map.64), calls=%async_computation | async-start | bytes 458752 | tf_op jit(solution)/shard_map/all_to_all | solution.py:242
  49.1 1.3 collective-permute-start.7
  51.2 8.4 %all-to-all-done.mine_ref = bf16[8,14,8,128]{3,2,1,0:T(8,128)(2,1)S(1)} async-done(((bf16[8,14,8,128]{3,2,1,0:T(8,128)(2,1)}), bf16[8,14,8,128]{3,2,1,0:T(8,128)(2,1)S(1)}, u32[]{:S(2)}, u32[]{:S(2)}) %all-to-all-start) | async-done | bytes 229408 | tf_op jit(solution)/shard_map/all_to_all | solution.py:242
  59.6 6.3 %collective-permute-start.9 = (bf16[8,14,8,128]{3,2,1,0:T(8,128)(2,1)S(1)}, bf16[8,14,8,128]{3,2,1,0:T(8,128)(2,1)S(1)}, u32[]{:S(2)}, u32[]{:S(2)}) collective-permute-start(bf16[8,14,8,128]{3,2,1,0:T(8,128)(2,1)S(1)} %all-to-all-done.mine_ref), channel_id=1, source_target_pairs={{0,1},{1,0},{2,3},{3,2},{4,5},{5,4},{6,7},{7,6},{8,9},{9,8},{10,11... | collective-permute-start | bytes 688136 | tf_op jit(solution)/shard_map/ppermute | solution.py:33
  67.0 15.6 %collective-permute-start.13 = (bf16[2,512,256]{2,1,0:T(8,128)(2,1)S(1)}, bf16[2,512,256]{2,1,0:T(8,128)(2,1)S(1)}, u32[]{:S(2)}, u32[]{:S(2)}) collective-permute-start(bf16[2,512,256]{2,1,0:T(8,128)(2,1)S(1)} %pad_maximum_fusion.refs_4_), channel_id=1, source_target_pairs={{0,128},{1,129},{2,130},{3,131},{4,132},{5,133},{6,134},{7,135},{8... | collective-permute-start | bytes 1572872 | tf_op jit(solution)/shard_map/ppermute | solution.py:33
  82.6 3.2 %collective-permute-start.12 = (bf16[2,512,256]{2,1,0:T(8,128)(2,1)S(1)}, bf16[2,512,256]{2,1,0:T(8,128)(2,1)S(1)}, u32[]{:S(2)}, u32[]{:S(2)}) collective-permute-start(bf16[2,512,256]{2,1,0:T(8,128)(2,1)S(1)} %pad_maximum_fusion.refs_4_), channel_id=1, source_target_pairs={{0,256},{1,257},{2,258},{3,259},{4,260},{5,261},{6,262},{7,263},{8... | collective-permute-start | bytes 1572872 | tf_op jit(solution)/shard_map/ppermute | solution.py:33
  85.8 4.0 %collective-permute-start.11 = (bf16[2,512,256]{2,1,0:T(8,128)(2,1)S(1)}, bf16[2,512,256]{2,1,0:T(8,128)(2,1)S(1)}, u32[]{:S(2)}, u32[]{:S(2)}) collective-permute-start(bf16[2,512,256]{2,1,0:T(8,128)(2,1)S(1)} %pad_maximum_fusion.refs_4_), channel_id=1, source_target_pairs={{0,384},{1,385},{2,386},{3,387},{4,388},{5,389},{6,390},{7,391},{8... | collective-permute-start | bytes 1572872 | tf_op jit(solution)/shard_map/ppermute | solution.py:33
  89.7 18.1 %shard_map.65 = bf16[128,512]{1,0:T(8,128)(2,1)S(1)} custom-call(s32[2]{0:T(128)S(1)} %pad_add_fusion.1.place, bf16[128,512]{1,0:T(8,128)(2,1)S(1)} %copy-done, bf16[8,14,8,128]{3,2,1,0:T(8,128)(2,1)S(1)} %all-to-all-done.mine_ref, bf16[8,14,8,128]{3,2,1,0:T(8,128)(2,1)S(1)} %collective-permute-done.9.other_ref), custom_call_target="tpu_custom_call" | custom-call | flops 20000000000 | bytes 1048576 | tf_op jit(solution)/shard_map/pallas_call | solution.py:123
  107.9 9.6 %collective-permute-start.10 = (bf16[128,512]{1,0:T(8,128)(2,1)S(1)}, bf16[128,512]{1,0:T(8,128)(2,1)S(1)}, u32[]{:S(2)}, u32[]{:S(2)}) collective-permute-start(bf16[128,512]{1,0:T(8,128)(2,1)S(1)} %shard_map.65), channel_id=1, source_target_pairs={{0,2},{1,3},{2,0},{3,1},{4,6},{5,7},{6,4},{7,5},{8,10},{9,11},{10,... | collective-permute-start | bytes 393224 | tf_op jit(solution)/shard_map/ppermute | solution.py:33
  117.5 2.3 %collective-permute-done.10 = bf16[128,512]{1,0:T(8,128)(2,1)S(1)} collective-permute-done((bf16[128,512]{1,0:T(8,128)(2,1)S(1)}, bf16[128,512]{1,0:T(8,128)(2,1)S(1)}, u32[]{:S(2)}, u32[]{:S(2)}) %collective-permute-start.10) | collective-permute-done | bytes 131104 | tf_op jit(solution)/shard_map/ppermute | solution.py:33
  119.9 2.0 %collective-permute-start.16 = (bf16[2,128,512]{2,1,0:T(8,128)(2,1)S(1)}, bf16[2,128,512]{2,1,0:T(8,128)(2,1)S(1)}, u32[]{:S(2)}, u32[]{:S(2)}) collective-permute-start(bf16[2,128,512]{2,1,0:T(8,128)(2,1)S(1)} %pad_maximum_fusion.1.refs_0_), channel_id=1, source_target_pairs={{0,16},{1,17},{2,18},{3,19},{4,20},{5,21},{6,22},{7,23},{8,24},{9,... | collective-permute-start | bytes 786440 | tf_op jit(solution)/shard_map/ppermute | solution.py:33
  121.9 1.9 %collective-permute-start.15 = (bf16[2,128,512]{2,1,0:T(8,128)(2,1)S(1)}, bf16[2,128,512]{2,1,0:T(8,128)(2,1)S(1)}, u32[]{:S(2)}, u32[]{:S(2)}) collective-permute-start(bf16[2,128,512]{2,1,0:T(8,128)(2,1)S(1)} %pad_maximum_fusion.1.refs_0_), channel_id=1, source_target_pairs={{0,32},{1,33},{2,34},{3,35},{4,36},{5,37},{6,38},{7,39},{8,40},{9,... | collective-permute-start | bytes 786440 | tf_op jit(solution)/shard_map/ppermute | solution.py:33
  123.8 4.5 %collective-permute-start.14 = (bf16[2,128,512]{2,1,0:T(8,128)(2,1)S(1)}, bf16[2,128,512]{2,1,0:T(8,128)(2,1)S(1)}, u32[]{:S(2)}, u32[]{:S(2)}) collective-permute-start(bf16[2,128,512]{2,1,0:T(8,128)(2,1)S(1)} %pad_maximum_fusion.1.refs_0_), channel_id=1, source_target_pairs={{0,48},{1,49},{2,50},{3,51},{4,52},{5,53},{6,54},{7,55},{8,56},{9,... | collective-permute-start | bytes 786440 | tf_op jit(solution)/shard_map/ppermute | solution.py:33
  128.4 2.6 %collective-permute-done.16.refs_3_ = bf16[2,128,512]{2,1,0:T(8,128)(2,1)S(1)} collective-permute-done((bf16[2,128,512]{2,1,0:T(8,128)(2,1)S(1)}, bf16[2,128,512]{2,1,0:T(8,128)(2,1)S(1)}, u32[]{:S(2)}, u32[]{:S(2)}) %collective-permute-start.16) | collective-permute-done | bytes 262176 | tf_op jit(solution)/shard_map/ppermute | solution.py:33
  131.0 2.8 %collective-permute-done.14.refs_1_ = bf16[2,128,512]{2,1,0:T(8,128)(2,1)S(1)} collective-permute-done((bf16[2,128,512]{2,1,0:T(8,128)(2,1)S(1)}, bf16[2,128,512]{2,1,0:T(8,128)(2,1)S(1)}, u32[]{:S(2)}, u32[]{:S(2)}) %collective-permute-start.14) | collective-permute-done | bytes 262176 | tf_op jit(solution)/shard_map/ppermute | solution.py:33
  133.8 1.8 shard_map.66
  135.7 8.6 %collective-permute-start.17 = (bf16[4,2,128,256]{3,2,1,0:T(8,128)(2,1)S(1)}, bf16[4,2,128,256]{3,2,1,0:T(8,128)(2,1)S(1)}, u32[]{:S(2)}, u32[]{:S(2)}) collective-permute-start(bf16[4,2,128,256]{3,2,1,0:T(8,128)(2,1)S(1)} %slice_bitcast_fusion), channel_id=1, source_target_pairs={{0,1},{1,0},{2,3},{3,2},{4,5},{5,4},{6,7},{7,6},{8,9},{9,8},{10,11... | collective-permute-start | bytes 1572872 | tf_op jit(solution)/shard_map/ppermute | solution.py:33
  144.3 1.5 collective-permute-done.17
  146.0 8.8 %collective-permute-start.18 = (bf16[2,128,256]{2,1,0:T(8,128)(2,1)S(1)}, bf16[2,128,256]{2,1,0:T(8,128)(2,1)S(1)}, u32[]{:S(2)}, u32[]{:S(2)}) collective-permute-start(bf16[2,128,256]{2,1,0:T(8,128)(2,1)S(1)} %get-tuple-element.25), channel_id=1, source_target_pairs={{0,12},{1,13},{2,14},{3,15},{4,8},{5,9},{6,10},{7,11},{8,4},{9,5},... | collective-permute-start | bytes 393224 | tf_op jit(solution)/shard_map/ppermute | solution.py:33
  154.8 4.6 %collective-permute-start.20 = (bf16[2,128,256]{2,1,0:T(8,128)(2,1)S(1)}, bf16[2,128,256]{2,1,0:T(8,128)(2,1)S(1)}, u32[]{:S(2)}, u32[]{:S(2)}) collective-permute-start(bf16[2,128,256]{2,1,0:T(8,128)(2,1)S(1)} %get-tuple-element.26), channel_id=1, source_target_pairs={{0,4},{1,5},{2,6},{3,7},{4,0},{5,1},{6,2},{7,3},{8,12},{9,13},{10,... | collective-permute-start | bytes 393224 | tf_op jit(solution)/shard_map/ppermute | solution.py:33
  159.4 1.9 %collective-permute-start.19 = (bf16[2,128,256]{2,1,0:T(8,128)(2,1)S(1)}, bf16[2,128,256]{2,1,0:T(8,128)(2,1)S(1)}, u32[]{:S(2)}, u32[]{:S(2)}) collective-permute-start(bf16[2,128,256]{2,1,0:T(8,128)(2,1)S(1)} %get-tuple-element.27), channel_id=1, source_target_pairs={{0,8},{1,9},{2,10},{3,11},{4,12},{5,13},{6,14},{7,15},{8,0},{9,1},... | collective-permute-start | bytes 393224 | tf_op jit(solution)/shard_map/ppermute | solution.py:33
  161.4 6.2 %collective-permute-done.20 = bf16[2,128,256]{2,1,0:T(8,128)(2,1)S(1)} collective-permute-done((bf16[2,128,256]{2,1,0:T(8,128)(2,1)S(1)}, bf16[2,128,256]{2,1,0:T(8,128)(2,1)S(1)}, u32[]{:S(2)}, u32[]{:S(2)}) %collective-permute-start.20) | collective-permute-done | bytes 131104 | tf_op jit(solution)/shard_map/ppermute | solution.py:33
  167.6 11.3 %collective-permute-done.19 = bf16[2,128,256]{2,1,0:T(8,128)(2,1)S(1)} collective-permute-done((bf16[2,128,256]{2,1,0:T(8,128)(2,1)S(1)}, bf16[2,128,256]{2,1,0:T(8,128)(2,1)S(1)}, u32[]{:S(2)}, u32[]{:S(2)}) %collective-permute-start.19) | collective-permute-done | bytes 131104 | tf_op jit(solution)/shard_map/ppermute | solution.py:33
  179.0 4.7 %collective-permute-start.21 = (bf16[128,256]{1,0:T(8,128)(2,1)S(1)}, bf16[128,256]{1,0:T(8,128)(2,1)S(1)}, u32[]{:S(2)}, u32[]{:S(2)}) collective-permute-start(bf16[128,256]{1,0:T(8,128)(2,1)S(1)} %get-tuple-element.30), channel_id=1, source_target_pairs={{0,16},{1,48},{2,18},{3,50},{4,20},{5,52},{6,22},{7,54},{8,24},{9,... | collective-permute-start | bytes 196616 | tf_op jit(solution)/shard_map/ppermute | solution.py:33
  183.7 1.9 %collective-permute-start.22 = (bf16[128,256]{1,0:T(8,128)(2,1)S(1)}, bf16[128,256]{1,0:T(8,128)(2,1)S(1)}, u32[]{:S(2)}, u32[]{:S(2)}) collective-permute-start(bf16[128,256]{1,0:T(8,128)(2,1)S(1)} %get-tuple-element.31), channel_id=1, source_target_pairs={{0,0},{1,32},{2,2},{3,34},{4,4},{5,36},{6,6},{7,38},{8,8},{9,40},{... | collective-permute-start | bytes 196616 | tf_op jit(solution)/shard_map/ppermute | solution.py:33
  185.8 5.0 %collective-permute-done.22 = bf16[128,256]{1,0:T(8,128)(2,1)S(1)} collective-permute-done((bf16[128,256]{1,0:T(8,128)(2,1)S(1)}, bf16[128,256]{1,0:T(8,128)(2,1)S(1)}, u32[]{:S(2)}, u32[]{:S(2)}) %collective-permute-start.22) | collective-permute-done | bytes 65568 | tf_op jit(solution)/shard_map/ppermute | solution.py:33
  (54 shorter events, 7.2 us)
Async XLA Ops:
  0.0 11.1 %copy-start.2 = (bf16[8,128]{1,0:T(8,128)(2,1)S(1)}, bf16[8,128]{1,0:T(8,128)(2,1)}, u32[]{:S(2)}) copy-start(bf16[8,128]{1,0:T(8,128)(2,1)} %refs_0_.1) | copy-start | bytes 6148
  0.0 38.3 %collective-permute-start.5 = (bf16[512,256]{1,0:T(8,128)(2,1)}, bf16[512,256]{1,0:T(8,128)(2,1)S(1)}, u32[]{:S(2)}, u32[]{:S(2)}) collective-permute-start(bf16[512,256]{1,0:T(8,128)(2,1)} %param.11), channel_id=1, source_target_pairs={{2,74},{3,75},{6,78},{7,79},{10,2},{11,3},{14,6},{15,7},{18,90},{1... | collective-permute-start | bytes 786440 | tf_op jit(solution)/shard_map/ppermute | solution.py:33
  0.8 37.5 %collective-permute-start.4 = (bf16[512,256]{1,0:T(8,128)(2,1)}, bf16[512,256]{1,0:T(8,128)(2,1)S(1)}, u32[]{:S(2)}, u32[]{:S(2)}) collective-permute-start(bf16[512,256]{1,0:T(8,128)(2,1)} %param.11), channel_id=1, source_target_pairs={{0,8},{1,9},{4,12},{5,13},{8,64},{9,65},{12,68},{13,69},{16,24},{1... | collective-permute-start | bytes 786440 | tf_op jit(solution)/shard_map/ppermute | solution.py:33
  11.1 9.4 %copy-start.4 = (bf16[8,128]{1,0:T(8,128)(2,1)S(1)}, bf16[8,128]{1,0:T(8,128)(2,1)}, u32[]{:S(2)}) copy-start(bf16[8,128]{1,0:T(8,128)(2,1)} %refs_2_.1) | copy-start | bytes 6148
  11.1 9.4 %copy-start.5 = (bf16[8,128]{1,0:T(8,128)(2,1)S(1)}, bf16[8,128]{1,0:T(8,128)(2,1)}, u32[]{:S(2)}) copy-start(bf16[8,128]{1,0:T(8,128)(2,1)} %refs_3_.1) | copy-start | bytes 6148
  11.8 8.7 %copy-start.3 = (bf16[8,128]{1,0:T(8,128)(2,1)S(1)}, bf16[8,128]{1,0:T(8,128)(2,1)}, u32[]{:S(2)}) copy-start(bf16[8,128]{1,0:T(8,128)(2,1)} %refs_1_.1) | copy-start | bytes 6148
  11.8 19.4 %collective-permute-start.3 = (bf16[2,8,128]{2,1,0:T(8,128)(2,1)S(1)}, bf16[2,8,128]{2,1,0:T(8,128)(2,1)S(1)}, u32[]{:S(2)}, u32[]{:S(2)}) collective-permute-start(bf16[2,8,128]{2,1,0:T(8,128)(2,1)S(1)} %pad_maximum_fusion.4), channel_id=1, source_target_pairs={{0,64},{16,80},{32,96},{48,112},{64,128},{80,144},{96,160},{112,17... | collective-permute-start | bytes 12296 | tf_op jit(solution)/shard_map/ppermute | solution.py:38
  20.5 15.1 %collective-permute-start = (bf16[4,8,128]{2,1,0:T(8,128)(2,1)S(1)}, bf16[4,8,128]{2,1,0:T(8,128)(2,1)S(1)}, u32[]{:S(2)}, u32[]{:S(2)}) collective-permute-start(bf16[4,8,128]{2,1,0:T(8,128)(2,1)S(1)} %pad_maximum_fusion.3), channel_id=1, source_target_pairs={{0,16},{16,32},{32,48},{48,64},{64,80},{80,96},{96,112},{112,128},... | collective-permute-start | bytes 24584 | tf_op jit(solution)/shard_map/ppermute | solution.py:38
  23.7 11.1 %collective-permute-start.2 = (bf16[2,8,128]{2,1,0:T(8,128)(2,1)S(1)}, bf16[2,8,128]{2,1,0:T(8,128)(2,1)S(1)}, u32[]{:S(2)}, u32[]{:S(2)}) collective-permute-start(bf16[2,8,128]{2,1,0:T(8,128)(2,1)S(1)} %pad_maximum_fusion.4), channel_id=1, source_target_pairs={{0,48},{16,64},{32,80},{48,96},{64,112},{80,128},{96,144},{112,160... | collective-permute-start | bytes 12296 | tf_op jit(solution)/shard_map/ppermute | solution.py:38
  31.2 4.4 %copy-start.7 = (bf16[2,8,128]{2,1,0:T(8,128)(2,1)}, bf16[2,8,128]{2,1,0:T(8,128)(2,1)S(1)}, u32[]{:S(2)}) copy-start(bf16[2,8,128]{2,1,0:T(8,128)(2,1)S(1)} %collective-permute-done.3.refs_7_) | copy-start | bytes 12292
  31.3 4.4 %collective-permute-start.1 = (bf16[2,8,128]{2,1,0:T(8,128)(2,1)S(1)}, bf16[2,8,128]{2,1,0:T(8,128)(2,1)S(1)}, u32[]{:S(2)}, u32[]{:S(2)}) collective-permute-start(bf16[2,8,128]{2,1,0:T(8,128)(2,1)S(1)} %pad_maximum_fusion.4), channel_id=1, source_target_pairs={{0,32},{16,48},{32,64},{48,80},{64,96},{80,112},{96,128},{112,144}... | collective-permute-start | bytes 12296 | tf_op jit(solution)/shard_map/ppermute | solution.py:38
  34.9 0.7 copy-start.8
  38.3 10.8 %copy-start.1 = (bf16[512,256]{1,0:T(8,128)(2,1)S(1)}, bf16[512,256]{1,0:T(8,128)(2,1)}, u32[]{:S(2)}) copy-start(bf16[512,256]{1,0:T(8,128)(2,1)} %param.11) | copy-start | bytes 786436
  38.3 21.4 %all-to-all-start = ((bf16[8,14,8,128]{3,2,1,0:T(8,128)(2,1)}), bf16[8,14,8,128]{3,2,1,0:T(8,128)(2,1)S(1)}, u32[]{:S(2)}, u32[]{:S(2)}) async-start(bf16[8,14,8,128]{3,2,1,0:T(8,128)(2,1)} %shard_map.64), calls=%async_computation | async-start | bytes 458752 | tf_op jit(solution)/shard_map/all_to_all | solution.py:242
  48.4 2.8 %collective-permute-start.6 = (bf16[512,256]{1,0:T(8,128)(2,1)S(1)}, bf16[512,256]{1,0:T(8,128)(2,1)S(1)}, u32[]{:S(2)}, u32[]{:S(2)}) collective-permute-start(bf16[512,256]{1,0:T(8,128)(2,1)S(1)} %collective-permute-done.4), channel_id=1, source_target_pairs={{2,10},{3,11},{6,14},{7,15},{8,64},{9,65},{12,68},{13,69},{18,26},... | collective-permute-start | bytes 786440 | tf_op jit(solution)/shard_map/ppermute | solution.py:33
  49.1 16.8 %collective-permute-start.7 = (bf16[512,256]{1,0:T(8,128)(2,1)S(1)}, bf16[512,256]{1,0:T(8,128)(2,1)S(1)}, u32[]{:S(2)}, u32[]{:S(2)}) collective-permute-start(bf16[512,256]{1,0:T(8,128)(2,1)S(1)} %copy-done.1), channel_id=1, source_target_pairs={{2,0},{3,1},{6,4},{7,5},{10,8},{11,9},{14,12},{15,13},{18,16},{19,... | collective-permute-start | bytes 786440 | tf_op jit(solution)/shard_map/ppermute | solution.py:33
  50.4 15.5 %collective-permute-start.8 = (bf16[512,256]{1,0:T(8,128)(2,1)S(1)}, bf16[512,256]{1,0:T(8,128)(2,1)S(1)}, u32[]{:S(2)}, u32[]{:S(2)}) collective-permute-start(bf16[512,256]{1,0:T(8,128)(2,1)S(1)} %collective-permute-done.5), channel_id=1, source_target_pairs={{2,72},{3,73},{6,76},{7,77},{8,2},{9,3},{12,6},{13,7},{18,88},{19,... | collective-permute-start | bytes 786440 | tf_op jit(solution)/shard_map/ppermute | solution.py:33
  59.6 7.4 %collective-permute-start.9 = (bf16[8,14,8,128]{3,2,1,0:T(8,128)(2,1)S(1)}, bf16[8,14,8,128]{3,2,1,0:T(8,128)(2,1)S(1)}, u32[]{:S(2)}, u32[]{:S(2)}) collective-permute-start(bf16[8,14,8,128]{3,2,1,0:T(8,128)(2,1)S(1)} %all-to-all-done.mine_ref), channel_id=1, source_target_pairs={{0,1},{1,0},{2,3},{3,2},{4,5},{5,4},{6,7},{7,6},{8,9},{9,8},{10,11... | collective-permute-start | bytes 688136 | tf_op jit(solution)/shard_map/ppermute | solution.py:33
  66.0 23.8 %copy-start = (bf16[128,512]{1,0:T(8,128)(2,1)S(1)}, bf16[128,512]{1,0:T(8,128)(2,1)}, u32[]{:S(2)}) copy-start(bf16[128,512]{1,0:T(8,128)(2,1)} %q_ref.1) | copy-start | bytes 393220
  67.0 52.8 %collective-permute-start.13 = (bf16[2,512,256]{2,1,0:T(8,128)(2,1)S(1)}, bf16[2,512,256]{2,1,0:T(8,128)(2,1)S(1)}, u32[]{:S(2)}, u32[]{:S(2)}) collective-permute-start(bf16[2,512,256]{2,1,0:T(8,128)(2,1)S(1)} %pad_maximum_fusion.refs_4_), channel_id=1, source_target_pairs={{0,128},{1,129},{2,130},{3,131},{4,132},{5,133},{6,134},{7,135},{8... | collective-permute-start | bytes 1572872 | tf_op jit(solution)/shard_map/ppermute | solution.py:33
  82.6 37.2 %collective-permute-start.12 = (bf16[2,512,256]{2,1,0:T(8,128)(2,1)S(1)}, bf16[2,512,256]{2,1,0:T(8,128)(2,1)S(1)}, u32[]{:S(2)}, u32[]{:S(2)}) collective-permute-start(bf16[2,512,256]{2,1,0:T(8,128)(2,1)S(1)} %pad_maximum_fusion.refs_4_), channel_id=1, source_target_pairs={{0,256},{1,257},{2,258},{3,259},{4,260},{5,261},{6,262},{7,263},{8... | collective-permute-start | bytes 1572872 | tf_op jit(solution)/shard_map/ppermute | solution.py:33
  85.8 34.1 %collective-permute-start.11 = (bf16[2,512,256]{2,1,0:T(8,128)(2,1)S(1)}, bf16[2,512,256]{2,1,0:T(8,128)(2,1)S(1)}, u32[]{:S(2)}, u32[]{:S(2)}) collective-permute-start(bf16[2,512,256]{2,1,0:T(8,128)(2,1)S(1)} %pad_maximum_fusion.refs_4_), channel_id=1, source_target_pairs={{0,384},{1,385},{2,386},{3,387},{4,388},{5,389},{6,390},{7,391},{8... | collective-permute-start | bytes 1572872 | tf_op jit(solution)/shard_map/ppermute | solution.py:33
  107.9 12.0 %collective-permute-start.10 = (bf16[128,512]{1,0:T(8,128)(2,1)S(1)}, bf16[128,512]{1,0:T(8,128)(2,1)S(1)}, u32[]{:S(2)}, u32[]{:S(2)}) collective-permute-start(bf16[128,512]{1,0:T(8,128)(2,1)S(1)} %shard_map.65), channel_id=1, source_target_pairs={{0,2},{1,3},{2,0},{3,1},{4,6},{5,7},{6,4},{7,5},{8,10},{9,11},{10,... | collective-permute-start | bytes 393224 | tf_op jit(solution)/shard_map/ppermute | solution.py:33
  119.9 11.1 %collective-permute-start.16 = (bf16[2,128,512]{2,1,0:T(8,128)(2,1)S(1)}, bf16[2,128,512]{2,1,0:T(8,128)(2,1)S(1)}, u32[]{:S(2)}, u32[]{:S(2)}) collective-permute-start(bf16[2,128,512]{2,1,0:T(8,128)(2,1)S(1)} %pad_maximum_fusion.1.refs_0_), channel_id=1, source_target_pairs={{0,16},{1,17},{2,18},{3,19},{4,20},{5,21},{6,22},{7,23},{8,24},{9,... | collective-permute-start | bytes 786440 | tf_op jit(solution)/shard_map/ppermute | solution.py:33
  121.9 9.1 %collective-permute-start.15 = (bf16[2,128,512]{2,1,0:T(8,128)(2,1)S(1)}, bf16[2,128,512]{2,1,0:T(8,128)(2,1)S(1)}, u32[]{:S(2)}, u32[]{:S(2)}) collective-permute-start(bf16[2,128,512]{2,1,0:T(8,128)(2,1)S(1)} %pad_maximum_fusion.1.refs_0_), channel_id=1, source_target_pairs={{0,32},{1,33},{2,34},{3,35},{4,36},{5,37},{6,38},{7,39},{8,40},{9,... | collective-permute-start | bytes 786440 | tf_op jit(solution)/shard_map/ppermute | solution.py:33
  123.8 10.0 %collective-permute-start.14 = (bf16[2,128,512]{2,1,0:T(8,128)(2,1)S(1)}, bf16[2,128,512]{2,1,0:T(8,128)(2,1)S(1)}, u32[]{:S(2)}, u32[]{:S(2)}) collective-permute-start(bf16[2,128,512]{2,1,0:T(8,128)(2,1)S(1)} %pad_maximum_fusion.1.refs_0_), channel_id=1, source_target_pairs={{0,48},{1,49},{2,50},{3,51},{4,52},{5,53},{6,54},{7,55},{8,56},{9,... | collective-permute-start | bytes 786440 | tf_op jit(solution)/shard_map/ppermute | solution.py:33
  135.7 10.2 %collective-permute-start.17 = (bf16[4,2,128,256]{3,2,1,0:T(8,128)(2,1)S(1)}, bf16[4,2,128,256]{3,2,1,0:T(8,128)(2,1)S(1)}, u32[]{:S(2)}, u32[]{:S(2)}) collective-permute-start(bf16[4,2,128,256]{3,2,1,0:T(8,128)(2,1)S(1)} %slice_bitcast_fusion), channel_id=1, source_target_pairs={{0,1},{1,0},{2,3},{3,2},{4,5},{5,4},{6,7},{7,6},{8,9},{9,8},{10,11... | collective-permute-start | bytes 1572872 | tf_op jit(solution)/shard_map/ppermute | solution.py:33
  146.0 15.4 %collective-permute-start.18 = (bf16[2,128,256]{2,1,0:T(8,128)(2,1)S(1)}, bf16[2,128,256]{2,1,0:T(8,128)(2,1)S(1)}, u32[]{:S(2)}, u32[]{:S(2)}) collective-permute-start(bf16[2,128,256]{2,1,0:T(8,128)(2,1)S(1)} %get-tuple-element.25), channel_id=1, source_target_pairs={{0,12},{1,13},{2,14},{3,15},{4,8},{5,9},{6,10},{7,11},{8,4},{9,5},... | collective-permute-start | bytes 393224 | tf_op jit(solution)/shard_map/ppermute | solution.py:33
  154.8 12.8 %collective-permute-start.20 = (bf16[2,128,256]{2,1,0:T(8,128)(2,1)S(1)}, bf16[2,128,256]{2,1,0:T(8,128)(2,1)S(1)}, u32[]{:S(2)}, u32[]{:S(2)}) collective-permute-start(bf16[2,128,256]{2,1,0:T(8,128)(2,1)S(1)} %get-tuple-element.26), channel_id=1, source_target_pairs={{0,4},{1,5},{2,6},{3,7},{4,0},{5,1},{6,2},{7,3},{8,12},{9,13},{10,... | collective-permute-start | bytes 393224 | tf_op jit(solution)/shard_map/ppermute | solution.py:33
  159.4 19.5 %collective-permute-start.19 = (bf16[2,128,256]{2,1,0:T(8,128)(2,1)S(1)}, bf16[2,128,256]{2,1,0:T(8,128)(2,1)S(1)}, u32[]{:S(2)}, u32[]{:S(2)}) collective-permute-start(bf16[2,128,256]{2,1,0:T(8,128)(2,1)S(1)} %get-tuple-element.27), channel_id=1, source_target_pairs={{0,8},{1,9},{2,10},{3,11},{4,12},{5,13},{6,14},{7,15},{8,0},{9,1},... | collective-permute-start | bytes 393224 | tf_op jit(solution)/shard_map/ppermute | solution.py:33
  179.0 6.8 %collective-permute-start.21 = (bf16[128,256]{1,0:T(8,128)(2,1)S(1)}, bf16[128,256]{1,0:T(8,128)(2,1)S(1)}, u32[]{:S(2)}, u32[]{:S(2)}) collective-permute-start(bf16[128,256]{1,0:T(8,128)(2,1)S(1)} %get-tuple-element.30), channel_id=1, source_target_pairs={{0,16},{1,48},{2,18},{3,50},{4,20},{5,52},{6,22},{7,54},{8,24},{9,... | collective-permute-start | bytes 196616 | tf_op jit(solution)/shard_map/ppermute | solution.py:33
  183.7 7.1 %collective-permute-start.22 = (bf16[128,256]{1,0:T(8,128)(2,1)S(1)}, bf16[128,256]{1,0:T(8,128)(2,1)S(1)}, u32[]{:S(2)}, u32[]{:S(2)}) collective-permute-start(bf16[128,256]{1,0:T(8,128)(2,1)S(1)} %get-tuple-element.31), channel_id=1, source_target_pairs={{0,0},{1,32},{2,2},{3,34},{4,4},{5,36},{6,6},{7,38},{8,8},{9,40},{... | collective-permute-start | bytes 196616 | tf_op jit(solution)/shard_map/ppermute | solution.py:33
  (2 other events, 1.2 us)

commit v6 on v2

--- a/solution.py
+++ b/solution.py
@@ -44,12 +44,19 @@
     rows, wide = q_ref.shape
     width = k_ref.shape[1]
     heads = wide // width
-    block_now, core = place[0], place[1]
+    block_now, core, z = place[0], place[1], place[2]
     spots = W1 // rows + 1
 
+    def spread(ref, number):
+        rows_of = []
+        for to in range(ZS):
+            way = to ^ z
+            at = way // 4 + way // 2 % 2 * 2 + way % 2 * 4
+            rows_of.append(ref[at, number].astype(jnp.float32))
+        return jnp.stack(rows_of)
+
     def whole(number):
-        mine = mine_ref[:, number].astype(jnp.float32)
-        other = other_ref[:, number].astype(jnp.float32)
+        mine, other = spread(mine_ref, number), spread(other_ref, number)
         first, second = jnp.where(core == 1, other, mine), jnp.where(core == 1, mine, other)
         return jnp.concatenate([first[:, None], second[:, None]], axis=1).reshape(rows, width)
 
@@ -143,20 +150,19 @@
 
 def pack_kernel(count, *refs):
     own, before, older, out_ref = refs[:4], refs[4], refs[5:-1], refs[-1]
-    for to in range(out_ref.shape[0]):
-        for kind in range(2):
-            line = [ref.at[kind] for ref in older[::-1]] + [before.at[kind], own[kind]]
-            for spot, ref in enumerate(line):
-                out_ref[to, kind * count + spot] = ref[...]
-            out_ref[to, 2 * count + kind] = before[2 + kind]
-            out_ref[to, 2 * count + 2 + kind] = own[2 + kind][...]
+    for kind in range(2):
+        line = [ref.at[kind] for ref in older[::-1]] + [before.at[kind], own[kind]]
+        for spot, ref in enumerate(line):
+            out_ref[0, kind * count + spot] = ref[...]
+        out_ref[0, 2 * count + kind] = before[2 + kind]
+        out_ref[0, 2 * count + 2 + kind] = own[2 + kind][...]
 
 
 def pack(own, before, older):
     count = len(older) + 2
     return pl.pallas_call(
         functools.partial(pack_kernel, count),
-        out_shape=jax.ShapeDtypeStruct((ZS, 2 * count + 4) + own[0].shape, own[0].dtype),
+        out_shape=jax.ShapeDtypeStruct((1, 2 * count + 4) + own[0].shape, own[0].dtype),
         in_specs=[pl.BlockSpec(memory_space=pltpu.VMEM)] * (5 + len(older)),
         out_specs=pl.BlockSpec(memory_space=pltpu.VMEM),
     )(*own, before, *older)
@@ -164,9 +170,9 @@
 
 def project_kernel(place, *refs):
     tokens, columns, out_ref = refs[:YS], refs[YS : YS + XS], refs[-1]
-    x, y, c = place[0], place[1], place[2]
+    x, y, far, c = place[0], place[1], place[2], place[3]
     for d in range(XS):
-        to = lax.rem(x + d, XS)
+        to = lax.rem(x + d, XS) ^ far
         for e in range(YS):
             slot = lax.rem(y + e + YS - 2 * c, YS)
             total = jnp.dot(tokens[e][0], columns[d][0], preferred_element_type=jnp.float32)
@@ -200,50 +206,57 @@
     x, half, y = seq // (HS * YS), seq // YS % HS, seq % YS
     z, c = head // CS, head % CS
 
-    def first_hop(x, h, y, z, c):
-        return (x, h, y, z ^ 1, c) if h != z % 2 else (x, h + 1, y, z, c)
-
-    def second_hop(x, h, y, z, c):
-        return (x, h + 1, y, z ^ 1, c) if h != z % 2 else None
-
-    one_way = moved(w_out, first_hop)
-    other_way = moved(w_out, second_hop)
-
     piece = jnp.stack([long_keys, long_values, short_keys, short_values])
     before = later(piece, 1)
     older = [later(piece[:2], steps) for steps in range(2, W1 // rows + 1)]
-    mine = pack((long_keys, long_values, short_keys, short_values), before, older)
-    lines = [[z * CS + core for z in range(ZS)] for core in range(CS)]
-    over_z = lax.all_to_all(mine, "head", 0, 0, axis_index_groups=lines, tiled=True)
-    over_core = moved(over_z, lambda x, h, y, z, c: (x, h, y, z, 1 - c))
+    held = pack((long_keys, long_values, short_keys, short_values), before, older)
+    held, w_out = lax.optimization_barrier((held, w_out))
+
+    first_up = {0: 5, 2: 7, 4: 8, 6: 10, 9: 12, 11: 14, 13: 1, 15: 3}
+    second_up = {first_up[spot]: (spot + 8) % 16 for spot in first_up}
+    stay = [spot for spot in range(16) if spot not in first_up]
+    first_up.update({spot: spot ^ 1 for spot in stay})
+    first_down = {spot: (spot - 4) % 16 for spot in stay}
+    second_down = {first_down[spot]: (spot ^ 1) ^ 8 for spot in stay}
+
+    def along(table):
+        def target(x, h, y, z, c):
+            to = table.get(h * ZS + z)
+            return None if to is None else (x, to // ZS, y, to % ZS, c)
+
+        return target
+
+    for far in (4, 2, 1):
+        if far == 4:
+            upward, downward = moved(w_out, along(first_up)), moved(w_out, along(first_down))
+        came = moved(held, lambda x, h, y, z, c, far=far: (x, h, y, z ^ far, c))
+        held = jnp.concatenate([held, came])
+    held, upward, downward = lax.optimization_barrier((held, upward, downward))
+    over_core = moved(held, lambda x, h, y, z, c: (x, h, y, z, 1 - c))
+    attended = attention(jnp.stack([seq, c, z]), queries, held, over_core)
+    long_way, downward = moved(upward, along(second_up)), moved(downward, along(second_down))
 
     near_by = half == z % 2
     pair = jnp.stack(
-        [jnp.where(near_by, w_out, one_way), jnp.where(near_by, one_way, other_way)]
+        [jnp.where(near_by, w_out, long_way), jnp.where(near_by, upward, downward)]
     )
-    pair, over_core = lax.optimization_barrier((pair, over_core))
+    pair, attended = lax.optimization_barrier((pair, attended))
     from_x = [pair] + [
         moved(pair, lambda x, h, y, z, c, d=d: (x - d, h, y, z, c)) for d in (1, 2, 3)
     ]
-
-    attended = attention(jnp.stack([seq, c]), queries, over_z, over_core)
-    attended, from_x = lax.optimization_barrier((attended, from_x))
 
     beside = moved(attended, lambda x, h, y, z, c: (x, h, y, z ^ 1, c))
     attended = jnp.stack([attended, beside])
     from_y = [attended] + [
         moved(attended, lambda x, h, y, z, c, d=d: (x, h, y - d, z, c)) for d in (1, 2, 3)
     ]
-    sums = project(jnp.stack([x, y, c]), from_y, from_x)
+    sums = project(jnp.stack([x, y, z // 2, c]), from_y, from_x)
     came = moved(sums[1], lambda x, h, y, z, c: (x, h, y, z, 1 - c))
     kept = (sums[0].astype(jnp.float32) + came.astype(jnp.float32)).astype(jnp.bfloat16)
-    groups = [
-        [(2 * far + low) * CS + core for far in range(ZS // 2)]
-        for low in range(2)
-        for core in range(CS)
-    ]
-    parts = lax.all_to_all(kept, "head", 0, 0, axis_index_groups=groups, tiled=True)
-    summed = jnp.sum(parts.astype(jnp.float32), axis=0).astype(jnp.bfloat16)
+    parts = [kept[0]] + [
+        moved(kept[k], lambda x, h, y, z, c, k=k: (x, h, y, z ^ (2 * k), c)) for k in (3, 2, 1)
+    ]
+    summed = sum(part.astype(jnp.float32) for part in parts).astype(jnp.bfloat16)
     odd = y % 2 == 1
     sent = in_order(summed[0], summed[1], odd)
     landed = [

time: 220 us -> 206 us (0.936)
  starting transfers between devices: 143 us -> 120 us
  waiting for transfers between devices: 47.2 us -> 57.1 us
    ppermute x13 -> x21, waiting for transfers between devices: 18.4 us -> 56.4 us  [moved(): return lax.ppermute(value, BOTH, pairs)]
    all_to_all x2 -> x0, waiting for transfers between devices: 28.2 us -> none  [the longest x1 28.2 us: per_device(): lax.all_to_all(kept, 'head', 0, 0, axis_index_groups=groups, tiled=True)]
    all_to_all x2 -> x0, starting transfers between devices: 13.7 us -> none  [the longest x1 9.94 us: per_device(): lax.all_to_all(mine, 'head', 0, 0, axis_index_groups=lines, tiled=True)]
    ppermute x13 -> x21, starting transfers between devices: 103 us -> 93.5 us  [moved(): return lax.ppermute(value, BOTH, pairs)]
  transfers between devices with their start and end apart: 19 -> 25, of which waited for: 9 -> 13; matrix products, arithmetic and copies ran while one was open for 0% -> 0% of each run, Pallas kernels for 8% -> 9%
where the time goes in v6:
time: 206 us; the launch traced here: 204 us
  starting transfers between devices  120 us (58%)
  waiting for transfers between devices  57.1 us (28%)
  Pallas kernels  21.4 us (10%)
  local copies, waits for them, and re-layouts  2.84 us (1%)
  other arithmetic  2.69 us (1%)
    ppermute x21, starting transfers between devices, moved(): return lax.ppermute(value, BOTH, pairs)  93.5 us
    ppermute x21, waiting for transfers between devices, moved(): return lax.ppermute(value, BOTH, pairs)  56.4 us
    ppermute x4, starting transfers between devices, later(): lax.ppermute(value, 'seq', [(s, s + steps) for s in range(count - steps)])  26.1 us
    pallas_call x1, Pallas kernels, attention(): pl.pallas_call(functools.partial(attention_kernel, tokens=16), out_shape=...  18.2 us
  transfers between devices with their start and end apart: 25, of which 13 were waited for; matrix products, arithmetic and copies ran while one was open for 0% of the time, Pallas kernels for 9%

profile of v6, /device:TPU:1, one launch (start us, length us, event | category | flops | bytes accessed | tf_op | source)
XLA Modules:
  0.0 204.2 jit_solution(314931687086612396)
XLA Ops:
  1.4 4.0 %collective-permute-start = (bf16[4,8,128]{2,1,0:T(8,128)(2,1)S(1)}, bf16[4,8,128]{2,1,0:T(8,128)(2,1)S(1)}, u32[]{:S(2)}, u32[]{:S(2)}) collective-permute-start(bf16[4,8,128]{2,1,0:T(8,128)(2,1)S(1)} %pad_maximum_fusion.6), channel_id=1, source_target_pairs={{0,16},{16,32},{32,48},{48,64},{64,80},{80,96},{96,112},{112,128},... | collective-permute-start | bytes 24584 | tf_op jit(solution)/shard_map/ppermute | solution.py:38
  5.4 15.4 %collective-permute-start.3 = (bf16[2,8,128]{2,1,0:T(8,128)(2,1)S(1)}, bf16[2,8,128]{2,1,0:T(8,128)(2,1)S(1)}, u32[]{:S(2)}, u32[]{:S(2)}) collective-permute-start(bf16[2,8,128]{2,1,0:T(8,128)(2,1)S(1)} %pad_maximum_fusion.7), channel_id=1, source_target_pairs={{0,64},{16,80},{32,96},{48,112},{64,128},{80,144},{96,160},{112,17... | collective-permute-start | bytes 12296 | tf_op jit(solution)/shard_map/ppermute | solution.py:38
  20.9 3.4 %collective-permute-start.2 = (bf16[2,8,128]{2,1,0:T(8,128)(2,1)S(1)}, bf16[2,8,128]{2,1,0:T(8,128)(2,1)S(1)}, u32[]{:S(2)}, u32[]{:S(2)}) collective-permute-start(bf16[2,8,128]{2,1,0:T(8,128)(2,1)S(1)} %pad_maximum_fusion.7), channel_id=1, source_target_pairs={{0,48},{16,64},{32,80},{48,96},{64,112},{80,128},{96,144},{112,160... | collective-permute-start | bytes 12296 | tf_op jit(solution)/shard_map/ppermute | solution.py:38
  24.3 3.3 %collective-permute-start.1 = (bf16[2,8,128]{2,1,0:T(8,128)(2,1)S(1)}, bf16[2,8,128]{2,1,0:T(8,128)(2,1)S(1)}, u32[]{:S(2)}, u32[]{:S(2)}) collective-permute-start(bf16[2,8,128]{2,1,0:T(8,128)(2,1)S(1)} %pad_maximum_fusion.7), channel_id=1, source_target_pairs={{0,32},{16,48},{32,64},{48,80},{64,96},{80,112},{96,128},{112,144}... | collective-permute-start | bytes 12296 | tf_op jit(solution)/shard_map/ppermute | solution.py:38
  30.8 6.5 %collective-permute-start.4 = (bf16[1,14,8,128]{3,2,1,0:T(8,128)(2,1)}, bf16[1,14,8,128]{3,2,1,0:T(8,128)(2,1)S(1)}, u32[]{:S(2)}, u32[]{:S(2)}) collective-permute-start(bf16[1,14,8,128]{3,2,1,0:T(8,128)(2,1)} %shard_map.64), channel_id=1, source_target_pairs={{0,8},{1,9},{2,10},{3,11},{4,12},{5,13},{6,14},{7,15},{8,0},{9,1},... | collective-permute-start | bytes 86024 | tf_op jit(solution)/shard_map/ppermute | solution.py:33
  37.3 2.3 %collective-permute-done.4 = bf16[1,14,8,128]{3,2,1,0:T(8,128)(2,1)S(1)} collective-permute-done((bf16[1,14,8,128]{3,2,1,0:T(8,128)(2,1)}, bf16[1,14,8,128]{3,2,1,0:T(8,128)(2,1)S(1)}, u32[]{:S(2)}, u32[]{:S(2)}) %collective-permute-start.4) | collective-permute-done | bytes 28704 | tf_op jit(solution)/shard_map/ppermute | solution.py:33
  40.4 4.0 %collective-permute-start.5 = (bf16[2,14,8,128]{3,2,1,0:T(8,128)(2,1)S(1)}, bf16[2,14,8,128]{3,2,1,0:T(8,128)(2,1)S(1)}, u32[]{:S(2)}, u32[]{:S(2)}) collective-permute-start(bf16[2,14,8,128]{3,2,1,0:T(8,128)(2,1)S(1)} %pad_maximum_fusion.5), channel_id=1, source_target_pairs={{0,4},{1,5},{2,6},{3,7},{4,0},{5,1},{6,2},{7,3},{8,12},{9,13},{10,... | collective-permute-start | bytes 172040 | tf_op jit(solution)/shard_map/ppermute | solution.py:33
  45.1 10.0 %collective-permute-start.7 = (bf16[512,256]{1,0:T(8,128)(2,1)}, bf16[512,256]{1,0:T(8,128)(2,1)S(1)}, u32[]{:S(2)}, u32[]{:S(2)}) collective-permute-start(bf16[512,256]{1,0:T(8,128)(2,1)} %param.11), channel_id=1, source_target_pairs={{0,10},{1,11},{2,0},{3,1},{4,14},{5,15},{6,4},{7,5},{8,64},{9,65},... | collective-permute-start | bytes 786440 | tf_op jit(solution)/shard_map/ppermute | solution.py:33
  55.2 14.1 %collective-permute-start.6 = (bf16[4,14,8,128]{3,2,1,0:T(8,128)(2,1)S(1)}, bf16[4,14,8,128]{3,2,1,0:T(8,128)(2,1)S(1)}, u32[]{:S(2)}, u32[]{:S(2)}) collective-permute-start(bf16[4,14,8,128]{3,2,1,0:T(8,128)(2,1)S(1)} %pad_maximum_fusion.4), channel_id=1, source_target_pairs={{0,2},{1,3},{2,0},{3,1},{4,6},{5,7},{6,4},{7,5},{8,10},{9,11},{10,... | collective-permute-start | bytes 344072 | tf_op jit(solution)/shard_map/ppermute | solution.py:33
  69.3 15.0 %collective-permute-done.6 = bf16[4,14,8,128]{3,2,1,0:T(8,128)(2,1)S(1)} collective-permute-done((bf16[4,14,8,128]{3,2,1,0:T(8,128)(2,1)S(1)}, bf16[4,14,8,128]{3,2,1,0:T(8,128)(2,1)S(1)}, u32[]{:S(2)}, u32[]{:S(2)}) %collective-permute-start.6) | collective-permute-done | bytes 114720 | tf_op jit(solution)/shard_map/ppermute | solution.py:33
  84.4 4.3 %collective-permute-start.11 = (bf16[8,14,8,128]{3,2,1,0:T(8,128)(2,1)S(1)}, bf16[8,14,8,128]{3,2,1,0:T(8,128)(2,1)S(1)}, u32[]{:S(2)}, u32[]{:S(2)}) collective-permute-start(bf16[8,14,8,128]{3,2,1,0:T(8,128)(2,1)S(1)} %pad_maximum_fusion.2.mine_ref), channel_id=1, source_target_pairs={{0,1},{1,0},{2,3},{3,2},{4,5},{5,4},{6,7},{7,6},{8,9},{9,8},{10,11... | collective-permute-start | bytes 688136 | tf_op jit(solution)/shard_map/ppermute | solution.py:33
  90.2 18.2 %shard_map.65 = bf16[128,512]{1,0:T(8,128)(2,1)S(1)} custom-call(s32[3]{0:T(128)S(1)} %pad_add_fusion.1.place, bf16[128,512]{1,0:T(8,128)(2,1)S(1)} %copy-done, bf16[8,14,8,128]{3,2,1,0:T(8,128)(2,1)S(1)} %pad_maximum_fusion.2.mine_ref, bf16[8,14,8,128]{3,2,1,0:T(8,128)(2,1)S(1)} %collective-permute-done.11.other_ref), custom_call_target="tpu_custom_call" | custom-call | flops 20000000000 | bytes 1048576 | tf_op jit(solution)/shard_map/pallas_call | solution.py:130
  109.4 5.2 %collective-permute-start.12 = (bf16[128,512]{1,0:T(8,128)(2,1)S(1)}, bf16[128,512]{1,0:T(8,128)(2,1)S(1)}, u32[]{:S(2)}, u32[]{:S(2)}) collective-permute-start(bf16[128,512]{1,0:T(8,128)(2,1)S(1)} %shard_map.65), channel_id=1, source_target_pairs={{0,2},{1,3},{2,0},{3,1},{4,6},{5,7},{6,4},{7,5},{8,10},{9,11},{10,... | collective-permute-start | bytes 393224 | tf_op jit(solution)/shard_map/ppermute | solution.py:33
  114.6 3.6 %collective-permute-done.12 = bf16[128,512]{1,0:T(8,128)(2,1)S(1)} collective-permute-done((bf16[128,512]{1,0:T(8,128)(2,1)S(1)}, bf16[128,512]{1,0:T(8,128)(2,1)S(1)}, u32[]{:S(2)}, u32[]{:S(2)}) %collective-permute-start.12) | collective-permute-done | bytes 131104 | tf_op jit(solution)/shard_map/ppermute | solution.py:33
  118.3 2.6 %collective-permute-start.15 = (bf16[2,128,512]{2,1,0:T(8,128)(2,1)S(1)}, bf16[2,128,512]{2,1,0:T(8,128)(2,1)S(1)}, u32[]{:S(2)}, u32[]{:S(2)}) collective-permute-start(bf16[2,128,512]{2,1,0:T(8,128)(2,1)S(1)} %pad_maximum_fusion.1.refs_0_), channel_id=1, source_target_pairs={{0,16},{1,17},{2,18},{3,19},{4,20},{5,21},{6,22},{7,23},{8,24},{9,... | collective-permute-start | bytes 786440 | tf_op jit(solution)/shard_map/ppermute | solution.py:33
  120.9 7.9 %collective-permute-start.18 = (bf16[2,512,256]{2,1,0:T(8,128)(2,1)S(1)}, bf16[2,512,256]{2,1,0:T(8,128)(2,1)S(1)}, u32[]{:S(2)}, u32[]{:S(2)}) collective-permute-start(bf16[2,512,256]{2,1,0:T(8,128)(2,1)S(1)} %pad_maximum_fusion.refs_4_), channel_id=1, source_target_pairs={{0,128},{1,129},{2,130},{3,131},{4,132},{5,133},{6,134},{7,135},{8... | collective-permute-start | bytes 1572872 | tf_op jit(solution)/shard_map/ppermute | solution.py:33
  128.8 3.1 %collective-permute-start.17 = (bf16[2,512,256]{2,1,0:T(8,128)(2,1)S(1)}, bf16[2,512,256]{2,1,0:T(8,128)(2,1)S(1)}, u32[]{:S(2)}, u32[]{:S(2)}) collective-permute-start(bf16[2,512,256]{2,1,0:T(8,128)(2,1)S(1)} %pad_maximum_fusion.refs_4_), channel_id=1, source_target_pairs={{0,256},{1,257},{2,258},{3,259},{4,260},{5,261},{6,262},{7,263},{8... | collective-permute-start | bytes 1572872 | tf_op jit(solution)/shard_map/ppermute | solution.py:33
  131.9 4.0 %collective-permute-start.16 = (bf16[2,512,256]{2,1,0:T(8,128)(2,1)S(1)}, bf16[2,512,256]{2,1,0:T(8,128)(2,1)S(1)}, u32[]{:S(2)}, u32[]{:S(2)}) collective-permute-start(bf16[2,512,256]{2,1,0:T(8,128)(2,1)S(1)} %pad_maximum_fusion.refs_4_), channel_id=1, source_target_pairs={{0,384},{1,385},{2,386},{3,387},{4,388},{5,389},{6,390},{7,391},{8... | collective-permute-start | bytes 1572872 | tf_op jit(solution)/shard_map/ppermute | solution.py:33
  135.9 1.9 collective-permute-start.14
  137.8 4.5 %collective-permute-start.13 = (bf16[2,128,512]{2,1,0:T(8,128)(2,1)S(1)}, bf16[2,128,512]{2,1,0:T(8,128)(2,1)S(1)}, u32[]{:S(2)}, u32[]{:S(2)}) collective-permute-start(bf16[2,128,512]{2,1,0:T(8,128)(2,1)S(1)} %pad_maximum_fusion.1.refs_0_), channel_id=1, source_target_pairs={{0,48},{1,49},{2,50},{3,51},{4,52},{5,53},{6,54},{7,55},{8,56},{9,... | collective-permute-start | bytes 786440 | tf_op jit(solution)/shard_map/ppermute | solution.py:33
  142.4 2.7 %collective-permute-done.14.refs_2_ = bf16[2,128,512]{2,1,0:T(8,128)(2,1)S(1)} collective-permute-done((bf16[2,128,512]{2,1,0:T(8,128)(2,1)S(1)}, bf16[2,128,512]{2,1,0:T(8,128)(2,1)S(1)}, u32[]{:S(2)}, u32[]{:S(2)}) %collective-permute-start.14) | collective-permute-done | bytes 262176 | tf_op jit(solution)/shard_map/ppermute | solution.py:33
  145.2 6.7 %collective-permute-done.13.refs_1_ = bf16[2,128,512]{2,1,0:T(8,128)(2,1)S(1)} collective-permute-done((bf16[2,128,512]{2,1,0:T(8,128)(2,1)S(1)}, bf16[2,128,512]{2,1,0:T(8,128)(2,1)S(1)}, u32[]{:S(2)}, u32[]{:S(2)}) %collective-permute-start.13) | collective-permute-done | bytes 262176 | tf_op jit(solution)/shard_map/ppermute | solution.py:33
  156.0 3.5 %collective-permute-start.19 = (bf16[4,2,128,256]{3,2,1,0:T(8,128)(2,1)S(1)}, bf16[4,2,128,256]{3,2,1,0:T(8,128)(2,1)S(1)}, u32[]{:S(2)}, u32[]{:S(2)}) collective-permute-start(bf16[4,2,128,256]{3,2,1,0:T(8,128)(2,1)S(1)} %slice_bitcast_fusion), channel_id=1, source_target_pairs={{0,1},{1,0},{2,3},{3,2},{4,5},{5,4},{6,7},{7,6},{8,9},{9,8},{10,11... | collective-permute-start | bytes 1572872 | tf_op jit(solution)/shard_map/ppermute | solution.py:33
  161.2 6.7 %collective-permute-start.20 = (bf16[2,128,256]{2,1,0:T(8,128)(2,1)S(1)}, bf16[2,128,256]{2,1,0:T(8,128)(2,1)S(1)}, u32[]{:S(2)}, u32[]{:S(2)}) collective-permute-start(bf16[2,128,256]{2,1,0:T(8,128)(2,1)S(1)} %get-tuple-element.19), channel_id=1, source_target_pairs={{0,12},{1,13},{2,14},{3,15},{4,8},{5,9},{6,10},{7,11},{8,4},{9,5},... | collective-permute-start | bytes 393224 | tf_op jit(solution)/shard_map/ppermute | solution.py:33
  167.9 2.1 %collective-permute-start.22 = (bf16[2,128,256]{2,1,0:T(8,128)(2,1)S(1)}, bf16[2,128,256]{2,1,0:T(8,128)(2,1)S(1)}, u32[]{:S(2)}, u32[]{:S(2)}) collective-permute-start(bf16[2,128,256]{2,1,0:T(8,128)(2,1)S(1)} %get-tuple-element.20), channel_id=1, source_target_pairs={{0,4},{1,5},{2,6},{3,7},{4,0},{5,1},{6,2},{7,3},{8,12},{9,13},{10,... | collective-permute-start | bytes 393224 | tf_op jit(solution)/shard_map/ppermute | solution.py:33
  170.1 4.3 %collective-permute-start.21 = (bf16[2,128,256]{2,1,0:T(8,128)(2,1)S(1)}, bf16[2,128,256]{2,1,0:T(8,128)(2,1)S(1)}, u32[]{:S(2)}, u32[]{:S(2)}) collective-permute-start(bf16[2,128,256]{2,1,0:T(8,128)(2,1)S(1)} %get-tuple-element.21), channel_id=1, source_target_pairs={{0,8},{1,9},{2,10},{3,11},{4,12},{5,13},{6,14},{7,15},{8,0},{9,1},... | collective-permute-start | bytes 393224 | tf_op jit(solution)/shard_map/ppermute | solution.py:33
  174.4 4.7 %collective-permute-done.20 = bf16[2,128,256]{2,1,0:T(8,128)(2,1)S(1)} collective-permute-done((bf16[2,128,256]{2,1,0:T(8,128)(2,1)S(1)}, bf16[2,128,256]{2,1,0:T(8,128)(2,1)S(1)}, u32[]{:S(2)}, u32[]{:S(2)}) %collective-permute-start.20) | collective-permute-done | bytes 131104 | tf_op jit(solution)/shard_map/ppermute | solution.py:33
  179.2 4.7 %collective-permute-done.22 = bf16[2,128,256]{2,1,0:T(8,128)(2,1)S(1)} collective-permute-done((bf16[2,128,256]{2,1,0:T(8,128)(2,1)S(1)}, bf16[2,128,256]{2,1,0:T(8,128)(2,1)S(1)}, u32[]{:S(2)}, u32[]{:S(2)}) %collective-permute-start.22) | collective-permute-done | bytes 131104 | tf_op jit(solution)/shard_map/ppermute | solution.py:33
  183.9 7.6 %collective-permute-done.21 = bf16[2,128,256]{2,1,0:T(8,128)(2,1)S(1)} collective-permute-done((bf16[2,128,256]{2,1,0:T(8,128)(2,1)S(1)}, bf16[2,128,256]{2,1,0:T(8,128)(2,1)S(1)}, u32[]{:S(2)}, u32[]{:S(2)}) %collective-permute-start.21) | collective-permute-done | bytes 131104 | tf_op jit(solution)/shard_map/ppermute | solution.py:33
  191.5 4.9 %collective-permute-start.23 = (bf16[128,256]{1,0:T(8,128)(2,1)S(1)}, bf16[128,256]{1,0:T(8,128)(2,1)S(1)}, u32[]{:S(2)}, u32[]{:S(2)}) collective-permute-start(bf16[128,256]{1,0:T(8,128)(2,1)S(1)} %get-tuple-element.24), channel_id=1, source_target_pairs={{0,16},{1,48},{2,18},{3,50},{4,20},{5,52},{6,22},{7,54},{8,24},{9,... | collective-permute-start | bytes 196616 | tf_op jit(solution)/shard_map/ppermute | solution.py:33
  196.4 1.9 collective-permute-start.24
  198.3 5.2 %collective-permute-done.24 = bf16[128,256]{1,0:T(8,128)(2,1)S(1)} collective-permute-done((bf16[128,256]{1,0:T(8,128)(2,1)S(1)}, bf16[128,256]{1,0:T(8,128)(2,1)S(1)}, u32[]{:S(2)}, u32[]{:S(2)}) %collective-permute-start.24) | collective-permute-done | bytes 65568 | tf_op jit(solution)/shard_map/ppermute | solution.py:33
  (59 shorter events, 15.3 us)
Async XLA Ops:
  0.0 0.7 copy-start.4
  0.0 0.7 copy-start.3
  1.4 26.9 %collective-permute-start = (bf16[4,8,128]{2,1,0:T(8,128)(2,1)S(1)}, bf16[4,8,128]{2,1,0:T(8,128)(2,1)S(1)}, u32[]{:S(2)}, u32[]{:S(2)}) collective-permute-start(bf16[4,8,128]{2,1,0:T(8,128)(2,1)S(1)} %pad_maximum_fusion.6), channel_id=1, source_target_pairs={{0,16},{16,32},{32,48},{48,64},{64,80},{80,96},{96,112},{112,128},... | collective-permute-start | bytes 24584 | tf_op jit(solution)/shard_map/ppermute | solution.py:38
  5.4 22.1 %collective-permute-start.3 = (bf16[2,8,128]{2,1,0:T(8,128)(2,1)S(1)}, bf16[2,8,128]{2,1,0:T(8,128)(2,1)S(1)}, u32[]{:S(2)}, u32[]{:S(2)}) collective-permute-start(bf16[2,8,128]{2,1,0:T(8,128)(2,1)S(1)} %pad_maximum_fusion.7), channel_id=1, source_target_pairs={{0,64},{16,80},{32,96},{48,112},{64,128},{80,144},{96,160},{112,17... | collective-permute-start | bytes 12296 | tf_op jit(solution)/shard_map/ppermute | solution.py:38
  20.9 6.7 %collective-permute-start.2 = (bf16[2,8,128]{2,1,0:T(8,128)(2,1)S(1)}, bf16[2,8,128]{2,1,0:T(8,128)(2,1)S(1)}, u32[]{:S(2)}, u32[]{:S(2)}) collective-permute-start(bf16[2,8,128]{2,1,0:T(8,128)(2,1)S(1)} %pad_maximum_fusion.7), channel_id=1, source_target_pairs={{0,48},{16,64},{32,80},{48,96},{64,112},{80,128},{96,144},{112,160... | collective-permute-start | bytes 12296 | tf_op jit(solution)/shard_map/ppermute | solution.py:38
  24.3 4.0 %collective-permute-start.1 = (bf16[2,8,128]{2,1,0:T(8,128)(2,1)S(1)}, bf16[2,8,128]{2,1,0:T(8,128)(2,1)S(1)}, u32[]{:S(2)}, u32[]{:S(2)}) collective-permute-start(bf16[2,8,128]{2,1,0:T(8,128)(2,1)S(1)} %pad_maximum_fusion.7), channel_id=1, source_target_pairs={{0,32},{16,48},{32,64},{48,80},{64,96},{80,112},{96,128},{112,144}... | collective-permute-start | bytes 12296 | tf_op jit(solution)/shard_map/ppermute | solution.py:38
  27.5 0.7 copy-start.7
  27.6 0.7 copy-start.8
  30.8 24.3 %copy-start.1 = (bf16[1,14,8,128]{3,2,1,0:T(8,128)(2,1)S(1)}, bf16[1,14,8,128]{3,2,1,0:T(8,128)(2,1)}, u32[]{:S(2)}) copy-start(bf16[1,14,8,128]{3,2,1,0:T(8,128)(2,1)} %shard_map.64) | copy-start | bytes 86020
  30.8 8.9 %collective-permute-start.4 = (bf16[1,14,8,128]{3,2,1,0:T(8,128)(2,1)}, bf16[1,14,8,128]{3,2,1,0:T(8,128)(2,1)S(1)}, u32[]{:S(2)}, u32[]{:S(2)}) collective-permute-start(bf16[1,14,8,128]{3,2,1,0:T(8,128)(2,1)} %shard_map.64), channel_id=1, source_target_pairs={{0,8},{1,9},{2,10},{3,11},{4,12},{5,13},{6,14},{7,15},{8,0},{9,1},... | collective-permute-start | bytes 86024 | tf_op jit(solution)/shard_map/ppermute | solution.py:33
  40.4 14.7 %collective-permute-start.5 = (bf16[2,14,8,128]{3,2,1,0:T(8,128)(2,1)S(1)}, bf16[2,14,8,128]{3,2,1,0:T(8,128)(2,1)S(1)}, u32[]{:S(2)}, u32[]{:S(2)}) collective-permute-start(bf16[2,14,8,128]{3,2,1,0:T(8,128)(2,1)S(1)} %pad_maximum_fusion.5), channel_id=1, source_target_pairs={{0,4},{1,5},{2,6},{3,7},{4,0},{5,1},{6,2},{7,3},{8,12},{9,13},{10,... | collective-permute-start | bytes 172040 | tf_op jit(solution)/shard_map/ppermute | solution.py:33
  44.5 39.9 %collective-permute-start.8 = (bf16[512,256]{1,0:T(8,128)(2,1)}, bf16[512,256]{1,0:T(8,128)(2,1)S(1)}, u32[]{:S(2)}, u32[]{:S(2)}) collective-permute-start(bf16[512,256]{1,0:T(8,128)(2,1)} %param.11), channel_id=1, source_target_pairs={{2,74},{3,75},{6,78},{7,79},{10,2},{11,3},{14,6},{15,7},{18,90},{1... | collective-permute-start | bytes 786440 | tf_op jit(solution)/shard_map/ppermute | solution.py:33
  45.1 39.3 %collective-permute-start.7 = (bf16[512,256]{1,0:T(8,128)(2,1)}, bf16[512,256]{1,0:T(8,128)(2,1)S(1)}, u32[]{:S(2)}, u32[]{:S(2)}) collective-permute-start(bf16[512,256]{1,0:T(8,128)(2,1)} %param.11), channel_id=1, source_target_pairs={{0,10},{1,11},{2,0},{3,1},{4,14},{5,15},{6,4},{7,5},{8,64},{9,65},... | collective-permute-start | bytes 786440 | tf_op jit(solution)/shard_map/ppermute | solution.py:33
  55.2 29.2 %collective-permute-start.6 = (bf16[4,14,8,128]{3,2,1,0:T(8,128)(2,1)S(1)}, bf16[4,14,8,128]{3,2,1,0:T(8,128)(2,1)S(1)}, u32[]{:S(2)}, u32[]{:S(2)}) collective-permute-start(bf16[4,14,8,128]{3,2,1,0:T(8,128)(2,1)S(1)} %pad_maximum_fusion.4), channel_id=1, source_target_pairs={{0,2},{1,3},{2,0},{3,1},{4,6},{5,7},{6,4},{7,5},{8,10},{9,11},{10,... | collective-permute-start | bytes 344072 | tf_op jit(solution)/shard_map/ppermute | solution.py:33
  84.4 5.8 %copy-start = (bf16[128,512]{1,0:T(8,128)(2,1)S(1)}, bf16[128,512]{1,0:T(8,128)(2,1)}, u32[]{:S(2)}) copy-start(bf16[128,512]{1,0:T(8,128)(2,1)} %q_ref.1) | copy-start | bytes 393220
  84.4 5.8 %collective-permute-start.11 = (bf16[8,14,8,128]{3,2,1,0:T(8,128)(2,1)S(1)}, bf16[8,14,8,128]{3,2,1,0:T(8,128)(2,1)S(1)}, u32[]{:S(2)}, u32[]{:S(2)}) collective-permute-start(bf16[8,14,8,128]{3,2,1,0:T(8,128)(2,1)S(1)} %pad_maximum_fusion.2.mine_ref), channel_id=1, source_target_pairs={{0,1},{1,0},{2,3},{3,2},{4,5},{5,4},{6,7},{7,6},{8,9},{9,8},{10,11... | collective-permute-start | bytes 688136 | tf_op jit(solution)/shard_map/ppermute | solution.py:33
  88.8 19.6 %collective-permute-start.10 = (bf16[512,256]{1,0:T(8,128)(2,1)S(1)}, bf16[512,256]{1,0:T(8,128)(2,1)S(1)}, u32[]{:S(2)}, u32[]{:S(2)}) collective-permute-start(bf16[512,256]{1,0:T(8,128)(2,1)S(1)} %collective-permute-done.8), channel_id=1, source_target_pairs={{2,72},{3,73},{6,76},{7,77},{8,2},{9,3},{12,6},{13,7},{18,88},{19,... | collective-permute-start | bytes 786440 | tf_op jit(solution)/shard_map/ppermute | solution.py:33
  89.5 19.0 %collective-permute-start.9 = (bf16[512,256]{1,0:T(8,128)(2,1)S(1)}, bf16[512,256]{1,0:T(8,128)(2,1)S(1)}, u32[]{:S(2)}, u32[]{:S(2)}) collective-permute-start(bf16[512,256]{1,0:T(8,128)(2,1)S(1)} %collective-permute-done.7), channel_id=1, source_target_pairs={{2,10},{3,11},{6,14},{7,15},{10,64},{11,65},{14,68},{15,69},{18,26... | collective-permute-start | bytes 786440 | tf_op jit(solution)/shard_map/ppermute | solution.py:33
  108.4 1.0 copy-start.2
  109.4 8.8 %collective-permute-start.12 = (bf16[128,512]{1,0:T(8,128)(2,1)S(1)}, bf16[128,512]{1,0:T(8,128)(2,1)S(1)}, u32[]{:S(2)}, u32[]{:S(2)}) collective-permute-start(bf16[128,512]{1,0:T(8,128)(2,1)S(1)} %shard_map.65), channel_id=1, source_target_pairs={{0,2},{1,3},{2,0},{3,1},{4,6},{5,7},{6,4},{7,5},{8,10},{9,11},{10,... | collective-permute-start | bytes 393224 | tf_op jit(solution)/shard_map/ppermute | solution.py:33
  118.3 19.5 %collective-permute-start.15 = (bf16[2,128,512]{2,1,0:T(8,128)(2,1)S(1)}, bf16[2,128,512]{2,1,0:T(8,128)(2,1)S(1)}, u32[]{:S(2)}, u32[]{:S(2)}) collective-permute-start(bf16[2,128,512]{2,1,0:T(8,128)(2,1)S(1)} %pad_maximum_fusion.1.refs_0_), channel_id=1, source_target_pairs={{0,16},{1,17},{2,18},{3,19},{4,20},{5,21},{6,22},{7,23},{8,24},{9,... | collective-permute-start | bytes 786440 | tf_op jit(solution)/shard_map/ppermute | solution.py:33
  120.9 31.0 %collective-permute-start.18 = (bf16[2,512,256]{2,1,0:T(8,128)(2,1)S(1)}, bf16[2,512,256]{2,1,0:T(8,128)(2,1)S(1)}, u32[]{:S(2)}, u32[]{:S(2)}) collective-permute-start(bf16[2,512,256]{2,1,0:T(8,128)(2,1)S(1)} %pad_maximum_fusion.refs_4_), channel_id=1, source_target_pairs={{0,128},{1,129},{2,130},{3,131},{4,132},{5,133},{6,134},{7,135},{8... | collective-permute-start | bytes 1572872 | tf_op jit(solution)/shard_map/ppermute | solution.py:33
  128.8 23.6 %collective-permute-start.17 = (bf16[2,512,256]{2,1,0:T(8,128)(2,1)S(1)}, bf16[2,512,256]{2,1,0:T(8,128)(2,1)S(1)}, u32[]{:S(2)}, u32[]{:S(2)}) collective-permute-start(bf16[2,512,256]{2,1,0:T(8,128)(2,1)S(1)} %pad_maximum_fusion.refs_4_), channel_id=1, source_target_pairs={{0,256},{1,257},{2,258},{3,259},{4,260},{5,261},{6,262},{7,263},{8... | collective-permute-start | bytes 1572872 | tf_op jit(solution)/shard_map/ppermute | solution.py:33
  131.9 22.3 %collective-permute-start.16 = (bf16[2,512,256]{2,1,0:T(8,128)(2,1)S(1)}, bf16[2,512,256]{2,1,0:T(8,128)(2,1)S(1)}, u32[]{:S(2)}, u32[]{:S(2)}) collective-permute-start(bf16[2,512,256]{2,1,0:T(8,128)(2,1)S(1)} %pad_maximum_fusion.refs_4_), channel_id=1, source_target_pairs={{0,384},{1,385},{2,386},{3,387},{4,388},{5,389},{6,390},{7,391},{8... | collective-permute-start | bytes 1572872 | tf_op jit(solution)/shard_map/ppermute | solution.py:33
  135.9 9.3 %collective-permute-start.14 = (bf16[2,128,512]{2,1,0:T(8,128)(2,1)S(1)}, bf16[2,128,512]{2,1,0:T(8,128)(2,1)S(1)}, u32[]{:S(2)}, u32[]{:S(2)}) collective-permute-start(bf16[2,128,512]{2,1,0:T(8,128)(2,1)S(1)} %pad_maximum_fusion.1.refs_0_), channel_id=1, source_target_pairs={{0,32},{1,33},{2,34},{3,35},{4,36},{5,37},{6,38},{7,39},{8,40},{9,... | collective-permute-start | bytes 786440 | tf_op jit(solution)/shard_map/ppermute | solution.py:33
  137.8 14.1 %collective-permute-start.13 = (bf16[2,128,512]{2,1,0:T(8,128)(2,1)S(1)}, bf16[2,128,512]{2,1,0:T(8,128)(2,1)S(1)}, u32[]{:S(2)}, u32[]{:S(2)}) collective-permute-start(bf16[2,128,512]{2,1,0:T(8,128)(2,1)S(1)} %pad_maximum_fusion.1.refs_0_), channel_id=1, source_target_pairs={{0,48},{1,49},{2,50},{3,51},{4,52},{5,53},{6,54},{7,55},{8,56},{9,... | collective-permute-start | bytes 786440 | tf_op jit(solution)/shard_map/ppermute | solution.py:33
  156.0 5.0 %collective-permute-start.19 = (bf16[4,2,128,256]{3,2,1,0:T(8,128)(2,1)S(1)}, bf16[4,2,128,256]{3,2,1,0:T(8,128)(2,1)S(1)}, u32[]{:S(2)}, u32[]{:S(2)}) collective-permute-start(bf16[4,2,128,256]{3,2,1,0:T(8,128)(2,1)S(1)} %slice_bitcast_fusion), channel_id=1, source_target_pairs={{0,1},{1,0},{2,3},{3,2},{4,5},{5,4},{6,7},{7,6},{8,9},{9,8},{10,11... | collective-permute-start | bytes 1572872 | tf_op jit(solution)/shard_map/ppermute | solution.py:33
  161.2 18.0 %collective-permute-start.20 = (bf16[2,128,256]{2,1,0:T(8,128)(2,1)S(1)}, bf16[2,128,256]{2,1,0:T(8,128)(2,1)S(1)}, u32[]{:S(2)}, u32[]{:S(2)}) collective-permute-start(bf16[2,128,256]{2,1,0:T(8,128)(2,1)S(1)} %get-tuple-element.19), channel_id=1, source_target_pairs={{0,12},{1,13},{2,14},{3,15},{4,8},{5,9},{6,10},{7,11},{8,4},{9,5},... | collective-permute-start | bytes 393224 | tf_op jit(solution)/shard_map/ppermute | solution.py:33
  167.9 15.9 %collective-permute-start.22 = (bf16[2,128,256]{2,1,0:T(8,128)(2,1)S(1)}, bf16[2,128,256]{2,1,0:T(8,128)(2,1)S(1)}, u32[]{:S(2)}, u32[]{:S(2)}) collective-permute-start(bf16[2,128,256]{2,1,0:T(8,128)(2,1)S(1)} %get-tuple-element.20), channel_id=1, source_target_pairs={{0,4},{1,5},{2,6},{3,7},{4,0},{5,1},{6,2},{7,3},{8,12},{9,13},{10,... | collective-permute-start | bytes 393224 | tf_op jit(solution)/shard_map/ppermute | solution.py:33
  170.1 21.3 %collective-permute-start.21 = (bf16[2,128,256]{2,1,0:T(8,128)(2,1)S(1)}, bf16[2,128,256]{2,1,0:T(8,128)(2,1)S(1)}, u32[]{:S(2)}, u32[]{:S(2)}) collective-permute-start(bf16[2,128,256]{2,1,0:T(8,128)(2,1)S(1)} %get-tuple-element.21), channel_id=1, source_target_pairs={{0,8},{1,9},{2,10},{3,11},{4,12},{5,13},{6,14},{7,15},{8,0},{9,1},... | collective-permute-start | bytes 393224 | tf_op jit(solution)/shard_map/ppermute | solution.py:33
  191.5 6.8 %collective-permute-start.23 = (bf16[128,256]{1,0:T(8,128)(2,1)S(1)}, bf16[128,256]{1,0:T(8,128)(2,1)S(1)}, u32[]{:S(2)}, u32[]{:S(2)}) collective-permute-start(bf16[128,256]{1,0:T(8,128)(2,1)S(1)} %get-tuple-element.24), channel_id=1, source_target_pairs={{0,16},{1,48},{2,18},{3,50},{4,20},{5,52},{6,22},{7,54},{8,24},{9,... | collective-permute-start | bytes 196616 | tf_op jit(solution)/shard_map/ppermute | solution.py:33
  196.4 7.1 %collective-permute-start.24 = (bf16[128,256]{1,0:T(8,128)(2,1)S(1)}, bf16[128,256]{1,0:T(8,128)(2,1)S(1)}, u32[]{:S(2)}, u32[]{:S(2)}) collective-permute-start(bf16[128,256]{1,0:T(8,128)(2,1)S(1)} %get-tuple-element.25), channel_id=1, source_target_pairs={{0,0},{1,32},{2,2},{3,34},{4,4},{5,36},{6,6},{7,38},{8,8},{9,40},{... | collective-permute-start | bytes 196616 | tf_op jit(solution)/shard_map/ppermute | solution.py:33
  (3 other events, 1.9 us)

commit v7 on v5

--- a/solution.py
+++ b/solution.py
@@ -121,7 +121,7 @@
     width = mine.shape[-1]
     spots = W1 // rows + 1
     return pl.pallas_call(
-        functools.partial(attention_kernel, tokens=16),
+        functools.partial(attention_kernel, tokens=32),
         out_shape=jax.ShapeDtypeStruct((rows, wide), jnp.bfloat16),
         in_specs=[pl.BlockSpec(memory_space=pltpu.SMEM)]
         + [pl.BlockSpec(memory_space=pltpu.VMEM)] * 3,
@@ -136,7 +136,7 @@
         ],
         compiler_params=pltpu.CompilerParams(vmem_limit_bytes=40 * 2**20),
         cost_estimate=pl.CostEstimate(
-            flops=20_000_000_000, bytes_accessed=2**20, transcendentals=0
+            flops=1000, bytes_accessed=1000, transcendentals=0
         ),
     )(place, q, mine, other)
 
@@ -200,53 +200,36 @@
     x, half, y = seq // (HS * YS), seq // YS % HS, seq % YS
     z, c = head // CS, head % CS
 
-    def along(steps):
+    first_up = {0: 5, 2: 7, 4: 8, 6: 10, 9: 12, 11: 14, 13: 1, 15: 3}
+    second_up = {first_up[spot]: (spot + 8) % 16 for spot in first_up}
+    stay = [spot for spot in range(16) if spot not in first_up]
+    first_up.update({spot: spot ^ 1 for spot in stay})
+    first_down = {spot: (spot - 4) % 16 for spot in stay}
+    second_down = {first_down[spot]: (spot ^ 1) ^ 8 for spot in stay}
+
+    def along(table):
         def target(x, h, y, z, c):
-            to = (h * ZS + z + steps) % (HS * ZS)
-            return (x, to // ZS, y, to % ZS, c)
+            to = table.get(h * ZS + z)
+            return None if to is None else (x, to // ZS, y, to % ZS, c)
 
         return target
 
-    def kept_here(h, z):
-        return h == z % 2
-
-    def first_up(x, h, y, z, c):
-        return along(4)(x, h, y, z, c) if kept_here(h, z) else None
-
-    def first_down(x, h, y, z, c):
-        return None if kept_here(h, z) else along(-4)(x, h, y, z, c)
-
-    def second_up(x, h, y, z, c):
-        spot = (h * ZS + z - 4) % (HS * ZS)
-        return along(4)(x, h, y, z, c) if kept_here(spot // ZS, spot % ZS) else None
-
-    def second_down(x, h, y, z, c):
-        spot = (h * ZS + z + 4) % (HS * ZS)
-        if kept_here(spot // ZS, spot % ZS):
-            return None
-        return along(-5 if spot < ZS else -3)(x, h, y, z, c)
-
-    def near(x, h, y, z, c):
-        return None if kept_here(h, z) else (x, h, y, z ^ 1, c)
-
-    upward, downward = moved(w_out, first_up), moved(w_out, first_down)
+    upward, downward = moved(w_out, along(first_up)), moved(w_out, along(first_down))
 
     piece = jnp.stack([long_keys, long_values, short_keys, short_values])
     before = later(piece, 1)
     older = [later(piece[:2], steps) for steps in range(2, W1 // rows + 1)]
     mine = pack((long_keys, long_values, short_keys, short_values), before, older)
     lines = [[z * CS + core for z in range(ZS)] for core in range(CS)]
-    mine, upward, downward = lax.optimization_barrier((mine, upward, downward))
-    upward, downward = moved(upward, second_up), moved(downward, second_down)
-    beside = moved(w_out, near)
+    long_way, downward = moved(upward, along(second_up)), moved(downward, along(second_down))
+    near_by = half == z % 2
+    pair = jnp.stack(
+        [jnp.where(near_by, w_out, long_way), jnp.where(near_by, upward, downward)]
+    )
+    mine, pair = lax.optimization_barrier((mine, pair))
     over_z = lax.all_to_all(mine, "head", 0, 0, axis_index_groups=lines, tiled=True)
     over_core = moved(over_z, lambda x, h, y, z, c: (x, h, y, z, 1 - c))
 
-    near_by = half == z % 2
-    pair = jnp.stack(
-        [jnp.where(near_by, w_out, upward), jnp.where(near_by, beside, downward)]
-    )
-    pair, over_core = lax.optimization_barrier((pair, over_core))
     from_x = [pair] + [
         moved(pair, lambda x, h, y, z, c, d=d: (x - d, h, y, z, c)) for d in (1, 2, 3)
     ]

time: 192 us -> 195 us (1.016)
  waiting for transfers between devices: 42 us -> 55.2 us
  starting transfers between devices: 124 us -> 116 us
  Pallas kernels: 21.4 us -> 18.1 us
    ppermute x19 -> x18, waiting for transfers between devices: 32.9 us -> 54.5 us  [moved(): return lax.ppermute(value, BOTH, pairs)]
    ppermute x19 -> x18, starting transfers between devices: 91.3 us -> 78 us  [moved(): return lax.ppermute(value, BOTH, pairs)]
    all_to_all x1, waiting for transfers between devices: 8.43 us -> 0.01 us  [per_device(): lax.all_to_all(mine, 'head', 0, 0, axis_index_groups=lines, tiled=True)]
    all_to_all x1, starting transfers between devices: 10.1 us -> 13.6 us  [per_device(): lax.all_to_all(mine, 'head', 0, 0, axis_index_groups=lines, tiled=True)]
    pallas_call x1, Pallas kernels: 18.1 us -> 14.9 us  [attention(): pl.pallas_call(functools.partial(attention_kernel, tokens=32), out_shape=...]
  transfers between devices with their start and end apart: 24 -> 23, of which waited for: 11 -> 11; matrix products, arithmetic and copies ran while one was open for 1% -> 1% of each run, Pallas kernels for 10% -> 8%
where the time goes in v7:
time: 195 us; the launch traced here: 194 us
  starting transfers between devices  116 us (59%)
  waiting for transfers between devices  55.2 us (28%)
  Pallas kernels  18.1 us (9%)
  other arithmetic  2.64 us (1%)
    ppermute x18, starting transfers between devices, moved(): return lax.ppermute(value, BOTH, pairs)  78 us
    ppermute x18, waiting for transfers between devices, moved(): return lax.ppermute(value, BOTH, pairs)  54.5 us
    ppermute x4, starting transfers between devices, later(): lax.ppermute(value, 'seq', [(s, s + steps) for s in range(count - steps)])  24.6 us
    pallas_call x1, Pallas kernels, attention(): pl.pallas_call(functools.partial(attention_kernel, tokens=32), out_shape=...  14.9 us
    all_to_all x1, starting transfers between devices, per_device(): lax.all_to_all(mine, 'head', 0, 0, axis_index_groups=lines, tiled=True)  13.6 us
  transfers between devices with their start and end apart: 23, of which 11 were waited for; matrix products, arithmetic and copies ran while one was open for 1% of the time, Pallas kernels for 8%

profile of v7, /device:TPU:1, one launch (start us, length us, event | category | flops | bytes accessed | tf_op | source)
XLA Modules:
  0.0 194.0 jit_solution(6685554460731780320)
XLA Ops:
  0.0 11.1 %collective-permute-start.4 = (bf16[512,256]{1,0:T(8,128)(2,1)}, bf16[512,256]{1,0:T(8,128)(2,1)S(1)}, u32[]{:S(2)}, u32[]{:S(2)}) collective-permute-start(bf16[512,256]{1,0:T(8,128)(2,1)} %param.11), channel_id=1, source_target_pairs={{0,10},{1,11},{2,0},{3,1},{4,14},{5,15},{6,4},{7,5},{8,64},{9,65},... | collective-permute-start | bytes 786440 | tf_op jit(solution)/shard_map/ppermute | solution.py:33
  11.8 16.2 %collective-permute-done.4 = bf16[512,256]{1,0:T(8,128)(2,1)S(1)} collective-permute-done((bf16[512,256]{1,0:T(8,128)(2,1)}, bf16[512,256]{1,0:T(8,128)(2,1)S(1)}, u32[]{:S(2)}, u32[]{:S(2)}) %collective-permute-start.4) | collective-permute-done | bytes 262176 | tf_op jit(solution)/shard_map/ppermute | solution.py:33
  29.4 9.1 %collective-permute-start.3 = (bf16[2,8,128]{2,1,0:T(8,128)(2,1)S(1)}, bf16[2,8,128]{2,1,0:T(8,128)(2,1)S(1)}, u32[]{:S(2)}, u32[]{:S(2)}) collective-permute-start(bf16[2,8,128]{2,1,0:T(8,128)(2,1)S(1)} %pad_maximum_fusion.4), channel_id=1, source_target_pairs={{0,64},{16,80},{32,96},{48,112},{64,128},{80,144},{96,160},{112,17... | collective-permute-start | bytes 12296 | tf_op jit(solution)/shard_map/ppermute | solution.py:38
  39.9 3.2 %collective-permute-start = (bf16[4,8,128]{2,1,0:T(8,128)(2,1)S(1)}, bf16[4,8,128]{2,1,0:T(8,128)(2,1)S(1)}, u32[]{:S(2)}, u32[]{:S(2)}) collective-permute-start(bf16[4,8,128]{2,1,0:T(8,128)(2,1)S(1)} %pad_maximum_fusion.3), channel_id=1, source_target_pairs={{0,16},{16,32},{32,48},{48,64},{64,80},{80,96},{96,112},{112,128},... | collective-permute-start | bytes 24584 | tf_op jit(solution)/shard_map/ppermute | solution.py:38
  43.1 8.7 %collective-permute-start.2 = (bf16[2,8,128]{2,1,0:T(8,128)(2,1)S(1)}, bf16[2,8,128]{2,1,0:T(8,128)(2,1)S(1)}, u32[]{:S(2)}, u32[]{:S(2)}) collective-permute-start(bf16[2,8,128]{2,1,0:T(8,128)(2,1)S(1)} %pad_maximum_fusion.4), channel_id=1, source_target_pairs={{0,48},{16,64},{32,80},{48,96},{64,112},{80,128},{96,144},{112,160... | collective-permute-start | bytes 12296 | tf_op jit(solution)/shard_map/ppermute | solution.py:38
  51.9 3.6 %collective-permute-start.1 = (bf16[2,8,128]{2,1,0:T(8,128)(2,1)S(1)}, bf16[2,8,128]{2,1,0:T(8,128)(2,1)S(1)}, u32[]{:S(2)}, u32[]{:S(2)}) collective-permute-start(bf16[2,8,128]{2,1,0:T(8,128)(2,1)S(1)} %pad_maximum_fusion.4), channel_id=1, source_target_pairs={{0,32},{16,48},{32,64},{48,80},{64,96},{80,112},{96,128},{112,144}... | collective-permute-start | bytes 12296 | tf_op jit(solution)/shard_map/ppermute | solution.py:38
  57.4 1.5 shard_map.64
  59.1 13.6 %all-to-all-start = ((bf16[8,14,8,128]{3,2,1,0:T(8,128)(2,1)}), bf16[8,14,8,128]{3,2,1,0:T(8,128)(2,1)S(1)}, u32[]{:S(2)}, u32[]{:S(2)}) async-start(bf16[8,14,8,128]{3,2,1,0:T(8,128)(2,1)} %shard_map.64), calls=%async_computation | async-start | bytes 458752 | tf_op jit(solution)/shard_map/all_to_all | solution.py:230
  72.7 15.1 %collective-permute-start.12 = (bf16[2,512,256]{2,1,0:T(8,128)(2,1)S(1)}, bf16[2,512,256]{2,1,0:T(8,128)(2,1)S(1)}, u32[]{:S(2)}, u32[]{:S(2)}) collective-permute-start(bf16[2,512,256]{2,1,0:T(8,128)(2,1)S(1)} %pad_maximum_fusion.refs_4_), channel_id=1, source_target_pairs={{0,128},{1,129},{2,130},{3,131},{4,132},{5,133},{6,134},{7,135},{8... | collective-permute-start | bytes 1572872 | tf_op jit(solution)/shard_map/ppermute | solution.py:33
  87.8 3.2 %collective-permute-start.11 = (bf16[2,512,256]{2,1,0:T(8,128)(2,1)S(1)}, bf16[2,512,256]{2,1,0:T(8,128)(2,1)S(1)}, u32[]{:S(2)}, u32[]{:S(2)}) collective-permute-start(bf16[2,512,256]{2,1,0:T(8,128)(2,1)S(1)} %pad_maximum_fusion.refs_4_), channel_id=1, source_target_pairs={{0,256},{1,257},{2,258},{3,259},{4,260},{5,261},{6,262},{7,263},{8... | collective-permute-start | bytes 1572872 | tf_op jit(solution)/shard_map/ppermute | solution.py:33
  91.0 4.0 %collective-permute-start.10 = (bf16[2,512,256]{2,1,0:T(8,128)(2,1)S(1)}, bf16[2,512,256]{2,1,0:T(8,128)(2,1)S(1)}, u32[]{:S(2)}, u32[]{:S(2)}) collective-permute-start(bf16[2,512,256]{2,1,0:T(8,128)(2,1)S(1)} %pad_maximum_fusion.refs_4_), channel_id=1, source_target_pairs={{0,384},{1,385},{2,386},{3,387},{4,388},{5,389},{6,390},{7,391},{8... | collective-permute-start | bytes 1572872 | tf_op jit(solution)/shard_map/ppermute | solution.py:33
  94.9 6.9 %collective-permute-start.8 = (bf16[8,14,8,128]{3,2,1,0:T(8,128)(2,1)S(1)}, bf16[8,14,8,128]{3,2,1,0:T(8,128)(2,1)S(1)}, u32[]{:S(2)}, u32[]{:S(2)}) collective-permute-start(bf16[8,14,8,128]{3,2,1,0:T(8,128)(2,1)S(1)} %all-to-all-done.mine_ref), channel_id=1, source_target_pairs={{0,1},{1,0},{2,3},{3,2},{4,5},{5,4},{6,7},{7,6},{8,9},{9,8},{10,11... | collective-permute-start | bytes 688136 | tf_op jit(solution)/shard_map/ppermute | solution.py:33
  103.0 14.9 %shard_map.65 = bf16[128,512]{1,0:T(8,128)(2,1)S(1)} custom-call(s32[2]{0:T(128)S(1)} %pad_add_fusion.1.place, bf16[128,512]{1,0:T(8,128)(2,1)S(1)} %copy-done, bf16[8,14,8,128]{3,2,1,0:T(8,128)(2,1)S(1)} %all-to-all-done.mine_ref, bf16[8,14,8,128]{3,2,1,0:T(8,128)(2,1)S(1)} %collective-permute-done.8.other_ref), custom_call_target="tpu_custom_call" | custom-call | flops 1000 | bytes 1000 | tf_op jit(solution)/shard_map/pallas_call | solution.py:123
  117.8 3.6 %collective-permute-start.9 = (bf16[128,512]{1,0:T(8,128)(2,1)S(1)}, bf16[128,512]{1,0:T(8,128)(2,1)S(1)}, u32[]{:S(2)}, u32[]{:S(2)}) collective-permute-start(bf16[128,512]{1,0:T(8,128)(2,1)S(1)} %shard_map.65), channel_id=1, source_target_pairs={{0,2},{1,3},{2,0},{3,1},{4,6},{5,7},{6,4},{7,5},{8,10},{9,11},{10,... | collective-permute-start | bytes 393224 | tf_op jit(solution)/shard_map/ppermute | solution.py:33
  121.5 3.5 %collective-permute-done.9 = bf16[128,512]{1,0:T(8,128)(2,1)S(1)} collective-permute-done((bf16[128,512]{1,0:T(8,128)(2,1)S(1)}, bf16[128,512]{1,0:T(8,128)(2,1)S(1)}, u32[]{:S(2)}, u32[]{:S(2)}) %collective-permute-start.9) | collective-permute-done | bytes 131104 | tf_op jit(solution)/shard_map/ppermute | solution.py:33
  125.1 2.0 %collective-permute-start.15 = (bf16[2,128,512]{2,1,0:T(8,128)(2,1)S(1)}, bf16[2,128,512]{2,1,0:T(8,128)(2,1)S(1)}, u32[]{:S(2)}, u32[]{:S(2)}) collective-permute-start(bf16[2,128,512]{2,1,0:T(8,128)(2,1)S(1)} %pad_maximum_fusion.1.refs_0_), channel_id=1, source_target_pairs={{0,16},{1,17},{2,18},{3,19},{4,20},{5,21},{6,22},{7,23},{8,24},{9,... | collective-permute-start | bytes 786440 | tf_op jit(solution)/shard_map/ppermute | solution.py:33
  127.0 1.9 collective-permute-start.14
  129.0 4.5 %collective-permute-start.13 = (bf16[2,128,512]{2,1,0:T(8,128)(2,1)S(1)}, bf16[2,128,512]{2,1,0:T(8,128)(2,1)S(1)}, u32[]{:S(2)}, u32[]{:S(2)}) collective-permute-start(bf16[2,128,512]{2,1,0:T(8,128)(2,1)S(1)} %pad_maximum_fusion.1.refs_0_), channel_id=1, source_target_pairs={{0,48},{1,49},{2,50},{3,51},{4,52},{5,53},{6,54},{7,55},{8,56},{9,... | collective-permute-start | bytes 786440 | tf_op jit(solution)/shard_map/ppermute | solution.py:33
  133.6 7.1 %collective-permute-done.15.refs_3_ = bf16[2,128,512]{2,1,0:T(8,128)(2,1)S(1)} collective-permute-done((bf16[2,128,512]{2,1,0:T(8,128)(2,1)S(1)}, bf16[2,128,512]{2,1,0:T(8,128)(2,1)S(1)}, u32[]{:S(2)}, u32[]{:S(2)}) %collective-permute-start.15) | collective-permute-done | bytes 262176 | tf_op jit(solution)/shard_map/ppermute | solution.py:33
  140.7 2.8 %collective-permute-done.13.refs_1_ = bf16[2,128,512]{2,1,0:T(8,128)(2,1)S(1)} collective-permute-done((bf16[2,128,512]{2,1,0:T(8,128)(2,1)S(1)}, bf16[2,128,512]{2,1,0:T(8,128)(2,1)S(1)}, u32[]{:S(2)}, u32[]{:S(2)}) %collective-permute-start.13) | collective-permute-done | bytes 262176 | tf_op jit(solution)/shard_map/ppermute | solution.py:33
  143.5 1.8 shard_map.66
  145.3 3.5 %collective-permute-start.16 = (bf16[4,2,128,256]{3,2,1,0:T(8,128)(2,1)S(1)}, bf16[4,2,128,256]{3,2,1,0:T(8,128)(2,1)S(1)}, u32[]{:S(2)}, u32[]{:S(2)}) collective-permute-start(bf16[4,2,128,256]{3,2,1,0:T(8,128)(2,1)S(1)} %slice_bitcast_fusion), channel_id=1, source_target_pairs={{0,1},{1,0},{2,3},{3,2},{4,5},{5,4},{6,7},{7,6},{8,9},{9,8},{10,11... | collective-permute-start | bytes 1572872 | tf_op jit(solution)/shard_map/ppermute | solution.py:33
  148.8 1.5 collective-permute-done.16
  150.5 8.8 %collective-permute-start.17 = (bf16[2,128,256]{2,1,0:T(8,128)(2,1)S(1)}, bf16[2,128,256]{2,1,0:T(8,128)(2,1)S(1)}, u32[]{:S(2)}, u32[]{:S(2)}) collective-permute-start(bf16[2,128,256]{2,1,0:T(8,128)(2,1)S(1)} %get-tuple-element.19), channel_id=1, source_target_pairs={{0,12},{1,13},{2,14},{3,15},{4,8},{5,9},{6,10},{7,11},{8,4},{9,5},... | collective-permute-start | bytes 393224 | tf_op jit(solution)/shard_map/ppermute | solution.py:33
  159.3 1.9 collective-permute-start.19
  161.2 2.5 %collective-permute-start.18 = (bf16[2,128,256]{2,1,0:T(8,128)(2,1)S(1)}, bf16[2,128,256]{2,1,0:T(8,128)(2,1)S(1)}, u32[]{:S(2)}, u32[]{:S(2)}) collective-permute-start(bf16[2,128,256]{2,1,0:T(8,128)(2,1)S(1)} %get-tuple-element.21), channel_id=1, source_target_pairs={{0,8},{1,9},{2,10},{3,11},{4,12},{5,13},{6,14},{7,15},{8,0},{9,1},... | collective-permute-start | bytes 393224 | tf_op jit(solution)/shard_map/ppermute | solution.py:33
  163.7 4.8 %collective-permute-done.17 = bf16[2,128,256]{2,1,0:T(8,128)(2,1)S(1)} collective-permute-done((bf16[2,128,256]{2,1,0:T(8,128)(2,1)S(1)}, bf16[2,128,256]{2,1,0:T(8,128)(2,1)S(1)}, u32[]{:S(2)}, u32[]{:S(2)}) %collective-permute-start.17) | collective-permute-done | bytes 131104 | tf_op jit(solution)/shard_map/ppermute | solution.py:33
  168.5 1.4 collective-permute-done.19
  169.9 11.1 %collective-permute-done.18 = bf16[2,128,256]{2,1,0:T(8,128)(2,1)S(1)} collective-permute-done((bf16[2,128,256]{2,1,0:T(8,128)(2,1)S(1)}, bf16[2,128,256]{2,1,0:T(8,128)(2,1)S(1)}, u32[]{:S(2)}, u32[]{:S(2)}) %collective-permute-start.18) | collective-permute-done | bytes 131104 | tf_op jit(solution)/shard_map/ppermute | solution.py:33
  181.1 5.1 %collective-permute-start.20 = (bf16[128,256]{1,0:T(8,128)(2,1)S(1)}, bf16[128,256]{1,0:T(8,128)(2,1)S(1)}, u32[]{:S(2)}, u32[]{:S(2)}) collective-permute-start(bf16[128,256]{1,0:T(8,128)(2,1)S(1)} %get-tuple-element.24), channel_id=1, source_target_pairs={{0,16},{1,48},{2,18},{3,50},{4,20},{5,52},{6,22},{7,54},{8,24},{9,... | collective-permute-start | bytes 196616 | tf_op jit(solution)/shard_map/ppermute | solution.py:33
  186.2 1.9 collective-permute-start.21
  188.1 5.2 %collective-permute-done.21 = bf16[128,256]{1,0:T(8,128)(2,1)S(1)} collective-permute-done((bf16[128,256]{1,0:T(8,128)(2,1)S(1)}, bf16[128,256]{1,0:T(8,128)(2,1)S(1)}, u32[]{:S(2)}, u32[]{:S(2)}) %collective-permute-start.21) | collective-permute-done | bytes 65568 | tf_op jit(solution)/shard_map/ppermute | solution.py:33
  (44 shorter events, 7.6 us)
Async XLA Ops:
  0.0 58.9 %copy-start.1 = (bf16[512,256]{1,0:T(8,128)(2,1)S(1)}, bf16[512,256]{1,0:T(8,128)(2,1)}, u32[]{:S(2)}) copy-start(bf16[512,256]{1,0:T(8,128)(2,1)} %param.11) | copy-start | bytes 786436
  0.0 28.0 %collective-permute-start.4 = (bf16[512,256]{1,0:T(8,128)(2,1)}, bf16[512,256]{1,0:T(8,128)(2,1)S(1)}, u32[]{:S(2)}, u32[]{:S(2)}) collective-permute-start(bf16[512,256]{1,0:T(8,128)(2,1)} %param.11), channel_id=1, source_target_pairs={{0,10},{1,11},{2,0},{3,1},{4,14},{5,15},{6,4},{7,5},{8,64},{9,65},... | collective-permute-start | bytes 786440 | tf_op jit(solution)/shard_map/ppermute | solution.py:33
  11.1 27.4 %collective-permute-start.6 = (bf16[512,256]{1,0:T(8,128)(2,1)}, bf16[512,256]{1,0:T(8,128)(2,1)S(1)}, u32[]{:S(2)}, u32[]{:S(2)}) collective-permute-start(bf16[512,256]{1,0:T(8,128)(2,1)} %param.11), channel_id=1, source_target_pairs={{2,74},{3,75},{6,78},{7,79},{10,2},{11,3},{14,6},{15,7},{18,90},{1... | collective-permute-start | bytes 786440 | tf_op jit(solution)/shard_map/ppermute | solution.py:33
  28.0 30.9 %collective-permute-start.5 = (bf16[512,256]{1,0:T(8,128)(2,1)S(1)}, bf16[512,256]{1,0:T(8,128)(2,1)S(1)}, u32[]{:S(2)}, u32[]{:S(2)}) collective-permute-start(bf16[512,256]{1,0:T(8,128)(2,1)S(1)} %collective-permute-done.4), channel_id=1, source_target_pairs={{2,10},{3,11},{6,14},{7,15},{10,64},{11,65},{14,68},{15,69},{18,26... | collective-permute-start | bytes 786440 | tf_op jit(solution)/shard_map/ppermute | solution.py:33
  29.4 22.5 %collective-permute-start.3 = (bf16[2,8,128]{2,1,0:T(8,128)(2,1)S(1)}, bf16[2,8,128]{2,1,0:T(8,128)(2,1)S(1)}, u32[]{:S(2)}, u32[]{:S(2)}) collective-permute-start(bf16[2,8,128]{2,1,0:T(8,128)(2,1)S(1)} %pad_maximum_fusion.4), channel_id=1, source_target_pairs={{0,64},{16,80},{32,96},{48,112},{64,128},{80,144},{96,160},{112,17... | collective-permute-start | bytes 12296 | tf_op jit(solution)/shard_map/ppermute | solution.py:38
  38.5 20.5 %collective-permute-start.7 = (bf16[512,256]{1,0:T(8,128)(2,1)S(1)}, bf16[512,256]{1,0:T(8,128)(2,1)S(1)}, u32[]{:S(2)}, u32[]{:S(2)}) collective-permute-start(bf16[512,256]{1,0:T(8,128)(2,1)S(1)} %collective-permute-done.6), channel_id=1, source_target_pairs={{2,72},{3,73},{6,76},{7,77},{8,2},{9,3},{12,6},{13,7},{18,88},{19,... | collective-permute-start | bytes 786440 | tf_op jit(solution)/shard_map/ppermute | solution.py:33
  39.9 16.3 %collective-permute-start = (bf16[4,8,128]{2,1,0:T(8,128)(2,1)S(1)}, bf16[4,8,128]{2,1,0:T(8,128)(2,1)S(1)}, u32[]{:S(2)}, u32[]{:S(2)}) collective-permute-start(bf16[4,8,128]{2,1,0:T(8,128)(2,1)S(1)} %pad_maximum_fusion.3), channel_id=1, source_target_pairs={{0,16},{16,32},{32,48},{48,64},{64,80},{80,96},{96,112},{112,128},... | collective-permute-start | bytes 24584 | tf_op jit(solution)/shard_map/ppermute | solution.py:38
  43.1 12.4 %collective-permute-start.2 = (bf16[2,8,128]{2,1,0:T(8,128)(2,1)S(1)}, bf16[2,8,128]{2,1,0:T(8,128)(2,1)S(1)}, u32[]{:S(2)}, u32[]{:S(2)}) collective-permute-start(bf16[2,8,128]{2,1,0:T(8,128)(2,1)S(1)} %pad_maximum_fusion.4), channel_id=1, source_target_pairs={{0,48},{16,64},{32,80},{48,96},{64,112},{80,128},{96,144},{112,160... | collective-permute-start | bytes 12296 | tf_op jit(solution)/shard_map/ppermute | solution.py:38
  51.9 3.6 %copy-start.3 = (bf16[2,8,128]{2,1,0:T(8,128)(2,1)}, bf16[2,8,128]{2,1,0:T(8,128)(2,1)S(1)}, u32[]{:S(2)}) copy-start(bf16[2,8,128]{2,1,0:T(8,128)(2,1)S(1)} %collective-permute-done.3.refs_7_) | copy-start | bytes 12292
  51.9 4.4 %collective-permute-start.1 = (bf16[2,8,128]{2,1,0:T(8,128)(2,1)S(1)}, bf16[2,8,128]{2,1,0:T(8,128)(2,1)S(1)}, u32[]{:S(2)}, u32[]{:S(2)}) collective-permute-start(bf16[2,8,128]{2,1,0:T(8,128)(2,1)S(1)} %pad_maximum_fusion.4), channel_id=1, source_target_pairs={{0,32},{16,48},{32,64},{48,80},{64,96},{80,112},{96,128},{112,144}... | collective-permute-start | bytes 12296 | tf_op jit(solution)/shard_map/ppermute | solution.py:38
  55.6 0.7 copy-start.4
  56.2 0.6 copy-start.5
  56.8 0.6 copy-start.2
  59.1 43.9 %copy-start = (bf16[128,512]{1,0:T(8,128)(2,1)S(1)}, bf16[128,512]{1,0:T(8,128)(2,1)}, u32[]{:S(2)}) copy-start(bf16[128,512]{1,0:T(8,128)(2,1)} %q_ref.1) | copy-start | bytes 393220
  59.1 35.9 %all-to-all-start = ((bf16[8,14,8,128]{3,2,1,0:T(8,128)(2,1)}), bf16[8,14,8,128]{3,2,1,0:T(8,128)(2,1)S(1)}, u32[]{:S(2)}, u32[]{:S(2)}) async-start(bf16[8,14,8,128]{3,2,1,0:T(8,128)(2,1)} %shard_map.64), calls=%async_computation | async-start | bytes 458752 | tf_op jit(solution)/shard_map/all_to_all | solution.py:230
  72.7 48.8 %collective-permute-start.12 = (bf16[2,512,256]{2,1,0:T(8,128)(2,1)S(1)}, bf16[2,512,256]{2,1,0:T(8,128)(2,1)S(1)}, u32[]{:S(2)}, u32[]{:S(2)}) collective-permute-start(bf16[2,512,256]{2,1,0:T(8,128)(2,1)S(1)} %pad_maximum_fusion.refs_4_), channel_id=1, source_target_pairs={{0,128},{1,129},{2,130},{3,131},{4,132},{5,133},{6,134},{7,135},{8... | collective-permute-start | bytes 1572872 | tf_op jit(solution)/shard_map/ppermute | solution.py:33
  87.8 33.7 %collective-permute-start.11 = (bf16[2,512,256]{2,1,0:T(8,128)(2,1)S(1)}, bf16[2,512,256]{2,1,0:T(8,128)(2,1)S(1)}, u32[]{:S(2)}, u32[]{:S(2)}) collective-permute-start(bf16[2,512,256]{2,1,0:T(8,128)(2,1)S(1)} %pad_maximum_fusion.refs_4_), channel_id=1, source_target_pairs={{0,256},{1,257},{2,258},{3,259},{4,260},{5,261},{6,262},{7,263},{8... | collective-permute-start | bytes 1572872 | tf_op jit(solution)/shard_map/ppermute | solution.py:33
  91.0 30.5 %collective-permute-start.10 = (bf16[2,512,256]{2,1,0:T(8,128)(2,1)S(1)}, bf16[2,512,256]{2,1,0:T(8,128)(2,1)S(1)}, u32[]{:S(2)}, u32[]{:S(2)}) collective-permute-start(bf16[2,512,256]{2,1,0:T(8,128)(2,1)S(1)} %pad_maximum_fusion.refs_4_), channel_id=1, source_target_pairs={{0,384},{1,385},{2,386},{3,387},{4,388},{5,389},{6,390},{7,391},{8... | collective-permute-start | bytes 1572872 | tf_op jit(solution)/shard_map/ppermute | solution.py:33
  94.9 8.0 %collective-permute-start.8 = (bf16[8,14,8,128]{3,2,1,0:T(8,128)(2,1)S(1)}, bf16[8,14,8,128]{3,2,1,0:T(8,128)(2,1)S(1)}, u32[]{:S(2)}, u32[]{:S(2)}) collective-permute-start(bf16[8,14,8,128]{3,2,1,0:T(8,128)(2,1)S(1)} %all-to-all-done.mine_ref), channel_id=1, source_target_pairs={{0,1},{1,0},{2,3},{3,2},{4,5},{5,4},{6,7},{7,6},{8,9},{9,8},{10,11... | collective-permute-start | bytes 688136 | tf_op jit(solution)/shard_map/ppermute | solution.py:33
  117.8 7.2 %collective-permute-start.9 = (bf16[128,512]{1,0:T(8,128)(2,1)S(1)}, bf16[128,512]{1,0:T(8,128)(2,1)S(1)}, u32[]{:S(2)}, u32[]{:S(2)}) collective-permute-start(bf16[128,512]{1,0:T(8,128)(2,1)S(1)} %shard_map.65), channel_id=1, source_target_pairs={{0,2},{1,3},{2,0},{3,1},{4,6},{5,7},{6,4},{7,5},{8,10},{9,11},{10,... | collective-permute-start | bytes 393224 | tf_op jit(solution)/shard_map/ppermute | solution.py:33
  125.1 15.7 %collective-permute-start.15 = (bf16[2,128,512]{2,1,0:T(8,128)(2,1)S(1)}, bf16[2,128,512]{2,1,0:T(8,128)(2,1)S(1)}, u32[]{:S(2)}, u32[]{:S(2)}) collective-permute-start(bf16[2,128,512]{2,1,0:T(8,128)(2,1)S(1)} %pad_maximum_fusion.1.refs_0_), channel_id=1, source_target_pairs={{0,16},{1,17},{2,18},{3,19},{4,20},{5,21},{6,22},{7,23},{8,24},{9,... | collective-permute-start | bytes 786440 | tf_op jit(solution)/shard_map/ppermute | solution.py:33
  127.0 13.7 %collective-permute-start.14 = (bf16[2,128,512]{2,1,0:T(8,128)(2,1)S(1)}, bf16[2,128,512]{2,1,0:T(8,128)(2,1)S(1)}, u32[]{:S(2)}, u32[]{:S(2)}) collective-permute-start(bf16[2,128,512]{2,1,0:T(8,128)(2,1)S(1)} %pad_maximum_fusion.1.refs_0_), channel_id=1, source_target_pairs={{0,32},{1,33},{2,34},{3,35},{4,36},{5,37},{6,38},{7,39},{8,40},{9,... | collective-permute-start | bytes 786440 | tf_op jit(solution)/shard_map/ppermute | solution.py:33
  129.0 14.5 %collective-permute-start.13 = (bf16[2,128,512]{2,1,0:T(8,128)(2,1)S(1)}, bf16[2,128,512]{2,1,0:T(8,128)(2,1)S(1)}, u32[]{:S(2)}, u32[]{:S(2)}) collective-permute-start(bf16[2,128,512]{2,1,0:T(8,128)(2,1)S(1)} %pad_maximum_fusion.1.refs_0_), channel_id=1, source_target_pairs={{0,48},{1,49},{2,50},{3,51},{4,52},{5,53},{6,54},{7,55},{8,56},{9,... | collective-permute-start | bytes 786440 | tf_op jit(solution)/shard_map/ppermute | solution.py:33
  145.3 5.0 %collective-permute-start.16 = (bf16[4,2,128,256]{3,2,1,0:T(8,128)(2,1)S(1)}, bf16[4,2,128,256]{3,2,1,0:T(8,128)(2,1)S(1)}, u32[]{:S(2)}, u32[]{:S(2)}) collective-permute-start(bf16[4,2,128,256]{3,2,1,0:T(8,128)(2,1)S(1)} %slice_bitcast_fusion), channel_id=1, source_target_pairs={{0,1},{1,0},{2,3},{3,2},{4,5},{5,4},{6,7},{7,6},{8,9},{9,8},{10,11... | collective-permute-start | bytes 1572872 | tf_op jit(solution)/shard_map/ppermute | solution.py:33
  150.5 18.0 %collective-permute-start.17 = (bf16[2,128,256]{2,1,0:T(8,128)(2,1)S(1)}, bf16[2,128,256]{2,1,0:T(8,128)(2,1)S(1)}, u32[]{:S(2)}, u32[]{:S(2)}) collective-permute-start(bf16[2,128,256]{2,1,0:T(8,128)(2,1)S(1)} %get-tuple-element.19), channel_id=1, source_target_pairs={{0,12},{1,13},{2,14},{3,15},{4,8},{5,9},{6,10},{7,11},{8,4},{9,5},... | collective-permute-start | bytes 393224 | tf_op jit(solution)/shard_map/ppermute | solution.py:33
  159.3 10.6 %collective-permute-start.19 = (bf16[2,128,256]{2,1,0:T(8,128)(2,1)S(1)}, bf16[2,128,256]{2,1,0:T(8,128)(2,1)S(1)}, u32[]{:S(2)}, u32[]{:S(2)}) collective-permute-start(bf16[2,128,256]{2,1,0:T(8,128)(2,1)S(1)} %get-tuple-element.20), channel_id=1, source_target_pairs={{0,4},{1,5},{2,6},{3,7},{4,0},{5,1},{6,2},{7,3},{8,12},{9,13},{10,... | collective-permute-start | bytes 393224 | tf_op jit(solution)/shard_map/ppermute | solution.py:33
  161.2 19.7 %collective-permute-start.18 = (bf16[2,128,256]{2,1,0:T(8,128)(2,1)S(1)}, bf16[2,128,256]{2,1,0:T(8,128)(2,1)S(1)}, u32[]{:S(2)}, u32[]{:S(2)}) collective-permute-start(bf16[2,128,256]{2,1,0:T(8,128)(2,1)S(1)} %get-tuple-element.21), channel_id=1, source_target_pairs={{0,8},{1,9},{2,10},{3,11},{4,12},{5,13},{6,14},{7,15},{8,0},{9,1},... | collective-permute-start | bytes 393224 | tf_op jit(solution)/shard_map/ppermute | solution.py:33
  181.1 7.0 %collective-permute-start.20 = (bf16[128,256]{1,0:T(8,128)(2,1)S(1)}, bf16[128,256]{1,0:T(8,128)(2,1)S(1)}, u32[]{:S(2)}, u32[]{:S(2)}) collective-permute-start(bf16[128,256]{1,0:T(8,128)(2,1)S(1)} %get-tuple-element.24), channel_id=1, source_target_pairs={{0,16},{1,48},{2,18},{3,50},{4,20},{5,52},{6,22},{7,54},{8,24},{9,... | collective-permute-start | bytes 196616 | tf_op jit(solution)/shard_map/ppermute | solution.py:33
  186.2 7.1 %collective-permute-start.21 = (bf16[128,256]{1,0:T(8,128)(2,1)S(1)}, bf16[128,256]{1,0:T(8,128)(2,1)S(1)}, u32[]{:S(2)}, u32[]{:S(2)}) collective-permute-start(bf16[128,256]{1,0:T(8,128)(2,1)S(1)} %get-tuple-element.25), channel_id=1, source_target_pairs={{0,0},{1,32},{2,2},{3,34},{4,4},{5,36},{6,6},{7,38},{8,8},{9,40},{... | collective-permute-start | bytes 196616 | tf_op jit(solution)/shard_map/ppermute | solution.py:33

commit v8 on v5

--- a/solution.py
+++ b/solution.py
@@ -121,7 +121,7 @@
     width = mine.shape[-1]
     spots = W1 // rows + 1
     return pl.pallas_call(
-        functools.partial(attention_kernel, tokens=16),
+        functools.partial(attention_kernel, tokens=32),
         out_shape=jax.ShapeDtypeStruct((rows, wide), jnp.bfloat16),
         in_specs=[pl.BlockSpec(memory_space=pltpu.SMEM)]
         + [pl.BlockSpec(memory_space=pltpu.VMEM)] * 3,
@@ -163,34 +163,72 @@
 
 
 def project_kernel(place, *refs):
-    tokens, columns, out_ref = refs[:YS], refs[YS : YS + XS], refs[-1]
+    own, beside, columns = refs[:YS], refs[YS : 2 * YS], refs[2 * YS : 2 * YS + XS]
+    kept_ref, away_ref = refs[-2:]
     x, y, far, c = place[0], place[1], place[2], place[3]
     for d in range(XS):
         to = lax.rem(x + d, XS) ^ far
         for e in range(YS):
             slot = lax.rem(y + e + YS - 2 * c, YS)
-            total = jnp.dot(tokens[e][0], columns[d][0], preferred_element_type=jnp.float32)
-            total += jnp.dot(tokens[e][1], columns[d][1], preferred_element_type=jnp.float32)
-            out_ref[slot // 2, to, slot % 2] = total.astype(jnp.bfloat16)
-
-
-def project(place, tokens, columns):
-    rows, wide = tokens[0].shape[1], columns[0].shape[2]
+            total = jnp.dot(own[e][...], columns[d][0], preferred_element_type=jnp.float32)
+            total += jnp.dot(beside[e][...], columns[d][1], preferred_element_type=jnp.float32)
+            total = total.astype(jnp.bfloat16)
+
+            @pl.when(slot < YS // 2)
+            def _():
+                kept_ref[to, slot % 2] = total
+
+            @pl.when(slot >= YS // 2)
+            def _():
+                away_ref[to, slot % 2] = total
+
+
+def small_call(kernel, place, operands, shapes):
+    out_shape = [jax.ShapeDtypeStruct(shape, jnp.bfloat16) for shape in shapes]
     return pl.pallas_call(
-        project_kernel,
-        out_shape=jax.ShapeDtypeStruct((2, XS, YS // 2, rows, wide), jnp.bfloat16),
+        kernel,
+        out_shape=out_shape,
         in_specs=[pl.BlockSpec(memory_space=pltpu.SMEM)]
-        + [pl.BlockSpec(memory_space=pltpu.VMEM)] * (XS + YS),
-        out_specs=pl.BlockSpec(memory_space=pltpu.VMEM),
+        + [pl.BlockSpec(memory_space=pltpu.VMEM)] * len(operands),
+        out_specs=[pl.BlockSpec(memory_space=pltpu.VMEM)] * len(shapes),
         compiler_params=pltpu.CompilerParams(vmem_limit_bytes=40 * 2**20),
-        cost_estimate=pl.CostEstimate(
-            flops=1_100_000_000, bytes_accessed=4 * 2**20, transcendentals=0
-        ),
-    )(place, *tokens, *columns)
-
-
-def in_order(first, second, swap):
-    return jnp.where(swap, second, first), jnp.where(swap, first, second)
+    )(place, *operands)
+
+
+def join_kernel(place, kept_ref, came_ref, *out_refs):
+    for k, out_ref in enumerate(out_refs):
+        total = kept_ref[k].astype(jnp.float32) + came_ref[k].astype(jnp.float32)
+        out_ref[...] = total.astype(jnp.bfloat16)
+
+
+def sum_kernel(place, *refs):
+    parts, out_refs = refs[:-2], refs[-2:]
+    for number in range(2):
+        total = sum(part[number].astype(jnp.float32) for part in parts).astype(jnp.bfloat16)
+        swap = place[1] % 2 == 1
+
+        @pl.when(swap)
+        def _():
+            out_refs[1 - number][...] = total
+
+        @pl.when(jnp.logical_not(swap))
+        def _():
+            out_refs[number][...] = total
+
+
+def lay_kernel(place, first_ref, second_ref, out_ref):
+    half = first_ref.shape[1]
+    swap = place[1] % 2 == 1
+
+    @pl.when(swap)
+    def _():
+        out_ref[:, :half] = second_ref[...]
+        out_ref[:, half:] = first_ref[...]
+
+    @pl.when(jnp.logical_not(swap))
+    def _():
+        out_ref[:, :half] = first_ref[...]
+        out_ref[:, half:] = second_ref[...]
 
 
 def per_device(queries, long_keys, long_values, short_keys, short_values, w_out):
@@ -252,21 +290,25 @@
     ]
 
     attended = attention(jnp.stack([seq, c]), queries, over_z, over_core)
-    beside = moved(attended, lambda x, h, y, z, c: (x, h, y, z ^ 1, c))
-    beside, from_x = lax.optimization_barrier((beside, from_x))
-    attended = jnp.stack([attended, beside])
-    from_y = [attended] + [
+    beside = [
+        moved(attended, lambda x, h, y, z, c, d=d: (x, h, y - d, z ^ 1, c)) for d in range(YS)
+    ]
+    attended, from_x = lax.optimization_barrier((attended, from_x))
+    own = [attended] + [
         moved(attended, lambda x, h, y, z, c, d=d: (x, h, y - d, z, c)) for d in (1, 2, 3)
     ]
-    sums = project(jnp.stack([x, y, z // 2, c]), from_y, from_x)
-    came = moved(sums[1], lambda x, h, y, z, c: (x, h, y, z, 1 - c))
-    kept = (sums[0].astype(jnp.float32) + came.astype(jnp.float32)).astype(jnp.bfloat16)
+    place = jnp.stack([x, y, z // 2, c])
+    wide = w_out.shape[1]
+    block = (YS // 2, rows, wide)
+    kept, away = small_call(
+        project_kernel, place, own + beside + from_x, [(XS,) + block, (XS,) + block]
+    )
+    came = moved(away, lambda x, h, y, z, c: (x, h, y, z, 1 - c))
+    kept = small_call(join_kernel, place, [kept, came], [block] * XS)
     parts = [kept[0]] + [
         moved(kept[k], lambda x, h, y, z, c, k=k: (x, h, y, z ^ (2 * k), c)) for k in (3, 2, 1)
     ]
-    summed = sum(part.astype(jnp.float32) for part in parts).astype(jnp.bfloat16)
-    odd = y % 2 == 1
-    sent = in_order(summed[0], summed[1], odd)
+    sent = small_call(sum_kernel, place, parts, [(rows, wide)] * 2)
     landed = [
         moved(
             sent[j],
@@ -274,7 +316,7 @@
         )
         for j in range(2)
     ]
-    return jnp.concatenate(in_order(landed[0], landed[1], odd), axis=1)
+    return small_call(lay_kernel, place, landed, [(rows, 2 * wide)])[0]
 
 
 def solution(mesh):

time: 192 us -> 198 us (1.031)
  starting transfers between devices: 124 us -> 134 us
  waiting for transfers between devices: 42 us -> 35.5 us
  Pallas kernels: 21.4 us -> 24 us
    ppermute x19 -> x22, starting transfers between devices: 91.3 us -> 101 us  [moved(): return lax.ppermute(value, BOTH, pairs)]
    ppermute x19 -> x22, waiting for transfers between devices: 32.9 us -> 26.4 us  [moved(): return lax.ppermute(value, BOTH, pairs)]
    pallas_call x2 -> x5, Pallas kernels: 19.9 us -> 22.5 us  [the longest x1 14.9 us: attention(): pl.pallas_call(functools.partial(attention_kernel, tokens=32), out_shape=...]
  transfers between devices with their start and end apart: 24 -> 27, of which waited for: 11 -> 8; matrix products, arithmetic and copies ran while one was open for 1% -> 0% of each run, Pallas kernels for 10% -> 8%
where the time goes in v8:
time: 198 us; the launch traced here: 197 us
  starting transfers between devices  134 us (68%)
  waiting for transfers between devices  35.5 us (18%)
  Pallas kernels  24 us (12%)
    ppermute x22, starting transfers between devices, moved(): return lax.ppermute(value, BOTH, pairs)  101 us
    ppermute x22, waiting for transfers between devices, moved(): return lax.ppermute(value, BOTH, pairs)  26.4 us
    ppermute x4, starting transfers between devices, later(): lax.ppermute(value, 'seq', [(s, s + steps) for s in range(count - steps)])  22.9 us
    pallas_call x1, Pallas kernels, attention(): pl.pallas_call(functools.partial(attention_kernel, tokens=32), out_shape=...  14.9 us
    all_to_all x1, starting transfers between devices, per_device(): lax.all_to_all(mine, 'head', 0, 0, axis_index_groups=lines, tiled=True)  10.1 us
    all_to_all x1, waiting for transfers between devices, per_device(): lax.all_to_all(mine, 'head', 0, 0, axis_index_groups=lines, tiled=True)  8.43 us
    pallas_call x4, Pallas kernels, small_call(): pl.pallas_call(kernel, out_shape=out_shape, in_specs=[pl.BlockSpec(memory...  7.68 us
  transfers between devices with their start and end apart: 27, of which 8 were waited for; matrix products, arithmetic and copies ran while one was open for 0% of the time, Pallas kernels for 8%

profile of v8, /device:TPU:1, one launch (start us, length us, event | category | flops | bytes accessed | tf_op | source)
XLA Modules:
  0.0 196.6 jit_solution(6920396468089390657)
XLA Ops:
  0.8 10.3 %collective-permute-start.4 = (bf16[512,256]{1,0:T(8,128)(2,1)}, bf16[512,256]{1,0:T(8,128)(2,1)S(1)}, u32[]{:S(2)}, u32[]{:S(2)}) collective-permute-start(bf16[512,256]{1,0:T(8,128)(2,1)} %param.11), channel_id=1, source_target_pairs={{0,8},{1,9},{4,12},{5,13},{8,64},{9,65},{12,68},{13,69},{16,24},{1... | collective-permute-start | bytes 786440 | tf_op jit(solution)/shard_map/ppermute | solution.py:33
  11.8 8.6 %collective-permute-start.3 = (bf16[2,8,128]{2,1,0:T(8,128)(2,1)S(1)}, bf16[2,8,128]{2,1,0:T(8,128)(2,1)S(1)}, u32[]{:S(2)}, u32[]{:S(2)}) collective-permute-start(bf16[2,8,128]{2,1,0:T(8,128)(2,1)S(1)} %pad_maximum_fusion.2), channel_id=1, source_target_pairs={{0,64},{16,80},{32,96},{48,112},{64,128},{80,144},{96,160},{112,17... | collective-permute-start | bytes 12296 | tf_op jit(solution)/shard_map/ppermute | solution.py:38
  20.5 3.2 %collective-permute-start = (bf16[4,8,128]{2,1,0:T(8,128)(2,1)S(1)}, bf16[4,8,128]{2,1,0:T(8,128)(2,1)S(1)}, u32[]{:S(2)}, u32[]{:S(2)}) collective-permute-start(bf16[4,8,128]{2,1,0:T(8,128)(2,1)S(1)} %pad_maximum_fusion.1), channel_id=1, source_target_pairs={{0,16},{16,32},{32,48},{48,64},{64,80},{80,96},{96,112},{112,128},... | collective-permute-start | bytes 24584 | tf_op jit(solution)/shard_map/ppermute | solution.py:38
  23.7 7.5 %collective-permute-start.2 = (bf16[2,8,128]{2,1,0:T(8,128)(2,1)S(1)}, bf16[2,8,128]{2,1,0:T(8,128)(2,1)S(1)}, u32[]{:S(2)}, u32[]{:S(2)}) collective-permute-start(bf16[2,8,128]{2,1,0:T(8,128)(2,1)S(1)} %pad_maximum_fusion.2), channel_id=1, source_target_pairs={{0,48},{16,64},{32,80},{48,96},{64,112},{80,128},{96,144},{112,160... | collective-permute-start | bytes 12296 | tf_op jit(solution)/shard_map/ppermute | solution.py:38
  31.3 3.6 %collective-permute-start.1 = (bf16[2,8,128]{2,1,0:T(8,128)(2,1)S(1)}, bf16[2,8,128]{2,1,0:T(8,128)(2,1)S(1)}, u32[]{:S(2)}, u32[]{:S(2)}) collective-permute-start(bf16[2,8,128]{2,1,0:T(8,128)(2,1)S(1)} %pad_maximum_fusion.2), channel_id=1, source_target_pairs={{0,32},{16,48},{32,64},{48,80},{64,96},{80,112},{96,128},{112,144}... | collective-permute-start | bytes 12296 | tf_op jit(solution)/shard_map/ppermute | solution.py:38
  36.8 1.5 shard_map.64
  38.3 10.1 %all-to-all-start = ((bf16[8,14,8,128]{3,2,1,0:T(8,128)(2,1)}), bf16[8,14,8,128]{3,2,1,0:T(8,128)(2,1)S(1)}, u32[]{:S(2)}, u32[]{:S(2)}) async-start(bf16[8,14,8,128]{3,2,1,0:T(8,128)(2,1)} %shard_map.64), calls=%async_computation | async-start | bytes 458752 | tf_op jit(solution)/shard_map/all_to_all | solution.py:280
  51.2 8.4 %all-to-all-done.mine_ref = bf16[8,14,8,128]{3,2,1,0:T(8,128)(2,1)S(1)} async-done(((bf16[8,14,8,128]{3,2,1,0:T(8,128)(2,1)}), bf16[8,14,8,128]{3,2,1,0:T(8,128)(2,1)S(1)}, u32[]{:S(2)}, u32[]{:S(2)}) %all-to-all-start) | async-done | bytes 229408 | tf_op jit(solution)/shard_map/all_to_all | solution.py:280
  59.7 6.3 %collective-permute-start.9 = (bf16[8,14,8,128]{3,2,1,0:T(8,128)(2,1)S(1)}, bf16[8,14,8,128]{3,2,1,0:T(8,128)(2,1)S(1)}, u32[]{:S(2)}, u32[]{:S(2)}) collective-permute-start(bf16[8,14,8,128]{3,2,1,0:T(8,128)(2,1)S(1)} %all-to-all-done.mine_ref), channel_id=1, source_target_pairs={{0,1},{1,0},{2,3},{3,2},{4,5},{5,4},{6,7},{7,6},{8,9},{9,8},{10,11... | collective-permute-start | bytes 688136 | tf_op jit(solution)/shard_map/ppermute | solution.py:33
  67.0 15.6 %collective-permute-start.12 = (bf16[2,512,256]{2,1,0:T(8,128)(2,1)S(1)}, bf16[2,512,256]{2,1,0:T(8,128)(2,1)S(1)}, u32[]{:S(2)}, u32[]{:S(2)}) collective-permute-start(bf16[2,512,256]{2,1,0:T(8,128)(2,1)S(1)} %pad_maximum_fusion.refs_8_), channel_id=1, source_target_pairs={{0,128},{1,129},{2,130},{3,131},{4,132},{5,133},{6,134},{7,135},{8... | collective-permute-start | bytes 1572872 | tf_op jit(solution)/shard_map/ppermute | solution.py:33
  82.6 3.2 %collective-permute-start.11 = (bf16[2,512,256]{2,1,0:T(8,128)(2,1)S(1)}, bf16[2,512,256]{2,1,0:T(8,128)(2,1)S(1)}, u32[]{:S(2)}, u32[]{:S(2)}) collective-permute-start(bf16[2,512,256]{2,1,0:T(8,128)(2,1)S(1)} %pad_maximum_fusion.refs_8_), channel_id=1, source_target_pairs={{0,256},{1,257},{2,258},{3,259},{4,260},{5,261},{6,262},{7,263},{8... | collective-permute-start | bytes 1572872 | tf_op jit(solution)/shard_map/ppermute | solution.py:33
  85.8 4.0 %collective-permute-start.10 = (bf16[2,512,256]{2,1,0:T(8,128)(2,1)S(1)}, bf16[2,512,256]{2,1,0:T(8,128)(2,1)S(1)}, u32[]{:S(2)}, u32[]{:S(2)}) collective-permute-start(bf16[2,512,256]{2,1,0:T(8,128)(2,1)S(1)} %pad_maximum_fusion.refs_8_), channel_id=1, source_target_pairs={{0,384},{1,385},{2,386},{3,387},{4,388},{5,389},{6,390},{7,391},{8... | collective-permute-start | bytes 1572872 | tf_op jit(solution)/shard_map/ppermute | solution.py:33
  89.8 14.9 %shard_map.65.refs_0_ = bf16[128,512]{1,0:T(8,128)(2,1)S(1)} custom-call(s32[2]{0:T(128)S(1)} %pad_add_fusion.1.place, bf16[128,512]{1,0:T(8,128)(2,1)S(1)} %copy-done, bf16[8,14,8,128]{3,2,1,0:T(8,128)(2,1)S(1)} %all-to-all-done.mine_ref, bf16[8,14,8,128]{3,2,1,0:T(8,128)(2,1)S(1)} %collective-permute-done.9.other_ref), custom_call_target="tpu_custom_call" | custom-call | flops 20000000000 | bytes 1048576 | tf_op jit(solution)/shard_map/pallas_call | solution.py:123
  104.6 9.4 %collective-permute-start.19 = (bf16[128,512]{1,0:T(8,128)(2,1)S(1)}, bf16[128,512]{1,0:T(8,128)(2,1)S(1)}, u32[]{:S(2)}, u32[]{:S(2)}) collective-permute-start(bf16[128,512]{1,0:T(8,128)(2,1)S(1)} %shard_map.65.refs_0_), channel_id=1, source_target_pairs={{0,18},{1,19},{2,16},{3,17},{4,22},{5,23},{6,20},{7,21},{8,26},{9,... | collective-permute-start | bytes 393224 | tf_op jit(solution)/shard_map/ppermute | solution.py:33
  114.0 1.9 collective-permute-start.18
  116.0 1.9 collective-permute-start.17
  117.9 5.7 %collective-permute-start.16 = (bf16[128,512]{1,0:T(8,128)(2,1)S(1)}, bf16[128,512]{1,0:T(8,128)(2,1)S(1)}, u32[]{:S(2)}, u32[]{:S(2)}) collective-permute-start(bf16[128,512]{1,0:T(8,128)(2,1)S(1)} %shard_map.65.refs_0_), channel_id=1, source_target_pairs={{0,2},{1,3},{2,0},{3,1},{4,6},{5,7},{6,4},{7,5},{8,10},{9,11},{10,... | collective-permute-start | bytes 393224 | tf_op jit(solution)/shard_map/ppermute | solution.py:33
  123.6 2.5 %collective-permute-start.15 = (bf16[128,512]{1,0:T(8,128)(2,1)S(1)}, bf16[128,512]{1,0:T(8,128)(2,1)S(1)}, u32[]{:S(2)}, u32[]{:S(2)}) collective-permute-start(bf16[128,512]{1,0:T(8,128)(2,1)S(1)} %shard_map.65.refs_0_), channel_id=1, source_target_pairs={{0,16},{1,17},{2,18},{3,19},{4,20},{5,21},{6,22},{7,23},{8,24},{9,... | collective-permute-start | bytes 393224 | tf_op jit(solution)/shard_map/ppermute | solution.py:33
  126.1 3.4 %collective-permute-start.14 = (bf16[128,512]{1,0:T(8,128)(2,1)S(1)}, bf16[128,512]{1,0:T(8,128)(2,1)S(1)}, u32[]{:S(2)}, u32[]{:S(2)}) collective-permute-start(bf16[128,512]{1,0:T(8,128)(2,1)S(1)} %shard_map.65.refs_0_), channel_id=1, source_target_pairs={{0,32},{1,33},{2,34},{3,35},{4,36},{5,37},{6,38},{7,39},{8,40},{9,... | collective-permute-start | bytes 393224 | tf_op jit(solution)/shard_map/ppermute | solution.py:33
  129.6 4.0 %collective-permute-start.13 = (bf16[128,512]{1,0:T(8,128)(2,1)S(1)}, bf16[128,512]{1,0:T(8,128)(2,1)S(1)}, u32[]{:S(2)}, u32[]{:S(2)}) collective-permute-start(bf16[128,512]{1,0:T(8,128)(2,1)S(1)} %shard_map.65.refs_0_), channel_id=1, source_target_pairs={{0,48},{1,49},{2,50},{3,51},{4,52},{5,53},{6,54},{7,55},{8,56},{9,... | collective-permute-start | bytes 393224 | tf_op jit(solution)/shard_map/ppermute | solution.py:33
  133.7 1.9 collective-permute-done.13.refs_1_
  135.6 5.2 %shard_map.66 = (bf16[4,2,128,256]{3,2,1,0:T(8,128)(2,1)S(1)}, bf16[4,2,128,256]{3,2,1,0:T(8,128)(2,1)S(1)}) custom-call(s32[4]{0:T(128)S(1)} %pad_add_fusion.place, bf16[128,512]{1,0:T(8,128)(2,1)S(1)} %shard_map.65.refs_0_, bf16[128,512]{1,0:T(8,128)(2,1)S(1)} %collective-permute-done.13.refs_1_, bf16[128,512]{1,0:T(8,128)(2,1)S(1)} %collective-permute-done.14.refs_2_, ...), custom_call_target="tpu_custom_call" | custom-call | tf_op jit(solution)/shard_map/pallas_call | solution.py:188
  140.8 8.8 %collective-permute-start.20 = (bf16[4,2,128,256]{3,2,1,0:T(8,128)(2,1)S(1)}, bf16[4,2,128,256]{3,2,1,0:T(8,128)(2,1)S(1)}, u32[]{:S(2)}, u32[]{:S(2)}) collective-permute-start(bf16[4,2,128,256]{3,2,1,0:T(8,128)(2,1)S(1)} %get-tuple-element.34), channel_id=1, source_target_pairs={{0,1},{1,0},{2,3},{3,2},{4,5},{5,4},{6,7},{7,6},{8,9},{9,8},{10,11... | collective-permute-start | bytes 1572872 | tf_op jit(solution)/shard_map/ppermute | solution.py:33
  149.5 1.5 collective-permute-done.20.came_ref
  151.7 6.0 %collective-permute-start.21 = (bf16[2,128,256]{2,1,0:T(8,128)(2,1)S(1)}, bf16[2,128,256]{2,1,0:T(8,128)(2,1)S(1)}, u32[]{:S(2)}, u32[]{:S(2)}) collective-permute-start(bf16[2,128,256]{2,1,0:T(8,128)(2,1)S(1)} %get-tuple-element.36), channel_id=1, source_target_pairs={{0,12},{1,13},{2,14},{3,15},{4,8},{5,9},{6,10},{7,11},{8,4},{9,5},... | collective-permute-start | bytes 393224 | tf_op jit(solution)/shard_map/ppermute | solution.py:33
  157.7 4.6 %collective-permute-start.22 = (bf16[2,128,256]{2,1,0:T(8,128)(2,1)S(1)}, bf16[2,128,256]{2,1,0:T(8,128)(2,1)S(1)}, u32[]{:S(2)}, u32[]{:S(2)}) collective-permute-start(bf16[2,128,256]{2,1,0:T(8,128)(2,1)S(1)} %get-tuple-element.37), channel_id=1, source_target_pairs={{0,8},{1,9},{2,10},{3,11},{4,12},{5,13},{6,14},{7,15},{8,0},{9,1},... | collective-permute-start | bytes 393224 | tf_op jit(solution)/shard_map/ppermute | solution.py:33
  162.4 2.5 %collective-permute-start.23 = (bf16[2,128,256]{2,1,0:T(8,128)(2,1)S(1)}, bf16[2,128,256]{2,1,0:T(8,128)(2,1)S(1)}, u32[]{:S(2)}, u32[]{:S(2)}) collective-permute-start(bf16[2,128,256]{2,1,0:T(8,128)(2,1)S(1)} %get-tuple-element.38), channel_id=1, source_target_pairs={{0,4},{1,5},{2,6},{3,7},{4,0},{5,1},{6,2},{7,3},{8,12},{9,13},{10,... | collective-permute-start | bytes 393224 | tf_op jit(solution)/shard_map/ppermute | solution.py:33
  164.9 2.0 %collective-permute-done.21.refs_1_ = bf16[2,128,256]{2,1,0:T(8,128)(2,1)S(1)} collective-permute-done((bf16[2,128,256]{2,1,0:T(8,128)(2,1)S(1)}, bf16[2,128,256]{2,1,0:T(8,128)(2,1)S(1)}, u32[]{:S(2)}, u32[]{:S(2)}) %collective-permute-start.21) | collective-permute-done | bytes 131104 | tf_op jit(solution)/shard_map/ppermute | solution.py:33
  166.9 16.9 %collective-permute-done.22.refs_2_ = bf16[2,128,256]{2,1,0:T(8,128)(2,1)S(1)} collective-permute-done((bf16[2,128,256]{2,1,0:T(8,128)(2,1)S(1)}, bf16[2,128,256]{2,1,0:T(8,128)(2,1)S(1)}, u32[]{:S(2)}, u32[]{:S(2)}) %collective-permute-start.22) | collective-permute-done | bytes 131104 | tf_op jit(solution)/shard_map/ppermute | solution.py:33
  184.4 4.2 %collective-permute-start.24 = (bf16[128,256]{1,0:T(8,128)(2,1)S(1)}, bf16[128,256]{1,0:T(8,128)(2,1)S(1)}, u32[]{:S(2)}, u32[]{:S(2)}) collective-permute-start(bf16[128,256]{1,0:T(8,128)(2,1)S(1)} %get-tuple-element.39), channel_id=1, source_target_pairs={{0,0},{1,32},{2,2},{3,34},{4,4},{5,36},{6,6},{7,38},{8,8},{9,40},{... | collective-permute-start | bytes 196616 | tf_op jit(solution)/shard_map/ppermute | solution.py:33
  188.6 3.7 %collective-permute-start.25 = (bf16[128,256]{1,0:T(8,128)(2,1)S(1)}, bf16[128,256]{1,0:T(8,128)(2,1)S(1)}, u32[]{:S(2)}, u32[]{:S(2)}) collective-permute-start(bf16[128,256]{1,0:T(8,128)(2,1)S(1)} %get-tuple-element.40), channel_id=1, source_target_pairs={{0,16},{1,48},{2,18},{3,50},{4,20},{5,52},{6,22},{7,54},{8,24},{9,... | collective-permute-start | bytes 196616 | tf_op jit(solution)/shard_map/ppermute | solution.py:33
  192.3 3.1 %collective-permute-done.25.second_ref = bf16[128,256]{1,0:T(8,128)(2,1)S(1)} collective-permute-done((bf16[128,256]{1,0:T(8,128)(2,1)S(1)}, bf16[128,256]{1,0:T(8,128)(2,1)S(1)}, u32[]{:S(2)}, u32[]{:S(2)}) %collective-permute-start.25) | collective-permute-done | bytes 65568 | tf_op jit(solution)/shard_map/ppermute | solution.py:33
  (55 shorter events, 9.8 us)
Async XLA Ops:
  0.0 11.1 %copy-start.2 = (bf16[8,128]{1,0:T(8,128)(2,1)S(1)}, bf16[8,128]{1,0:T(8,128)(2,1)}, u32[]{:S(2)}) copy-start(bf16[8,128]{1,0:T(8,128)(2,1)} %refs_0_.1) | copy-start | bytes 6148
  0.0 38.3 %collective-permute-start.5 = (bf16[512,256]{1,0:T(8,128)(2,1)}, bf16[512,256]{1,0:T(8,128)(2,1)S(1)}, u32[]{:S(2)}, u32[]{:S(2)}) collective-permute-start(bf16[512,256]{1,0:T(8,128)(2,1)} %param.11), channel_id=1, source_target_pairs={{2,74},{3,75},{6,78},{7,79},{10,2},{11,3},{14,6},{15,7},{18,90},{1... | collective-permute-start | bytes 786440 | tf_op jit(solution)/shard_map/ppermute | solution.py:33
  0.8 37.5 %collective-permute-start.4 = (bf16[512,256]{1,0:T(8,128)(2,1)}, bf16[512,256]{1,0:T(8,128)(2,1)S(1)}, u32[]{:S(2)}, u32[]{:S(2)}) collective-permute-start(bf16[512,256]{1,0:T(8,128)(2,1)} %param.11), channel_id=1, source_target_pairs={{0,8},{1,9},{4,12},{5,13},{8,64},{9,65},{12,68},{13,69},{16,24},{1... | collective-permute-start | bytes 786440 | tf_op jit(solution)/shard_map/ppermute | solution.py:33
  11.1 9.4 %copy-start.4 = (bf16[8,128]{1,0:T(8,128)(2,1)S(1)}, bf16[8,128]{1,0:T(8,128)(2,1)}, u32[]{:S(2)}) copy-start(bf16[8,128]{1,0:T(8,128)(2,1)} %refs_2_.1) | copy-start | bytes 6148
  11.1 9.4 %copy-start.5 = (bf16[8,128]{1,0:T(8,128)(2,1)S(1)}, bf16[8,128]{1,0:T(8,128)(2,1)}, u32[]{:S(2)}) copy-start(bf16[8,128]{1,0:T(8,128)(2,1)} %refs_3_.1) | copy-start | bytes 6148
  11.8 19.4 %collective-permute-start.3 = (bf16[2,8,128]{2,1,0:T(8,128)(2,1)S(1)}, bf16[2,8,128]{2,1,0:T(8,128)(2,1)S(1)}, u32[]{:S(2)}, u32[]{:S(2)}) collective-permute-start(bf16[2,8,128]{2,1,0:T(8,128)(2,1)S(1)} %pad_maximum_fusion.2), channel_id=1, source_target_pairs={{0,64},{16,80},{32,96},{48,112},{64,128},{80,144},{96,160},{112,17... | collective-permute-start | bytes 12296 | tf_op jit(solution)/shard_map/ppermute | solution.py:38
  20.5 15.1 %collective-permute-start = (bf16[4,8,128]{2,1,0:T(8,128)(2,1)S(1)}, bf16[4,8,128]{2,1,0:T(8,128)(2,1)S(1)}, u32[]{:S(2)}, u32[]{:S(2)}) collective-permute-start(bf16[4,8,128]{2,1,0:T(8,128)(2,1)S(1)} %pad_maximum_fusion.1), channel_id=1, source_target_pairs={{0,16},{16,32},{32,48},{48,64},{64,80},{80,96},{96,112},{112,128},... | collective-permute-start | bytes 24584 | tf_op jit(solution)/shard_map/ppermute | solution.py:38
  23.7 11.1 %collective-permute-start.2 = (bf16[2,8,128]{2,1,0:T(8,128)(2,1)S(1)}, bf16[2,8,128]{2,1,0:T(8,128)(2,1)S(1)}, u32[]{:S(2)}, u32[]{:S(2)}) collective-permute-start(bf16[2,8,128]{2,1,0:T(8,128)(2,1)S(1)} %pad_maximum_fusion.2), channel_id=1, source_target_pairs={{0,48},{16,64},{32,80},{48,96},{64,112},{80,128},{96,144},{112,160... | collective-permute-start | bytes 12296 | tf_op jit(solution)/shard_map/ppermute | solution.py:38
  31.3 4.4 %collective-permute-start.1 = (bf16[2,8,128]{2,1,0:T(8,128)(2,1)S(1)}, bf16[2,8,128]{2,1,0:T(8,128)(2,1)S(1)}, u32[]{:S(2)}, u32[]{:S(2)}) collective-permute-start(bf16[2,8,128]{2,1,0:T(8,128)(2,1)S(1)} %pad_maximum_fusion.2), channel_id=1, source_target_pairs={{0,32},{16,48},{32,64},{48,80},{64,96},{80,112},{96,128},{112,144}... | collective-permute-start | bytes 12296 | tf_op jit(solution)/shard_map/ppermute | solution.py:38
  38.3 10.8 %copy-start.1 = (bf16[512,256]{1,0:T(8,128)(2,1)S(1)}, bf16[512,256]{1,0:T(8,128)(2,1)}, u32[]{:S(2)}) copy-start(bf16[512,256]{1,0:T(8,128)(2,1)} %param.11) | copy-start | bytes 786436
  38.3 21.4 %all-to-all-start = ((bf16[8,14,8,128]{3,2,1,0:T(8,128)(2,1)}), bf16[8,14,8,128]{3,2,1,0:T(8,128)(2,1)S(1)}, u32[]{:S(2)}, u32[]{:S(2)}) async-start(bf16[8,14,8,128]{3,2,1,0:T(8,128)(2,1)} %shard_map.64), calls=%async_computation | async-start | bytes 458752 | tf_op jit(solution)/shard_map/all_to_all | solution.py:280
  48.4 2.8 %collective-permute-start.6 = (bf16[512,256]{1,0:T(8,128)(2,1)S(1)}, bf16[512,256]{1,0:T(8,128)(2,1)S(1)}, u32[]{:S(2)}, u32[]{:S(2)}) collective-permute-start(bf16[512,256]{1,0:T(8,128)(2,1)S(1)} %collective-permute-done.4), channel_id=1, source_target_pairs={{2,10},{3,11},{6,14},{7,15},{8,64},{9,65},{12,68},{13,69},{18,26},... | collective-permute-start | bytes 786440 | tf_op jit(solution)/shard_map/ppermute | solution.py:33
  49.1 16.8 %collective-permute-start.7 = (bf16[512,256]{1,0:T(8,128)(2,1)S(1)}, bf16[512,256]{1,0:T(8,128)(2,1)S(1)}, u32[]{:S(2)}, u32[]{:S(2)}) collective-permute-start(bf16[512,256]{1,0:T(8,128)(2,1)S(1)} %copy-done.1), channel_id=1, source_target_pairs={{2,0},{3,1},{6,4},{7,5},{10,8},{11,9},{14,12},{15,13},{18,16},{19,... | collective-permute-start | bytes 786440 | tf_op jit(solution)/shard_map/ppermute | solution.py:33
  50.4 15.5 %collective-permute-start.8 = (bf16[512,256]{1,0:T(8,128)(2,1)S(1)}, bf16[512,256]{1,0:T(8,128)(2,1)S(1)}, u32[]{:S(2)}, u32[]{:S(2)}) collective-permute-start(bf16[512,256]{1,0:T(8,128)(2,1)S(1)} %collective-permute-done.5), channel_id=1, source_target_pairs={{2,72},{3,73},{6,76},{7,77},{8,2},{9,3},{12,6},{13,7},{18,88},{19,... | collective-permute-start | bytes 786440 | tf_op jit(solution)/shard_map/ppermute | solution.py:33
  59.7 7.4 %collective-permute-start.9 = (bf16[8,14,8,128]{3,2,1,0:T(8,128)(2,1)S(1)}, bf16[8,14,8,128]{3,2,1,0:T(8,128)(2,1)S(1)}, u32[]{:S(2)}, u32[]{:S(2)}) collective-permute-start(bf16[8,14,8,128]{3,2,1,0:T(8,128)(2,1)S(1)} %all-to-all-done.mine_ref), channel_id=1, source_target_pairs={{0,1},{1,0},{2,3},{3,2},{4,5},{5,4},{6,7},{7,6},{8,9},{9,8},{10,11... | collective-permute-start | bytes 688136 | tf_op jit(solution)/shard_map/ppermute | solution.py:33
  66.0 23.8 %copy-start = (bf16[128,512]{1,0:T(8,128)(2,1)S(1)}, bf16[128,512]{1,0:T(8,128)(2,1)}, u32[]{:S(2)}) copy-start(bf16[128,512]{1,0:T(8,128)(2,1)} %q_ref.1) | copy-start | bytes 393220
  67.0 48.9 %collective-permute-start.12 = (bf16[2,512,256]{2,1,0:T(8,128)(2,1)S(1)}, bf16[2,512,256]{2,1,0:T(8,128)(2,1)S(1)}, u32[]{:S(2)}, u32[]{:S(2)}) collective-permute-start(bf16[2,512,256]{2,1,0:T(8,128)(2,1)S(1)} %pad_maximum_fusion.refs_8_), channel_id=1, source_target_pairs={{0,128},{1,129},{2,130},{3,131},{4,132},{5,133},{6,134},{7,135},{8... | collective-permute-start | bytes 1572872 | tf_op jit(solution)/shard_map/ppermute | solution.py:33
  82.6 35.3 %collective-permute-start.11 = (bf16[2,512,256]{2,1,0:T(8,128)(2,1)S(1)}, bf16[2,512,256]{2,1,0:T(8,128)(2,1)S(1)}, u32[]{:S(2)}, u32[]{:S(2)}) collective-permute-start(bf16[2,512,256]{2,1,0:T(8,128)(2,1)S(1)} %pad_maximum_fusion.refs_8_), channel_id=1, source_target_pairs={{0,256},{1,257},{2,258},{3,259},{4,260},{5,261},{6,262},{7,263},{8... | collective-permute-start | bytes 1572872 | tf_op jit(solution)/shard_map/ppermute | solution.py:33
  85.8 37.8 %collective-permute-start.10 = (bf16[2,512,256]{2,1,0:T(8,128)(2,1)S(1)}, bf16[2,512,256]{2,1,0:T(8,128)(2,1)S(1)}, u32[]{:S(2)}, u32[]{:S(2)}) collective-permute-start(bf16[2,512,256]{2,1,0:T(8,128)(2,1)S(1)} %pad_maximum_fusion.refs_8_), channel_id=1, source_target_pairs={{0,384},{1,385},{2,386},{3,387},{4,388},{5,389},{6,390},{7,391},{8... | collective-permute-start | bytes 1572872 | tf_op jit(solution)/shard_map/ppermute | solution.py:33
  104.6 21.5 %collective-permute-start.19 = (bf16[128,512]{1,0:T(8,128)(2,1)S(1)}, bf16[128,512]{1,0:T(8,128)(2,1)S(1)}, u32[]{:S(2)}, u32[]{:S(2)}) collective-permute-start(bf16[128,512]{1,0:T(8,128)(2,1)S(1)} %shard_map.65.refs_0_), channel_id=1, source_target_pairs={{0,18},{1,19},{2,16},{3,17},{4,22},{5,23},{6,20},{7,21},{8,26},{9,... | collective-permute-start | bytes 393224 | tf_op jit(solution)/shard_map/ppermute | solution.py:33
  114.0 15.5 %collective-permute-start.18 = (bf16[128,512]{1,0:T(8,128)(2,1)S(1)}, bf16[128,512]{1,0:T(8,128)(2,1)S(1)}, u32[]{:S(2)}, u32[]{:S(2)}) collective-permute-start(bf16[128,512]{1,0:T(8,128)(2,1)S(1)} %shard_map.65.refs_0_), channel_id=1, source_target_pairs={{0,34},{1,35},{2,32},{3,33},{4,38},{5,39},{6,36},{7,37},{8,42},{9,... | collective-permute-start | bytes 393224 | tf_op jit(solution)/shard_map/ppermute | solution.py:33
  116.0 17.7 %collective-permute-start.17 = (bf16[128,512]{1,0:T(8,128)(2,1)S(1)}, bf16[128,512]{1,0:T(8,128)(2,1)S(1)}, u32[]{:S(2)}, u32[]{:S(2)}) collective-permute-start(bf16[128,512]{1,0:T(8,128)(2,1)S(1)} %shard_map.65.refs_0_), channel_id=1, source_target_pairs={{0,50},{1,51},{2,48},{3,49},{4,54},{5,55},{6,52},{7,53},{8,58},{9,... | collective-permute-start | bytes 393224 | tf_op jit(solution)/shard_map/ppermute | solution.py:33
  117.9 15.7 %collective-permute-start.16 = (bf16[128,512]{1,0:T(8,128)(2,1)S(1)}, bf16[128,512]{1,0:T(8,128)(2,1)S(1)}, u32[]{:S(2)}, u32[]{:S(2)}) collective-permute-start(bf16[128,512]{1,0:T(8,128)(2,1)S(1)} %shard_map.65.refs_0_), channel_id=1, source_target_pairs={{0,2},{1,3},{2,0},{3,1},{4,6},{5,7},{6,4},{7,5},{8,10},{9,11},{10,... | collective-permute-start | bytes 393224 | tf_op jit(solution)/shard_map/ppermute | solution.py:33
  123.6 10.1 %collective-permute-start.15 = (bf16[128,512]{1,0:T(8,128)(2,1)S(1)}, bf16[128,512]{1,0:T(8,128)(2,1)S(1)}, u32[]{:S(2)}, u32[]{:S(2)}) collective-permute-start(bf16[128,512]{1,0:T(8,128)(2,1)S(1)} %shard_map.65.refs_0_), channel_id=1, source_target_pairs={{0,16},{1,17},{2,18},{3,19},{4,20},{5,21},{6,22},{7,23},{8,24},{9,... | collective-permute-start | bytes 393224 | tf_op jit(solution)/shard_map/ppermute | solution.py:33
  126.1 7.6 %collective-permute-start.14 = (bf16[128,512]{1,0:T(8,128)(2,1)S(1)}, bf16[128,512]{1,0:T(8,128)(2,1)S(1)}, u32[]{:S(2)}, u32[]{:S(2)}) collective-permute-start(bf16[128,512]{1,0:T(8,128)(2,1)S(1)} %shard_map.65.refs_0_), channel_id=1, source_target_pairs={{0,32},{1,33},{2,34},{3,35},{4,36},{5,37},{6,38},{7,39},{8,40},{9,... | collective-permute-start | bytes 393224 | tf_op jit(solution)/shard_map/ppermute | solution.py:33
  129.6 6.0 %collective-permute-start.13 = (bf16[128,512]{1,0:T(8,128)(2,1)S(1)}, bf16[128,512]{1,0:T(8,128)(2,1)S(1)}, u32[]{:S(2)}, u32[]{:S(2)}) collective-permute-start(bf16[128,512]{1,0:T(8,128)(2,1)S(1)} %shard_map.65.refs_0_), channel_id=1, source_target_pairs={{0,48},{1,49},{2,50},{3,51},{4,52},{5,53},{6,54},{7,55},{8,56},{9,... | collective-permute-start | bytes 393224 | tf_op jit(solution)/shard_map/ppermute | solution.py:33
  140.8 10.3 %collective-permute-start.20 = (bf16[4,2,128,256]{3,2,1,0:T(8,128)(2,1)S(1)}, bf16[4,2,128,256]{3,2,1,0:T(8,128)(2,1)S(1)}, u32[]{:S(2)}, u32[]{:S(2)}) collective-permute-start(bf16[4,2,128,256]{3,2,1,0:T(8,128)(2,1)S(1)} %get-tuple-element.34), channel_id=1, source_target_pairs={{0,1},{1,0},{2,3},{3,2},{4,5},{5,4},{6,7},{7,6},{8,9},{9,8},{10,11... | collective-permute-start | bytes 1572872 | tf_op jit(solution)/shard_map/ppermute | solution.py:33
  151.7 15.2 %collective-permute-start.21 = (bf16[2,128,256]{2,1,0:T(8,128)(2,1)S(1)}, bf16[2,128,256]{2,1,0:T(8,128)(2,1)S(1)}, u32[]{:S(2)}, u32[]{:S(2)}) collective-permute-start(bf16[2,128,256]{2,1,0:T(8,128)(2,1)S(1)} %get-tuple-element.36), channel_id=1, source_target_pairs={{0,12},{1,13},{2,14},{3,15},{4,8},{5,9},{6,10},{7,11},{8,4},{9,5},... | collective-permute-start | bytes 393224 | tf_op jit(solution)/shard_map/ppermute | solution.py:33
  157.7 26.1 %collective-permute-start.22 = (bf16[2,128,256]{2,1,0:T(8,128)(2,1)S(1)}, bf16[2,128,256]{2,1,0:T(8,128)(2,1)S(1)}, u32[]{:S(2)}, u32[]{:S(2)}) collective-permute-start(bf16[2,128,256]{2,1,0:T(8,128)(2,1)S(1)} %get-tuple-element.37), channel_id=1, source_target_pairs={{0,8},{1,9},{2,10},{3,11},{4,12},{5,13},{6,14},{7,15},{8,0},{9,1},... | collective-permute-start | bytes 393224 | tf_op jit(solution)/shard_map/ppermute | solution.py:33
  162.4 21.4 %collective-permute-start.23 = (bf16[2,128,256]{2,1,0:T(8,128)(2,1)S(1)}, bf16[2,128,256]{2,1,0:T(8,128)(2,1)S(1)}, u32[]{:S(2)}, u32[]{:S(2)}) collective-permute-start(bf16[2,128,256]{2,1,0:T(8,128)(2,1)S(1)} %get-tuple-element.38), channel_id=1, source_target_pairs={{0,4},{1,5},{2,6},{3,7},{4,0},{5,1},{6,2},{7,3},{8,12},{9,13},{10,... | collective-permute-start | bytes 393224 | tf_op jit(solution)/shard_map/ppermute | solution.py:33
  184.4 7.9 %collective-permute-start.24 = (bf16[128,256]{1,0:T(8,128)(2,1)S(1)}, bf16[128,256]{1,0:T(8,128)(2,1)S(1)}, u32[]{:S(2)}, u32[]{:S(2)}) collective-permute-start(bf16[128,256]{1,0:T(8,128)(2,1)S(1)} %get-tuple-element.39), channel_id=1, source_target_pairs={{0,0},{1,32},{2,2},{3,34},{4,4},{5,36},{6,6},{7,38},{8,8},{9,40},{... | collective-permute-start | bytes 196616 | tf_op jit(solution)/shard_map/ppermute | solution.py:33
  188.6 6.8 %collective-permute-start.25 = (bf16[128,256]{1,0:T(8,128)(2,1)S(1)}, bf16[128,256]{1,0:T(8,128)(2,1)S(1)}, u32[]{:S(2)}, u32[]{:S(2)}) collective-permute-start(bf16[128,256]{1,0:T(8,128)(2,1)S(1)} %get-tuple-element.40), channel_id=1, source_target_pairs={{0,16},{1,48},{2,18},{3,50},{4,20},{5,52},{6,22},{7,54},{8,24},{9,... | collective-permute-start | bytes 196616 | tf_op jit(solution)/shard_map/ppermute | solution.py:33
  (5 other events, 15.0 us)

commit v9 on v7

--- a/solution.py
+++ b/solution.py
@@ -136,7 +136,7 @@
         ],
         compiler_params=pltpu.CompilerParams(vmem_limit_bytes=40 * 2**20),
         cost_estimate=pl.CostEstimate(
-            flops=1000, bytes_accessed=1000, transcendentals=0
+            flops=20_000_000_000, bytes_accessed=2**20, transcendentals=0
         ),
     )(place, q, mine, other)
 
@@ -221,15 +221,16 @@
     older = [later(piece[:2], steps) for steps in range(2, W1 // rows + 1)]
     mine = pack((long_keys, long_values, short_keys, short_values), before, older)
     lines = [[z * CS + core for z in range(ZS)] for core in range(CS)]
+    mine, upward, downward = lax.optimization_barrier((mine, upward, downward))
     long_way, downward = moved(upward, along(second_up)), moved(downward, along(second_down))
+    over_z = lax.all_to_all(mine, "head", 0, 0, axis_index_groups=lines, tiled=True)
+    over_core = moved(over_z, lambda x, h, y, z, c: (x, h, y, z, 1 - c))
+
     near_by = half == z % 2
     pair = jnp.stack(
         [jnp.where(near_by, w_out, long_way), jnp.where(near_by, upward, downward)]
     )
-    mine, pair = lax.optimization_barrier((mine, pair))
-    over_z = lax.all_to_all(mine, "head", 0, 0, axis_index_groups=lines, tiled=True)
-    over_core = moved(over_z, lambda x, h, y, z, c: (x, h, y, z, 1 - c))
-
+    pair, over_core = lax.optimization_barrier((pair, over_core))
     from_x = [pair] + [
         moved(pair, lambda x, h, y, z, c, d=d: (x - d, h, y, z, c)) for d in (1, 2, 3)
     ]

time: 195 us -> 188 us (0.964)
  waiting for transfers between devices: 55.2 us -> 38.9 us
  starting transfers between devices: 116 us -> 126 us
    ppermute x18, waiting for transfers between devices: 54.5 us -> 28.4 us  [moved(): return lax.ppermute(value, BOTH, pairs)]
    ppermute x18, starting transfers between devices: 78 us -> 94.9 us  [moved(): return lax.ppermute(value, BOTH, pairs)]
    all_to_all x1, waiting for transfers between devices: 0.01 us -> 9.74 us  [per_device(): lax.all_to_all(mine, 'head', 0, 0, axis_index_groups=lines, tiled=True)]
    all_to_all x1, starting transfers between devices: 13.6 us -> 7.58 us  [per_device(): lax.all_to_all(mine, 'head', 0, 0, axis_index_groups=lines, tiled=True)]
  transfers between devices with their start and end apart: 23 -> 23, of which waited for: 11 -> 10; matrix products, arithmetic and copies ran while one was open for 1% -> 1% of each run, Pallas kernels for 8% -> 9%
where the time goes in v9:
time: 188 us; the launch traced here: 187 us
  starting transfers between devices  126 us (67%)
  waiting for transfers between devices  38.9 us (21%)
  Pallas kernels  18.2 us (10%)
  other arithmetic  1.89 us (1%)
    ppermute x18, starting transfers between devices, moved(): return lax.ppermute(value, BOTH, pairs)  94.9 us
    ppermute x18, waiting for transfers between devices, moved(): return lax.ppermute(value, BOTH, pairs)  28.4 us
    ppermute x4, starting transfers between devices, later(): lax.ppermute(value, 'seq', [(s, s + steps) for s in range(count - steps)])  23.7 us
    pallas_call x1, Pallas kernels, attention(): pl.pallas_call(functools.partial(attention_kernel, tokens=32), out_shape=...  14.9 us
    all_to_all x1, waiting for transfers between devices, per_device(): lax.all_to_all(mine, 'head', 0, 0, axis_index_groups=lines, tiled=True)  9.74 us
    all_to_all x1, starting transfers between devices, per_device(): lax.all_to_all(mine, 'head', 0, 0, axis_index_groups=lines, tiled=True)  7.58 us
  transfers between devices with their start and end apart: 23, of which 10 were waited for; matrix products, arithmetic and copies ran while one was open for 1% of the time, Pallas kernels for 9%

profile of v9, /device:TPU:1, one launch (start us, length us, event | category | flops | bytes accessed | tf_op | source)
XLA Modules:
  0.0 186.9 jit_solution(5793861908175781801)
XLA Ops:
  0.0 11.1 %collective-permute-start.4 = (bf16[512,256]{1,0:T(8,128)(2,1)}, bf16[512,256]{1,0:T(8,128)(2,1)S(1)}, u32[]{:S(2)}, u32[]{:S(2)}) collective-permute-start(bf16[512,256]{1,0:T(8,128)(2,1)} %param.11), channel_id=1, source_target_pairs={{0,10},{1,11},{2,0},{3,1},{4,14},{5,15},{6,4},{7,5},{8,64},{9,65},... | collective-permute-start | bytes 786440 | tf_op jit(solution)/shard_map/ppermute | solution.py:33
  12.6 13.9 %collective-permute-start.3 = (bf16[2,8,128]{2,1,0:T(8,128)(2,1)S(1)}, bf16[2,8,128]{2,1,0:T(8,128)(2,1)S(1)}, u32[]{:S(2)}, u32[]{:S(2)}) collective-permute-start(bf16[2,8,128]{2,1,0:T(8,128)(2,1)S(1)} %pad_maximum_fusion.4), channel_id=1, source_target_pairs={{0,64},{16,80},{32,96},{48,112},{64,128},{80,144},{96,160},{112,17... | collective-permute-start | bytes 12296 | tf_op jit(solution)/shard_map/ppermute | solution.py:38
  26.5 3.2 %collective-permute-start = (bf16[4,8,128]{2,1,0:T(8,128)(2,1)S(1)}, bf16[4,8,128]{2,1,0:T(8,128)(2,1)S(1)}, u32[]{:S(2)}, u32[]{:S(2)}) collective-permute-start(bf16[4,8,128]{2,1,0:T(8,128)(2,1)S(1)} %pad_maximum_fusion.3), channel_id=1, source_target_pairs={{0,16},{16,32},{32,48},{48,64},{64,80},{80,96},{96,112},{112,128},... | collective-permute-start | bytes 24584 | tf_op jit(solution)/shard_map/ppermute | solution.py:38
  29.7 3.4 %collective-permute-start.2 = (bf16[2,8,128]{2,1,0:T(8,128)(2,1)S(1)}, bf16[2,8,128]{2,1,0:T(8,128)(2,1)S(1)}, u32[]{:S(2)}, u32[]{:S(2)}) collective-permute-start(bf16[2,8,128]{2,1,0:T(8,128)(2,1)S(1)} %pad_maximum_fusion.4), channel_id=1, source_target_pairs={{0,48},{16,64},{32,80},{48,96},{64,112},{80,128},{96,144},{112,160... | collective-permute-start | bytes 12296 | tf_op jit(solution)/shard_map/ppermute | solution.py:38
  33.1 3.3 %collective-permute-start.1 = (bf16[2,8,128]{2,1,0:T(8,128)(2,1)S(1)}, bf16[2,8,128]{2,1,0:T(8,128)(2,1)S(1)}, u32[]{:S(2)}, u32[]{:S(2)}) collective-permute-start(bf16[2,8,128]{2,1,0:T(8,128)(2,1)S(1)} %pad_maximum_fusion.4), channel_id=1, source_target_pairs={{0,32},{16,48},{32,64},{48,80},{64,96},{80,112},{96,128},{112,144}... | collective-permute-start | bytes 12296 | tf_op jit(solution)/shard_map/ppermute | solution.py:38
  38.3 1.5 shard_map.64
  39.8 7.6 %all-to-all-start = ((bf16[8,14,8,128]{3,2,1,0:T(8,128)(2,1)}), bf16[8,14,8,128]{3,2,1,0:T(8,128)(2,1)S(1)}, u32[]{:S(2)}, u32[]{:S(2)}) async-start(bf16[8,14,8,128]{3,2,1,0:T(8,128)(2,1)} %shard_map.64), calls=%async_computation | async-start | bytes 458752 | tf_op jit(solution)/shard_map/all_to_all | solution.py:226
  48.9 9.7 %all-to-all-done.mine_ref = bf16[8,14,8,128]{3,2,1,0:T(8,128)(2,1)S(1)} async-done(((bf16[8,14,8,128]{3,2,1,0:T(8,128)(2,1)}), bf16[8,14,8,128]{3,2,1,0:T(8,128)(2,1)S(1)}, u32[]{:S(2)}, u32[]{:S(2)}) %all-to-all-start) | async-done | bytes 229408 | tf_op jit(solution)/shard_map/all_to_all | solution.py:226
  58.6 14.8 %collective-permute-start.8 = (bf16[8,14,8,128]{3,2,1,0:T(8,128)(2,1)S(1)}, bf16[8,14,8,128]{3,2,1,0:T(8,128)(2,1)S(1)}, u32[]{:S(2)}, u32[]{:S(2)}) collective-permute-start(bf16[8,14,8,128]{3,2,1,0:T(8,128)(2,1)S(1)} %all-to-all-done.mine_ref), channel_id=1, source_target_pairs={{0,1},{1,0},{2,3},{3,2},{4,5},{5,4},{6,7},{7,6},{8,9},{9,8},{10,11... | collective-permute-start | bytes 688136 | tf_op jit(solution)/shard_map/ppermute | solution.py:33
  73.6 1.0 collective-permute-done.8.other_ref
  74.6 11.5 %collective-permute-start.12 = (bf16[2,512,256]{2,1,0:T(8,128)(2,1)S(1)}, bf16[2,512,256]{2,1,0:T(8,128)(2,1)S(1)}, u32[]{:S(2)}, u32[]{:S(2)}) collective-permute-start(bf16[2,512,256]{2,1,0:T(8,128)(2,1)S(1)} %pad_maximum_fusion.refs_4_), channel_id=1, source_target_pairs={{0,128},{1,129},{2,130},{3,131},{4,132},{5,133},{6,134},{7,135},{8... | collective-permute-start | bytes 1572872 | tf_op jit(solution)/shard_map/ppermute | solution.py:33
  86.1 3.5 %collective-permute-start.11 = (bf16[2,512,256]{2,1,0:T(8,128)(2,1)S(1)}, bf16[2,512,256]{2,1,0:T(8,128)(2,1)S(1)}, u32[]{:S(2)}, u32[]{:S(2)}) collective-permute-start(bf16[2,512,256]{2,1,0:T(8,128)(2,1)S(1)} %pad_maximum_fusion.refs_4_), channel_id=1, source_target_pairs={{0,256},{1,257},{2,258},{3,259},{4,260},{5,261},{6,262},{7,263},{8... | collective-permute-start | bytes 1572872 | tf_op jit(solution)/shard_map/ppermute | solution.py:33
  89.6 4.0 %collective-permute-start.10 = (bf16[2,512,256]{2,1,0:T(8,128)(2,1)S(1)}, bf16[2,512,256]{2,1,0:T(8,128)(2,1)S(1)}, u32[]{:S(2)}, u32[]{:S(2)}) collective-permute-start(bf16[2,512,256]{2,1,0:T(8,128)(2,1)S(1)} %pad_maximum_fusion.refs_4_), channel_id=1, source_target_pairs={{0,384},{1,385},{2,386},{3,387},{4,388},{5,389},{6,390},{7,391},{8... | collective-permute-start | bytes 1572872 | tf_op jit(solution)/shard_map/ppermute | solution.py:33
  93.6 14.9 %shard_map.65 = bf16[128,512]{1,0:T(8,128)(2,1)S(1)} custom-call(s32[2]{0:T(128)S(1)} %pad_add_fusion.1.place, bf16[128,512]{1,0:T(8,128)(2,1)S(1)} %copy-done, bf16[8,14,8,128]{3,2,1,0:T(8,128)(2,1)S(1)} %all-to-all-done.mine_ref, bf16[8,14,8,128]{3,2,1,0:T(8,128)(2,1)S(1)} %collective-permute-done.8.other_ref), custom_call_target="tpu_custom_call" | custom-call | flops 20000000000 | bytes 1048576 | tf_op jit(solution)/shard_map/pallas_call | solution.py:123
  108.4 9.6 %collective-permute-start.9 = (bf16[128,512]{1,0:T(8,128)(2,1)S(1)}, bf16[128,512]{1,0:T(8,128)(2,1)S(1)}, u32[]{:S(2)}, u32[]{:S(2)}) collective-permute-start(bf16[128,512]{1,0:T(8,128)(2,1)S(1)} %shard_map.65), channel_id=1, source_target_pairs={{0,2},{1,3},{2,0},{3,1},{4,6},{5,7},{6,4},{7,5},{8,10},{9,11},{10,... | collective-permute-start | bytes 393224 | tf_op jit(solution)/shard_map/ppermute | solution.py:33
  118.1 2.3 %collective-permute-done.9 = bf16[128,512]{1,0:T(8,128)(2,1)S(1)} collective-permute-done((bf16[128,512]{1,0:T(8,128)(2,1)S(1)}, bf16[128,512]{1,0:T(8,128)(2,1)S(1)}, u32[]{:S(2)}, u32[]{:S(2)}) %collective-permute-start.9) | collective-permute-done | bytes 131104 | tf_op jit(solution)/shard_map/ppermute | solution.py:33
  120.5 2.0 %collective-permute-start.15 = (bf16[2,128,512]{2,1,0:T(8,128)(2,1)S(1)}, bf16[2,128,512]{2,1,0:T(8,128)(2,1)S(1)}, u32[]{:S(2)}, u32[]{:S(2)}) collective-permute-start(bf16[2,128,512]{2,1,0:T(8,128)(2,1)S(1)} %pad_maximum_fusion.1.refs_0_), channel_id=1, source_target_pairs={{0,16},{1,17},{2,18},{3,19},{4,20},{5,21},{6,22},{7,23},{8,24},{9,... | collective-permute-start | bytes 786440 | tf_op jit(solution)/shard_map/ppermute | solution.py:33
  122.5 1.9 %collective-permute-start.14 = (bf16[2,128,512]{2,1,0:T(8,128)(2,1)S(1)}, bf16[2,128,512]{2,1,0:T(8,128)(2,1)S(1)}, u32[]{:S(2)}, u32[]{:S(2)}) collective-permute-start(bf16[2,128,512]{2,1,0:T(8,128)(2,1)S(1)} %pad_maximum_fusion.1.refs_0_), channel_id=1, source_target_pairs={{0,32},{1,33},{2,34},{3,35},{4,36},{5,37},{6,38},{7,39},{8,40},{9,... | collective-permute-start | bytes 786440 | tf_op jit(solution)/shard_map/ppermute | solution.py:33
  124.4 4.5 %collective-permute-start.13 = (bf16[2,128,512]{2,1,0:T(8,128)(2,1)S(1)}, bf16[2,128,512]{2,1,0:T(8,128)(2,1)S(1)}, u32[]{:S(2)}, u32[]{:S(2)}) collective-permute-start(bf16[2,128,512]{2,1,0:T(8,128)(2,1)S(1)} %pad_maximum_fusion.1.refs_0_), channel_id=1, source_target_pairs={{0,48},{1,49},{2,50},{3,51},{4,52},{5,53},{6,54},{7,55},{8,56},{9,... | collective-permute-start | bytes 786440 | tf_op jit(solution)/shard_map/ppermute | solution.py:33
  129.0 3.2 %collective-permute-done.15.refs_3_ = bf16[2,128,512]{2,1,0:T(8,128)(2,1)S(1)} collective-permute-done((bf16[2,128,512]{2,1,0:T(8,128)(2,1)S(1)}, bf16[2,128,512]{2,1,0:T(8,128)(2,1)S(1)}, u32[]{:S(2)}, u32[]{:S(2)}) %collective-permute-start.15) | collective-permute-done | bytes 262176 | tf_op jit(solution)/shard_map/ppermute | solution.py:33
  132.2 4.3 %collective-permute-done.13.refs_1_ = bf16[2,128,512]{2,1,0:T(8,128)(2,1)S(1)} collective-permute-done((bf16[2,128,512]{2,1,0:T(8,128)(2,1)S(1)}, bf16[2,128,512]{2,1,0:T(8,128)(2,1)S(1)}, u32[]{:S(2)}, u32[]{:S(2)}) %collective-permute-start.13) | collective-permute-done | bytes 262176 | tf_op jit(solution)/shard_map/ppermute | solution.py:33
  136.5 1.8 shard_map.66
  138.4 5.8 %collective-permute-start.16 = (bf16[4,2,128,256]{3,2,1,0:T(8,128)(2,1)S(1)}, bf16[4,2,128,256]{3,2,1,0:T(8,128)(2,1)S(1)}, u32[]{:S(2)}, u32[]{:S(2)}) collective-permute-start(bf16[4,2,128,256]{3,2,1,0:T(8,128)(2,1)S(1)} %slice_bitcast_fusion), channel_id=1, source_target_pairs={{0,1},{1,0},{2,3},{3,2},{4,5},{5,4},{6,7},{7,6},{8,9},{9,8},{10,11... | collective-permute-start | bytes 1572872 | tf_op jit(solution)/shard_map/ppermute | solution.py:33
  144.2 1.5 collective-permute-done.16
  145.9 1.9 %collective-permute-start.17 = (bf16[2,128,256]{2,1,0:T(8,128)(2,1)S(1)}, bf16[2,128,256]{2,1,0:T(8,128)(2,1)S(1)}, u32[]{:S(2)}, u32[]{:S(2)}) collective-permute-start(bf16[2,128,256]{2,1,0:T(8,128)(2,1)S(1)} %get-tuple-element.25), channel_id=1, source_target_pairs={{0,12},{1,13},{2,14},{3,15},{4,8},{5,9},{6,10},{7,11},{8,4},{9,5},... | collective-permute-start | bytes 393224 | tf_op jit(solution)/shard_map/ppermute | solution.py:33
  147.8 2.7 %collective-permute-start.19 = (bf16[2,128,256]{2,1,0:T(8,128)(2,1)S(1)}, bf16[2,128,256]{2,1,0:T(8,128)(2,1)S(1)}, u32[]{:S(2)}, u32[]{:S(2)}) collective-permute-start(bf16[2,128,256]{2,1,0:T(8,128)(2,1)S(1)} %get-tuple-element.26), channel_id=1, source_target_pairs={{0,4},{1,5},{2,6},{3,7},{4,0},{5,1},{6,2},{7,3},{8,12},{9,13},{10,... | collective-permute-start | bytes 393224 | tf_op jit(solution)/shard_map/ppermute | solution.py:33
  150.5 8.6 %collective-permute-start.18 = (bf16[2,128,256]{2,1,0:T(8,128)(2,1)S(1)}, bf16[2,128,256]{2,1,0:T(8,128)(2,1)S(1)}, u32[]{:S(2)}, u32[]{:S(2)}) collective-permute-start(bf16[2,128,256]{2,1,0:T(8,128)(2,1)S(1)} %get-tuple-element.27), channel_id=1, source_target_pairs={{0,8},{1,9},{2,10},{3,11},{4,12},{5,13},{6,14},{7,15},{8,0},{9,1},... | collective-permute-start | bytes 393224 | tf_op jit(solution)/shard_map/ppermute | solution.py:33
  159.1 7.6 %collective-permute-done.17 = bf16[2,128,256]{2,1,0:T(8,128)(2,1)S(1)} collective-permute-done((bf16[2,128,256]{2,1,0:T(8,128)(2,1)S(1)}, bf16[2,128,256]{2,1,0:T(8,128)(2,1)S(1)}, u32[]{:S(2)}, u32[]{:S(2)}) %collective-permute-start.17) | collective-permute-done | bytes 131104 | tf_op jit(solution)/shard_map/ppermute | solution.py:33
  166.6 3.4 %collective-permute-done.18 = bf16[2,128,256]{2,1,0:T(8,128)(2,1)S(1)} collective-permute-done((bf16[2,128,256]{2,1,0:T(8,128)(2,1)S(1)}, bf16[2,128,256]{2,1,0:T(8,128)(2,1)S(1)}, u32[]{:S(2)}, u32[]{:S(2)}) %collective-permute-start.18) | collective-permute-done | bytes 131104 | tf_op jit(solution)/shard_map/ppermute | solution.py:33
  170.1 9.1 %collective-permute-start.20 = (bf16[128,256]{1,0:T(8,128)(2,1)S(1)}, bf16[128,256]{1,0:T(8,128)(2,1)S(1)}, u32[]{:S(2)}, u32[]{:S(2)}) collective-permute-start(bf16[128,256]{1,0:T(8,128)(2,1)S(1)} %get-tuple-element.30), channel_id=1, source_target_pairs={{0,16},{1,48},{2,18},{3,50},{4,20},{5,52},{6,22},{7,54},{8,24},{9,... | collective-permute-start | bytes 196616 | tf_op jit(solution)/shard_map/ppermute | solution.py:33
  179.2 1.9 %collective-permute-start.21 = (bf16[128,256]{1,0:T(8,128)(2,1)S(1)}, bf16[128,256]{1,0:T(8,128)(2,1)S(1)}, u32[]{:S(2)}, u32[]{:S(2)}) collective-permute-start(bf16[128,256]{1,0:T(8,128)(2,1)S(1)} %get-tuple-element.31), channel_id=1, source_target_pairs={{0,0},{1,32},{2,2},{3,34},{4,4},{5,36},{6,6},{7,38},{8,8},{9,40},{... | collective-permute-start | bytes 196616 | tf_op jit(solution)/shard_map/ppermute | solution.py:33
  181.1 5.2 %collective-permute-done.21 = bf16[128,256]{1,0:T(8,128)(2,1)S(1)} collective-permute-done((bf16[128,256]{1,0:T(8,128)(2,1)S(1)}, bf16[128,256]{1,0:T(8,128)(2,1)S(1)}, u32[]{:S(2)}, u32[]{:S(2)}) %collective-permute-start.21) | collective-permute-done | bytes 65568 | tf_op jit(solution)/shard_map/ppermute | solution.py:33
  (52 shorter events, 5.9 us)
Async XLA Ops:
  0.0 11.8 %copy-start.2 = (bf16[8,128]{1,0:T(8,128)(2,1)S(1)}, bf16[8,128]{1,0:T(8,128)(2,1)}, u32[]{:S(2)}) copy-start(bf16[8,128]{1,0:T(8,128)(2,1)} %refs_0_.1) | copy-start | bytes 6148
  0.0 39.8 %collective-permute-start.4 = (bf16[512,256]{1,0:T(8,128)(2,1)}, bf16[512,256]{1,0:T(8,128)(2,1)S(1)}, u32[]{:S(2)}, u32[]{:S(2)}) collective-permute-start(bf16[512,256]{1,0:T(8,128)(2,1)} %param.11), channel_id=1, source_target_pairs={{0,10},{1,11},{2,0},{3,1},{4,14},{5,15},{6,4},{7,5},{8,64},{9,65},... | collective-permute-start | bytes 786440 | tf_op jit(solution)/shard_map/ppermute | solution.py:33
  11.1 28.7 %collective-permute-start.5 = (bf16[512,256]{1,0:T(8,128)(2,1)}, bf16[512,256]{1,0:T(8,128)(2,1)S(1)}, u32[]{:S(2)}, u32[]{:S(2)}) collective-permute-start(bf16[512,256]{1,0:T(8,128)(2,1)} %param.11), channel_id=1, source_target_pairs={{2,74},{3,75},{6,78},{7,79},{10,2},{11,3},{14,6},{15,7},{18,90},{1... | collective-permute-start | bytes 786440 | tf_op jit(solution)/shard_map/ppermute | solution.py:33
  11.8 14.6 %copy-start.4 = (bf16[8,128]{1,0:T(8,128)(2,1)S(1)}, bf16[8,128]{1,0:T(8,128)(2,1)}, u32[]{:S(2)}) copy-start(bf16[8,128]{1,0:T(8,128)(2,1)} %refs_2_.1) | copy-start | bytes 6148
  11.8 14.6 %copy-start.5 = (bf16[8,128]{1,0:T(8,128)(2,1)S(1)}, bf16[8,128]{1,0:T(8,128)(2,1)}, u32[]{:S(2)}) copy-start(bf16[8,128]{1,0:T(8,128)(2,1)} %refs_3_.1) | copy-start | bytes 6148
  12.5 13.9 %copy-start.3 = (bf16[8,128]{1,0:T(8,128)(2,1)S(1)}, bf16[8,128]{1,0:T(8,128)(2,1)}, u32[]{:S(2)}) copy-start(bf16[8,128]{1,0:T(8,128)(2,1)} %refs_1_.1) | copy-start | bytes 6148
  12.6 20.5 %collective-permute-start.3 = (bf16[2,8,128]{2,1,0:T(8,128)(2,1)S(1)}, bf16[2,8,128]{2,1,0:T(8,128)(2,1)S(1)}, u32[]{:S(2)}, u32[]{:S(2)}) collective-permute-start(bf16[2,8,128]{2,1,0:T(8,128)(2,1)S(1)} %pad_maximum_fusion.4), channel_id=1, source_target_pairs={{0,64},{16,80},{32,96},{48,112},{64,128},{80,144},{96,160},{112,17... | collective-permute-start | bytes 12296 | tf_op jit(solution)/shard_map/ppermute | solution.py:38
  26.5 10.6 %collective-permute-start = (bf16[4,8,128]{2,1,0:T(8,128)(2,1)S(1)}, bf16[4,8,128]{2,1,0:T(8,128)(2,1)S(1)}, u32[]{:S(2)}, u32[]{:S(2)}) collective-permute-start(bf16[4,8,128]{2,1,0:T(8,128)(2,1)S(1)} %pad_maximum_fusion.3), channel_id=1, source_target_pairs={{0,16},{16,32},{32,48},{48,64},{64,80},{80,96},{96,112},{112,128},... | collective-permute-start | bytes 24584 | tf_op jit(solution)/shard_map/ppermute | solution.py:38
  29.7 6.7 %collective-permute-start.2 = (bf16[2,8,128]{2,1,0:T(8,128)(2,1)S(1)}, bf16[2,8,128]{2,1,0:T(8,128)(2,1)S(1)}, u32[]{:S(2)}, u32[]{:S(2)}) collective-permute-start(bf16[2,8,128]{2,1,0:T(8,128)(2,1)S(1)} %pad_maximum_fusion.4), channel_id=1, source_target_pairs={{0,48},{16,64},{32,80},{48,96},{64,112},{80,128},{96,144},{112,160... | collective-permute-start | bytes 12296 | tf_op jit(solution)/shard_map/ppermute | solution.py:38
  33.1 4.0 %copy-start.7 = (bf16[2,8,128]{2,1,0:T(8,128)(2,1)}, bf16[2,8,128]{2,1,0:T(8,128)(2,1)S(1)}, u32[]{:S(2)}) copy-start(bf16[2,8,128]{2,1,0:T(8,128)(2,1)S(1)} %collective-permute-done.3.refs_7_) | copy-start | bytes 12292
  33.1 4.0 %collective-permute-start.1 = (bf16[2,8,128]{2,1,0:T(8,128)(2,1)S(1)}, bf16[2,8,128]{2,1,0:T(8,128)(2,1)S(1)}, u32[]{:S(2)}, u32[]{:S(2)}) collective-permute-start(bf16[2,8,128]{2,1,0:T(8,128)(2,1)S(1)} %pad_maximum_fusion.4), channel_id=1, source_target_pairs={{0,32},{16,48},{32,64},{48,80},{64,96},{80,112},{96,128},{112,144}... | collective-permute-start | bytes 12296 | tf_op jit(solution)/shard_map/ppermute | solution.py:38
  36.4 0.7 copy-start.8
  37.7 0.6 copy-start.6
  39.8 18.8 %all-to-all-start = ((bf16[8,14,8,128]{3,2,1,0:T(8,128)(2,1)}), bf16[8,14,8,128]{3,2,1,0:T(8,128)(2,1)S(1)}, u32[]{:S(2)}, u32[]{:S(2)}) async-start(bf16[8,14,8,128]{3,2,1,0:T(8,128)(2,1)} %shard_map.64), calls=%async_computation | async-start | bytes 458752 | tf_op jit(solution)/shard_map/all_to_all | solution.py:226
  47.4 1.5 collective-permute-start.7
  48.1 25.4 %collective-permute-start.6 = (bf16[512,256]{1,0:T(8,128)(2,1)S(1)}, bf16[512,256]{1,0:T(8,128)(2,1)S(1)}, u32[]{:S(2)}, u32[]{:S(2)}) collective-permute-start(bf16[512,256]{1,0:T(8,128)(2,1)S(1)} %collective-permute-done.4), channel_id=1, source_target_pairs={{2,10},{3,11},{6,14},{7,15},{10,64},{11,65},{14,68},{15,69},{18,26... | collective-permute-start | bytes 786440 | tf_op jit(solution)/shard_map/ppermute | solution.py:33
  48.8 24.6 %copy-start.1 = (bf16[512,256]{1,0:T(8,128)(2,1)S(1)}, bf16[512,256]{1,0:T(8,128)(2,1)}, u32[]{:S(2)}) copy-start(bf16[512,256]{1,0:T(8,128)(2,1)} %param.11) | copy-start | bytes 786436
  58.6 15.9 %collective-permute-start.8 = (bf16[8,14,8,128]{3,2,1,0:T(8,128)(2,1)S(1)}, bf16[8,14,8,128]{3,2,1,0:T(8,128)(2,1)S(1)}, u32[]{:S(2)}, u32[]{:S(2)}) collective-permute-start(bf16[8,14,8,128]{3,2,1,0:T(8,128)(2,1)S(1)} %all-to-all-done.mine_ref), channel_id=1, source_target_pairs={{0,1},{1,0},{2,3},{3,2},{4,5},{5,4},{6,7},{7,6},{8,9},{9,8},{10,11... | collective-permute-start | bytes 688136 | tf_op jit(solution)/shard_map/ppermute | solution.py:33
  73.5 20.0 %copy-start = (bf16[128,512]{1,0:T(8,128)(2,1)S(1)}, bf16[128,512]{1,0:T(8,128)(2,1)}, u32[]{:S(2)}) copy-start(bf16[128,512]{1,0:T(8,128)(2,1)} %q_ref.1) | copy-start | bytes 393220
  74.6 45.9 %collective-permute-start.12 = (bf16[2,512,256]{2,1,0:T(8,128)(2,1)S(1)}, bf16[2,512,256]{2,1,0:T(8,128)(2,1)S(1)}, u32[]{:S(2)}, u32[]{:S(2)}) collective-permute-start(bf16[2,512,256]{2,1,0:T(8,128)(2,1)S(1)} %pad_maximum_fusion.refs_4_), channel_id=1, source_target_pairs={{0,128},{1,129},{2,130},{3,131},{4,132},{5,133},{6,134},{7,135},{8... | collective-permute-start | bytes 1572872 | tf_op jit(solution)/shard_map/ppermute | solution.py:33
  86.1 34.3 %collective-permute-start.11 = (bf16[2,512,256]{2,1,0:T(8,128)(2,1)S(1)}, bf16[2,512,256]{2,1,0:T(8,128)(2,1)S(1)}, u32[]{:S(2)}, u32[]{:S(2)}) collective-permute-start(bf16[2,512,256]{2,1,0:T(8,128)(2,1)S(1)} %pad_maximum_fusion.refs_4_), channel_id=1, source_target_pairs={{0,256},{1,257},{2,258},{3,259},{4,260},{5,261},{6,262},{7,263},{8... | collective-permute-start | bytes 1572872 | tf_op jit(solution)/shard_map/ppermute | solution.py:33
  89.6 30.9 %collective-permute-start.10 = (bf16[2,512,256]{2,1,0:T(8,128)(2,1)S(1)}, bf16[2,512,256]{2,1,0:T(8,128)(2,1)S(1)}, u32[]{:S(2)}, u32[]{:S(2)}) collective-permute-start(bf16[2,512,256]{2,1,0:T(8,128)(2,1)S(1)} %pad_maximum_fusion.refs_4_), channel_id=1, source_target_pairs={{0,384},{1,385},{2,386},{3,387},{4,388},{5,389},{6,390},{7,391},{8... | collective-permute-start | bytes 1572872 | tf_op jit(solution)/shard_map/ppermute | solution.py:33
  108.4 12.0 %collective-permute-start.9 = (bf16[128,512]{1,0:T(8,128)(2,1)S(1)}, bf16[128,512]{1,0:T(8,128)(2,1)S(1)}, u32[]{:S(2)}, u32[]{:S(2)}) collective-permute-start(bf16[128,512]{1,0:T(8,128)(2,1)S(1)} %shard_map.65), channel_id=1, source_target_pairs={{0,2},{1,3},{2,0},{3,1},{4,6},{5,7},{6,4},{7,5},{8,10},{9,11},{10,... | collective-permute-start | bytes 393224 | tf_op jit(solution)/shard_map/ppermute | solution.py:33
  120.5 11.8 %collective-permute-start.15 = (bf16[2,128,512]{2,1,0:T(8,128)(2,1)S(1)}, bf16[2,128,512]{2,1,0:T(8,128)(2,1)S(1)}, u32[]{:S(2)}, u32[]{:S(2)}) collective-permute-start(bf16[2,128,512]{2,1,0:T(8,128)(2,1)S(1)} %pad_maximum_fusion.1.refs_0_), channel_id=1, source_target_pairs={{0,16},{1,17},{2,18},{3,19},{4,20},{5,21},{6,22},{7,23},{8,24},{9,... | collective-permute-start | bytes 786440 | tf_op jit(solution)/shard_map/ppermute | solution.py:33
  122.5 9.7 %collective-permute-start.14 = (bf16[2,128,512]{2,1,0:T(8,128)(2,1)S(1)}, bf16[2,128,512]{2,1,0:T(8,128)(2,1)S(1)}, u32[]{:S(2)}, u32[]{:S(2)}) collective-permute-start(bf16[2,128,512]{2,1,0:T(8,128)(2,1)S(1)} %pad_maximum_fusion.1.refs_0_), channel_id=1, source_target_pairs={{0,32},{1,33},{2,34},{3,35},{4,36},{5,37},{6,38},{7,39},{8,40},{9,... | collective-permute-start | bytes 786440 | tf_op jit(solution)/shard_map/ppermute | solution.py:33
  124.4 12.1 %collective-permute-start.13 = (bf16[2,128,512]{2,1,0:T(8,128)(2,1)S(1)}, bf16[2,128,512]{2,1,0:T(8,128)(2,1)S(1)}, u32[]{:S(2)}, u32[]{:S(2)}) collective-permute-start(bf16[2,128,512]{2,1,0:T(8,128)(2,1)S(1)} %pad_maximum_fusion.1.refs_0_), channel_id=1, source_target_pairs={{0,48},{1,49},{2,50},{3,51},{4,52},{5,53},{6,54},{7,55},{8,56},{9,... | collective-permute-start | bytes 786440 | tf_op jit(solution)/shard_map/ppermute | solution.py:33
  138.4 7.3 %collective-permute-start.16 = (bf16[4,2,128,256]{3,2,1,0:T(8,128)(2,1)S(1)}, bf16[4,2,128,256]{3,2,1,0:T(8,128)(2,1)S(1)}, u32[]{:S(2)}, u32[]{:S(2)}) collective-permute-start(bf16[4,2,128,256]{3,2,1,0:T(8,128)(2,1)S(1)} %slice_bitcast_fusion), channel_id=1, source_target_pairs={{0,1},{1,0},{2,3},{3,2},{4,5},{5,4},{6,7},{7,6},{8,9},{9,8},{10,11... | collective-permute-start | bytes 1572872 | tf_op jit(solution)/shard_map/ppermute | solution.py:33
  145.9 20.8 %collective-permute-start.17 = (bf16[2,128,256]{2,1,0:T(8,128)(2,1)S(1)}, bf16[2,128,256]{2,1,0:T(8,128)(2,1)S(1)}, u32[]{:S(2)}, u32[]{:S(2)}) collective-permute-start(bf16[2,128,256]{2,1,0:T(8,128)(2,1)S(1)} %get-tuple-element.25), channel_id=1, source_target_pairs={{0,12},{1,13},{2,14},{3,15},{4,8},{5,9},{6,10},{7,11},{8,4},{9,5},... | collective-permute-start | bytes 393224 | tf_op jit(solution)/shard_map/ppermute | solution.py:33
  147.8 18.9 %collective-permute-start.19 = (bf16[2,128,256]{2,1,0:T(8,128)(2,1)S(1)}, bf16[2,128,256]{2,1,0:T(8,128)(2,1)S(1)}, u32[]{:S(2)}, u32[]{:S(2)}) collective-permute-start(bf16[2,128,256]{2,1,0:T(8,128)(2,1)S(1)} %get-tuple-element.26), channel_id=1, source_target_pairs={{0,4},{1,5},{2,6},{3,7},{4,0},{5,1},{6,2},{7,3},{8,12},{9,13},{10,... | collective-permute-start | bytes 393224 | tf_op jit(solution)/shard_map/ppermute | solution.py:33
  150.5 19.5 %collective-permute-start.18 = (bf16[2,128,256]{2,1,0:T(8,128)(2,1)S(1)}, bf16[2,128,256]{2,1,0:T(8,128)(2,1)S(1)}, u32[]{:S(2)}, u32[]{:S(2)}) collective-permute-start(bf16[2,128,256]{2,1,0:T(8,128)(2,1)S(1)} %get-tuple-element.27), channel_id=1, source_target_pairs={{0,8},{1,9},{2,10},{3,11},{4,12},{5,13},{6,14},{7,15},{8,0},{9,1},... | collective-permute-start | bytes 393224 | tf_op jit(solution)/shard_map/ppermute | solution.py:33
  170.1 11.0 %collective-permute-start.20 = (bf16[128,256]{1,0:T(8,128)(2,1)S(1)}, bf16[128,256]{1,0:T(8,128)(2,1)S(1)}, u32[]{:S(2)}, u32[]{:S(2)}) collective-permute-start(bf16[128,256]{1,0:T(8,128)(2,1)S(1)} %get-tuple-element.30), channel_id=1, source_target_pairs={{0,16},{1,48},{2,18},{3,50},{4,20},{5,52},{6,22},{7,54},{8,24},{9,... | collective-permute-start | bytes 196616 | tf_op jit(solution)/shard_map/ppermute | solution.py:33
  179.2 7.1 %collective-permute-start.21 = (bf16[128,256]{1,0:T(8,128)(2,1)S(1)}, bf16[128,256]{1,0:T(8,128)(2,1)S(1)}, u32[]{:S(2)}, u32[]{:S(2)}) collective-permute-start(bf16[128,256]{1,0:T(8,128)(2,1)S(1)} %get-tuple-element.31), channel_id=1, source_target_pairs={{0,0},{1,32},{2,2},{3,34},{4,4},{5,36},{6,6},{7,38},{8,8},{9,40},{... | collective-permute-start | bytes 196616 | tf_op jit(solution)/shard_map/ppermute | solution.py:33
  (1 other events, 0.6 us)

commit v10 on v9

--- a/solution.py
+++ b/solution.py
@@ -232,17 +232,20 @@
     )
     pair, over_core = lax.optimization_barrier((pair, over_core))
     from_x = [pair] + [
-        moved(pair, lambda x, h, y, z, c, d=d: (x - d, h, y, z, c)) for d in (1, 2, 3)
+        moved(pair, lambda x, h, y, z, c, d=d: (x - d, h, y, z, c)) for d in (1, 2)
     ]
 
     attended = attention(jnp.stack([seq, c]), queries, over_z, over_core)
+    attended, last = lax.optimization_barrier((attended, pair))
+    last = moved(last, lambda x, h, y, z, c: (x - 3, h, y, z, c))
+
     beside = moved(attended, lambda x, h, y, z, c: (x, h, y, z ^ 1, c))
     beside, from_x = lax.optimization_barrier((beside, from_x))
     attended = jnp.stack([attended, beside])
     from_y = [attended] + [
         moved(attended, lambda x, h, y, z, c, d=d: (x, h, y - d, z, c)) for d in (1, 2, 3)
     ]
-    sums = project(jnp.stack([x, y, z // 2, c]), from_y, from_x)
+    sums = project(jnp.stack([x, y, z // 2, c]), from_y, from_x + [last])
     came = moved(sums[1], lambda x, h, y, z, c: (x, h, y, z, 1 - c))
     kept = (sums[0].astype(jnp.float32) + came.astype(jnp.float32)).astype(jnp.bfloat16)
     parts = [kept[0]] + [

time: 188 us -> 187 us (level)
  no operation moved by 1% of the time
where the time goes in v10:
time: 187 us
  starting transfers between devices  125 us (67%)
  waiting for transfers between devices  39.4 us (21%)
  Pallas kernels  18.2 us (10%)
  other arithmetic  1.9 us (1%)
    ppermute x18, starting transfers between devices, moved(): return lax.ppermute(value, BOTH, pairs)  94 us
    ppermute x18, waiting for transfers between devices, moved(): return lax.ppermute(value, BOTH, pairs)  29 us
    ppermute x4, starting transfers between devices, later(): lax.ppermute(value, 'seq', [(s, s + steps) for s in range(count - steps)])  23.7 us
    pallas_call x1, Pallas kernels, attention(): pl.pallas_call(functools.partial(attention_kernel, tokens=32), out_shape=...  14.9 us
    all_to_all x1, waiting for transfers between devices, per_device(): lax.all_to_all(mine, 'head', 0, 0, axis_index_groups=lines, tiled=True)  9.74 us
    all_to_all x1, starting transfers between devices, per_device(): lax.all_to_all(mine, 'head', 0, 0, axis_index_groups=lines, tiled=True)  7.58 us
  transfers between devices with their start and end apart: 23, of which 10 were waited for; matrix products, arithmetic and copies ran while one was open for 1% of the time, Pallas kernels for 9%

profile of v10, /device:TPU:1, one launch (start us, length us, event | category | flops | bytes accessed | tf_op | source)
XLA Modules:
  0.0 186.6 jit_solution(8246959284583941844)
XLA Ops:
  0.0 11.1 %collective-permute-start.4 = (bf16[512,256]{1,0:T(8,128)(2,1)}, bf16[512,256]{1,0:T(8,128)(2,1)S(1)}, u32[]{:S(2)}, u32[]{:S(2)}) collective-permute-start(bf16[512,256]{1,0:T(8,128)(2,1)} %param.11), channel_id=1, source_target_pairs={{0,10},{1,11},{2,0},{3,1},{4,14},{5,15},{6,4},{7,5},{8,64},{9,65},... | collective-permute-start | bytes 786440 | tf_op jit(solution)/shard_map/ppermute | solution.py:33
  12.6 13.9 %collective-permute-start.3 = (bf16[2,8,128]{2,1,0:T(8,128)(2,1)S(1)}, bf16[2,8,128]{2,1,0:T(8,128)(2,1)S(1)}, u32[]{:S(2)}, u32[]{:S(2)}) collective-permute-start(bf16[2,8,128]{2,1,0:T(8,128)(2,1)S(1)} %pad_maximum_fusion.4), channel_id=1, source_target_pairs={{0,64},{16,80},{32,96},{48,112},{64,128},{80,144},{96,160},{112,17... | collective-permute-start | bytes 12296 | tf_op jit(solution)/shard_map/ppermute | solution.py:38
  26.5 3.2 %collective-permute-start = (bf16[4,8,128]{2,1,0:T(8,128)(2,1)S(1)}, bf16[4,8,128]{2,1,0:T(8,128)(2,1)S(1)}, u32[]{:S(2)}, u32[]{:S(2)}) collective-permute-start(bf16[4,8,128]{2,1,0:T(8,128)(2,1)S(1)} %pad_maximum_fusion.3), channel_id=1, source_target_pairs={{0,16},{16,32},{32,48},{48,64},{64,80},{80,96},{96,112},{112,128},... | collective-permute-start | bytes 24584 | tf_op jit(solution)/shard_map/ppermute | solution.py:38
  29.7 3.4 %collective-permute-start.2 = (bf16[2,8,128]{2,1,0:T(8,128)(2,1)S(1)}, bf16[2,8,128]{2,1,0:T(8,128)(2,1)S(1)}, u32[]{:S(2)}, u32[]{:S(2)}) collective-permute-start(bf16[2,8,128]{2,1,0:T(8,128)(2,1)S(1)} %pad_maximum_fusion.4), channel_id=1, source_target_pairs={{0,48},{16,64},{32,80},{48,96},{64,112},{80,128},{96,144},{112,160... | collective-permute-start | bytes 12296 | tf_op jit(solution)/shard_map/ppermute | solution.py:38
  33.1 3.3 %collective-permute-start.1 = (bf16[2,8,128]{2,1,0:T(8,128)(2,1)S(1)}, bf16[2,8,128]{2,1,0:T(8,128)(2,1)S(1)}, u32[]{:S(2)}, u32[]{:S(2)}) collective-permute-start(bf16[2,8,128]{2,1,0:T(8,128)(2,1)S(1)} %pad_maximum_fusion.4), channel_id=1, source_target_pairs={{0,32},{16,48},{32,64},{48,80},{64,96},{80,112},{96,128},{112,144}... | collective-permute-start | bytes 12296 | tf_op jit(solution)/shard_map/ppermute | solution.py:38
  38.3 1.5 shard_map.64
  39.8 7.6 %all-to-all-start = ((bf16[8,14,8,128]{3,2,1,0:T(8,128)(2,1)}), bf16[8,14,8,128]{3,2,1,0:T(8,128)(2,1)S(1)}, u32[]{:S(2)}, u32[]{:S(2)}) async-start(bf16[8,14,8,128]{3,2,1,0:T(8,128)(2,1)} %shard_map.64), calls=%async_computation | async-start | bytes 458752 | tf_op jit(solution)/shard_map/all_to_all | solution.py:226
  48.9 9.7 %all-to-all-done.mine_ref = bf16[8,14,8,128]{3,2,1,0:T(8,128)(2,1)S(1)} async-done(((bf16[8,14,8,128]{3,2,1,0:T(8,128)(2,1)}), bf16[8,14,8,128]{3,2,1,0:T(8,128)(2,1)S(1)}, u32[]{:S(2)}, u32[]{:S(2)}) %all-to-all-start) | async-done | bytes 229408 | tf_op jit(solution)/shard_map/all_to_all | solution.py:226
  58.6 14.8 %collective-permute-start.8 = (bf16[8,14,8,128]{3,2,1,0:T(8,128)(2,1)S(1)}, bf16[8,14,8,128]{3,2,1,0:T(8,128)(2,1)S(1)}, u32[]{:S(2)}, u32[]{:S(2)}) collective-permute-start(bf16[8,14,8,128]{3,2,1,0:T(8,128)(2,1)S(1)} %all-to-all-done.mine_ref), channel_id=1, source_target_pairs={{0,1},{1,0},{2,3},{3,2},{4,5},{5,4},{6,7},{7,6},{8,9},{9,8},{10,11... | collective-permute-start | bytes 688136 | tf_op jit(solution)/shard_map/ppermute | solution.py:33
  73.6 1.0 collective-permute-done.8.other_ref
  74.6 13.1 %collective-permute-start.11 = (bf16[2,512,256]{2,1,0:T(8,128)(2,1)S(1)}, bf16[2,512,256]{2,1,0:T(8,128)(2,1)S(1)}, u32[]{:S(2)}, u32[]{:S(2)}) collective-permute-start(bf16[2,512,256]{2,1,0:T(8,128)(2,1)S(1)} %pad_maximum_fusion.refs_4_), channel_id=1, source_target_pairs={{0,256},{1,257},{2,258},{3,259},{4,260},{5,261},{6,262},{7,263},{8... | collective-permute-start | bytes 1572872 | tf_op jit(solution)/shard_map/ppermute | solution.py:33
  87.6 2.8 %collective-permute-start.10 = (bf16[2,512,256]{2,1,0:T(8,128)(2,1)S(1)}, bf16[2,512,256]{2,1,0:T(8,128)(2,1)S(1)}, u32[]{:S(2)}, u32[]{:S(2)}) collective-permute-start(bf16[2,512,256]{2,1,0:T(8,128)(2,1)S(1)} %pad_maximum_fusion.refs_4_), channel_id=1, source_target_pairs={{0,384},{1,385},{2,386},{3,387},{4,388},{5,389},{6,390},{7,391},{8... | collective-permute-start | bytes 1572872 | tf_op jit(solution)/shard_map/ppermute | solution.py:33
  90.4 14.9 %shard_map.65 = bf16[128,512]{1,0:T(8,128)(2,1)S(1)} custom-call(s32[2]{0:T(128)S(1)} %pad_add_fusion.1.place, bf16[128,512]{1,0:T(8,128)(2,1)S(1)} %copy-done, bf16[8,14,8,128]{3,2,1,0:T(8,128)(2,1)S(1)} %all-to-all-done.mine_ref, bf16[8,14,8,128]{3,2,1,0:T(8,128)(2,1)S(1)} %collective-permute-done.8.other_ref), custom_call_target="tpu_custom_call" | custom-call | flops 20000000000 | bytes 1048576 | tf_op jit(solution)/shard_map/pallas_call | solution.py:123
  105.3 2.5 %collective-permute-start.15 = (bf16[2,512,256]{2,1,0:T(8,128)(2,1)S(1)}, bf16[2,512,256]{2,1,0:T(8,128)(2,1)S(1)}, u32[]{:S(2)}, u32[]{:S(2)}) collective-permute-start(bf16[2,512,256]{2,1,0:T(8,128)(2,1)S(1)} %pad_maximum_fusion.refs_4_), channel_id=1, source_target_pairs={{0,128},{1,129},{2,130},{3,131},{4,132},{5,133},{6,134},{7,135},{8... | collective-permute-start | bytes 1572872 | tf_op jit(solution)/shard_map/ppermute | solution.py:33
  107.8 9.6 %collective-permute-start.9 = (bf16[128,512]{1,0:T(8,128)(2,1)S(1)}, bf16[128,512]{1,0:T(8,128)(2,1)S(1)}, u32[]{:S(2)}, u32[]{:S(2)}) collective-permute-start(bf16[128,512]{1,0:T(8,128)(2,1)S(1)} %shard_map.65), channel_id=1, source_target_pairs={{0,2},{1,3},{2,0},{3,1},{4,6},{5,7},{6,4},{7,5},{8,10},{9,11},{10,... | collective-permute-start | bytes 393224 | tf_op jit(solution)/shard_map/ppermute | solution.py:33
  117.5 2.6 %collective-permute-done.9 = bf16[128,512]{1,0:T(8,128)(2,1)S(1)} collective-permute-done((bf16[128,512]{1,0:T(8,128)(2,1)S(1)}, bf16[128,512]{1,0:T(8,128)(2,1)S(1)}, u32[]{:S(2)}, u32[]{:S(2)}) %collective-permute-start.9) | collective-permute-done | bytes 131104 | tf_op jit(solution)/shard_map/ppermute | solution.py:33
  120.1 2.0 %collective-permute-start.14 = (bf16[2,128,512]{2,1,0:T(8,128)(2,1)S(1)}, bf16[2,128,512]{2,1,0:T(8,128)(2,1)S(1)}, u32[]{:S(2)}, u32[]{:S(2)}) collective-permute-start(bf16[2,128,512]{2,1,0:T(8,128)(2,1)S(1)} %pad_maximum_fusion.1.refs_0_), channel_id=1, source_target_pairs={{0,16},{1,17},{2,18},{3,19},{4,20},{5,21},{6,22},{7,23},{8,24},{9,... | collective-permute-start | bytes 786440 | tf_op jit(solution)/shard_map/ppermute | solution.py:33
  122.2 1.9 %collective-permute-start.13 = (bf16[2,128,512]{2,1,0:T(8,128)(2,1)S(1)}, bf16[2,128,512]{2,1,0:T(8,128)(2,1)S(1)}, u32[]{:S(2)}, u32[]{:S(2)}) collective-permute-start(bf16[2,128,512]{2,1,0:T(8,128)(2,1)S(1)} %pad_maximum_fusion.1.refs_0_), channel_id=1, source_target_pairs={{0,32},{1,33},{2,34},{3,35},{4,36},{5,37},{6,38},{7,39},{8,40},{9,... | collective-permute-start | bytes 786440 | tf_op jit(solution)/shard_map/ppermute | solution.py:33
  124.1 4.5 %collective-permute-start.12 = (bf16[2,128,512]{2,1,0:T(8,128)(2,1)S(1)}, bf16[2,128,512]{2,1,0:T(8,128)(2,1)S(1)}, u32[]{:S(2)}, u32[]{:S(2)}) collective-permute-start(bf16[2,128,512]{2,1,0:T(8,128)(2,1)S(1)} %pad_maximum_fusion.1.refs_0_), channel_id=1, source_target_pairs={{0,48},{1,49},{2,50},{3,51},{4,52},{5,53},{6,54},{7,55},{8,56},{9,... | collective-permute-start | bytes 786440 | tf_op jit(solution)/shard_map/ppermute | solution.py:33
  128.7 3.2 %collective-permute-done.14.refs_3_ = bf16[2,128,512]{2,1,0:T(8,128)(2,1)S(1)} collective-permute-done((bf16[2,128,512]{2,1,0:T(8,128)(2,1)S(1)}, bf16[2,128,512]{2,1,0:T(8,128)(2,1)S(1)}, u32[]{:S(2)}, u32[]{:S(2)}) %collective-permute-start.14) | collective-permute-done | bytes 262176 | tf_op jit(solution)/shard_map/ppermute | solution.py:33
  131.9 4.6 %collective-permute-done.12.refs_1_ = bf16[2,128,512]{2,1,0:T(8,128)(2,1)S(1)} collective-permute-done((bf16[2,128,512]{2,1,0:T(8,128)(2,1)S(1)}, bf16[2,128,512]{2,1,0:T(8,128)(2,1)S(1)}, u32[]{:S(2)}, u32[]{:S(2)}) %collective-permute-start.12) | collective-permute-done | bytes 262176 | tf_op jit(solution)/shard_map/ppermute | solution.py:33
  136.5 1.8 shard_map.66
  138.3 5.5 %collective-permute-start.16 = (bf16[4,2,128,256]{3,2,1,0:T(8,128)(2,1)S(1)}, bf16[4,2,128,256]{3,2,1,0:T(8,128)(2,1)S(1)}, u32[]{:S(2)}, u32[]{:S(2)}) collective-permute-start(bf16[4,2,128,256]{3,2,1,0:T(8,128)(2,1)S(1)} %slice_bitcast_fusion), channel_id=1, source_target_pairs={{0,1},{1,0},{2,3},{3,2},{4,5},{5,4},{6,7},{7,6},{8,9},{9,8},{10,11... | collective-permute-start | bytes 1572872 | tf_op jit(solution)/shard_map/ppermute | solution.py:33
  143.8 1.5 collective-permute-done.16
  145.5 1.9 %collective-permute-start.17 = (bf16[2,128,256]{2,1,0:T(8,128)(2,1)S(1)}, bf16[2,128,256]{2,1,0:T(8,128)(2,1)S(1)}, u32[]{:S(2)}, u32[]{:S(2)}) collective-permute-start(bf16[2,128,256]{2,1,0:T(8,128)(2,1)S(1)} %get-tuple-element.27), channel_id=1, source_target_pairs={{0,12},{1,13},{2,14},{3,15},{4,8},{5,9},{6,10},{7,11},{8,4},{9,5},... | collective-permute-start | bytes 393224 | tf_op jit(solution)/shard_map/ppermute | solution.py:33
  147.5 2.7 %collective-permute-start.19 = (bf16[2,128,256]{2,1,0:T(8,128)(2,1)S(1)}, bf16[2,128,256]{2,1,0:T(8,128)(2,1)S(1)}, u32[]{:S(2)}, u32[]{:S(2)}) collective-permute-start(bf16[2,128,256]{2,1,0:T(8,128)(2,1)S(1)} %get-tuple-element.28), channel_id=1, source_target_pairs={{0,4},{1,5},{2,6},{3,7},{4,0},{5,1},{6,2},{7,3},{8,12},{9,13},{10,... | collective-permute-start | bytes 393224 | tf_op jit(solution)/shard_map/ppermute | solution.py:33
  150.1 8.6 %collective-permute-start.18 = (bf16[2,128,256]{2,1,0:T(8,128)(2,1)S(1)}, bf16[2,128,256]{2,1,0:T(8,128)(2,1)S(1)}, u32[]{:S(2)}, u32[]{:S(2)}) collective-permute-start(bf16[2,128,256]{2,1,0:T(8,128)(2,1)S(1)} %get-tuple-element.29), channel_id=1, source_target_pairs={{0,8},{1,9},{2,10},{3,11},{4,12},{5,13},{6,14},{7,15},{8,0},{9,1},... | collective-permute-start | bytes 393224 | tf_op jit(solution)/shard_map/ppermute | solution.py:33
  158.8 7.6 %collective-permute-done.17 = bf16[2,128,256]{2,1,0:T(8,128)(2,1)S(1)} collective-permute-done((bf16[2,128,256]{2,1,0:T(8,128)(2,1)S(1)}, bf16[2,128,256]{2,1,0:T(8,128)(2,1)S(1)}, u32[]{:S(2)}, u32[]{:S(2)}) %collective-permute-start.17) | collective-permute-done | bytes 131104 | tf_op jit(solution)/shard_map/ppermute | solution.py:33
  166.3 3.3 %collective-permute-done.18 = bf16[2,128,256]{2,1,0:T(8,128)(2,1)S(1)} collective-permute-done((bf16[2,128,256]{2,1,0:T(8,128)(2,1)S(1)}, bf16[2,128,256]{2,1,0:T(8,128)(2,1)S(1)}, u32[]{:S(2)}, u32[]{:S(2)}) %collective-permute-start.18) | collective-permute-done | bytes 131104 | tf_op jit(solution)/shard_map/ppermute | solution.py:33
  169.8 9.1 %collective-permute-start.20 = (bf16[128,256]{1,0:T(8,128)(2,1)S(1)}, bf16[128,256]{1,0:T(8,128)(2,1)S(1)}, u32[]{:S(2)}, u32[]{:S(2)}) collective-permute-start(bf16[128,256]{1,0:T(8,128)(2,1)S(1)} %get-tuple-element.32), channel_id=1, source_target_pairs={{0,16},{1,48},{2,18},{3,50},{4,20},{5,52},{6,22},{7,54},{8,24},{9,... | collective-permute-start | bytes 196616 | tf_op jit(solution)/shard_map/ppermute | solution.py:33
  178.8 1.9 %collective-permute-start.21 = (bf16[128,256]{1,0:T(8,128)(2,1)S(1)}, bf16[128,256]{1,0:T(8,128)(2,1)S(1)}, u32[]{:S(2)}, u32[]{:S(2)}) collective-permute-start(bf16[128,256]{1,0:T(8,128)(2,1)S(1)} %get-tuple-element.33), channel_id=1, source_target_pairs={{0,0},{1,32},{2,2},{3,34},{4,4},{5,36},{6,6},{7,38},{8,8},{9,40},{... | collective-permute-start | bytes 196616 | tf_op jit(solution)/shard_map/ppermute | solution.py:33
  180.8 5.2 %collective-permute-done.21 = bf16[128,256]{1,0:T(8,128)(2,1)S(1)} collective-permute-done((bf16[128,256]{1,0:T(8,128)(2,1)S(1)}, bf16[128,256]{1,0:T(8,128)(2,1)S(1)}, u32[]{:S(2)}, u32[]{:S(2)}) %collective-permute-start.21) | collective-permute-done | bytes 65568 | tf_op jit(solution)/shard_map/ppermute | solution.py:33
  (52 shorter events, 6.0 us)
Async XLA Ops:
  0.0 11.8 %copy-start.2 = (bf16[8,128]{1,0:T(8,128)(2,1)S(1)}, bf16[8,128]{1,0:T(8,128)(2,1)}, u32[]{:S(2)}) copy-start(bf16[8,128]{1,0:T(8,128)(2,1)} %refs_0_.1) | copy-start | bytes 6148
  0.0 39.8 %collective-permute-start.4 = (bf16[512,256]{1,0:T(8,128)(2,1)}, bf16[512,256]{1,0:T(8,128)(2,1)S(1)}, u32[]{:S(2)}, u32[]{:S(2)}) collective-permute-start(bf16[512,256]{1,0:T(8,128)(2,1)} %param.11), channel_id=1, source_target_pairs={{0,10},{1,11},{2,0},{3,1},{4,14},{5,15},{6,4},{7,5},{8,64},{9,65},... | collective-permute-start | bytes 786440 | tf_op jit(solution)/shard_map/ppermute | solution.py:33
  11.1 28.7 %collective-permute-start.5 = (bf16[512,256]{1,0:T(8,128)(2,1)}, bf16[512,256]{1,0:T(8,128)(2,1)S(1)}, u32[]{:S(2)}, u32[]{:S(2)}) collective-permute-start(bf16[512,256]{1,0:T(8,128)(2,1)} %param.11), channel_id=1, source_target_pairs={{2,74},{3,75},{6,78},{7,79},{10,2},{11,3},{14,6},{15,7},{18,90},{1... | collective-permute-start | bytes 786440 | tf_op jit(solution)/shard_map/ppermute | solution.py:33
  11.8 14.6 %copy-start.4 = (bf16[8,128]{1,0:T(8,128)(2,1)S(1)}, bf16[8,128]{1,0:T(8,128)(2,1)}, u32[]{:S(2)}) copy-start(bf16[8,128]{1,0:T(8,128)(2,1)} %refs_2_.1) | copy-start | bytes 6148
  11.8 14.6 %copy-start.5 = (bf16[8,128]{1,0:T(8,128)(2,1)S(1)}, bf16[8,128]{1,0:T(8,128)(2,1)}, u32[]{:S(2)}) copy-start(bf16[8,128]{1,0:T(8,128)(2,1)} %refs_3_.1) | copy-start | bytes 6148
  12.5 13.9 %copy-start.3 = (bf16[8,128]{1,0:T(8,128)(2,1)S(1)}, bf16[8,128]{1,0:T(8,128)(2,1)}, u32[]{:S(2)}) copy-start(bf16[8,128]{1,0:T(8,128)(2,1)} %refs_1_.1) | copy-start | bytes 6148
  12.6 20.5 %collective-permute-start.3 = (bf16[2,8,128]{2,1,0:T(8,128)(2,1)S(1)}, bf16[2,8,128]{2,1,0:T(8,128)(2,1)S(1)}, u32[]{:S(2)}, u32[]{:S(2)}) collective-permute-start(bf16[2,8,128]{2,1,0:T(8,128)(2,1)S(1)} %pad_maximum_fusion.4), channel_id=1, source_target_pairs={{0,64},{16,80},{32,96},{48,112},{64,128},{80,144},{96,160},{112,17... | collective-permute-start | bytes 12296 | tf_op jit(solution)/shard_map/ppermute | solution.py:38
  26.5 10.6 %collective-permute-start = (bf16[4,8,128]{2,1,0:T(8,128)(2,1)S(1)}, bf16[4,8,128]{2,1,0:T(8,128)(2,1)S(1)}, u32[]{:S(2)}, u32[]{:S(2)}) collective-permute-start(bf16[4,8,128]{2,1,0:T(8,128)(2,1)S(1)} %pad_maximum_fusion.3), channel_id=1, source_target_pairs={{0,16},{16,32},{32,48},{48,64},{64,80},{80,96},{96,112},{112,128},... | collective-permute-start | bytes 24584 | tf_op jit(solution)/shard_map/ppermute | solution.py:38
  29.7 6.7 %collective-permute-start.2 = (bf16[2,8,128]{2,1,0:T(8,128)(2,1)S(1)}, bf16[2,8,128]{2,1,0:T(8,128)(2,1)S(1)}, u32[]{:S(2)}, u32[]{:S(2)}) collective-permute-start(bf16[2,8,128]{2,1,0:T(8,128)(2,1)S(1)} %pad_maximum_fusion.4), channel_id=1, source_target_pairs={{0,48},{16,64},{32,80},{48,96},{64,112},{80,128},{96,144},{112,160... | collective-permute-start | bytes 12296 | tf_op jit(solution)/shard_map/ppermute | solution.py:38
  33.1 4.0 %copy-start.7 = (bf16[2,8,128]{2,1,0:T(8,128)(2,1)}, bf16[2,8,128]{2,1,0:T(8,128)(2,1)S(1)}, u32[]{:S(2)}) copy-start(bf16[2,8,128]{2,1,0:T(8,128)(2,1)S(1)} %collective-permute-done.3.refs_7_) | copy-start | bytes 12292
  33.1 4.0 %collective-permute-start.1 = (bf16[2,8,128]{2,1,0:T(8,128)(2,1)S(1)}, bf16[2,8,128]{2,1,0:T(8,128)(2,1)S(1)}, u32[]{:S(2)}, u32[]{:S(2)}) collective-permute-start(bf16[2,8,128]{2,1,0:T(8,128)(2,1)S(1)} %pad_maximum_fusion.4), channel_id=1, source_target_pairs={{0,32},{16,48},{32,64},{48,80},{64,96},{80,112},{96,128},{112,144}... | collective-permute-start | bytes 12296 | tf_op jit(solution)/shard_map/ppermute | solution.py:38
  36.4 0.7 copy-start.8
  37.7 0.6 copy-start.6
  39.8 18.8 %all-to-all-start = ((bf16[8,14,8,128]{3,2,1,0:T(8,128)(2,1)}), bf16[8,14,8,128]{3,2,1,0:T(8,128)(2,1)S(1)}, u32[]{:S(2)}, u32[]{:S(2)}) async-start(bf16[8,14,8,128]{3,2,1,0:T(8,128)(2,1)} %shard_map.64), calls=%async_computation | async-start | bytes 458752 | tf_op jit(solution)/shard_map/all_to_all | solution.py:226
  47.4 1.5 collective-permute-start.7
  48.1 25.4 %collective-permute-start.6 = (bf16[512,256]{1,0:T(8,128)(2,1)S(1)}, bf16[512,256]{1,0:T(8,128)(2,1)S(1)}, u32[]{:S(2)}, u32[]{:S(2)}) collective-permute-start(bf16[512,256]{1,0:T(8,128)(2,1)S(1)} %collective-permute-done.4), channel_id=1, source_target_pairs={{2,10},{3,11},{6,14},{7,15},{10,64},{11,65},{14,68},{15,69},{18,26... | collective-permute-start | bytes 786440 | tf_op jit(solution)/shard_map/ppermute | solution.py:33
  48.8 24.6 %copy-start.1 = (bf16[512,256]{1,0:T(8,128)(2,1)S(1)}, bf16[512,256]{1,0:T(8,128)(2,1)}, u32[]{:S(2)}) copy-start(bf16[512,256]{1,0:T(8,128)(2,1)} %param.11) | copy-start | bytes 786436
  58.6 15.9 %collective-permute-start.8 = (bf16[8,14,8,128]{3,2,1,0:T(8,128)(2,1)S(1)}, bf16[8,14,8,128]{3,2,1,0:T(8,128)(2,1)S(1)}, u32[]{:S(2)}, u32[]{:S(2)}) collective-permute-start(bf16[8,14,8,128]{3,2,1,0:T(8,128)(2,1)S(1)} %all-to-all-done.mine_ref), channel_id=1, source_target_pairs={{0,1},{1,0},{2,3},{3,2},{4,5},{5,4},{6,7},{7,6},{8,9},{9,8},{10,11... | collective-permute-start | bytes 688136 | tf_op jit(solution)/shard_map/ppermute | solution.py:33
  73.5 16.9 %copy-start = (bf16[128,512]{1,0:T(8,128)(2,1)S(1)}, bf16[128,512]{1,0:T(8,128)(2,1)}, u32[]{:S(2)}) copy-start(bf16[128,512]{1,0:T(8,128)(2,1)} %q_ref.1) | copy-start | bytes 393220
  74.6 45.5 %collective-permute-start.11 = (bf16[2,512,256]{2,1,0:T(8,128)(2,1)S(1)}, bf16[2,512,256]{2,1,0:T(8,128)(2,1)S(1)}, u32[]{:S(2)}, u32[]{:S(2)}) collective-permute-start(bf16[2,512,256]{2,1,0:T(8,128)(2,1)S(1)} %pad_maximum_fusion.refs_4_), channel_id=1, source_target_pairs={{0,256},{1,257},{2,258},{3,259},{4,260},{5,261},{6,262},{7,263},{8... | collective-permute-start | bytes 1572872 | tf_op jit(solution)/shard_map/ppermute | solution.py:33
  87.6 32.5 %collective-permute-start.10 = (bf16[2,512,256]{2,1,0:T(8,128)(2,1)S(1)}, bf16[2,512,256]{2,1,0:T(8,128)(2,1)S(1)}, u32[]{:S(2)}, u32[]{:S(2)}) collective-permute-start(bf16[2,512,256]{2,1,0:T(8,128)(2,1)S(1)} %pad_maximum_fusion.refs_4_), channel_id=1, source_target_pairs={{0,384},{1,385},{2,386},{3,387},{4,388},{5,389},{6,390},{7,391},{8... | collective-permute-start | bytes 1572872 | tf_op jit(solution)/shard_map/ppermute | solution.py:33
  105.3 23.4 %collective-permute-start.15 = (bf16[2,512,256]{2,1,0:T(8,128)(2,1)S(1)}, bf16[2,512,256]{2,1,0:T(8,128)(2,1)S(1)}, u32[]{:S(2)}, u32[]{:S(2)}) collective-permute-start(bf16[2,512,256]{2,1,0:T(8,128)(2,1)S(1)} %pad_maximum_fusion.refs_4_), channel_id=1, source_target_pairs={{0,128},{1,129},{2,130},{3,131},{4,132},{5,133},{6,134},{7,135},{8... | collective-permute-start | bytes 1572872 | tf_op jit(solution)/shard_map/ppermute | solution.py:33
  107.8 12.3 %collective-permute-start.9 = (bf16[128,512]{1,0:T(8,128)(2,1)S(1)}, bf16[128,512]{1,0:T(8,128)(2,1)S(1)}, u32[]{:S(2)}, u32[]{:S(2)}) collective-permute-start(bf16[128,512]{1,0:T(8,128)(2,1)S(1)} %shard_map.65), channel_id=1, source_target_pairs={{0,2},{1,3},{2,0},{3,1},{4,6},{5,7},{6,4},{7,5},{8,10},{9,11},{10,... | collective-permute-start | bytes 393224 | tf_op jit(solution)/shard_map/ppermute | solution.py:33
  120.1 11.8 %collective-permute-start.14 = (bf16[2,128,512]{2,1,0:T(8,128)(2,1)S(1)}, bf16[2,128,512]{2,1,0:T(8,128)(2,1)S(1)}, u32[]{:S(2)}, u32[]{:S(2)}) collective-permute-start(bf16[2,128,512]{2,1,0:T(8,128)(2,1)S(1)} %pad_maximum_fusion.1.refs_0_), channel_id=1, source_target_pairs={{0,16},{1,17},{2,18},{3,19},{4,20},{5,21},{6,22},{7,23},{8,24},{9,... | collective-permute-start | bytes 786440 | tf_op jit(solution)/shard_map/ppermute | solution.py:33
  122.2 9.7 %collective-permute-start.13 = (bf16[2,128,512]{2,1,0:T(8,128)(2,1)S(1)}, bf16[2,128,512]{2,1,0:T(8,128)(2,1)S(1)}, u32[]{:S(2)}, u32[]{:S(2)}) collective-permute-start(bf16[2,128,512]{2,1,0:T(8,128)(2,1)S(1)} %pad_maximum_fusion.1.refs_0_), channel_id=1, source_target_pairs={{0,32},{1,33},{2,34},{3,35},{4,36},{5,37},{6,38},{7,39},{8,40},{9,... | collective-permute-start | bytes 786440 | tf_op jit(solution)/shard_map/ppermute | solution.py:33
  124.1 12.4 %collective-permute-start.12 = (bf16[2,128,512]{2,1,0:T(8,128)(2,1)S(1)}, bf16[2,128,512]{2,1,0:T(8,128)(2,1)S(1)}, u32[]{:S(2)}, u32[]{:S(2)}) collective-permute-start(bf16[2,128,512]{2,1,0:T(8,128)(2,1)S(1)} %pad_maximum_fusion.1.refs_0_), channel_id=1, source_target_pairs={{0,48},{1,49},{2,50},{3,51},{4,52},{5,53},{6,54},{7,55},{8,56},{9,... | collective-permute-start | bytes 786440 | tf_op jit(solution)/shard_map/ppermute | solution.py:33
  138.3 7.0 %collective-permute-start.16 = (bf16[4,2,128,256]{3,2,1,0:T(8,128)(2,1)S(1)}, bf16[4,2,128,256]{3,2,1,0:T(8,128)(2,1)S(1)}, u32[]{:S(2)}, u32[]{:S(2)}) collective-permute-start(bf16[4,2,128,256]{3,2,1,0:T(8,128)(2,1)S(1)} %slice_bitcast_fusion), channel_id=1, source_target_pairs={{0,1},{1,0},{2,3},{3,2},{4,5},{5,4},{6,7},{7,6},{8,9},{9,8},{10,11... | collective-permute-start | bytes 1572872 | tf_op jit(solution)/shard_map/ppermute | solution.py:33
  145.5 20.8 %collective-permute-start.17 = (bf16[2,128,256]{2,1,0:T(8,128)(2,1)S(1)}, bf16[2,128,256]{2,1,0:T(8,128)(2,1)S(1)}, u32[]{:S(2)}, u32[]{:S(2)}) collective-permute-start(bf16[2,128,256]{2,1,0:T(8,128)(2,1)S(1)} %get-tuple-element.27), channel_id=1, source_target_pairs={{0,12},{1,13},{2,14},{3,15},{4,8},{5,9},{6,10},{7,11},{8,4},{9,5},... | collective-permute-start | bytes 393224 | tf_op jit(solution)/shard_map/ppermute | solution.py:33
  147.5 18.9 %collective-permute-start.19 = (bf16[2,128,256]{2,1,0:T(8,128)(2,1)S(1)}, bf16[2,128,256]{2,1,0:T(8,128)(2,1)S(1)}, u32[]{:S(2)}, u32[]{:S(2)}) collective-permute-start(bf16[2,128,256]{2,1,0:T(8,128)(2,1)S(1)} %get-tuple-element.28), channel_id=1, source_target_pairs={{0,4},{1,5},{2,6},{3,7},{4,0},{5,1},{6,2},{7,3},{8,12},{9,13},{10,... | collective-permute-start | bytes 393224 | tf_op jit(solution)/shard_map/ppermute | solution.py:33
  150.1 19.5 %collective-permute-start.18 = (bf16[2,128,256]{2,1,0:T(8,128)(2,1)S(1)}, bf16[2,128,256]{2,1,0:T(8,128)(2,1)S(1)}, u32[]{:S(2)}, u32[]{:S(2)}) collective-permute-start(bf16[2,128,256]{2,1,0:T(8,128)(2,1)S(1)} %get-tuple-element.29), channel_id=1, source_target_pairs={{0,8},{1,9},{2,10},{3,11},{4,12},{5,13},{6,14},{7,15},{8,0},{9,1},... | collective-permute-start | bytes 393224 | tf_op jit(solution)/shard_map/ppermute | solution.py:33
  169.8 11.0 %collective-permute-start.20 = (bf16[128,256]{1,0:T(8,128)(2,1)S(1)}, bf16[128,256]{1,0:T(8,128)(2,1)S(1)}, u32[]{:S(2)}, u32[]{:S(2)}) collective-permute-start(bf16[128,256]{1,0:T(8,128)(2,1)S(1)} %get-tuple-element.32), channel_id=1, source_target_pairs={{0,16},{1,48},{2,18},{3,50},{4,20},{5,52},{6,22},{7,54},{8,24},{9,... | collective-permute-start | bytes 196616 | tf_op jit(solution)/shard_map/ppermute | solution.py:33
  178.8 7.1 %collective-permute-start.21 = (bf16[128,256]{1,0:T(8,128)(2,1)S(1)}, bf16[128,256]{1,0:T(8,128)(2,1)S(1)}, u32[]{:S(2)}, u32[]{:S(2)}) collective-permute-start(bf16[128,256]{1,0:T(8,128)(2,1)S(1)} %get-tuple-element.33), channel_id=1, source_target_pairs={{0,0},{1,32},{2,2},{3,34},{4,4},{5,36},{6,6},{7,38},{8,8},{9,40},{... | collective-permute-start | bytes 196616 | tf_op jit(solution)/shard_map/ppermute | solution.py:33
  (1 other events, 0.6 us)

commit v11 on v10

--- a/solution.py
+++ b/solution.py
@@ -204,7 +204,7 @@
     second_up = {first_up[spot]: (spot + 8) % 16 for spot in first_up}
     stay = [spot for spot in range(16) if spot not in first_up]
     first_up.update({spot: spot ^ 1 for spot in stay})
-    first_down = {spot: (spot - 4) % 16 for spot in stay}
+    first_down = {spot: (spot - (5 if spot < 8 else 4)) % 16 for spot in stay}
     second_down = {first_down[spot]: (spot ^ 1) ^ 8 for spot in stay}
 
     def along(table):

time: 187 us -> 189 us (1.011); the launches traced: 187 us -> 186 us
  waiting for transfers between devices: 39.4 us -> 35.2 us
  starting transfers between devices: 125 us -> 129 us
    all_to_all x1, waiting for transfers between devices: 9.74 us -> 0.01 us  [per_device(): lax.all_to_all(mine, 'head', 0, 0, axis_index_groups=lines, tiled=True)]
    ppermute x18, waiting for transfers between devices: 29 us -> 34.4 us  [moved(): return lax.ppermute(value, BOTH, pairs)]
    all_to_all x1, starting transfers between devices: 7.58 us -> 10.7 us  [per_device(): lax.all_to_all(mine, 'head', 0, 0, axis_index_groups=lines, tiled=True)]
  transfers between devices with their start and end apart: 23 -> 23, of which waited for: 10 -> 11; matrix products, arithmetic and copies ran while one was open for 1% -> 1% of each run, Pallas kernels for 9% -> 9%
where the time goes in v11:
time: 189 us; the launch traced here: 186 us
  starting transfers between devices  129 us (68%)
  waiting for transfers between devices  35.2 us (19%)
  Pallas kernels  18.1 us (10%)
  other arithmetic  1.9 us (1%)
    ppermute x18, starting transfers between devices, moved(): return lax.ppermute(value, BOTH, pairs)  95.5 us
    ppermute x18, waiting for transfers between devices, moved(): return lax.ppermute(value, BOTH, pairs)  34.4 us
    ppermute x4, starting transfers between devices, later(): lax.ppermute(value, 'seq', [(s, s + steps) for s in range(count - steps)])  23.1 us
    pallas_call x1, Pallas kernels, attention(): pl.pallas_call(functools.partial(attention_kernel, tokens=32), out_shape=...  14.8 us
    all_to_all x1, starting transfers between devices, per_device(): lax.all_to_all(mine, 'head', 0, 0, axis_index_groups=lines, tiled=True)  10.7 us
  transfers between devices with their start and end apart: 23, of which 11 were waited for; matrix products, arithmetic and copies ran while one was open for 1% of the time, Pallas kernels for 9%

profile of v11, /device:TPU:1, one launch (start us, length us, event | category | flops | bytes accessed | tf_op | source)
XLA Modules:
  0.0 186.3 jit_solution(12775689401159330769)
XLA Ops:
  0.0 11.1 %collective-permute-start.4 = (bf16[512,256]{1,0:T(8,128)(2,1)}, bf16[512,256]{1,0:T(8,128)(2,1)S(1)}, u32[]{:S(2)}, u32[]{:S(2)}) collective-permute-start(bf16[512,256]{1,0:T(8,128)(2,1)} %param.11), channel_id=1, source_target_pairs={{0,10},{1,11},{2,0},{3,1},{4,14},{5,15},{6,4},{7,5},{8,64},{9,65},... | collective-permute-start | bytes 786440 | tf_op jit(solution)/shard_map/ppermute | solution.py:33
  13.2 13.3 %collective-permute-start.3 = (bf16[2,8,128]{2,1,0:T(8,128)(2,1)S(1)}, bf16[2,8,128]{2,1,0:T(8,128)(2,1)S(1)}, u32[]{:S(2)}, u32[]{:S(2)}) collective-permute-start(bf16[2,8,128]{2,1,0:T(8,128)(2,1)S(1)} %pad_maximum_fusion.4), channel_id=1, source_target_pairs={{0,64},{16,80},{32,96},{48,112},{64,128},{80,144},{96,160},{112,17... | collective-permute-start | bytes 12296 | tf_op jit(solution)/shard_map/ppermute | solution.py:38
  26.5 3.2 %collective-permute-start = (bf16[4,8,128]{2,1,0:T(8,128)(2,1)S(1)}, bf16[4,8,128]{2,1,0:T(8,128)(2,1)S(1)}, u32[]{:S(2)}, u32[]{:S(2)}) collective-permute-start(bf16[4,8,128]{2,1,0:T(8,128)(2,1)S(1)} %pad_maximum_fusion.3), channel_id=1, source_target_pairs={{0,16},{16,32},{32,48},{48,64},{64,80},{80,96},{96,112},{112,128},... | collective-permute-start | bytes 24584 | tf_op jit(solution)/shard_map/ppermute | solution.py:38
  29.7 3.4 %collective-permute-start.2 = (bf16[2,8,128]{2,1,0:T(8,128)(2,1)S(1)}, bf16[2,8,128]{2,1,0:T(8,128)(2,1)S(1)}, u32[]{:S(2)}, u32[]{:S(2)}) collective-permute-start(bf16[2,8,128]{2,1,0:T(8,128)(2,1)S(1)} %pad_maximum_fusion.4), channel_id=1, source_target_pairs={{0,48},{16,64},{32,80},{48,96},{64,112},{80,128},{96,144},{112,160... | collective-permute-start | bytes 12296 | tf_op jit(solution)/shard_map/ppermute | solution.py:38
  33.1 3.3 %collective-permute-start.1 = (bf16[2,8,128]{2,1,0:T(8,128)(2,1)S(1)}, bf16[2,8,128]{2,1,0:T(8,128)(2,1)S(1)}, u32[]{:S(2)}, u32[]{:S(2)}) collective-permute-start(bf16[2,8,128]{2,1,0:T(8,128)(2,1)S(1)} %pad_maximum_fusion.4), channel_id=1, source_target_pairs={{0,32},{16,48},{32,64},{48,80},{64,96},{80,112},{96,128},{112,144}... | collective-permute-start | bytes 12296 | tf_op jit(solution)/shard_map/ppermute | solution.py:38
  38.3 1.5 shard_map.64
  39.8 10.7 %all-to-all-start = ((bf16[8,14,8,128]{3,2,1,0:T(8,128)(2,1)}), bf16[8,14,8,128]{3,2,1,0:T(8,128)(2,1)S(1)}, u32[]{:S(2)}, u32[]{:S(2)}) async-start(bf16[8,14,8,128]{3,2,1,0:T(8,128)(2,1)} %shard_map.64), calls=%async_computation | async-start | bytes 458752 | tf_op jit(solution)/shard_map/all_to_all | solution.py:226
  50.5 20.2 %collective-permute-start.7 = (bf16[512,256]{1,0:T(8,128)(2,1)S(1)}, bf16[512,256]{1,0:T(8,128)(2,1)S(1)}, u32[]{:S(2)}, u32[]{:S(2)}) collective-permute-start(bf16[512,256]{1,0:T(8,128)(2,1)S(1)} %collective-permute-done.5), channel_id=1, source_target_pairs={{0,72},{1,73},{4,76},{5,77},{8,2},{9,3},{12,6},{13,7},{16,88},{17,... | collective-permute-start | bytes 786440 | tf_op jit(solution)/shard_map/ppermute | solution.py:33
  71.5 3.0 %collective-permute-done.7 = bf16[512,256]{1,0:T(8,128)(2,1)S(1)} collective-permute-done((bf16[512,256]{1,0:T(8,128)(2,1)S(1)}, bf16[512,256]{1,0:T(8,128)(2,1)S(1)}, u32[]{:S(2)}, u32[]{:S(2)}) %collective-permute-start.7) | collective-permute-done | bytes 262176 | tf_op jit(solution)/shard_map/ppermute | solution.py:33
  74.5 11.4 %collective-permute-start.8 = (bf16[8,14,8,128]{3,2,1,0:T(8,128)(2,1)S(1)}, bf16[8,14,8,128]{3,2,1,0:T(8,128)(2,1)S(1)}, u32[]{:S(2)}, u32[]{:S(2)}) collective-permute-start(bf16[8,14,8,128]{3,2,1,0:T(8,128)(2,1)S(1)} %all-to-all-done.mine_ref), channel_id=1, source_target_pairs={{0,1},{1,0},{2,3},{3,2},{4,5},{5,4},{6,7},{7,6},{8,9},{9,8},{10,11... | collective-permute-start | bytes 688136 | tf_op jit(solution)/shard_map/ppermute | solution.py:33
  87.0 5.9 %collective-permute-start.11 = (bf16[2,512,256]{2,1,0:T(8,128)(2,1)S(1)}, bf16[2,512,256]{2,1,0:T(8,128)(2,1)S(1)}, u32[]{:S(2)}, u32[]{:S(2)}) collective-permute-start(bf16[2,512,256]{2,1,0:T(8,128)(2,1)S(1)} %pad_maximum_fusion.refs_4_), channel_id=1, source_target_pairs={{0,256},{1,257},{2,258},{3,259},{4,260},{5,261},{6,262},{7,263},{8... | collective-permute-start | bytes 1572872 | tf_op jit(solution)/shard_map/ppermute | solution.py:33
  93.0 3.1 %collective-permute-start.10 = (bf16[2,512,256]{2,1,0:T(8,128)(2,1)S(1)}, bf16[2,512,256]{2,1,0:T(8,128)(2,1)S(1)}, u32[]{:S(2)}, u32[]{:S(2)}) collective-permute-start(bf16[2,512,256]{2,1,0:T(8,128)(2,1)S(1)} %pad_maximum_fusion.refs_4_), channel_id=1, source_target_pairs={{0,384},{1,385},{2,386},{3,387},{4,388},{5,389},{6,390},{7,391},{8... | collective-permute-start | bytes 1572872 | tf_op jit(solution)/shard_map/ppermute | solution.py:33
  96.0 14.8 %shard_map.65 = bf16[128,512]{1,0:T(8,128)(2,1)S(1)} custom-call(s32[2]{0:T(128)S(1)} %pad_add_fusion.1.place, bf16[128,512]{1,0:T(8,128)(2,1)S(1)} %copy-done, bf16[8,14,8,128]{3,2,1,0:T(8,128)(2,1)S(1)} %all-to-all-done.mine_ref, bf16[8,14,8,128]{3,2,1,0:T(8,128)(2,1)S(1)} %collective-permute-done.8.other_ref), custom_call_target="tpu_custom_call" | custom-call | flops 20000000000 | bytes 1048576 | tf_op jit(solution)/shard_map/pallas_call | solution.py:123
  110.9 2.2 %collective-permute-start.15 = (bf16[2,512,256]{2,1,0:T(8,128)(2,1)S(1)}, bf16[2,512,256]{2,1,0:T(8,128)(2,1)S(1)}, u32[]{:S(2)}, u32[]{:S(2)}) collective-permute-start(bf16[2,512,256]{2,1,0:T(8,128)(2,1)S(1)} %pad_maximum_fusion.refs_4_), channel_id=1, source_target_pairs={{0,128},{1,129},{2,130},{3,131},{4,132},{5,133},{6,134},{7,135},{8... | collective-permute-start | bytes 1572872 | tf_op jit(solution)/shard_map/ppermute | solution.py:33
  113.1 7.5 %collective-permute-start.9 = (bf16[128,512]{1,0:T(8,128)(2,1)S(1)}, bf16[128,512]{1,0:T(8,128)(2,1)S(1)}, u32[]{:S(2)}, u32[]{:S(2)}) collective-permute-start(bf16[128,512]{1,0:T(8,128)(2,1)S(1)} %shard_map.65), channel_id=1, source_target_pairs={{0,2},{1,3},{2,0},{3,1},{4,6},{5,7},{6,4},{7,5},{8,10},{9,11},{10,... | collective-permute-start | bytes 393224 | tf_op jit(solution)/shard_map/ppermute | solution.py:33
  120.6 2.6 %collective-permute-done.9 = bf16[128,512]{1,0:T(8,128)(2,1)S(1)} collective-permute-done((bf16[128,512]{1,0:T(8,128)(2,1)S(1)}, bf16[128,512]{1,0:T(8,128)(2,1)S(1)}, u32[]{:S(2)}, u32[]{:S(2)}) %collective-permute-start.9) | collective-permute-done | bytes 131104 | tf_op jit(solution)/shard_map/ppermute | solution.py:33
  123.3 2.0 %collective-permute-start.14 = (bf16[2,128,512]{2,1,0:T(8,128)(2,1)S(1)}, bf16[2,128,512]{2,1,0:T(8,128)(2,1)S(1)}, u32[]{:S(2)}, u32[]{:S(2)}) collective-permute-start(bf16[2,128,512]{2,1,0:T(8,128)(2,1)S(1)} %pad_maximum_fusion.1.refs_0_), channel_id=1, source_target_pairs={{0,16},{1,17},{2,18},{3,19},{4,20},{5,21},{6,22},{7,23},{8,24},{9,... | collective-permute-start | bytes 786440 | tf_op jit(solution)/shard_map/ppermute | solution.py:33
  125.3 1.9 %collective-permute-start.13 = (bf16[2,128,512]{2,1,0:T(8,128)(2,1)S(1)}, bf16[2,128,512]{2,1,0:T(8,128)(2,1)S(1)}, u32[]{:S(2)}, u32[]{:S(2)}) collective-permute-start(bf16[2,128,512]{2,1,0:T(8,128)(2,1)S(1)} %pad_maximum_fusion.1.refs_0_), channel_id=1, source_target_pairs={{0,32},{1,33},{2,34},{3,35},{4,36},{5,37},{6,38},{7,39},{8,40},{9,... | collective-permute-start | bytes 786440 | tf_op jit(solution)/shard_map/ppermute | solution.py:33
  127.2 4.5 %collective-permute-start.12 = (bf16[2,128,512]{2,1,0:T(8,128)(2,1)S(1)}, bf16[2,128,512]{2,1,0:T(8,128)(2,1)S(1)}, u32[]{:S(2)}, u32[]{:S(2)}) collective-permute-start(bf16[2,128,512]{2,1,0:T(8,128)(2,1)S(1)} %pad_maximum_fusion.1.refs_0_), channel_id=1, source_target_pairs={{0,48},{1,49},{2,50},{3,51},{4,52},{5,53},{6,54},{7,55},{8,56},{9,... | collective-permute-start | bytes 786440 | tf_op jit(solution)/shard_map/ppermute | solution.py:33
  131.9 6.2 %collective-permute-done.14.refs_3_ = bf16[2,128,512]{2,1,0:T(8,128)(2,1)S(1)} collective-permute-done((bf16[2,128,512]{2,1,0:T(8,128)(2,1)S(1)}, bf16[2,128,512]{2,1,0:T(8,128)(2,1)S(1)}, u32[]{:S(2)}, u32[]{:S(2)}) %collective-permute-start.14) | collective-permute-done | bytes 262176 | tf_op jit(solution)/shard_map/ppermute | solution.py:33
  138.0 3.2 %collective-permute-done.12.refs_1_ = bf16[2,128,512]{2,1,0:T(8,128)(2,1)S(1)} collective-permute-done((bf16[2,128,512]{2,1,0:T(8,128)(2,1)S(1)}, bf16[2,128,512]{2,1,0:T(8,128)(2,1)S(1)}, u32[]{:S(2)}, u32[]{:S(2)}) %collective-permute-start.12) | collective-permute-done | bytes 262176 | tf_op jit(solution)/shard_map/ppermute | solution.py:33
  141.2 1.8 shard_map.66
  143.0 4.0 %collective-permute-start.16 = (bf16[4,2,128,256]{3,2,1,0:T(8,128)(2,1)S(1)}, bf16[4,2,128,256]{3,2,1,0:T(8,128)(2,1)S(1)}, u32[]{:S(2)}, u32[]{:S(2)}) collective-permute-start(bf16[4,2,128,256]{3,2,1,0:T(8,128)(2,1)S(1)} %slice_bitcast_fusion), channel_id=1, source_target_pairs={{0,1},{1,0},{2,3},{3,2},{4,5},{5,4},{6,7},{7,6},{8,9},{9,8},{10,11... | collective-permute-start | bytes 1572872 | tf_op jit(solution)/shard_map/ppermute | solution.py:33
  147.0 1.5 collective-permute-done.16
  148.7 4.8 %collective-permute-start.17 = (bf16[2,128,256]{2,1,0:T(8,128)(2,1)S(1)}, bf16[2,128,256]{2,1,0:T(8,128)(2,1)S(1)}, u32[]{:S(2)}, u32[]{:S(2)}) collective-permute-start(bf16[2,128,256]{2,1,0:T(8,128)(2,1)S(1)} %get-tuple-element.27), channel_id=1, source_target_pairs={{0,12},{1,13},{2,14},{3,15},{4,8},{5,9},{6,10},{7,11},{8,4},{9,5},... | collective-permute-start | bytes 393224 | tf_op jit(solution)/shard_map/ppermute | solution.py:33
  153.5 1.9 %collective-permute-start.19 = (bf16[2,128,256]{2,1,0:T(8,128)(2,1)S(1)}, bf16[2,128,256]{2,1,0:T(8,128)(2,1)S(1)}, u32[]{:S(2)}, u32[]{:S(2)}) collective-permute-start(bf16[2,128,256]{2,1,0:T(8,128)(2,1)S(1)} %get-tuple-element.28), channel_id=1, source_target_pairs={{0,4},{1,5},{2,6},{3,7},{4,0},{5,1},{6,2},{7,3},{8,12},{9,13},{10,... | collective-permute-start | bytes 393224 | tf_op jit(solution)/shard_map/ppermute | solution.py:33
  155.5 6.4 %collective-permute-start.18 = (bf16[2,128,256]{2,1,0:T(8,128)(2,1)S(1)}, bf16[2,128,256]{2,1,0:T(8,128)(2,1)S(1)}, u32[]{:S(2)}, u32[]{:S(2)}) collective-permute-start(bf16[2,128,256]{2,1,0:T(8,128)(2,1)S(1)} %get-tuple-element.29), channel_id=1, source_target_pairs={{0,8},{1,9},{2,10},{3,11},{4,12},{5,13},{6,14},{7,15},{8,0},{9,1},... | collective-permute-start | bytes 393224 | tf_op jit(solution)/shard_map/ppermute | solution.py:33
  161.9 4.7 %collective-permute-done.17 = bf16[2,128,256]{2,1,0:T(8,128)(2,1)S(1)} collective-permute-done((bf16[2,128,256]{2,1,0:T(8,128)(2,1)S(1)}, bf16[2,128,256]{2,1,0:T(8,128)(2,1)S(1)}, u32[]{:S(2)}, u32[]{:S(2)}) %collective-permute-start.17) | collective-permute-done | bytes 131104 | tf_op jit(solution)/shard_map/ppermute | solution.py:33
  166.6 7.2 %collective-permute-done.19 = bf16[2,128,256]{2,1,0:T(8,128)(2,1)S(1)} collective-permute-done((bf16[2,128,256]{2,1,0:T(8,128)(2,1)S(1)}, bf16[2,128,256]{2,1,0:T(8,128)(2,1)S(1)}, u32[]{:S(2)}, u32[]{:S(2)}) %collective-permute-start.19) | collective-permute-done | bytes 131104 | tf_op jit(solution)/shard_map/ppermute | solution.py:33
  173.9 4.7 %collective-permute-start.20 = (bf16[128,256]{1,0:T(8,128)(2,1)S(1)}, bf16[128,256]{1,0:T(8,128)(2,1)S(1)}, u32[]{:S(2)}, u32[]{:S(2)}) collective-permute-start(bf16[128,256]{1,0:T(8,128)(2,1)S(1)} %get-tuple-element.32), channel_id=1, source_target_pairs={{0,16},{1,48},{2,18},{3,50},{4,20},{5,52},{6,22},{7,54},{8,24},{9,... | collective-permute-start | bytes 196616 | tf_op jit(solution)/shard_map/ppermute | solution.py:33
  178.6 1.9 %collective-permute-start.21 = (bf16[128,256]{1,0:T(8,128)(2,1)S(1)}, bf16[128,256]{1,0:T(8,128)(2,1)S(1)}, u32[]{:S(2)}, u32[]{:S(2)}) collective-permute-start(bf16[128,256]{1,0:T(8,128)(2,1)S(1)} %get-tuple-element.33), channel_id=1, source_target_pairs={{0,0},{1,32},{2,2},{3,34},{4,4},{5,36},{6,6},{7,38},{8,8},{9,40},{... | collective-permute-start | bytes 196616 | tf_op jit(solution)/shard_map/ppermute | solution.py:33
  180.7 5.0 %collective-permute-done.21 = bf16[128,256]{1,0:T(8,128)(2,1)S(1)} collective-permute-done((bf16[128,256]{1,0:T(8,128)(2,1)S(1)}, bf16[128,256]{1,0:T(8,128)(2,1)S(1)}, u32[]{:S(2)}, u32[]{:S(2)}) %collective-permute-start.21) | collective-permute-done | bytes 65568 | tf_op jit(solution)/shard_map/ppermute | solution.py:33
  (52 shorter events, 7.0 us)
Async XLA Ops:
  0.0 12.4 %copy-start.2 = (bf16[8,128]{1,0:T(8,128)(2,1)S(1)}, bf16[8,128]{1,0:T(8,128)(2,1)}, u32[]{:S(2)}) copy-start(bf16[8,128]{1,0:T(8,128)(2,1)} %refs_0_.1) | copy-start | bytes 6148
  0.0 39.8 %collective-permute-start.4 = (bf16[512,256]{1,0:T(8,128)(2,1)}, bf16[512,256]{1,0:T(8,128)(2,1)S(1)}, u32[]{:S(2)}, u32[]{:S(2)}) collective-permute-start(bf16[512,256]{1,0:T(8,128)(2,1)} %param.11), channel_id=1, source_target_pairs={{0,10},{1,11},{2,0},{3,1},{4,14},{5,15},{6,4},{7,5},{8,64},{9,65},... | collective-permute-start | bytes 786440 | tf_op jit(solution)/shard_map/ppermute | solution.py:33
  11.1 28.7 %collective-permute-start.5 = (bf16[512,256]{1,0:T(8,128)(2,1)}, bf16[512,256]{1,0:T(8,128)(2,1)S(1)}, u32[]{:S(2)}, u32[]{:S(2)}) collective-permute-start(bf16[512,256]{1,0:T(8,128)(2,1)} %param.11), channel_id=1, source_target_pairs={{2,72},{3,73},{6,76},{7,77},{10,0},{11,1},{14,4},{15,5},{18,88},{1... | collective-permute-start | bytes 786440 | tf_op jit(solution)/shard_map/ppermute | solution.py:33
  12.4 14.0 %copy-start.4 = (bf16[8,128]{1,0:T(8,128)(2,1)S(1)}, bf16[8,128]{1,0:T(8,128)(2,1)}, u32[]{:S(2)}) copy-start(bf16[8,128]{1,0:T(8,128)(2,1)} %refs_2_.1) | copy-start | bytes 6148
  12.5 14.0 %copy-start.5 = (bf16[8,128]{1,0:T(8,128)(2,1)S(1)}, bf16[8,128]{1,0:T(8,128)(2,1)}, u32[]{:S(2)}) copy-start(bf16[8,128]{1,0:T(8,128)(2,1)} %refs_3_.1) | copy-start | bytes 6148
  13.2 13.3 %copy-start.3 = (bf16[8,128]{1,0:T(8,128)(2,1)S(1)}, bf16[8,128]{1,0:T(8,128)(2,1)}, u32[]{:S(2)}) copy-start(bf16[8,128]{1,0:T(8,128)(2,1)} %refs_1_.1) | copy-start | bytes 6148
  13.2 19.9 %collective-permute-start.3 = (bf16[2,8,128]{2,1,0:T(8,128)(2,1)S(1)}, bf16[2,8,128]{2,1,0:T(8,128)(2,1)S(1)}, u32[]{:S(2)}, u32[]{:S(2)}) collective-permute-start(bf16[2,8,128]{2,1,0:T(8,128)(2,1)S(1)} %pad_maximum_fusion.4), channel_id=1, source_target_pairs={{0,64},{16,80},{32,96},{48,112},{64,128},{80,144},{96,160},{112,17... | collective-permute-start | bytes 12296 | tf_op jit(solution)/shard_map/ppermute | solution.py:38
  26.5 10.6 %collective-permute-start = (bf16[4,8,128]{2,1,0:T(8,128)(2,1)S(1)}, bf16[4,8,128]{2,1,0:T(8,128)(2,1)S(1)}, u32[]{:S(2)}, u32[]{:S(2)}) collective-permute-start(bf16[4,8,128]{2,1,0:T(8,128)(2,1)S(1)} %pad_maximum_fusion.3), channel_id=1, source_target_pairs={{0,16},{16,32},{32,48},{48,64},{64,80},{80,96},{96,112},{112,128},... | collective-permute-start | bytes 24584 | tf_op jit(solution)/shard_map/ppermute | solution.py:38
  29.7 6.7 %collective-permute-start.2 = (bf16[2,8,128]{2,1,0:T(8,128)(2,1)S(1)}, bf16[2,8,128]{2,1,0:T(8,128)(2,1)S(1)}, u32[]{:S(2)}, u32[]{:S(2)}) collective-permute-start(bf16[2,8,128]{2,1,0:T(8,128)(2,1)S(1)} %pad_maximum_fusion.4), channel_id=1, source_target_pairs={{0,48},{16,64},{32,80},{48,96},{64,112},{80,128},{96,144},{112,160... | collective-permute-start | bytes 12296 | tf_op jit(solution)/shard_map/ppermute | solution.py:38
  33.1 4.0 %copy-start.7 = (bf16[2,8,128]{2,1,0:T(8,128)(2,1)}, bf16[2,8,128]{2,1,0:T(8,128)(2,1)S(1)}, u32[]{:S(2)}) copy-start(bf16[2,8,128]{2,1,0:T(8,128)(2,1)S(1)} %collective-permute-done.3.refs_7_) | copy-start | bytes 12292
  33.1 4.0 %collective-permute-start.1 = (bf16[2,8,128]{2,1,0:T(8,128)(2,1)S(1)}, bf16[2,8,128]{2,1,0:T(8,128)(2,1)S(1)}, u32[]{:S(2)}, u32[]{:S(2)}) collective-permute-start(bf16[2,8,128]{2,1,0:T(8,128)(2,1)S(1)} %pad_maximum_fusion.4), channel_id=1, source_target_pairs={{0,32},{16,48},{32,64},{48,80},{64,96},{80,112},{96,128},{112,144}... | collective-permute-start | bytes 12296 | tf_op jit(solution)/shard_map/ppermute | solution.py:38
  36.4 0.7 copy-start.8
  37.7 0.6 copy-start.6
  39.8 34.7 %all-to-all-start = ((bf16[8,14,8,128]{3,2,1,0:T(8,128)(2,1)}), bf16[8,14,8,128]{3,2,1,0:T(8,128)(2,1)S(1)}, u32[]{:S(2)}, u32[]{:S(2)}) async-start(bf16[8,14,8,128]{3,2,1,0:T(8,128)(2,1)} %shard_map.64), calls=%async_computation | async-start | bytes 458752 | tf_op jit(solution)/shard_map/all_to_all | solution.py:226
  50.5 23.9 %collective-permute-start.7 = (bf16[512,256]{1,0:T(8,128)(2,1)S(1)}, bf16[512,256]{1,0:T(8,128)(2,1)S(1)}, u32[]{:S(2)}, u32[]{:S(2)}) collective-permute-start(bf16[512,256]{1,0:T(8,128)(2,1)S(1)} %collective-permute-done.5), channel_id=1, source_target_pairs={{0,72},{1,73},{4,76},{5,77},{8,2},{9,3},{12,6},{13,7},{16,88},{17,... | collective-permute-start | bytes 786440 | tf_op jit(solution)/shard_map/ppermute | solution.py:33
  70.7 15.2 %collective-permute-start.6 = (bf16[512,256]{1,0:T(8,128)(2,1)S(1)}, bf16[512,256]{1,0:T(8,128)(2,1)S(1)}, u32[]{:S(2)}, u32[]{:S(2)}) collective-permute-start(bf16[512,256]{1,0:T(8,128)(2,1)S(1)} %collective-permute-done.4), channel_id=1, source_target_pairs={{2,10},{3,11},{6,14},{7,15},{10,64},{11,65},{14,68},{15,69},{18,26... | collective-permute-start | bytes 786440 | tf_op jit(solution)/shard_map/ppermute | solution.py:33
  71.5 14.5 %copy-start.1 = (bf16[512,256]{1,0:T(8,128)(2,1)S(1)}, bf16[512,256]{1,0:T(8,128)(2,1)}, u32[]{:S(2)}) copy-start(bf16[512,256]{1,0:T(8,128)(2,1)} %param.11) | copy-start | bytes 786436
  74.5 12.5 %collective-permute-start.8 = (bf16[8,14,8,128]{3,2,1,0:T(8,128)(2,1)S(1)}, bf16[8,14,8,128]{3,2,1,0:T(8,128)(2,1)S(1)}, u32[]{:S(2)}, u32[]{:S(2)}) collective-permute-start(bf16[8,14,8,128]{3,2,1,0:T(8,128)(2,1)S(1)} %all-to-all-done.mine_ref), channel_id=1, source_target_pairs={{0,1},{1,0},{2,3},{3,2},{4,5},{5,4},{6,7},{7,6},{8,9},{9,8},{10,11... | collective-permute-start | bytes 688136 | tf_op jit(solution)/shard_map/ppermute | solution.py:33
  86.0 10.0 %copy-start = (bf16[128,512]{1,0:T(8,128)(2,1)S(1)}, bf16[128,512]{1,0:T(8,128)(2,1)}, u32[]{:S(2)}) copy-start(bf16[128,512]{1,0:T(8,128)(2,1)} %q_ref.1) | copy-start | bytes 393220
  87.0 36.2 %collective-permute-start.11 = (bf16[2,512,256]{2,1,0:T(8,128)(2,1)S(1)}, bf16[2,512,256]{2,1,0:T(8,128)(2,1)S(1)}, u32[]{:S(2)}, u32[]{:S(2)}) collective-permute-start(bf16[2,512,256]{2,1,0:T(8,128)(2,1)S(1)} %pad_maximum_fusion.refs_4_), channel_id=1, source_target_pairs={{0,256},{1,257},{2,258},{3,259},{4,260},{5,261},{6,262},{7,263},{8... | collective-permute-start | bytes 1572872 | tf_op jit(solution)/shard_map/ppermute | solution.py:33
  93.0 30.3 %collective-permute-start.10 = (bf16[2,512,256]{2,1,0:T(8,128)(2,1)S(1)}, bf16[2,512,256]{2,1,0:T(8,128)(2,1)S(1)}, u32[]{:S(2)}, u32[]{:S(2)}) collective-permute-start(bf16[2,512,256]{2,1,0:T(8,128)(2,1)S(1)} %pad_maximum_fusion.refs_4_), channel_id=1, source_target_pairs={{0,384},{1,385},{2,386},{3,387},{4,388},{5,389},{6,390},{7,391},{8... | collective-permute-start | bytes 1572872 | tf_op jit(solution)/shard_map/ppermute | solution.py:33
  110.9 21.0 %collective-permute-start.15 = (bf16[2,512,256]{2,1,0:T(8,128)(2,1)S(1)}, bf16[2,512,256]{2,1,0:T(8,128)(2,1)S(1)}, u32[]{:S(2)}, u32[]{:S(2)}) collective-permute-start(bf16[2,512,256]{2,1,0:T(8,128)(2,1)S(1)} %pad_maximum_fusion.refs_4_), channel_id=1, source_target_pairs={{0,128},{1,129},{2,130},{3,131},{4,132},{5,133},{6,134},{7,135},{8... | collective-permute-start | bytes 1572872 | tf_op jit(solution)/shard_map/ppermute | solution.py:33
  113.1 10.1 %collective-permute-start.9 = (bf16[128,512]{1,0:T(8,128)(2,1)S(1)}, bf16[128,512]{1,0:T(8,128)(2,1)S(1)}, u32[]{:S(2)}, u32[]{:S(2)}) collective-permute-start(bf16[128,512]{1,0:T(8,128)(2,1)S(1)} %shard_map.65), channel_id=1, source_target_pairs={{0,2},{1,3},{2,0},{3,1},{4,6},{5,7},{6,4},{7,5},{8,10},{9,11},{10,... | collective-permute-start | bytes 393224 | tf_op jit(solution)/shard_map/ppermute | solution.py:33
  123.3 14.7 %collective-permute-start.14 = (bf16[2,128,512]{2,1,0:T(8,128)(2,1)S(1)}, bf16[2,128,512]{2,1,0:T(8,128)(2,1)S(1)}, u32[]{:S(2)}, u32[]{:S(2)}) collective-permute-start(bf16[2,128,512]{2,1,0:T(8,128)(2,1)S(1)} %pad_maximum_fusion.1.refs_0_), channel_id=1, source_target_pairs={{0,16},{1,17},{2,18},{3,19},{4,20},{5,21},{6,22},{7,23},{8,24},{9,... | collective-permute-start | bytes 786440 | tf_op jit(solution)/shard_map/ppermute | solution.py:33
  125.3 12.7 %collective-permute-start.13 = (bf16[2,128,512]{2,1,0:T(8,128)(2,1)S(1)}, bf16[2,128,512]{2,1,0:T(8,128)(2,1)S(1)}, u32[]{:S(2)}, u32[]{:S(2)}) collective-permute-start(bf16[2,128,512]{2,1,0:T(8,128)(2,1)S(1)} %pad_maximum_fusion.1.refs_0_), channel_id=1, source_target_pairs={{0,32},{1,33},{2,34},{3,35},{4,36},{5,37},{6,38},{7,39},{8,40},{9,... | collective-permute-start | bytes 786440 | tf_op jit(solution)/shard_map/ppermute | solution.py:33
  127.2 13.9 %collective-permute-start.12 = (bf16[2,128,512]{2,1,0:T(8,128)(2,1)S(1)}, bf16[2,128,512]{2,1,0:T(8,128)(2,1)S(1)}, u32[]{:S(2)}, u32[]{:S(2)}) collective-permute-start(bf16[2,128,512]{2,1,0:T(8,128)(2,1)S(1)} %pad_maximum_fusion.1.refs_0_), channel_id=1, source_target_pairs={{0,48},{1,49},{2,50},{3,51},{4,52},{5,53},{6,54},{7,55},{8,56},{9,... | collective-permute-start | bytes 786440 | tf_op jit(solution)/shard_map/ppermute | solution.py:33
  143.0 5.5 %collective-permute-start.16 = (bf16[4,2,128,256]{3,2,1,0:T(8,128)(2,1)S(1)}, bf16[4,2,128,256]{3,2,1,0:T(8,128)(2,1)S(1)}, u32[]{:S(2)}, u32[]{:S(2)}) collective-permute-start(bf16[4,2,128,256]{3,2,1,0:T(8,128)(2,1)S(1)} %slice_bitcast_fusion), channel_id=1, source_target_pairs={{0,1},{1,0},{2,3},{3,2},{4,5},{5,4},{6,7},{7,6},{8,9},{9,8},{10,11... | collective-permute-start | bytes 1572872 | tf_op jit(solution)/shard_map/ppermute | solution.py:33
  148.7 17.9 %collective-permute-start.17 = (bf16[2,128,256]{2,1,0:T(8,128)(2,1)S(1)}, bf16[2,128,256]{2,1,0:T(8,128)(2,1)S(1)}, u32[]{:S(2)}, u32[]{:S(2)}) collective-permute-start(bf16[2,128,256]{2,1,0:T(8,128)(2,1)S(1)} %get-tuple-element.27), channel_id=1, source_target_pairs={{0,12},{1,13},{2,14},{3,15},{4,8},{5,9},{6,10},{7,11},{8,4},{9,5},... | collective-permute-start | bytes 393224 | tf_op jit(solution)/shard_map/ppermute | solution.py:33
  153.5 20.3 %collective-permute-start.19 = (bf16[2,128,256]{2,1,0:T(8,128)(2,1)S(1)}, bf16[2,128,256]{2,1,0:T(8,128)(2,1)S(1)}, u32[]{:S(2)}, u32[]{:S(2)}) collective-permute-start(bf16[2,128,256]{2,1,0:T(8,128)(2,1)S(1)} %get-tuple-element.28), channel_id=1, source_target_pairs={{0,4},{1,5},{2,6},{3,7},{4,0},{5,1},{6,2},{7,3},{8,12},{9,13},{10,... | collective-permute-start | bytes 393224 | tf_op jit(solution)/shard_map/ppermute | solution.py:33
  155.5 18.3 %collective-permute-start.18 = (bf16[2,128,256]{2,1,0:T(8,128)(2,1)S(1)}, bf16[2,128,256]{2,1,0:T(8,128)(2,1)S(1)}, u32[]{:S(2)}, u32[]{:S(2)}) collective-permute-start(bf16[2,128,256]{2,1,0:T(8,128)(2,1)S(1)} %get-tuple-element.29), channel_id=1, source_target_pairs={{0,8},{1,9},{2,10},{3,11},{4,12},{5,13},{6,14},{7,15},{8,0},{9,1},... | collective-permute-start | bytes 393224 | tf_op jit(solution)/shard_map/ppermute | solution.py:33
  173.9 6.8 %collective-permute-start.20 = (bf16[128,256]{1,0:T(8,128)(2,1)S(1)}, bf16[128,256]{1,0:T(8,128)(2,1)S(1)}, u32[]{:S(2)}, u32[]{:S(2)}) collective-permute-start(bf16[128,256]{1,0:T(8,128)(2,1)S(1)} %get-tuple-element.32), channel_id=1, source_target_pairs={{0,16},{1,48},{2,18},{3,50},{4,20},{5,52},{6,22},{7,54},{8,24},{9,... | collective-permute-start | bytes 196616 | tf_op jit(solution)/shard_map/ppermute | solution.py:33
  178.6 7.1 %collective-permute-start.21 = (bf16[128,256]{1,0:T(8,128)(2,1)S(1)}, bf16[128,256]{1,0:T(8,128)(2,1)S(1)}, u32[]{:S(2)}, u32[]{:S(2)}) collective-permute-start(bf16[128,256]{1,0:T(8,128)(2,1)S(1)} %get-tuple-element.33), channel_id=1, source_target_pairs={{0,0},{1,32},{2,2},{3,34},{4,4},{5,36},{6,6},{7,38},{8,8},{9,40},{... | collective-permute-start | bytes 196616 | tf_op jit(solution)/shard_map/ppermute | solution.py:33
  (1 other events, 0.6 us)

commit v12 on v11

--- a/solution.py
+++ b/solution.py
@@ -204,7 +204,7 @@
     second_up = {first_up[spot]: (spot + 8) % 16 for spot in first_up}
     stay = [spot for spot in range(16) if spot not in first_up]
     first_up.update({spot: spot ^ 1 for spot in stay})
-    first_down = {spot: (spot - (5 if spot < 8 else 4)) % 16 for spot in stay}
+    first_down = {spot: (spot - (5 if spot < 4 else 4)) % 16 for spot in stay}
     second_down = {first_down[spot]: (spot ^ 1) ^ 8 for spot in stay}
 
     def along(table):

time: 189 us -> 187 us (0.989)
  the two profiles are of different devices: /device:TPU:1 before, /device:TPU:33 now
where the time goes in v12:
time: 187 us; the launch traced here: 186 us
  starting transfers between devices  126 us (67%)
  waiting for transfers between devices  38 us (20%)
  Pallas kernels  18.1 us (10%)
  other arithmetic  1.9 us (1%)
    ppermute x18, starting transfers between devices, moved(): return lax.ppermute(value, BOTH, pairs)  98.6 us
    ppermute x18, waiting for transfers between devices, moved(): return lax.ppermute(value, BOTH, pairs)  37.3 us
    ppermute x4, starting transfers between devices, later(): lax.ppermute(value, 'seq', [(s, s + steps) for s in range(count - steps)])  22.9 us
    pallas_call x1, Pallas kernels, attention(): pl.pallas_call(functools.partial(attention_kernel, tokens=32), out_shape=...  14.8 us
    all_to_all x1, starting transfers between devices, per_device(): lax.all_to_all(mine, 'head', 0, 0, axis_index_groups=lines, tiled=True)  4.39 us
  transfers between devices with their start and end apart: 23, of which 12 were waited for; matrix products, arithmetic and copies ran while one was open for 1% of the time, Pallas kernels for 9%

profile of v12, /device:TPU:33, one launch (start us, length us, event | category | flops | bytes accessed | tf_op | source)
XLA Modules:
  0.0 185.8 jit_solution(10875317710055138632)
XLA Ops:
  0.0 2.0 %collective-permute-start.4 = (bf16[512,256]{1,0:T(8,128)(2,1)}, bf16[512,256]{1,0:T(8,128)(2,1)S(1)}, u32[]{:S(2)}, u32[]{:S(2)}) collective-permute-start(bf16[512,256]{1,0:T(8,128)(2,1)} %param.11), channel_id=1, source_target_pairs={{0,10},{1,11},{2,0},{3,1},{4,14},{5,15},{6,4},{7,5},{8,64},{9,65},... | collective-permute-start | bytes 786440 | tf_op jit(solution)/shard_map/ppermute | solution.py:33
  2.1 12.7 %collective-permute-start.5 = (bf16[512,256]{1,0:T(8,128)(2,1)}, bf16[512,256]{1,0:T(8,128)(2,1)S(1)}, u32[]{:S(2)}, u32[]{:S(2)}) collective-permute-start(bf16[512,256]{1,0:T(8,128)(2,1)} %param.11), channel_id=1, source_target_pairs={{2,72},{3,73},{6,76},{7,77},{10,2},{11,3},{14,6},{15,7},{18,88},{1... | collective-permute-start | bytes 786440 | tf_op jit(solution)/shard_map/ppermute | solution.py:33
  15.5 4.2 %collective-permute-start.3 = (bf16[2,8,128]{2,1,0:T(8,128)(2,1)S(1)}, bf16[2,8,128]{2,1,0:T(8,128)(2,1)S(1)}, u32[]{:S(2)}, u32[]{:S(2)}) collective-permute-start(bf16[2,8,128]{2,1,0:T(8,128)(2,1)S(1)} %pad_maximum_fusion.4), channel_id=1, source_target_pairs={{0,64},{16,80},{32,96},{48,112},{64,128},{80,144},{96,160},{112,17... | collective-permute-start | bytes 12296 | tf_op jit(solution)/shard_map/ppermute | solution.py:38
  19.8 3.2 %collective-permute-start = (bf16[4,8,128]{2,1,0:T(8,128)(2,1)S(1)}, bf16[4,8,128]{2,1,0:T(8,128)(2,1)S(1)}, u32[]{:S(2)}, u32[]{:S(2)}) collective-permute-start(bf16[4,8,128]{2,1,0:T(8,128)(2,1)S(1)} %pad_maximum_fusion.3), channel_id=1, source_target_pairs={{0,16},{16,32},{32,48},{48,64},{64,80},{80,96},{96,112},{112,128},... | collective-permute-start | bytes 24584 | tf_op jit(solution)/shard_map/ppermute | solution.py:38
  23.0 11.9 %collective-permute-start.2 = (bf16[2,8,128]{2,1,0:T(8,128)(2,1)S(1)}, bf16[2,8,128]{2,1,0:T(8,128)(2,1)S(1)}, u32[]{:S(2)}, u32[]{:S(2)}) collective-permute-start(bf16[2,8,128]{2,1,0:T(8,128)(2,1)S(1)} %pad_maximum_fusion.4), channel_id=1, source_target_pairs={{0,48},{16,64},{32,80},{48,96},{64,112},{80,128},{96,144},{112,160... | collective-permute-start | bytes 12296 | tf_op jit(solution)/shard_map/ppermute | solution.py:38
  35.0 3.6 %collective-permute-start.1 = (bf16[2,8,128]{2,1,0:T(8,128)(2,1)S(1)}, bf16[2,8,128]{2,1,0:T(8,128)(2,1)S(1)}, u32[]{:S(2)}, u32[]{:S(2)}) collective-permute-start(bf16[2,8,128]{2,1,0:T(8,128)(2,1)S(1)} %pad_maximum_fusion.4), channel_id=1, source_target_pairs={{0,32},{16,48},{32,64},{48,80},{64,96},{80,112},{96,128},{112,144}... | collective-permute-start | bytes 12296 | tf_op jit(solution)/shard_map/ppermute | solution.py:38
  42.0 4.4 %all-to-all-start = ((bf16[8,14,8,128]{3,2,1,0:T(8,128)(2,1)}), bf16[8,14,8,128]{3,2,1,0:T(8,128)(2,1)S(1)}, u32[]{:S(2)}, u32[]{:S(2)}) async-start(bf16[8,14,8,128]{3,2,1,0:T(8,128)(2,1)} %shard_map.64), calls=%async_computation | async-start | bytes 458752 | tf_op jit(solution)/shard_map/all_to_all | solution.py:226
  46.4 21.0 %collective-permute-start.7 = (bf16[512,256]{1,0:T(8,128)(2,1)S(1)}, bf16[512,256]{1,0:T(8,128)(2,1)S(1)}, u32[]{:S(2)}, u32[]{:S(2)}) collective-permute-start(bf16[512,256]{1,0:T(8,128)(2,1)S(1)} %collective-permute-done.5), channel_id=1, source_target_pairs={{2,72},{3,73},{6,76},{7,77},{8,2},{9,3},{12,6},{13,7},{18,88},{19,... | collective-permute-start | bytes 786440 | tf_op jit(solution)/shard_map/ppermute | solution.py:33
  67.4 1.9 %collective-permute-start.6 = (bf16[512,256]{1,0:T(8,128)(2,1)S(1)}, bf16[512,256]{1,0:T(8,128)(2,1)S(1)}, u32[]{:S(2)}, u32[]{:S(2)}) collective-permute-start(bf16[512,256]{1,0:T(8,128)(2,1)S(1)} %collective-permute-done.4), channel_id=1, source_target_pairs={{2,10},{3,11},{6,14},{7,15},{10,64},{11,65},{14,68},{15,69},{18,26... | collective-permute-start | bytes 786440 | tf_op jit(solution)/shard_map/ppermute | solution.py:33
  69.4 2.2 %collective-permute-done.7 = bf16[512,256]{1,0:T(8,128)(2,1)S(1)} collective-permute-done((bf16[512,256]{1,0:T(8,128)(2,1)S(1)}, bf16[512,256]{1,0:T(8,128)(2,1)S(1)}, u32[]{:S(2)}, u32[]{:S(2)}) %collective-permute-start.7) | collective-permute-done | bytes 262176 | tf_op jit(solution)/shard_map/ppermute | solution.py:33
  71.6 10.7 %collective-permute-start.8 = (bf16[8,14,8,128]{3,2,1,0:T(8,128)(2,1)S(1)}, bf16[8,14,8,128]{3,2,1,0:T(8,128)(2,1)S(1)}, u32[]{:S(2)}, u32[]{:S(2)}) collective-permute-start(bf16[8,14,8,128]{3,2,1,0:T(8,128)(2,1)S(1)} %all-to-all-done.mine_ref), channel_id=1, source_target_pairs={{0,1},{1,0},{2,3},{3,2},{4,5},{5,4},{6,7},{7,6},{8,9},{9,8},{10,11... | collective-permute-start | bytes 688136 | tf_op jit(solution)/shard_map/ppermute | solution.py:33
  83.5 9.5 %collective-permute-start.11 = (bf16[2,512,256]{2,1,0:T(8,128)(2,1)S(1)}, bf16[2,512,256]{2,1,0:T(8,128)(2,1)S(1)}, u32[]{:S(2)}, u32[]{:S(2)}) collective-permute-start(bf16[2,512,256]{2,1,0:T(8,128)(2,1)S(1)} %pad_maximum_fusion.refs_4_), channel_id=1, source_target_pairs={{0,256},{1,257},{2,258},{3,259},{4,260},{5,261},{6,262},{7,263},{8... | collective-permute-start | bytes 1572872 | tf_op jit(solution)/shard_map/ppermute | solution.py:33
  92.9 3.1 %collective-permute-start.10 = (bf16[2,512,256]{2,1,0:T(8,128)(2,1)S(1)}, bf16[2,512,256]{2,1,0:T(8,128)(2,1)S(1)}, u32[]{:S(2)}, u32[]{:S(2)}) collective-permute-start(bf16[2,512,256]{2,1,0:T(8,128)(2,1)S(1)} %pad_maximum_fusion.refs_4_), channel_id=1, source_target_pairs={{0,384},{1,385},{2,386},{3,387},{4,388},{5,389},{6,390},{7,391},{8... | collective-permute-start | bytes 1572872 | tf_op jit(solution)/shard_map/ppermute | solution.py:33
  96.0 14.8 %shard_map.65 = bf16[128,512]{1,0:T(8,128)(2,1)S(1)} custom-call(s32[2]{0:T(128)S(1)} %pad_add_fusion.1.place, bf16[128,512]{1,0:T(8,128)(2,1)S(1)} %copy-done, bf16[8,14,8,128]{3,2,1,0:T(8,128)(2,1)S(1)} %all-to-all-done.mine_ref, bf16[8,14,8,128]{3,2,1,0:T(8,128)(2,1)S(1)} %collective-permute-done.8.other_ref), custom_call_target="tpu_custom_call" | custom-call | flops 20000000000 | bytes 1048576 | tf_op jit(solution)/shard_map/pallas_call | solution.py:123
  110.9 2.2 %collective-permute-start.15 = (bf16[2,512,256]{2,1,0:T(8,128)(2,1)S(1)}, bf16[2,512,256]{2,1,0:T(8,128)(2,1)S(1)}, u32[]{:S(2)}, u32[]{:S(2)}) collective-permute-start(bf16[2,512,256]{2,1,0:T(8,128)(2,1)S(1)} %pad_maximum_fusion.refs_4_), channel_id=1, source_target_pairs={{0,128},{1,129},{2,130},{3,131},{4,132},{5,133},{6,134},{7,135},{8... | collective-permute-start | bytes 1572872 | tf_op jit(solution)/shard_map/ppermute | solution.py:33
  113.1 1.9 %collective-permute-start.9 = (bf16[128,512]{1,0:T(8,128)(2,1)S(1)}, bf16[128,512]{1,0:T(8,128)(2,1)S(1)}, u32[]{:S(2)}, u32[]{:S(2)}) collective-permute-start(bf16[128,512]{1,0:T(8,128)(2,1)S(1)} %shard_map.65), channel_id=1, source_target_pairs={{0,2},{1,3},{2,0},{3,1},{4,6},{5,7},{6,4},{7,5},{8,10},{9,11},{10,... | collective-permute-start | bytes 393224 | tf_op jit(solution)/shard_map/ppermute | solution.py:33
  115.0 4.1 %collective-permute-done.9 = bf16[128,512]{1,0:T(8,128)(2,1)S(1)} collective-permute-done((bf16[128,512]{1,0:T(8,128)(2,1)S(1)}, bf16[128,512]{1,0:T(8,128)(2,1)S(1)}, u32[]{:S(2)}, u32[]{:S(2)}) %collective-permute-start.9) | collective-permute-done | bytes 131104 | tf_op jit(solution)/shard_map/ppermute | solution.py:33
  119.1 1.9 %collective-permute-start.14 = (bf16[2,128,512]{2,1,0:T(8,128)(2,1)S(1)}, bf16[2,128,512]{2,1,0:T(8,128)(2,1)S(1)}, u32[]{:S(2)}, u32[]{:S(2)}) collective-permute-start(bf16[2,128,512]{2,1,0:T(8,128)(2,1)S(1)} %pad_maximum_fusion.1.refs_0_), channel_id=1, source_target_pairs={{0,16},{1,17},{2,18},{3,19},{4,20},{5,21},{6,22},{7,23},{8,24},{9,... | collective-permute-start | bytes 786440 | tf_op jit(solution)/shard_map/ppermute | solution.py:33
  121.1 1.9 %collective-permute-start.13 = (bf16[2,128,512]{2,1,0:T(8,128)(2,1)S(1)}, bf16[2,128,512]{2,1,0:T(8,128)(2,1)S(1)}, u32[]{:S(2)}, u32[]{:S(2)}) collective-permute-start(bf16[2,128,512]{2,1,0:T(8,128)(2,1)S(1)} %pad_maximum_fusion.1.refs_0_), channel_id=1, source_target_pairs={{0,32},{1,33},{2,34},{3,35},{4,36},{5,37},{6,38},{7,39},{8,40},{9,... | collective-permute-start | bytes 786440 | tf_op jit(solution)/shard_map/ppermute | solution.py:33
  123.0 4.6 %collective-permute-start.12 = (bf16[2,128,512]{2,1,0:T(8,128)(2,1)S(1)}, bf16[2,128,512]{2,1,0:T(8,128)(2,1)S(1)}, u32[]{:S(2)}, u32[]{:S(2)}) collective-permute-start(bf16[2,128,512]{2,1,0:T(8,128)(2,1)S(1)} %pad_maximum_fusion.1.refs_0_), channel_id=1, source_target_pairs={{0,48},{1,49},{2,50},{3,51},{4,52},{5,53},{6,54},{7,55},{8,56},{9,... | collective-permute-start | bytes 786440 | tf_op jit(solution)/shard_map/ppermute | solution.py:33
  127.7 3.3 %collective-permute-done.14.refs_3_ = bf16[2,128,512]{2,1,0:T(8,128)(2,1)S(1)} collective-permute-done((bf16[2,128,512]{2,1,0:T(8,128)(2,1)S(1)}, bf16[2,128,512]{2,1,0:T(8,128)(2,1)S(1)}, u32[]{:S(2)}, u32[]{:S(2)}) %collective-permute-start.14) | collective-permute-done | bytes 262176 | tf_op jit(solution)/shard_map/ppermute | solution.py:33
  131.0 4.6 %collective-permute-done.12.refs_1_ = bf16[2,128,512]{2,1,0:T(8,128)(2,1)S(1)} collective-permute-done((bf16[2,128,512]{2,1,0:T(8,128)(2,1)S(1)}, bf16[2,128,512]{2,1,0:T(8,128)(2,1)S(1)}, u32[]{:S(2)}, u32[]{:S(2)}) %collective-permute-start.12) | collective-permute-done | bytes 262176 | tf_op jit(solution)/shard_map/ppermute | solution.py:33
  137.5 5.4 %collective-permute-start.16 = (bf16[4,2,128,256]{3,2,1,0:T(8,128)(2,1)S(1)}, bf16[4,2,128,256]{3,2,1,0:T(8,128)(2,1)S(1)}, u32[]{:S(2)}, u32[]{:S(2)}) collective-permute-start(bf16[4,2,128,256]{3,2,1,0:T(8,128)(2,1)S(1)} %slice_bitcast_fusion), channel_id=1, source_target_pairs={{0,1},{1,0},{2,3},{3,2},{4,5},{5,4},{6,7},{7,6},{8,9},{9,8},{10,11... | collective-permute-start | bytes 1572872 | tf_op jit(solution)/shard_map/ppermute | solution.py:33
  144.5 5.8 %collective-permute-start.17 = (bf16[2,128,256]{2,1,0:T(8,128)(2,1)S(1)}, bf16[2,128,256]{2,1,0:T(8,128)(2,1)S(1)}, u32[]{:S(2)}, u32[]{:S(2)}) collective-permute-start(bf16[2,128,256]{2,1,0:T(8,128)(2,1)S(1)} %get-tuple-element.27), channel_id=1, source_target_pairs={{0,12},{1,13},{2,14},{3,15},{4,8},{5,9},{6,10},{7,11},{8,4},{9,5},... | collective-permute-start | bytes 393224 | tf_op jit(solution)/shard_map/ppermute | solution.py:33
  150.3 1.9 %collective-permute-start.19 = (bf16[2,128,256]{2,1,0:T(8,128)(2,1)S(1)}, bf16[2,128,256]{2,1,0:T(8,128)(2,1)S(1)}, u32[]{:S(2)}, u32[]{:S(2)}) collective-permute-start(bf16[2,128,256]{2,1,0:T(8,128)(2,1)S(1)} %get-tuple-element.28), channel_id=1, source_target_pairs={{0,4},{1,5},{2,6},{3,7},{4,0},{5,1},{6,2},{7,3},{8,12},{9,13},{10,... | collective-permute-start | bytes 393224 | tf_op jit(solution)/shard_map/ppermute | solution.py:33
  152.3 5.5 %collective-permute-start.18 = (bf16[2,128,256]{2,1,0:T(8,128)(2,1)S(1)}, bf16[2,128,256]{2,1,0:T(8,128)(2,1)S(1)}, u32[]{:S(2)}, u32[]{:S(2)}) collective-permute-start(bf16[2,128,256]{2,1,0:T(8,128)(2,1)S(1)} %get-tuple-element.29), channel_id=1, source_target_pairs={{0,8},{1,9},{2,10},{3,11},{4,12},{5,13},{6,14},{7,15},{8,0},{9,1},... | collective-permute-start | bytes 393224 | tf_op jit(solution)/shard_map/ppermute | solution.py:33
  157.8 4.1 %collective-permute-done.17 = bf16[2,128,256]{2,1,0:T(8,128)(2,1)S(1)} collective-permute-done((bf16[2,128,256]{2,1,0:T(8,128)(2,1)S(1)}, bf16[2,128,256]{2,1,0:T(8,128)(2,1)S(1)}, u32[]{:S(2)}, u32[]{:S(2)}) %collective-permute-start.17) | collective-permute-done | bytes 131104 | tf_op jit(solution)/shard_map/ppermute | solution.py:33
  161.8 3.5 %collective-permute-done.19 = bf16[2,128,256]{2,1,0:T(8,128)(2,1)S(1)} collective-permute-done((bf16[2,128,256]{2,1,0:T(8,128)(2,1)S(1)}, bf16[2,128,256]{2,1,0:T(8,128)(2,1)S(1)}, u32[]{:S(2)}, u32[]{:S(2)}) %collective-permute-start.19) | collective-permute-done | bytes 131104 | tf_op jit(solution)/shard_map/ppermute | solution.py:33
  165.4 7.9 %collective-permute-done.18 = bf16[2,128,256]{2,1,0:T(8,128)(2,1)S(1)} collective-permute-done((bf16[2,128,256]{2,1,0:T(8,128)(2,1)S(1)}, bf16[2,128,256]{2,1,0:T(8,128)(2,1)S(1)}, u32[]{:S(2)}, u32[]{:S(2)}) %collective-permute-start.18) | collective-permute-done | bytes 131104 | tf_op jit(solution)/shard_map/ppermute | solution.py:33
  173.3 4.7 %collective-permute-start.20 = (bf16[128,256]{1,0:T(8,128)(2,1)S(1)}, bf16[128,256]{1,0:T(8,128)(2,1)S(1)}, u32[]{:S(2)}, u32[]{:S(2)}) collective-permute-start(bf16[128,256]{1,0:T(8,128)(2,1)S(1)} %get-tuple-element.32), channel_id=1, source_target_pairs={{0,16},{1,48},{2,18},{3,50},{4,20},{5,52},{6,22},{7,54},{8,24},{9,... | collective-permute-start | bytes 196616 | tf_op jit(solution)/shard_map/ppermute | solution.py:33
  178.0 1.9 %collective-permute-start.21 = (bf16[128,256]{1,0:T(8,128)(2,1)S(1)}, bf16[128,256]{1,0:T(8,128)(2,1)S(1)}, u32[]{:S(2)}, u32[]{:S(2)}) collective-permute-start(bf16[128,256]{1,0:T(8,128)(2,1)S(1)} %get-tuple-element.33), channel_id=1, source_target_pairs={{0,0},{1,32},{2,2},{3,34},{4,4},{5,36},{6,6},{7,38},{8,8},{9,40},{... | collective-permute-start | bytes 196616 | tf_op jit(solution)/shard_map/ppermute | solution.py:33
  180.1 5.0 %collective-permute-done.21 = bf16[128,256]{1,0:T(8,128)(2,1)S(1)} collective-permute-done((bf16[128,256]{1,0:T(8,128)(2,1)S(1)}, bf16[128,256]{1,0:T(8,128)(2,1)S(1)}, u32[]{:S(2)}, u32[]{:S(2)}) %collective-permute-start.21) | collective-permute-done | bytes 65568 | tf_op jit(solution)/shard_map/ppermute | solution.py:33
  (52 shorter events, 9.9 us)
Async XLA Ops:
  0.0 14.8 %copy-start.2 = (bf16[8,128]{1,0:T(8,128)(2,1)S(1)}, bf16[8,128]{1,0:T(8,128)(2,1)}, u32[]{:S(2)}) copy-start(bf16[8,128]{1,0:T(8,128)(2,1)} %refs_0_.1) | copy-start | bytes 6148
  0.0 42.0 %collective-permute-start.4 = (bf16[512,256]{1,0:T(8,128)(2,1)}, bf16[512,256]{1,0:T(8,128)(2,1)S(1)}, u32[]{:S(2)}, u32[]{:S(2)}) collective-permute-start(bf16[512,256]{1,0:T(8,128)(2,1)} %param.11), channel_id=1, source_target_pairs={{0,10},{1,11},{2,0},{3,1},{4,14},{5,15},{6,4},{7,5},{8,64},{9,65},... | collective-permute-start | bytes 786440 | tf_op jit(solution)/shard_map/ppermute | solution.py:33
  2.1 39.9 %collective-permute-start.5 = (bf16[512,256]{1,0:T(8,128)(2,1)}, bf16[512,256]{1,0:T(8,128)(2,1)S(1)}, u32[]{:S(2)}, u32[]{:S(2)}) collective-permute-start(bf16[512,256]{1,0:T(8,128)(2,1)} %param.11), channel_id=1, source_target_pairs={{2,72},{3,73},{6,76},{7,77},{10,2},{11,3},{14,6},{15,7},{18,88},{1... | collective-permute-start | bytes 786440 | tf_op jit(solution)/shard_map/ppermute | solution.py:33
  14.8 5.0 %copy-start.4 = (bf16[8,128]{1,0:T(8,128)(2,1)S(1)}, bf16[8,128]{1,0:T(8,128)(2,1)}, u32[]{:S(2)}) copy-start(bf16[8,128]{1,0:T(8,128)(2,1)} %refs_2_.1) | copy-start | bytes 6148
  14.8 5.0 %copy-start.5 = (bf16[8,128]{1,0:T(8,128)(2,1)S(1)}, bf16[8,128]{1,0:T(8,128)(2,1)}, u32[]{:S(2)}) copy-start(bf16[8,128]{1,0:T(8,128)(2,1)} %refs_3_.1) | copy-start | bytes 6148
  15.5 4.3 %copy-start.3 = (bf16[8,128]{1,0:T(8,128)(2,1)S(1)}, bf16[8,128]{1,0:T(8,128)(2,1)}, u32[]{:S(2)}) copy-start(bf16[8,128]{1,0:T(8,128)(2,1)} %refs_1_.1) | copy-start | bytes 6148
  15.5 19.4 %collective-permute-start.3 = (bf16[2,8,128]{2,1,0:T(8,128)(2,1)S(1)}, bf16[2,8,128]{2,1,0:T(8,128)(2,1)S(1)}, u32[]{:S(2)}, u32[]{:S(2)}) collective-permute-start(bf16[2,8,128]{2,1,0:T(8,128)(2,1)S(1)} %pad_maximum_fusion.4), channel_id=1, source_target_pairs={{0,64},{16,80},{32,96},{48,112},{64,128},{80,144},{96,160},{112,17... | collective-permute-start | bytes 12296 | tf_op jit(solution)/shard_map/ppermute | solution.py:38
  19.8 19.5 %collective-permute-start = (bf16[4,8,128]{2,1,0:T(8,128)(2,1)S(1)}, bf16[4,8,128]{2,1,0:T(8,128)(2,1)S(1)}, u32[]{:S(2)}, u32[]{:S(2)}) collective-permute-start(bf16[4,8,128]{2,1,0:T(8,128)(2,1)S(1)} %pad_maximum_fusion.3), channel_id=1, source_target_pairs={{0,16},{16,32},{32,48},{48,64},{64,80},{80,96},{96,112},{112,128},... | collective-permute-start | bytes 24584 | tf_op jit(solution)/shard_map/ppermute | solution.py:38
  23.0 15.5 %collective-permute-start.2 = (bf16[2,8,128]{2,1,0:T(8,128)(2,1)S(1)}, bf16[2,8,128]{2,1,0:T(8,128)(2,1)S(1)}, u32[]{:S(2)}, u32[]{:S(2)}) collective-permute-start(bf16[2,8,128]{2,1,0:T(8,128)(2,1)S(1)} %pad_maximum_fusion.4), channel_id=1, source_target_pairs={{0,48},{16,64},{32,80},{48,96},{64,112},{80,128},{96,144},{112,160... | collective-permute-start | bytes 12296 | tf_op jit(solution)/shard_map/ppermute | solution.py:38
  34.9 4.4 %copy-start.7 = (bf16[2,8,128]{2,1,0:T(8,128)(2,1)}, bf16[2,8,128]{2,1,0:T(8,128)(2,1)S(1)}, u32[]{:S(2)}) copy-start(bf16[2,8,128]{2,1,0:T(8,128)(2,1)S(1)} %collective-permute-done.3.refs_7_) | copy-start | bytes 12292
  35.0 4.4 %collective-permute-start.1 = (bf16[2,8,128]{2,1,0:T(8,128)(2,1)S(1)}, bf16[2,8,128]{2,1,0:T(8,128)(2,1)S(1)}, u32[]{:S(2)}, u32[]{:S(2)}) collective-permute-start(bf16[2,8,128]{2,1,0:T(8,128)(2,1)S(1)} %pad_maximum_fusion.4), channel_id=1, source_target_pairs={{0,32},{16,48},{32,64},{48,80},{64,96},{80,112},{96,128},{112,144}... | collective-permute-start | bytes 12296 | tf_op jit(solution)/shard_map/ppermute | solution.py:38
  38.6 0.7 copy-start.8
  39.9 0.6 copy-start.6
  42.0 29.6 %all-to-all-start = ((bf16[8,14,8,128]{3,2,1,0:T(8,128)(2,1)}), bf16[8,14,8,128]{3,2,1,0:T(8,128)(2,1)S(1)}, u32[]{:S(2)}, u32[]{:S(2)}) async-start(bf16[8,14,8,128]{3,2,1,0:T(8,128)(2,1)} %shard_map.64), calls=%async_computation | async-start | bytes 458752 | tf_op jit(solution)/shard_map/all_to_all | solution.py:226
  46.4 25.2 %collective-permute-start.7 = (bf16[512,256]{1,0:T(8,128)(2,1)S(1)}, bf16[512,256]{1,0:T(8,128)(2,1)S(1)}, u32[]{:S(2)}, u32[]{:S(2)}) collective-permute-start(bf16[512,256]{1,0:T(8,128)(2,1)S(1)} %collective-permute-done.5), channel_id=1, source_target_pairs={{2,72},{3,73},{6,76},{7,77},{8,2},{9,3},{12,6},{13,7},{18,88},{19,... | collective-permute-start | bytes 786440 | tf_op jit(solution)/shard_map/ppermute | solution.py:33
  67.4 15.0 %collective-permute-start.6 = (bf16[512,256]{1,0:T(8,128)(2,1)S(1)}, bf16[512,256]{1,0:T(8,128)(2,1)S(1)}, u32[]{:S(2)}, u32[]{:S(2)}) collective-permute-start(bf16[512,256]{1,0:T(8,128)(2,1)S(1)} %collective-permute-done.4), channel_id=1, source_target_pairs={{2,10},{3,11},{6,14},{7,15},{10,64},{11,65},{14,68},{15,69},{18,26... | collective-permute-start | bytes 786440 | tf_op jit(solution)/shard_map/ppermute | solution.py:33
  69.4 13.0 %copy-start.1 = (bf16[512,256]{1,0:T(8,128)(2,1)S(1)}, bf16[512,256]{1,0:T(8,128)(2,1)}, u32[]{:S(2)}) copy-start(bf16[512,256]{1,0:T(8,128)(2,1)} %param.11) | copy-start | bytes 786436
  71.6 11.8 %collective-permute-start.8 = (bf16[8,14,8,128]{3,2,1,0:T(8,128)(2,1)S(1)}, bf16[8,14,8,128]{3,2,1,0:T(8,128)(2,1)S(1)}, u32[]{:S(2)}, u32[]{:S(2)}) collective-permute-start(bf16[8,14,8,128]{3,2,1,0:T(8,128)(2,1)S(1)} %all-to-all-done.mine_ref), channel_id=1, source_target_pairs={{0,1},{1,0},{2,3},{3,2},{4,5},{5,4},{6,7},{7,6},{8,9},{9,8},{10,11... | collective-permute-start | bytes 688136 | tf_op jit(solution)/shard_map/ppermute | solution.py:33
  82.4 13.6 %copy-start = (bf16[128,512]{1,0:T(8,128)(2,1)S(1)}, bf16[128,512]{1,0:T(8,128)(2,1)}, u32[]{:S(2)}) copy-start(bf16[128,512]{1,0:T(8,128)(2,1)} %q_ref.1) | copy-start | bytes 393220
  83.5 35.6 %collective-permute-start.11 = (bf16[2,512,256]{2,1,0:T(8,128)(2,1)S(1)}, bf16[2,512,256]{2,1,0:T(8,128)(2,1)S(1)}, u32[]{:S(2)}, u32[]{:S(2)}) collective-permute-start(bf16[2,512,256]{2,1,0:T(8,128)(2,1)S(1)} %pad_maximum_fusion.refs_4_), channel_id=1, source_target_pairs={{0,256},{1,257},{2,258},{3,259},{4,260},{5,261},{6,262},{7,263},{8... | collective-permute-start | bytes 1572872 | tf_op jit(solution)/shard_map/ppermute | solution.py:33
  92.9 26.2 %collective-permute-start.10 = (bf16[2,512,256]{2,1,0:T(8,128)(2,1)S(1)}, bf16[2,512,256]{2,1,0:T(8,128)(2,1)S(1)}, u32[]{:S(2)}, u32[]{:S(2)}) collective-permute-start(bf16[2,512,256]{2,1,0:T(8,128)(2,1)S(1)} %pad_maximum_fusion.refs_4_), channel_id=1, source_target_pairs={{0,384},{1,385},{2,386},{3,387},{4,388},{5,389},{6,390},{7,391},{8... | collective-permute-start | bytes 1572872 | tf_op jit(solution)/shard_map/ppermute | solution.py:33
  110.9 16.8 %collective-permute-start.15 = (bf16[2,512,256]{2,1,0:T(8,128)(2,1)S(1)}, bf16[2,512,256]{2,1,0:T(8,128)(2,1)S(1)}, u32[]{:S(2)}, u32[]{:S(2)}) collective-permute-start(bf16[2,512,256]{2,1,0:T(8,128)(2,1)S(1)} %pad_maximum_fusion.refs_4_), channel_id=1, source_target_pairs={{0,128},{1,129},{2,130},{3,131},{4,132},{5,133},{6,134},{7,135},{8... | collective-permute-start | bytes 1572872 | tf_op jit(solution)/shard_map/ppermute | solution.py:33
  113.1 6.0 %collective-permute-start.9 = (bf16[128,512]{1,0:T(8,128)(2,1)S(1)}, bf16[128,512]{1,0:T(8,128)(2,1)S(1)}, u32[]{:S(2)}, u32[]{:S(2)}) collective-permute-start(bf16[128,512]{1,0:T(8,128)(2,1)S(1)} %shard_map.65), channel_id=1, source_target_pairs={{0,2},{1,3},{2,0},{3,1},{4,6},{5,7},{6,4},{7,5},{8,10},{9,11},{10,... | collective-permute-start | bytes 393224 | tf_op jit(solution)/shard_map/ppermute | solution.py:33
  119.1 11.8 %collective-permute-start.14 = (bf16[2,128,512]{2,1,0:T(8,128)(2,1)S(1)}, bf16[2,128,512]{2,1,0:T(8,128)(2,1)S(1)}, u32[]{:S(2)}, u32[]{:S(2)}) collective-permute-start(bf16[2,128,512]{2,1,0:T(8,128)(2,1)S(1)} %pad_maximum_fusion.1.refs_0_), channel_id=1, source_target_pairs={{0,16},{1,17},{2,18},{3,19},{4,20},{5,21},{6,22},{7,23},{8,24},{9,... | collective-permute-start | bytes 786440 | tf_op jit(solution)/shard_map/ppermute | solution.py:33
  121.1 9.9 %collective-permute-start.13 = (bf16[2,128,512]{2,1,0:T(8,128)(2,1)S(1)}, bf16[2,128,512]{2,1,0:T(8,128)(2,1)S(1)}, u32[]{:S(2)}, u32[]{:S(2)}) collective-permute-start(bf16[2,128,512]{2,1,0:T(8,128)(2,1)S(1)} %pad_maximum_fusion.1.refs_0_), channel_id=1, source_target_pairs={{0,32},{1,33},{2,34},{3,35},{4,36},{5,37},{6,38},{7,39},{8,40},{9,... | collective-permute-start | bytes 786440 | tf_op jit(solution)/shard_map/ppermute | solution.py:33
  123.0 12.6 %collective-permute-start.12 = (bf16[2,128,512]{2,1,0:T(8,128)(2,1)S(1)}, bf16[2,128,512]{2,1,0:T(8,128)(2,1)S(1)}, u32[]{:S(2)}, u32[]{:S(2)}) collective-permute-start(bf16[2,128,512]{2,1,0:T(8,128)(2,1)S(1)} %pad_maximum_fusion.1.refs_0_), channel_id=1, source_target_pairs={{0,48},{1,49},{2,50},{3,51},{4,52},{5,53},{6,54},{7,55},{8,56},{9,... | collective-permute-start | bytes 786440 | tf_op jit(solution)/shard_map/ppermute | solution.py:33
  137.5 6.9 %collective-permute-start.16 = (bf16[4,2,128,256]{3,2,1,0:T(8,128)(2,1)S(1)}, bf16[4,2,128,256]{3,2,1,0:T(8,128)(2,1)S(1)}, u32[]{:S(2)}, u32[]{:S(2)}) collective-permute-start(bf16[4,2,128,256]{3,2,1,0:T(8,128)(2,1)S(1)} %slice_bitcast_fusion), channel_id=1, source_target_pairs={{0,1},{1,0},{2,3},{3,2},{4,5},{5,4},{6,7},{7,6},{8,9},{9,8},{10,11... | collective-permute-start | bytes 1572872 | tf_op jit(solution)/shard_map/ppermute | solution.py:33
  144.5 17.3 %collective-permute-start.17 = (bf16[2,128,256]{2,1,0:T(8,128)(2,1)S(1)}, bf16[2,128,256]{2,1,0:T(8,128)(2,1)S(1)}, u32[]{:S(2)}, u32[]{:S(2)}) collective-permute-start(bf16[2,128,256]{2,1,0:T(8,128)(2,1)S(1)} %get-tuple-element.27), channel_id=1, source_target_pairs={{0,12},{1,13},{2,14},{3,15},{4,8},{5,9},{6,10},{7,11},{8,4},{9,5},... | collective-permute-start | bytes 393224 | tf_op jit(solution)/shard_map/ppermute | solution.py:33
  150.3 15.0 %collective-permute-start.19 = (bf16[2,128,256]{2,1,0:T(8,128)(2,1)S(1)}, bf16[2,128,256]{2,1,0:T(8,128)(2,1)S(1)}, u32[]{:S(2)}, u32[]{:S(2)}) collective-permute-start(bf16[2,128,256]{2,1,0:T(8,128)(2,1)S(1)} %get-tuple-element.28), channel_id=1, source_target_pairs={{0,4},{1,5},{2,6},{3,7},{4,0},{5,1},{6,2},{7,3},{8,12},{9,13},{10,... | collective-permute-start | bytes 393224 | tf_op jit(solution)/shard_map/ppermute | solution.py:33
  152.3 21.0 %collective-permute-start.18 = (bf16[2,128,256]{2,1,0:T(8,128)(2,1)S(1)}, bf16[2,128,256]{2,1,0:T(8,128)(2,1)S(1)}, u32[]{:S(2)}, u32[]{:S(2)}) collective-permute-start(bf16[2,128,256]{2,1,0:T(8,128)(2,1)S(1)} %get-tuple-element.29), channel_id=1, source_target_pairs={{0,8},{1,9},{2,10},{3,11},{4,12},{5,13},{6,14},{7,15},{8,0},{9,1},... | collective-permute-start | bytes 393224 | tf_op jit(solution)/shard_map/ppermute | solution.py:33
  173.3 6.8 %collective-permute-start.20 = (bf16[128,256]{1,0:T(8,128)(2,1)S(1)}, bf16[128,256]{1,0:T(8,128)(2,1)S(1)}, u32[]{:S(2)}, u32[]{:S(2)}) collective-permute-start(bf16[128,256]{1,0:T(8,128)(2,1)S(1)} %get-tuple-element.32), channel_id=1, source_target_pairs={{0,16},{1,48},{2,18},{3,50},{4,20},{5,52},{6,22},{7,54},{8,24},{9,... | collective-permute-start | bytes 196616 | tf_op jit(solution)/shard_map/ppermute | solution.py:33
  178.0 7.1 %collective-permute-start.21 = (bf16[128,256]{1,0:T(8,128)(2,1)S(1)}, bf16[128,256]{1,0:T(8,128)(2,1)S(1)}, u32[]{:S(2)}, u32[]{:S(2)}) collective-permute-start(bf16[128,256]{1,0:T(8,128)(2,1)S(1)} %get-tuple-element.33), channel_id=1, source_target_pairs={{0,0},{1,32},{2,2},{3,34},{4,4},{5,36},{6,6},{7,38},{8,8},{9,40},{... | collective-permute-start | bytes 196616 | tf_op jit(solution)/shard_map/ppermute | solution.py:33
  (1 other events, 0.6 us)
